TPU v7x, 32 devices: a whole 2x2x4 slice. The times are simulated.
32 devices in a mesh: seq: 4 (over y, x), mem: 8 (over z, core).
Axes of the slice: x: 2, y: 2, z: 4, core: 2. Of those that a mesh axis runs over, the one named last changes fastest.
Arguments:
- query: bfloat16 [4096, 2048], P(('seq', 'mem')), may hold values from -64 to 64
- key: bfloat16 [4096, 2048], P(('seq', 'mem')), may hold values from -64 to 64
- value: bfloat16 [4096, 2048], P(('seq', 'mem')), may hold values from -6 to 6
- mem_key: bfloat16 [1024, 2048], P('mem'), may hold values from -6 to 6
- mem_value: bfloat16 [1024, 2048], P('mem'), may hold values from -6 to 6
- block_ids: int32 [512, 2], P(('seq', 'mem')), may hold values from 0 to 7, all different within a row; in each aligned block of 16 rows (0 to 15, 16 to 31, ...) at most 8 rows name the same one
- gate_logit: float32 [16], replicated, may hold values from -2 to 2
- d_out: bfloat16 [4096, 2048], P(('seq', 'mem')), may hold values from -16 to 16
Outputs:
- out: bfloat16 [4096, 2048], P(('seq', 'mem'))
- d_query: bfloat16 [4096, 2048], P(('seq', 'mem'))
- gate_grad: float32 [16], replicated
Inputs may be any that keep to these rules, and one draw needn't show every extreme that they name: `block_ids`: each row names 2 different memory blocks. Among the query groups of one device no block is named by more than 8 rows, and some device names some block exactly 8 times.
All inputs are finite; a program needn't handle non-finite values.
Results may differ from a plain program's by a relative error of at most 0.015.
Values may be sent and summed in bfloat16 or wider, within the bound.
No kernel may reach another device: no remote copies, remote signals or barrier semaphores. Data moves between devices by JAX's collectives and lax.ppermute only.
A program may use at most 64 MiB of HBM per device.

v0:
```python
import math

import jax
import jax.numpy as jnp
from jax import lax
from jax.sharding import PartitionSpec as P


def head_split(array, heads):
    return array.reshape(array.shape[0], heads, array.shape[1] // heads)


def body(query, key, value, mem_key, mem_value, block_ids, gate_logit, d_out):
    tok_rows, width = query.shape
    heads = gate_logit.shape[0]
    head_dim = width // heads
    softmax_scale = head_dim ** (-0.5)
    mem_devices = lax.axis_size("mem")
    groups, fetched = block_ids.shape
    group_rows = tok_rows // groups
    capacity = max(2, 2 * tok_rows * fetched // (group_rows * mem_devices))
    slot_count = mem_devices * capacity
    all_tokens = tok_rows * lax.axis_size("seq") * lax.axis_size("mem")
    gate_open = jax.nn.sigmoid(gate_logit)[None, :, None]
    q_heads = head_split(query, heads)
    k_heads = head_split(key, heads)
    v_heads = head_split(value, heads)
    grad_f = head_split(d_out, heads).astype(jnp.float32)
    local_scores = (
        jnp.einsum("qhd,khd->hqk", q_heads, k_heads, preferred_element_type=jnp.float32)
        * softmax_scale
    )
    row_index = lax.broadcasted_iota(jnp.int32, (tok_rows, tok_rows), 0)
    col_index = lax.broadcasted_iota(jnp.int32, (tok_rows, tok_rows), 1)
    local_scores = jnp.where((row_index >= col_index)[None], local_scores, -1e30)
    local_peak = jnp.max(local_scores, axis=-1, keepdims=True)
    local_exp = jnp.exp(local_scores - local_peak)
    local_prob = local_exp / jnp.sum(local_exp, axis=-1, keepdims=True)
    local_out = jnp.einsum(
        "hqk,khd->qhd", local_prob.astype(jnp.bfloat16), v_heads, preferred_element_type=jnp.float32
    )
    pair_owner = block_ids.reshape(groups * fetched)
    owner_hot = (pair_owner[:, None] == jnp.arange(mem_devices, dtype=jnp.int32)[None, :]).astype(
        jnp.int32
    )
    earlier = jnp.cumsum(owner_hot, axis=0) - owner_hot
    pair_slot = pair_owner * capacity + jnp.sum(earlier * owner_hot, axis=1)
    dispatch = (pair_slot[:, None] == jnp.arange(slot_count, dtype=jnp.int32)[None, :]).astype(
        jnp.float32
    )
    to_slots = jnp.transpose(jnp.sum(dispatch.reshape(groups, fetched, slot_count), axis=1))
    to_slots_half = to_slots.astype(jnp.bfloat16)
    dispatch_half = dispatch.astype(jnp.bfloat16)

    def place_rows(rows_half):
        placed = jnp.dot(to_slots_half, rows_half, preferred_element_type=jnp.float32)
        return placed.astype(jnp.bfloat16).reshape(mem_devices, capacity, rows_half.shape[1])

    mem_dout = (gate_open * grad_f).astype(jnp.bfloat16)
    dout_groups = mem_dout.reshape(groups, group_rows * width)
    query_groups = query.reshape(groups, group_rows * width)
    got_query = lax.all_to_all(
        place_rows(query_groups), "mem", split_axis=0, concat_axis=0, tiled=True
    )
    slot_query = got_query.reshape(slot_count, group_rows, heads, head_dim)
    mem_k_heads = head_split(mem_key, heads)
    mem_v_heads = head_split(mem_value, heads)
    mem_scores = (
        jnp.einsum("sqhd,khd->shqk", slot_query, mem_k_heads, preferred_element_type=jnp.float32)
        * softmax_scale
    )
    slot_peak = jnp.max(mem_scores, axis=-1, keepdims=True)
    slot_lse = slot_peak + jnp.log(jnp.sum(jnp.exp(mem_scores - slot_peak), axis=-1, keepdims=True))
    slot_weight = jnp.exp(mem_scores - slot_lse).astype(jnp.bfloat16)
    slot_out = jnp.einsum(
        "shqk,khd->sqhd", slot_weight, mem_v_heads, preferred_element_type=jnp.float32
    ).astype(jnp.bfloat16)
    slot_out_wire = slot_out.reshape(mem_devices, capacity, group_rows * width)
    slot_lse_wire = jnp.transpose(slot_lse[..., 0], (0, 2, 1)).reshape(
        mem_devices, capacity, group_rows * heads
    )
    back_out = lax.all_to_all(slot_out_wire, "mem", split_axis=0, concat_axis=0, tiled=True)
    back_lse = lax.all_to_all(slot_lse_wire, "mem", split_axis=0, concat_axis=0, tiled=True)
    pair_out = jnp.dot(
        dispatch_half,
        back_out.reshape(slot_count, group_rows * width),
        preferred_element_type=jnp.float32,
    )
    pair_lse = jnp.dot(
        dispatch, back_lse.reshape(slot_count, group_rows * heads), precision=lax.Precision.HIGHEST
    )
    pair_lse = pair_lse.reshape(groups, fetched, group_rows, heads)
    lse_peak = jnp.max(pair_lse, axis=1, keepdims=True)
    total_lse = lse_peak + jnp.log(jnp.sum(jnp.exp(pair_lse - lse_peak), axis=1, keepdims=True))
    pair_share = jnp.exp(pair_lse - total_lse)
    pair_view = pair_out.reshape(groups, fetched, group_rows, heads, head_dim)
    mem_out = jnp.sum(pair_share[..., None] * pair_view, axis=1).reshape(tok_rows, heads, head_dim)
    mixed = gate_open * mem_out + (1.0 - gate_open) * local_out
    out = mixed.astype(jnp.bfloat16).reshape(tok_rows, width)
    gate_term = (
        jnp.sum(grad_f * (mem_out - local_out), axis=(0, 2))
        * (gate_open * (1.0 - gate_open))[0, :, 0]
    )
    gate_grad = lax.psum(gate_term, ("seq", "mem")) / math.sqrt(all_tokens)
    local_dout = ((1.0 - gate_open) * grad_f).astype(jnp.bfloat16)
    local_delta = jnp.sum(local_dout.astype(jnp.float32) * local_out, axis=-1)
    local_dp = jnp.einsum("qhd,khd->hqk", local_dout, v_heads, preferred_element_type=jnp.float32)
    local_ds = (local_prob * (local_dp - jnp.transpose(local_delta)[:, :, None])).astype(
        jnp.bfloat16
    )
    local_dq = (
        jnp.einsum("hqk,khd->qhd", local_ds, k_heads, preferred_element_type=jnp.float32)
        * softmax_scale
    )
    mem_delta = jnp.sum(mem_dout.astype(jnp.float32) * mem_out, axis=-1)
    group_stats = jnp.stack([total_lse[:, 0], mem_delta.reshape(groups, group_rows, heads)], axis=1)
    group_stats = group_stats.reshape(groups, 2 * group_rows * heads)
    slot_stats = jnp.dot(to_slots, group_stats, precision=lax.Precision.HIGHEST).reshape(
        mem_devices, capacity, 2 * group_rows * heads
    )
    got_stats = lax.all_to_all(slot_stats, "mem", split_axis=0, concat_axis=0, tiled=True)
    got_grad = lax.all_to_all(
        place_rows(dout_groups), "mem", split_axis=0, concat_axis=0, tiled=True
    )
    slot_grad = got_grad.reshape(slot_count, group_rows, heads, head_dim)
    stats_view = got_stats.reshape(slot_count, 2, group_rows, heads)
    slot_total = jnp.transpose(stats_view[:, 0], (0, 2, 1))[..., None]
    slot_delta = jnp.transpose(stats_view[:, 1], (0, 2, 1))[..., None]
    slot_prob = jnp.exp(mem_scores - slot_total)
    slot_dp = jnp.einsum(
        "sqhd,khd->shqk", slot_grad, mem_v_heads, preferred_element_type=jnp.float32
    )
    slot_ds = (slot_prob * (slot_dp - slot_delta)).astype(jnp.bfloat16)
    slot_dq = (
        jnp.einsum("shqk,khd->sqhd", slot_ds, mem_k_heads, preferred_element_type=jnp.float32)
        * softmax_scale
    )
    slot_dq = slot_dq.astype(jnp.bfloat16).reshape(mem_devices, capacity, group_rows * width)
    back_dq = lax.all_to_all(slot_dq, "mem", split_axis=0, concat_axis=0, tiled=True)
    pair_dq = jnp.dot(
        dispatch_half,
        back_dq.reshape(slot_count, group_rows * width),
        preferred_element_type=jnp.float32,
    )
    mem_dq = jnp.sum(pair_dq.reshape(groups, fetched, group_rows * width), axis=1).reshape(
        tok_rows, width
    )
    d_query = (local_dq.reshape(tok_rows, width) + mem_dq).astype(jnp.bfloat16)
    return (out, d_query, gate_grad)


def solution(mesh):
    placed = (
        P(("seq", "mem"), None),
        P(("seq", "mem"), None),
        P(("seq", "mem"), None),
        P("mem", None),
        P("mem", None),
        P(("seq", "mem"), None),
        P(),
        P(("seq", "mem"), None),
    )
    return jax.shard_map(
        body,
        mesh=mesh,
        in_specs=placed,
        out_specs=(P(("seq", "mem"), None), P(("seq", "mem"), None), P()),
        check_vma=False,
    )
```

profile of v0, /device:TPU:0, one launch (start us, length us, event | category | flops | bytes accessed | tf_op | source)
XLA Modules:
  0.0 293.6 jit_solution(14479915250246480982)
XLA Ops:
  4.1 2.1 fusion.1
  6.2 6.3 %all-to-all-start = ((bf16[8,8,16384]{2,1,0:T(8,128)(2,1)}), bf16[8,8,16384]{2,1,0:T(8,128)(2,1)S(1)}, u32[]{:S(2)}, u32[]{:S(2)}) async-start(bf16[8,8,16384]{2,1,0:T(8,128)(2,1)} %fusion.1), calls=%async_computation | async-start | bytes 4194304 | tf_op jit(solution)/shard_map/all_to_all | solution.py:62
  13.7 2.1 copy.320
  15.8 45.8 %all-to-all-done = bf16[8,8,16384]{2,1,0:T(8,128)(2,1)S(1)} async-done(((bf16[8,8,16384]{2,1,0:T(8,128)(2,1)}), bf16[8,8,16384]{2,1,0:T(8,128)(2,1)S(1)}, u32[]{:S(2)}, u32[]{:S(2)}) %all-to-all-start) | async-done | bytes 2097184 | tf_op jit(solution)/shard_map/all_to_all | solution.py:62
  62.2 1.5 bitcast_reduce_fusion
  63.7 2.4 fusion.6
  67.2 3.3 %all-to-all-start.1 = ((f32[8,8,128]{2,1,0:T(8,128)}), f32[8,8,128]{2,1,0:T(8,128)S(1)}, u32[]{:S(2)}, u32[]{:S(2)}) async-start(f32[8,8,128]{2,1,0:T(8,128)} %reshape.221), calls=%async_computation.1 | async-start | bytes 65536 | tf_op jit(solution)/shard_map/all_to_all | solution.py:83
  70.6 3.1 %convert_bitcast_fusion = bf16[64,8,16,128]{3,1,0,2:T(8,128)(2,1)S(1)} fusion(f32[16,64,8,128]{3,2,1,0:T(8,128)} %copy-done.1, f32[64,16,8]{2,0,1:T(8,128)S(1)} %log_add_fusion, bf16[128,16,128,1]{2,1,0,3:T(8,128)(2,1)S(1)} %bitcast.219), kind=kOutput, calls=%fused_computation.30 | convolution fusion | flops 272629760 | bytes 6848512 | tf_op jit(solution)/shard_map/shqk,khd->sqhd/dot_general | solution.py:75
  73.7 2.4 copy.264
  76.2 2.3 reshape.224
  78.5 5.1 %all-to-all-start.2 = ((bf16[8,8,16384]{2,1,0:T(8,128)(2,1)}), bf16[8,8,16384]{2,1,0:T(8,128)(2,1)S(1)}, u32[]{:S(2)}, u32[]{:S(2)}) async-start(bf16[8,8,16384]{2,1,0:T(8,128)(2,1)} %reshape.224), calls=%async_computation.2 | async-start | bytes 4194304 | tf_op jit(solution)/shard_map/all_to_all | solution.py:82
  84.8 2.5 mul.129
  88.5 3.6 %fusion.2 = bf16[8,8,16384]{2,1,0:T(8,128)(2,1)} fusion(f32[16,16384]{1,0:T(8,128)} %mul.129, f32[16,16384]{1,0:T(8,128)} %reshape.241, f32[16,64]{1,0:T(8,128)S(1)} %convert_reduce_fusion), kind=kOutput, calls=%fused_computation.4 | convolution fusion | flops 34078720 | bytes 4198400 | tf_op jit(solution)/shard_map/dot_general | solution.py:56
  92.1 40.6 %all-to-all-done.2 = bf16[8,8,16384]{2,1,0:T(8,128)(2,1)S(1)} async-done(((bf16[8,8,16384]{2,1,0:T(8,128)(2,1)}), bf16[8,8,16384]{2,1,0:T(8,128)(2,1)S(1)}, u32[]{:S(2)}, u32[]{:S(2)}) %all-to-all-start.2) | async-done | bytes 2097184 | tf_op jit(solution)/shard_map/all_to_all | solution.py:82
  134.1 3.8 %all-to-all-start.4 = ((bf16[8,8,16384]{2,1,0:T(8,128)(2,1)}), bf16[8,8,16384]{2,1,0:T(8,128)(2,1)S(1)}, u32[]{:S(2)}, u32[]{:S(2)}) async-start(bf16[8,8,16384]{2,1,0:T(8,128)(2,1)} %fusion.2), calls=%async_computation.4 | async-start | bytes 4194304 | tf_op jit(solution)/shard_map/all_to_all | solution.py:122
  139.9 2.2 copy.321
  142.1 1.9 multiply_reduce_fusion
  146.8 39.8 %all-to-all-done.4 = bf16[8,8,16384]{2,1,0:T(8,128)(2,1)S(1)} async-done(((bf16[8,8,16384]{2,1,0:T(8,128)(2,1)}), bf16[8,8,16384]{2,1,0:T(8,128)(2,1)S(1)}, u32[]{:S(2)}, u32[]{:S(2)}) %all-to-all-start.4) | async-done | bytes 2097184 | tf_op jit(solution)/shard_map/all_to_all | solution.py:122
  186.7 3.3 %all-to-all-start.3 = ((f32[8,8,256]{2,1,0:T(8,128)}), f32[8,8,256]{2,1,0:T(8,128)S(1)}, u32[]{:S(2)}, u32[]{:S(2)}) async-start(f32[8,8,256]{2,1,0:T(8,128)} %fusion.57), calls=%async_computation.3 | async-start | bytes 131072 | tf_op jit(solution)/shard_map/all_to_all | solution.py:121
  190.0 1.9 copy.323
  191.9 3.9 %all-to-all-done.3 = f32[8,8,256]{2,1,0:T(8,128)S(1)} async-done(((f32[8,8,256]{2,1,0:T(8,128)}), f32[8,8,256]{2,1,0:T(8,128)S(1)}, u32[]{:S(2)}, u32[]{:S(2)}) %all-to-all-start.3) | async-done | bytes 65568 | tf_op jit(solution)/shard_map/all_to_all | solution.py:121
  197.2 6.0 %fusion.30 = bf16[64,8,16,128]{3,1,0,2:T(8,128)(2,1)} fusion(f32[16,64,8,128]{3,2,1,0:T(8,128)} %copy-done.1, bf16[64,8,16,128]{3,2,1,0:T(8,128)(2,1)} %bitcast.209, f32[64,16,8]{2,0,1:T(8,128)S(1)} %copy.287, f32[64,16,8]{2,0,1:T(8,128)S(1)} %copy.283, bf16[128,16,128,1]{2,1,0,3:T(8,128)(2,1)} %bitcast.218, bf16[128,16,128,1]{2,1,0,3:T(8,128)(2,1)S(1)} %bitcast.207), kind=kOutput, calls=%fused_computation.34 | convolution fusion | flops 544210944 | bytes 9502720 | tf_op jit(solution)/shard_map/shqk,khd->sqhd/dot_general | solution.py:135
  203.2 4.0 %copy.289 = bf16[64,8,16,128]{3,2,1,0:T(8,128)(2,1)S(1)} copy(bf16[64,8,16,128]{3,1,0,2:T(8,128)(2,1)} %fusion.30) | data formatting | bytes 4194304 | tf_op jit(solution)/shard_map/convert_element_type | solution.py:138
  207.2 2.3 reshape.236
  209.5 3.6 %all-to-all-start.5 = ((bf16[8,8,16384]{2,1,0:T(8,128)(2,1)}), bf16[8,8,16384]{2,1,0:T(8,128)(2,1)S(1)}, u32[]{:S(2)}, u32[]{:S(2)}) async-start(bf16[8,8,16384]{2,1,0:T(8,128)(2,1)} %reshape.236), calls=%async_computation.5 | async-start | bytes 4194304 | tf_op jit(solution)/shard_map/all_to_all | solution.py:139
  215.7 1.6 fusion.39
  220.0 2.6 copy.267
  222.6 4.1 %multiply_reduce_fusion.1 = (f32[16]{0:T(128)S(1)}, f32[128,16]{0,1:T(8,128)S(1)}, bf16[128,16,128]{0,2,1:T(8,128)(2,1)}) fusion(f32[128,16,128]{0,2,1:T(8,128)} %bitcast.213, f32[128,16,128]{0,2,1:T(8,128)} %copy.267, f32[128,2048]{0,1:T(8,128)} %copy.272, f32[16]{0:T(128)S(1)} %get-tuple-element.29, f32[16]{0:T(128)S(1)} %get-tuple-element.30, ...), kind=kOutput, calls=%fused_computation.48 | convolution fusion | flops 71041136 | bytes 5259456 | tf_op jit(solution)/shard_map/hqk,khd->qhd/dot_general | solution.py:39
  226.7 55.7 %psum.7 = f32[16]{0:T(128)S(1)} all-reduce(f32[16]{0:T(128)S(1)} %multiply_multiply_fusion), channel_id=1, replica_groups=mesh['seq'=4,'mem'=8] {'seq','mem'}, use_global_device_ids=true, to_apply=%region_14.15 | all-reduce | flops 16 | bytes 128 | tf_op jit(solution)/shard_map/psum | solution.py:104
  282.4 3.0 %convolution_multiply_fusion = f32[16,128,128]{1,2,0:T(8,128)} fusion(bf16[128,16,128]{0,2,1:T(8,128)(2,1)S(1)} %bitcast.212, f32[16,128]{1,0:T(8,128)S(1)} %bitcast.225, f32[16,128,128]{1,2,0:T(8,128)} %get-tuple-element.39, f32[16,128]{1,0:T(8,128)S(1)} %get-tuple-element.38, f32[16]{0:T(128)S(1)} %get-tuple-element.29, f32[128,2048]{0,1:T(8,128)} %copy.272, ...), kind=kOutput, calls=%fused_computation.38 | convolution fusion | flops 136052736 | bytes 4210752 | tf_op jit(solution)/shard_map/hqk,khd->qhd/dot_general | solution.py:112
  285.5 2.6 copy.290
  289.6 1.6 fusion.33
  (77 shorter events, 25.2 us)
Async XLA Ops:
  0.6 222.0 %copy-start = (bf16[128,2048]{1,0:T(8,128)(2,1)S(1)}, bf16[128,2048]{1,0:T(8,128)(2,1)}, u32[]{:S(2)}) copy-start(bf16[128,2048]{1,0:T(8,128)(2,1)} %param.10) | copy-start | bytes 1572868
  6.2 55.4 %all-to-all-start = ((bf16[8,8,16384]{2,1,0:T(8,128)(2,1)}), bf16[8,8,16384]{2,1,0:T(8,128)(2,1)S(1)}, u32[]{:S(2)}, u32[]{:S(2)}) async-start(bf16[8,8,16384]{2,1,0:T(8,128)(2,1)} %fusion.1), calls=%async_computation | async-start | bytes 4194304 | tf_op jit(solution)/shard_map/all_to_all | solution.py:62
  13.7 48.5 %copy-start.9 = (bf16[16,8,16,128]{3,2,1,0:T(8,128)(2,1)}, bf16[16,8,16,128]{3,2,1,0:T(8,128)(2,1)S(1)}, u32[]{:S(2)}) copy-start(bf16[16,8,16,128]{3,2,1,0:T(8,128)(2,1)S(1)} %copy.319) | copy-start | bytes 1572868
  63.7 2.4 copy-start.1
  66.1 4.5 %copy-start.11 = (bf16[16,8,16,128]{3,2,1,0:T(8,128)(2,1)S(1)}, bf16[16,8,16,128]{3,2,1,0:T(8,128)(2,1)}, u32[]{:S(2)}) copy-start(bf16[16,8,16,128]{3,2,1,0:T(8,128)(2,1)} %copy.320) | copy-start | bytes 1572868
  67.2 11.3 %all-to-all-start.1 = ((f32[8,8,128]{2,1,0:T(8,128)}), f32[8,8,128]{2,1,0:T(8,128)S(1)}, u32[]{:S(2)}, u32[]{:S(2)}) async-start(f32[8,8,128]{2,1,0:T(8,128)} %reshape.221), calls=%async_computation.1 | async-start | bytes 65536 | tf_op jit(solution)/shard_map/all_to_all | solution.py:83
  78.5 5.2 %copy-start.13 = (f32[16]{0:T(128)S(1)}, f32[16]{0:T(128)}, u32[]{:S(2)}) copy-start(f32[16]{0:T(128)} %param.14) | copy-start | bytes 196
  78.5 54.2 %all-to-all-start.2 = ((bf16[8,8,16384]{2,1,0:T(8,128)(2,1)}), bf16[8,8,16384]{2,1,0:T(8,128)(2,1)S(1)}, u32[]{:S(2)}, u32[]{:S(2)}) async-start(bf16[8,8,16384]{2,1,0:T(8,128)(2,1)} %reshape.224), calls=%async_computation.2 | async-start | bytes 4194304 | tf_op jit(solution)/shard_map/all_to_all | solution.py:82
  83.7 3.6 %copy-start.3 = (bf16[128,2048]{1,0:T(8,128)(2,1)S(1)}, bf16[128,2048]{1,0:T(8,128)(2,1)}, u32[]{:S(2)}) copy-start(bf16[128,2048]{1,0:T(8,128)(2,1)} %param.15) | copy-start | bytes 1572868
  132.7 1.3 copy-start.2
  134.1 52.6 %all-to-all-start.4 = ((bf16[8,8,16384]{2,1,0:T(8,128)(2,1)}), bf16[8,8,16384]{2,1,0:T(8,128)(2,1)S(1)}, u32[]{:S(2)}, u32[]{:S(2)}) async-start(bf16[8,8,16384]{2,1,0:T(8,128)(2,1)} %fusion.2), calls=%async_computation.4 | async-start | bytes 4194304 | tf_op jit(solution)/shard_map/all_to_all | solution.py:122
  142.1 3.0 %copy-start.6 = (f32[16,8,16,128]{3,2,1,0:T(8,128)S(1)}, f32[16,8,16,128]{3,2,1,0:T(8,128)}, u32[]{:S(2)}) copy-start(f32[16,8,16,128]{3,2,1,0:T(8,128)} %copy.371) | copy-start | bytes 3145732
  144.0 1.1 copy-start.4
  186.7 9.2 %all-to-all-start.3 = ((f32[8,8,256]{2,1,0:T(8,128)}), f32[8,8,256]{2,1,0:T(8,128)S(1)}, u32[]{:S(2)}, u32[]{:S(2)}) async-start(f32[8,8,256]{2,1,0:T(8,128)} %fusion.57), calls=%async_computation.3 | async-start | bytes 131072 | tf_op jit(solution)/shard_map/all_to_all | solution.py:121
  191.9 5.2 %copy-start.10 = (bf16[16,8,16,128]{3,2,1,0:T(8,128)(2,1)S(1)}, bf16[16,8,16,128]{3,2,1,0:T(8,128)(2,1)}, u32[]{:S(2)}) copy-start(bf16[16,8,16,128]{3,2,1,0:T(8,128)(2,1)} %copy-done.9) | copy-start | bytes 1572868
  209.5 80.1 %all-to-all-start.5 = ((bf16[8,8,16384]{2,1,0:T(8,128)(2,1)}), bf16[8,8,16384]{2,1,0:T(8,128)(2,1)S(1)}, u32[]{:S(2)}, u32[]{:S(2)}) async-start(bf16[8,8,16384]{2,1,0:T(8,128)(2,1)} %reshape.236), calls=%async_computation.5 | async-start | bytes 4194304 | tf_op jit(solution)/shard_map/all_to_all | solution.py:139
  215.7 3.0 %copy-start.5 = (f32[16,8,16,128]{3,0,2,1:T(8,128)S(1)}, f32[16,8,16,128]{3,0,2,1:T(8,128)}, u32[]{:S(2)}) copy-start(f32[16,8,16,128]{3,0,2,1:T(8,128)} %copy-done.4) | copy-start | bytes 3145732
  217.3 2.7 copy-start.8
  285.5 2.6 copy-start.12
  291.2 1.5 copy-start.7
where the time goes:
time: 295 us; the launch traced here: 294 us
  waiting for transfers between devices  130 us (44%)
  blocking collectives  55.7 us (19%)
  local copies, waits for them, and re-layouts  44.1 us (15%)
  matrix products  29.8 us (10%)
  starting transfers between devices  25.5 us (9%)
  other arithmetic  7.23 us (2%)
    psum x1, blocking collectives, body(): gate_grad = lax.psum(gate_term, ('seq', 'mem')) / math.sqrt(all_tokens)  55.7 us
    all_to_all x1, waiting for transfers between devices, body(): lax.all_to_all(place_rows(query_groups), 'mem', split_axis=0, concat_axis...  45.8 us
    all_to_all x1, waiting for transfers between devices, body(): lax.all_to_all(slot_out_wire, 'mem', split_axis=0, concat_axis=0, tiled=T...  40.6 us
    all_to_all x1, waiting for transfers between devices, body(): lax.all_to_all(place_rows(dout_groups), 'mem', split_axis=0, concat_axis=...  39.8 us
    unnamed x36, local copies, waits for them, and re-layouts  13.4 us
    all_to_all x1, starting transfers between devices, body(): lax.all_to_all(place_rows(query_groups), 'mem', split_axis=0, concat_axis...  6.32 us
    dot_general x1, matrix products, body(): jnp.einsum('shqk,khd->sqhd', slot_ds, mem_k_heads, preferred_element_type...  6 us
  transfers between devices with their start and end apart: 6, of which 4 were waited for; matrix products, arithmetic and copies ran while one was open for 17% of the time, Pallas kernels for 0%

commit v1 on v0

v1 whole, which is shorter than its diff:
```python
import functools
import math

import jax
import jax.numpy as jnp
from jax import lax
from jax.experimental import pallas as pl
from jax.experimental.pallas import tpu as pltpu
from jax.sharding import Mesh, PartitionSpec as P

HEAD_DIM = 128
PAIR = 2
CHUNK = PAIR * HEAD_DIM
TILE = 2
NEG = -1e30
LOG2E = math.log2(math.e)
MIB = 1024 * 1024
F32 = jnp.float32
BF16 = jnp.bfloat16
NT = (((1,), (1,)), ((), ()))
NN = (((1,), (0,)), ((), ()))
PLANE = ("sb", "core")
MEM = ("z", "core")
ALL = ("sa", "sb", "z", "core")


def dot(a, b, dims=NN):
    return lax.dot_general(a, b, dims, preferred_element_type=F32)


def head_cols(h):
    return slice(h * HEAD_DIM, (h + 1) * HEAD_DIM)


def chunk_columns(chunk):
    return pl.ds(pl.multiple_of(chunk * CHUNK, CHUNK), CHUNK)


def plane_index():
    return lax.axis_index("sb") * 2 + lax.axis_index("core")


def row_sums(x):
    high = x.astype(BF16)
    low = (x - high.astype(F32)).astype(BF16)
    return dot(jnp.concatenate([high, low], axis=1), jnp.ones((2 * HEAD_DIM, HEAD_DIM), BF16))


def prologue_kernel(
    blocks, mk_hbm, mv_hbm, q_hbm, g_hbm, ids_ref, both_ref, *refs
):
    *out_refs, mem_sems, in_sems = refs
    tok = q_hbm.shape[0]
    fetched, groups = ids_ref.shape
    chunk = plane_index()
    copies = [
        pltpu.make_async_copy(
            ref.at[:, chunk_columns(chunk ^ i)], both_ref.at[i, t], mem_sems.at[i, t]
        )
        for i in range(2)
        for t, ref in enumerate((mk_hbm, mv_hbm))
    ]
    for k, out_ref in enumerate(out_refs):
        for t, ref in enumerate((q_hbm, g_hbm)):
            span = slice(t * tok, (t + 1) * tok)
            copies.append(
                pltpu.make_async_copy(
                    ref.at[:, chunk_columns(chunk ^ k)], out_ref.at[span], in_sems.at[k, t]
                )
            )
    for copy in copies:
        copy.start()
    row = lax.broadcasted_iota(jnp.int32, (out_refs[0].shape[0] - 2 * tok, groups), 0)
    owner = lax.axis_index("z") * 2 + lax.axis_index("core")
    for core in range(2):
        hot = row >= blocks
        for t in range(fetched):
            hot = hot | (row == (ids_ref[t : t + 1, :] ^ owner ^ core))
        shun = jnp.where(hot, 0.0, 1.0).astype(BF16)
        for out_ref in out_refs[core::2]:
            out_ref[2 * tok :, :groups] = shun
    for copy in copies:
        copy.wait()


def local_forward_kernel(scale, q_ref, k_ref, v_ref, g_ref, out_ref, prob_ref, part_ref):
    tok = q_ref.shape[0]
    heads = part_ref.shape[1]
    row = lax.broadcasted_iota(jnp.int32, (tok, tok), 0)
    col = lax.broadcasted_iota(jnp.int32, (tok, tok), 1)
    causal = row >= col
    s = [dot(q_ref[:, head_cols(h)], k_ref[:, head_cols(h)], NT) for h in range(heads)]
    s = [jnp.where(causal, x, NEG) for x in s]
    e = [jnp.exp2((x - jnp.max(x, axis=1, keepdims=True)) * (scale * LOG2E)) for x in s]
    p = [x * (1.0 / row_sums(x)) for x in e]
    p = [x.astype(BF16) for x in p]
    for h in range(heads):
        cols = head_cols(h)
        o = dot(p[h], v_ref[:, cols])
        prob_ref[h] = p[h]
        out_ref[:, cols] = o
        part_ref[0, h : h + 1, :] = jnp.sum(g_ref[:, cols].astype(F32) * o, axis=0, keepdims=True)


def local_backward_kernel(scale, k_ref, v_ref, g_ref, gate_ref, out_ref, prob_ref, lo_ref, dq_ref):
    heads = prob_ref.shape[0]
    for h in range(heads):
        shut = 1.0 - gate_ref[:, head_cols(h)]
        lo_ref[:, head_cols(h)] = (shut * out_ref[:, head_cols(h)]).astype(BF16)
    dout = [
        ((1.0 - gate_ref[:, head_cols(h)]) * g_ref[:, head_cols(h)].astype(F32)).astype(BF16)
        for h in range(heads)
    ]
    delta = [row_sums(dout[h].astype(F32) * out_ref[:, head_cols(h)]) for h in range(heads)]
    dp = [dot(dout[h], v_ref[:, head_cols(h)], NT) for h in range(heads)]
    for h in range(heads):
        ds = (prob_ref[h].astype(F32) * (dp[h] - delta[h])).astype(BF16)
        dq_ref[:, head_cols(h)] = (dot(ds, k_ref[:, head_cols(h)]) * scale).astype(BF16)


def attend_kernel(scale, groups, peers, gate_ref, local_ref, *refs):
    *refs, k_all, v_all = refs
    got, mem_refs, back = refs[:peers], refs[peers:-peers], refs[-peers:]
    packet_rows = got[0].shape[0]
    blocks = len(mem_refs)
    rows = mem_refs[0].shape[2]
    heads = local_ref.shape[0]
    tok = (back[0].shape[0] - heads) // 2
    extra = packet_rows - 2 * tok
    chunk = plane_index()
    lane = lax.broadcasted_iota(jnp.int32, (rows, HEAD_DIM), 1)
    for h in range(PAIR):
        for b, ref in enumerate(mem_refs):
            span = slice(b * rows, (b + 1) * rows)
            k_all[h, span, :HEAD_DIM] = ref[b % 2, 0, :, head_cols(h)]
            k_all[h, span, HEAD_DIM:] = jnp.where(lane == b, NEG, 0.0).astype(BF16)
            v_all[h, span, :HEAD_DIM] = ref[b % 2, 1, :, head_cols(h)]
            v_all[h, span, HEAD_DIM:] = jnp.ones((rows, HEAD_DIM), BF16)
    spread = (
        lax.broadcasted_iota(jnp.int32, (tok, groups), 0) // (tok // groups)
        == lax.broadcasted_iota(jnp.int32, (tok, groups), 1)
    )
    spread = jnp.where(spread, 1.0, 0.0).astype(BF16)
    gates = gate_ref[:, chunk_columns(chunk)]
    pad = jnp.zeros((HEAD_DIM - extra, groups), BF16)

    def rows_of(first, start, cols):
        return jnp.concatenate(
            [got[first + t][start : start + tok, cols] for t in range(TILE)], axis=0
        )

    units = [(first, h) for first in range(0, peers, TILE) for h in range(PAIR)]
    shunned, scores, weights, parts = {}, {}, {}, [0.0] * PAIR
    for step in range(len(units) + 2):
        if step < len(units):
            first, h = units[step]
            if first not in shunned:
                shun = [
                    jnp.concatenate([got[first + t][2 * tok :, :groups], pad], axis=0)
                    for t in range(TILE)
                ]
                shunned[first] = jnp.concatenate(
                    [dot(spread, x, NT).astype(BF16) for x in shun], axis=0
                )
            q = jnp.concatenate([rows_of(first, 0, head_cols(h)), shunned[first]], axis=1)
            scores[step] = dot(q, k_all[h], NT)
        if 1 <= step <= len(units):
            u = step - 1
            first, h = units[u]
            gate = gates[:, head_cols(h)]
            s = scores.pop(u)
            peak = jnp.max(s, axis=1, keepdims=True)
            e = jnp.exp2((s - peak) * (scale * LOG2E)).astype(BF16)
            o = dot(e, v_all[h])
            inv = 1.0 / o[:, HEAD_DIM:]
            o = o[:, :HEAD_DIM] * inv
            g32 = rows_of(first, tok, head_cols(h)).astype(F32)
            dout = (gate * g32).astype(BF16)
            delta = row_sums(dout.astype(F32) * o)
            mixed = (gate * o).astype(BF16)
            for t in range(TILE):
                back[first + t][:tok, head_cols(h)] = mixed[t * tok : (t + 1) * tok]
            parts[h] = parts[h] + jnp.sum(g32 * o, axis=0, keepdims=True)
            weights[u] = (e, dout, delta, inv)
        if 2 <= step:
            u = step - 2
            first, h = units[u]
            e, dout, delta, inv = weights.pop(u)
            dp = dot(dout, v_all[h, :, :HEAD_DIM], NT)
            ds = (e.astype(F32) * (dp - jnp.concatenate([delta] * blocks, axis=1))).astype(BF16)
            dq = (dot(ds, k_all[h, :, :HEAD_DIM]) * (inv * scale)).astype(BF16)
            for t in range(TILE):
                back[first + t][tok : 2 * tok, head_cols(h)] = dq[t * tok : (t + 1) * tok]

    head = lax.broadcasted_iota(jnp.int32, (heads, HEAD_DIM), 0)
    total = -local_ref[...]
    for h in range(PAIR):
        total = total + jnp.where(head == chunk * PAIR + h, parts[h], 0.0)
    total = jnp.sum(total, axis=1, keepdims=True)
    high = total.astype(BF16).astype(F32)
    middle = (total - high).astype(BF16).astype(F32)
    low = total - high - middle
    lane = lax.broadcasted_iota(jnp.int32, (heads, CHUNK), 1)
    terms = jnp.where(lane == 0, high, jnp.where(lane == 1, middle, jnp.where(lane == 2, low, 0.0)))
    for ref in back:
        ref[2 * tok :, :] = terms.astype(BF16)


def merge_kernel(lo_ref, ldq_ref, *refs):
    *back_refs, out_ref, dq_ref = refs
    tok = lo_ref.shape[0]
    chunk = plane_index()
    for k, back_ref in enumerate(back_refs):
        cols = chunk_columns(chunk ^ k)
        for t, (ref, local_ref) in enumerate(((out_ref, lo_ref), (dq_ref, ldq_ref))):
            arrived = back_ref[t * tok : (t + 1) * tok].astype(F32)
            ref[:, cols] = (arrived + local_ref[:, cols].astype(F32)).astype(BF16)


def send_xor(array, axes, k):
    return lax.ppermute(array, axes, [(i, i ^ k) for i in range(lax.axis_size(axes))])


def spread_along(array, axis, ready):
    held = {0: array}
    step = lax.axis_size(axis) // 2
    while step:
        for k in sorted(held):
            source = held[k]
            if k and step == 1:
                source, held[1], ready = lax.optimization_barrier((source, held[1], ready))
            held[k + step] = send_xor(source, axis, step)
        step //= 2
    return held, ready


def exchange(arrays, axes):
    return [arrays[0]] + [send_xor(arrays[k], axes, k) for k in range(1, len(arrays))]


def sum_over(array, axis):
    arrived = [send_xor(array, axis, k) for k in range(1, lax.axis_size(axis))]
    return functools.reduce(jnp.add, arrived, array)


def body(query, key, value, mem_key, mem_value, block_ids, gate_logit, d_out):
    tok, width = query.shape
    heads = gate_logit.shape[0]
    scale = HEAD_DIM ** (-0.5)
    rows = mem_key.shape[0]
    groups = block_ids.shape[0]
    blocks = lax.axis_size(MEM)
    peers = width // CHUNK
    devices = lax.axis_size(ALL)

    params = pltpu.CompilerParams(vmem_limit_bytes=(6 + 5 * blocks // 4) * MIB)
    alone = pltpu.CompilerParams(vmem_limit_bytes=60 * MIB)
    hbm_spec = pl.BlockSpec(memory_space=pltpu.HBM)
    vmem_spec = pl.BlockSpec(memory_space=pltpu.VMEM)
    packet = jax.ShapeDtypeStruct((2 * tok + max(16, blocks), CHUNK), BF16)
    reply = jax.ShapeDtypeStruct((2 * tok + heads, CHUNK), BF16)
    both, *send = pl.pallas_call(
        functools.partial(prologue_kernel, blocks),
        out_shape=(jax.ShapeDtypeStruct((2, 2, rows, CHUNK), BF16),) + (packet,) * peers,
        in_specs=[hbm_spec] * 4 + [vmem_spec],
        out_specs=(vmem_spec,) * (peers + 1),
        scratch_shapes=[pltpu.SemaphoreType.DMA((2, 2)), pltpu.SemaphoreType.DMA((peers, 2))],
        compiler_params=alone,
        name="chunks",
    )(mem_key, mem_value, query, d_out, jnp.transpose(block_ids))
    got = exchange(send, PLANE)

    gate = jax.nn.sigmoid(gate_logit)
    gate_cols = jnp.repeat(gate, HEAD_DIM)[None, :]
    steps = 4
    step_heads = heads // steps
    col_spec = pl.BlockSpec((tok, step_heads * HEAD_DIM), lambda j: (0, j))
    prob_spec = pl.BlockSpec((step_heads, tok, tok), lambda j: (j, 0, 0))
    local_out, local_prob, local_part = pl.pallas_call(
        functools.partial(local_forward_kernel, scale),
        grid=(steps,),
        out_shape=(
            jax.ShapeDtypeStruct((tok, width), F32),
            jax.ShapeDtypeStruct((heads, tok, tok), BF16),
            jax.ShapeDtypeStruct((steps, step_heads, HEAD_DIM), F32),
        ),
        in_specs=[col_spec] * 4,
        out_specs=(
            col_spec,
            prob_spec,
            pl.BlockSpec((1, step_heads, HEAD_DIM), lambda j: (j, 0, 0)),
        ),
        compiler_params=params,
        cost_estimate=pl.CostEstimate(
            flops=4 * heads * tok * tok * HEAD_DIM, bytes_accessed=12 * tok * width,
            transcendentals=heads * tok * tok,
        ),
        name="local_forward",
    )(query, key, value, d_out)

    spread, (got[4:], local_part) = spread_along(both, "z", (got[4:], local_part))
    memory = []
    for k in range(blocks // 2):
        memory += [spread[k], send_xor(spread[k], "core", 1)]

    keys_shape = (PAIR, blocks * rows, CHUNK)
    send_back = pl.pallas_call(
        functools.partial(attend_kernel, scale, groups, peers),
        out_shape=(reply,) * peers,
        in_specs=[vmem_spec] * (2 + peers + blocks),
        out_specs=(vmem_spec,) * peers,
        scratch_shapes=[pltpu.VMEM(keys_shape, BF16), pltpu.VMEM(keys_shape, BF16)],
        compiler_params=params,
        cost_estimate=pl.CostEstimate(
            flops=8 * peers * tok * blocks * rows * CHUNK, bytes_accessed=10 * tok * width,
            transcendentals=heads * tok * blocks * rows,
        ),
        name="memory_attention",
    )(gate_cols, local_part.reshape(heads, HEAD_DIM), *got, *memory)
    whole = jax.ShapeDtypeStruct((tok, width), BF16)
    local_mix, local_dq = pl.pallas_call(
        functools.partial(local_backward_kernel, scale),
        grid=(steps,),
        out_shape=(whole, whole),
        in_specs=[col_spec] * 3
        + [pl.BlockSpec((1, step_heads * HEAD_DIM), lambda j: (0, j)), col_spec, prob_spec],
        out_specs=(col_spec, col_spec),
        compiler_params=params,
        cost_estimate=pl.CostEstimate(
            flops=4 * heads * tok * tok * HEAD_DIM, bytes_accessed=16 * tok * width,
            transcendentals=0,
        ),
        name="local_backward",
    )(key, value, d_out, gate_cols, local_out, local_prob)

    send_back = list(send_back)
    send_back[1], local_mix, local_dq = lax.optimization_barrier(
        (send_back[1], local_mix, local_dq)
    )
    back = exchange(send_back, PLANE)

    sums = functools.reduce(jnp.add, [x[2 * tok :, :HEAD_DIM].astype(F32) for x in back])
    sums = jnp.sum(sum_over(sum_over(sums, "z"), "sa")[:, :3], axis=1)
    gate_grad = sums * gate * (1.0 - gate) / math.sqrt(tok * devices)

    out, d_query = pl.pallas_call(
        merge_kernel,
        out_shape=(whole, whole),
        in_specs=[vmem_spec] * (2 + peers),
        out_specs=(vmem_spec, vmem_spec),
        compiler_params=params,
        name="merge",
    )(local_mix, local_dq, *back)
    return (out, d_query, gate_grad)


def solution(mesh):
    seq, mem = mesh.devices.shape
    sb = min(seq, 4)
    fine = Mesh(mesh.devices.reshape(seq // sb, sb, mem // 2, 2), ALL)
    tokens = P(ALL, None)
    blocks = P(MEM, None)
    return jax.shard_map(
        body,
        mesh=fine,
        in_specs=(tokens, tokens, tokens, blocks, blocks, tokens, P(), tokens),
        out_specs=(tokens, tokens, P()),
        check_vma=False,
    )
```

time: 295 us -> 69.2 us (0.23)
  waiting for transfers between devices: 130 us -> 23.4 us
  blocking collectives: 55.7 us -> 0 us
  local copies, waits for them, and re-layouts: 44.1 us -> 0.12 us
  matrix products: 29.8 us -> 0 us
  Pallas kernels: 0 us -> 17.2 us
  other arithmetic: 7.23 us -> 0.67 us
    all_to_all x6 -> x0, waiting for transfers between devices: 130 us -> none  [the longest x1 45.8 us: body(): lax.all_to_all(place_rows(query_groups), 'mem', split_axis=0, concat_axis...]
    psum x1 -> x0, blocking collectives: 55.7 us -> none  [body(): gate_grad = lax.psum(gate_term, ('seq', 'mem')) / math.sqrt(all_tokens)]
    dot_general x12 -> x0, matrix products: 29.8 us -> none  [the longest x1 6 us: body(): jnp.einsum('shqk,khd->sqhd', slot_ds, mem_k_heads, preferred_element_type...]
    ppermute x0 -> x24, starting transfers between devices: none -> 26.8 us  [send_xor(): lax.ppermute(array, axes, [(i, i ^ k) for i in range(lax.axis_size(axes))])]
    all_to_all x6 -> x0, starting transfers between devices: 25.5 us -> none  [the longest x1 6.32 us: body(): lax.all_to_all(place_rows(query_groups), 'mem', split_axis=0, concat_axis...]
    ppermute x0 -> x24, waiting for transfers between devices: none -> 23.4 us  [send_xor(): lax.ppermute(array, axes, [(i, i ^ k) for i in range(lax.axis_size(axes))])]
    pallas_call x0 -> x5, Pallas kernels: none -> 17.2 us  [the longest x1 7.83 us: body(): pl.pallas_call(functools.partial(attend_kernel, scale, groups, peers), ou...]
    reshape x10 -> x0, local copies, waits for them, and re-layouts: 15 us -> none  [the longest x1 2.6 us: body(): d_query = (local_dq.reshape(tok_rows, width) + mem_dq).astype(jnp.bfloat16)]
  transfers between devices with their start and end apart: 6 -> 24, of which waited for: 4 -> 7; matrix products, arithmetic and copies ran while one was open for 17% -> 0% of each run, Pallas kernels for 0% -> 9%
where the time goes in v1:
time: 69.2 us; the launch traced here: 69 us
  starting transfers between devices  26.8 us (39%)
  waiting for transfers between devices  23.4 us (34%)
  Pallas kernels  17.2 us (25%)
  between operations  0.78 us (1%)
    ppermute x24, starting transfers between devices, send_xor(): lax.ppermute(array, axes, [(i, i ^ k) for i in range(lax.axis_size(axes))])  26.8 us
    ppermute x24, waiting for transfers between devices, send_xor(): lax.ppermute(array, axes, [(i, i ^ k) for i in range(lax.axis_size(axes))])  23.4 us
    pallas_call x1, Pallas kernels, body(): pl.pallas_call(functools.partial(attend_kernel, scale, groups, peers), ou...  7.83 us
    pallas_call x1, Pallas kernels, body(): pl.pallas_call(functools.partial(prologue_kernel, blocks), out_shape=(jax...  3.44 us
    pallas_call x1, Pallas kernels, body(): pl.pallas_call(functools.partial(local_forward_kernel, scale), grid=(step...  2.61 us
    pallas_call x1, Pallas kernels, body(): pl.pallas_call(functools.partial(local_backward_kernel, scale), grid=(ste...  2.02 us
  transfers between devices with their start and end apart: 24, of which 7 were waited for; matrix products, arithmetic and copies ran while one was open for 0% of the time, Pallas kernels for 9%

profile of v1, /device:TPU:0, one launch (start us, length us, event | category | flops | bytes accessed | tf_op | source)
XLA Modules:
  0.0 69.0 jit_solution(6987168470009942904)
XLA Ops:
  0.7 3.4 %chunks.1 = (bf16[2,2,128,256]{3,2,1,0:T(8,128)(2,1)}, bf16[272,256]{1,0:T(8,128)(2,1)}, bf16[272,256]{1,0:T(8,128)(2,1)}, bf16[272,256]{1,0:T(8,128)(2,1)}, bf1...) custom-call(bf16[128,2048]{1,0:T(8,128)(2,1)} %mk_hbm.1, ...), custom_call_target="tpu_custom_call" | custom-call | tf_op jit(solution)/shard_map/chunks/pallas_call | solution.py:262
  4.1 3.0 %collective-permute-start.2 = (bf16[272,256]{1,0:T(8,128)(2,1)}, bf16[272,256]{1,0:T(8,128)(2,1)S(1)}, u32[]{:S(2)}, u32[]{:S(2)}) collective-permute-start(bf16[272,256]{1,0:T(8,128)(2,1)} %get-tuple-element.38), channel_id=1, source_target_pairs={{0,16},{1,17},{8,24},{9,25},{16,0},{17,1},{24,8},{25,9},{2,18},{3,... | collective-permute-start | bytes 417800 | tf_op jit(solution)/shard_map/ppermute | solution.py:221
  7.1 1.6 %collective-permute-start.1 = (bf16[2,2,128,256]{3,2,1,0:T(8,128)(2,1)}, bf16[2,2,128,256]{3,2,1,0:T(8,128)(2,1)S(1)}, u32[]{:S(2)}, u32[]{:S(2)}) collective-permute-start(bf16[2,2,128,256]{3,2,1,0:T(8,128)(2,1)} %get-tuple-element.37.refs_8_), channel_id=1, source_target_pairs={{0,2},{2,0},{4,6},{6,4},{1,3},{3,1},{5,7},{7,5},{8,10},{10,8},{12,... | collective-permute-start | bytes 786440 | tf_op jit(solution)/shard_map/ppermute | solution.py:221
  8.7 2.6 %collective-permute-start = (bf16[2,2,128,256]{3,2,1,0:T(8,128)(2,1)}, bf16[2,2,128,256]{3,2,1,0:T(8,128)(2,1)S(1)}, u32[]{:S(2)}, u32[]{:S(2)}) collective-permute-start(bf16[2,2,128,256]{3,2,1,0:T(8,128)(2,1)} %get-tuple-element.37.refs_8_), channel_id=1, source_target_pairs={{0,4},{2,6},{4,0},{6,2},{1,5},{3,7},{5,1},{7,3},{8,12},{10,14},{12... | collective-permute-start | bytes 786440 | tf_op jit(solution)/shard_map/ppermute | solution.py:221
  11.3 1.6 %collective-permute-start.4 = (bf16[272,256]{1,0:T(8,128)(2,1)}, bf16[272,256]{1,0:T(8,128)(2,1)S(1)}, u32[]{:S(2)}, u32[]{:S(2)}) collective-permute-start(bf16[272,256]{1,0:T(8,128)(2,1)} %get-tuple-element.40), channel_id=1, source_target_pairs={{0,24},{1,25},{8,16},{9,17},{16,8},{17,9},{24,0},{25,1},{2,26},{3,... | collective-permute-start | bytes 417800 | tf_op jit(solution)/shard_map/ppermute | solution.py:221
  12.9 1.4 %collective-permute-start.5 = (bf16[272,256]{1,0:T(8,128)(2,1)}, bf16[272,256]{1,0:T(8,128)(2,1)S(1)}, u32[]{:S(2)}, u32[]{:S(2)}) collective-permute-start(bf16[272,256]{1,0:T(8,128)(2,1)} %get-tuple-element.41), channel_id=1, source_target_pairs={{0,25},{1,24},{8,17},{9,16},{16,9},{17,8},{24,1},{25,0},{2,27},{3,... | collective-permute-start | bytes 417800 | tf_op jit(solution)/shard_map/ppermute | solution.py:221
  14.3 2.6 %local_forward.1 = (f32[128,2048]{1,0:T(8,128)S(1)}, bf16[16,128,128]{2,1,0:T(8,128)(2,1)S(1)}, f32[4,4,128]{2,1,0:T(4,128)S(1)}) custom-call(bf16[128,2048]{1,0:T(8,128)(2,1)S(1)} %copy-done.1, bf16[128,2048]{1,0:T(8,128)(2,1)S(1)} %copy-done.2, bf16[128,2048]{1,0:T(8,128)(2,1)S(1)} %copy-done.3, bf16[128,2048]{1,0:T(8,128)(2,1)S(1)} %copy-done), custom_call_target="tpu_custom_call" | custom-call | flops 134217728 | bytes 3145728 | tf_op jit(solution)/shard_map/local_forward/pallas_call | solution.py:279
  16.9 5.7 %collective-permute-done.3.refs_5_ = bf16[272,256]{1,0:T(8,128)(2,1)S(1)} collective-permute-done((bf16[272,256]{1,0:T(8,128)(2,1)}, bf16[272,256]{1,0:T(8,128)(2,1)S(1)}, u32[]{:S(2)}, u32[]{:S(2)}) %collective-permute-start.3) | collective-permute-done | bytes 139296 | tf_op jit(solution)/shard_map/ppermute | solution.py:221
  22.7 0.3 collective-permute-done.refs_12_
  23.0 0.4 collective-permute-start.12
  23.5 1.6 %collective-permute-start.7 = (bf16[272,256]{1,0:T(8,128)(2,1)S(1)}, bf16[272,256]{1,0:T(8,128)(2,1)S(1)}, u32[]{:S(2)}, u32[]{:S(2)}) collective-permute-start(bf16[272,256]{1,0:T(8,128)(2,1)S(1)} %copy-done.7), channel_id=1, source_target_pairs={{0,8},{1,9},{8,0},{9,1},{16,24},{17,25},{24,16},{25,17},{2,10},{3,... | collective-permute-start | bytes 417800 | tf_op jit(solution)/shard_map/ppermute | solution.py:221
  25.0 0.2 collective-permute-start.9
  25.2 0.3 collective-permute-start.10
  25.5 0.2 collective-permute-start.11
  25.7 4.6 %collective-permute-done.12.refs_14_ = bf16[2,2,128,256]{3,2,1,0:T(8,128)(2,1)S(1)} collective-permute-done((bf16[2,2,128,256]{3,2,1,0:T(8,128)(2,1)S(1)}, bf16[2,2,128,256]{3,2,1,0:T(8,128)(2,1)S(1)}, u32[]{:S(2)}, u32[]{:S(2)}) %collective-permute-start.12) | collective-permute-done | bytes 262176 | tf_op jit(solution)/shard_map/ppermute | solution.py:221
  30.3 1.6 %collective-permute-start.8 = (bf16[272,256]{1,0:T(8,128)(2,1)S(1)}, bf16[272,256]{1,0:T(8,128)(2,1)S(1)}, u32[]{:S(2)}, u32[]{:S(2)}) collective-permute-start(bf16[272,256]{1,0:T(8,128)(2,1)S(1)} %copy-done.6), channel_id=1, source_target_pairs={{0,9},{1,8},{8,1},{9,0},{16,25},{17,24},{24,17},{25,16},{2,11},{3,... | collective-permute-start | bytes 417800 | tf_op jit(solution)/shard_map/ppermute | solution.py:221
  32.0 2.0 %local_backward.1 = (bf16[128,2048]{1,0:T(8,128)(2,1)S(1)}, bf16[128,2048]{1,0:T(8,128)(2,1)S(1)}) custom-call(bf16[128,2048]{1,0:T(8,128)(2,1)S(1)} %copy-done.2, bf16[128,2048]{1,0:T(8,128)(2,1)S(1)} %copy-done.3, bf16[128,2048]{1,0:T(8,128)(2,1)S(1)} %copy-done, f32[1,2048]{1,0:T(1,128)S(1)} %bitcast.3, f32[128,2048]{1,0:T(8,128)S(1)} %get-tuple-element.55.out_ref, ...), custom_call_target="tpu_custom_call" | custom-call | flops 134217728 | bytes 4194304 | tf_op jit(solution)/shard_map/local_backward/pallas_call | solution.py:321
  34.0 1.8 %collective-permute-done.8.refs_3_ = bf16[272,256]{1,0:T(8,128)(2,1)S(1)} collective-permute-done((bf16[272,256]{1,0:T(8,128)(2,1)S(1)}, bf16[272,256]{1,0:T(8,128)(2,1)S(1)}, u32[]{:S(2)}, u32[]{:S(2)}) %collective-permute-start.8) | collective-permute-done | bytes 139296 | tf_op jit(solution)/shard_map/ppermute | solution.py:221
  35.8 7.8 %memory_attention.1 = (bf16[272,256]{1,0:T(8,128)(2,1)S(1)}, bf16[272,256]{1,0:T(8,128)(2,1)S(1)}, bf16[272,256]{1,0:T(8,128)(2,1)S(1)}, bf16[272,256]{1,0:T(8,1...) custom-call(f32[1,2048]{1,0:T(1,128)S(1)} %bitcast.4, ...), custom_call_target="tpu_custom_call" | custom-call | flops 2147483648 | bytes 2621440 | tf_op jit(solution)/shard_map/memory_attention/pallas_call | solution.py:307
  43.6 0.5 collective-permute-start.14
  44.1 1.5 %collective-permute-start.15 = (bf16[272,256]{1,0:T(8,128)(2,1)S(1)}, bf16[272,256]{1,0:T(8,128)(2,1)S(1)}, u32[]{:S(2)}, u32[]{:S(2)}) collective-permute-start(bf16[272,256]{1,0:T(8,128)(2,1)S(1)} %get-tuple-element.63), channel_id=1, source_target_pairs={{0,8},{1,9},{8,0},{9,1},{16,24},{17,25},{24,16},{25,17},{2,10},{3,... | collective-permute-start | bytes 417800 | tf_op jit(solution)/shard_map/ppermute | solution.py:221
  45.6 2.1 %collective-permute-start.17 = (bf16[272,256]{1,0:T(8,128)(2,1)S(1)}, bf16[272,256]{1,0:T(8,128)(2,1)S(1)}, u32[]{:S(2)}, u32[]{:S(2)}) collective-permute-start(bf16[272,256]{1,0:T(8,128)(2,1)S(1)} %get-tuple-element.65), channel_id=1, source_target_pairs={{0,16},{1,17},{8,24},{9,25},{16,0},{17,1},{24,8},{25,9},{2,18},{3,... | collective-permute-start | bytes 417800 | tf_op jit(solution)/shard_map/ppermute | solution.py:221
  47.6 0.3 collective-permute-start.18
  47.9 2.7 %collective-permute-start.19 = (bf16[272,256]{1,0:T(8,128)(2,1)S(1)}, bf16[272,256]{1,0:T(8,128)(2,1)S(1)}, u32[]{:S(2)}, u32[]{:S(2)}) collective-permute-start(bf16[272,256]{1,0:T(8,128)(2,1)S(1)} %get-tuple-element.67), channel_id=1, source_target_pairs={{0,24},{1,25},{8,16},{9,17},{16,8},{17,9},{24,0},{25,1},{2,26},{3,... | collective-permute-start | bytes 417800 | tf_op jit(solution)/shard_map/ppermute | solution.py:221
  50.6 1.0 %collective-permute-start.20 = (bf16[272,256]{1,0:T(8,128)(2,1)S(1)}, bf16[272,256]{1,0:T(8,128)(2,1)S(1)}, u32[]{:S(2)}, u32[]{:S(2)}) collective-permute-start(bf16[272,256]{1,0:T(8,128)(2,1)S(1)} %get-tuple-element.68), channel_id=1, source_target_pairs={{0,25},{1,24},{8,17},{9,16},{16,9},{17,8},{24,1},{25,0},{2,27},{3,... | collective-permute-start | bytes 417800 | tf_op jit(solution)/shard_map/ppermute | solution.py:221
  51.6 1.0 %collective-permute-done.16.refs_3_ = bf16[272,256]{1,0:T(8,128)(2,1)S(1)} collective-permute-done((bf16[272,256]{1,0:T(8,128)(2,1)S(1)}, bf16[272,256]{1,0:T(8,128)(2,1)S(1)}, u32[]{:S(2)}, u32[]{:S(2)}) %collective-permute-start.16) | collective-permute-done | bytes 139296 | tf_op jit(solution)/shard_map/ppermute | solution.py:221
  52.6 8.4 %collective-permute-done.18.refs_5_ = bf16[272,256]{1,0:T(8,128)(2,1)S(1)} collective-permute-done((bf16[272,256]{1,0:T(8,128)(2,1)S(1)}, bf16[272,256]{1,0:T(8,128)(2,1)S(1)}, u32[]{:S(2)}, u32[]{:S(2)}) %collective-permute-start.18) | collective-permute-done | bytes 139296 | tf_op jit(solution)/shard_map/ppermute | solution.py:221
  61.0 2.8 %collective-permute-start.23 = (f32[16,128]{1,0:T(8,128)S(1)}, f32[16,128]{1,0:T(8,128)S(1)}, u32[]{:S(2)}, u32[]{:S(2)}) collective-permute-start(f32[16,128]{1,0:T(8,128)S(1)} %convert_add_fusion), channel_id=1, source_target_pairs={{0,6},{2,4},{4,2},{6,0},{1,7},{3,5},{5,3},{7,1},{8,14},{10,12},{12... | collective-permute-start | bytes 24584 | tf_op jit(solution)/shard_map/ppermute | solution.py:221
  63.8 1.7 %collective-permute-start.21 = (f32[16,128]{1,0:T(8,128)S(1)}, f32[16,128]{1,0:T(8,128)S(1)}, u32[]{:S(2)}, u32[]{:S(2)}) collective-permute-start(f32[16,128]{1,0:T(8,128)S(1)} %convert_add_fusion), channel_id=1, source_target_pairs={{0,2},{2,0},{4,6},{6,4},{1,3},{3,1},{5,7},{7,5},{8,10},{10,8},{12,... | collective-permute-start | bytes 24584 | tf_op jit(solution)/shard_map/ppermute | solution.py:221
  65.4 1.3 %merge.1 = (bf16[128,2048]{1,0:T(8,128)(2,1)}, bf16[128,2048]{1,0:T(8,128)(2,1)}) custom-call(bf16[128,2048]{1,0:T(8,128)(2,1)S(1)} %get-tuple-element.59.lo_ref, bf16[128,2048]{1,0:T(8,128)(2,1)S(1)} %get-tuple-element.60.ldq_ref, bf16[272,256]{1,0:T(8,128)(2,1)S(1)} %get-tuple-element.61.refs_0_, bf16[272,256]{1,0:T(8,128)(2,1)S(1)} %collective-permute-done.14.refs_1_, ...), custom_call_target="tpu_custom_call" | custom-call | tf_op jit(solution)/shard_map/merge/pallas_call | solution.py:346
  66.7 1.6 %collective-permute-done.22 = f32[16,128]{1,0:T(8,128)S(1)} collective-permute-done((f32[16,128]{1,0:T(8,128)S(1)}, f32[16,128]{1,0:T(8,128)S(1)}, u32[]{:S(2)}, u32[]{:S(2)}) %collective-permute-start.22) | collective-permute-done | bytes 8224 | tf_op jit(solution)/shard_map/ppermute | solution.py:221
  68.4 0.5 multiply_multiply_fusion
  (46 shorter events, 0.3 us)
Async XLA Ops:
  0.6 13.6 %copy-start = (bf16[128,2048]{1,0:T(8,128)(2,1)S(1)}, bf16[128,2048]{1,0:T(8,128)(2,1)}, u32[]{:S(2)}) copy-start(bf16[128,2048]{1,0:T(8,128)(2,1)} %g_ref.3) | copy-start | bytes 1572868
  0.6 13.6 %copy-start.1 = (bf16[128,2048]{1,0:T(8,128)(2,1)S(1)}, bf16[128,2048]{1,0:T(8,128)(2,1)}, u32[]{:S(2)}) copy-start(bf16[128,2048]{1,0:T(8,128)(2,1)} %q_ref.1) | copy-start | bytes 1572868
  0.7 13.6 %copy-start.2 = (bf16[128,2048]{1,0:T(8,128)(2,1)S(1)}, bf16[128,2048]{1,0:T(8,128)(2,1)}, u32[]{:S(2)}) copy-start(bf16[128,2048]{1,0:T(8,128)(2,1)} %k_ref.3) | copy-start | bytes 1572868
  0.7 13.6 %copy-start.3 = (bf16[128,2048]{1,0:T(8,128)(2,1)S(1)}, bf16[128,2048]{1,0:T(8,128)(2,1)}, u32[]{:S(2)}) copy-start(bf16[128,2048]{1,0:T(8,128)(2,1)} %v_ref.3) | copy-start | bytes 1572868
  4.1 8.8 %collective-permute-start.2 = (bf16[272,256]{1,0:T(8,128)(2,1)}, bf16[272,256]{1,0:T(8,128)(2,1)S(1)}, u32[]{:S(2)}, u32[]{:S(2)}) collective-permute-start(bf16[272,256]{1,0:T(8,128)(2,1)} %get-tuple-element.38), channel_id=1, source_target_pairs={{0,16},{1,17},{8,24},{9,25},{16,0},{17,1},{24,8},{25,9},{2,18},{3,... | collective-permute-start | bytes 417800 | tf_op jit(solution)/shard_map/ppermute | solution.py:221
  7.1 15.5 %collective-permute-start.1 = (bf16[2,2,128,256]{3,2,1,0:T(8,128)(2,1)}, bf16[2,2,128,256]{3,2,1,0:T(8,128)(2,1)S(1)}, u32[]{:S(2)}, u32[]{:S(2)}) collective-permute-start(bf16[2,2,128,256]{3,2,1,0:T(8,128)(2,1)} %get-tuple-element.37.refs_8_), channel_id=1, source_target_pairs={{0,2},{2,0},{4,6},{6,4},{1,3},{3,1},{5,7},{7,5},{8,10},{10,8},{12,... | collective-permute-start | bytes 786440 | tf_op jit(solution)/shard_map/ppermute | solution.py:221
  8.7 14.3 %collective-permute-start = (bf16[2,2,128,256]{3,2,1,0:T(8,128)(2,1)}, bf16[2,2,128,256]{3,2,1,0:T(8,128)(2,1)S(1)}, u32[]{:S(2)}, u32[]{:S(2)}) collective-permute-start(bf16[2,2,128,256]{3,2,1,0:T(8,128)(2,1)} %get-tuple-element.37.refs_8_), channel_id=1, source_target_pairs={{0,4},{2,6},{4,0},{6,2},{1,5},{3,7},{5,1},{7,3},{8,12},{10,14},{12... | collective-permute-start | bytes 786440 | tf_op jit(solution)/shard_map/ppermute | solution.py:221
  11.3 11.3 %collective-permute-start.3 = (bf16[272,256]{1,0:T(8,128)(2,1)}, bf16[272,256]{1,0:T(8,128)(2,1)S(1)}, u32[]{:S(2)}, u32[]{:S(2)}) collective-permute-start(bf16[272,256]{1,0:T(8,128)(2,1)} %get-tuple-element.39), channel_id=1, source_target_pairs={{0,17},{1,16},{8,25},{9,24},{16,1},{17,0},{24,9},{25,8},{2,19},{3,... | collective-permute-start | bytes 417800 | tf_op jit(solution)/shard_map/ppermute | solution.py:221
  11.3 11.3 %collective-permute-start.4 = (bf16[272,256]{1,0:T(8,128)(2,1)}, bf16[272,256]{1,0:T(8,128)(2,1)S(1)}, u32[]{:S(2)}, u32[]{:S(2)}) collective-permute-start(bf16[272,256]{1,0:T(8,128)(2,1)} %get-tuple-element.40), channel_id=1, source_target_pairs={{0,24},{1,25},{8,16},{9,17},{16,8},{17,9},{24,0},{25,1},{2,26},{3,... | collective-permute-start | bytes 417800 | tf_op jit(solution)/shard_map/ppermute | solution.py:221
  12.9 10.6 %copy-start.8 = (bf16[272,256]{1,0:T(8,128)(2,1)S(1)}, bf16[272,256]{1,0:T(8,128)(2,1)}, u32[]{:S(2)}) copy-start(bf16[272,256]{1,0:T(8,128)(2,1)} %get-tuple-element.45) | copy-start | bytes 417796
  12.9 10.6 %copy-start.7 = (bf16[272,256]{1,0:T(8,128)(2,1)S(1)}, bf16[272,256]{1,0:T(8,128)(2,1)}, u32[]{:S(2)}) copy-start(bf16[272,256]{1,0:T(8,128)(2,1)} %get-tuple-element.46) | copy-start | bytes 417796
  12.9 12.1 %copy-start.4 = (bf16[2,2,128,256]{3,2,1,0:T(8,128)(2,1)S(1)}, bf16[2,2,128,256]{3,2,1,0:T(8,128)(2,1)}, u32[]{:S(2)}) copy-start(bf16[2,2,128,256]{3,2,1,0:T(8,128)(2,1)} %get-tuple-element.37.refs_8_) | copy-start | bytes 786436
  12.9 17.4 %copy-start.6 = (bf16[272,256]{1,0:T(8,128)(2,1)S(1)}, bf16[272,256]{1,0:T(8,128)(2,1)}, u32[]{:S(2)}) copy-start(bf16[272,256]{1,0:T(8,128)(2,1)} %get-tuple-element.47) | copy-start | bytes 417796
  12.9 9.8 %collective-permute-start.5 = (bf16[272,256]{1,0:T(8,128)(2,1)}, bf16[272,256]{1,0:T(8,128)(2,1)S(1)}, u32[]{:S(2)}, u32[]{:S(2)}) collective-permute-start(bf16[272,256]{1,0:T(8,128)(2,1)} %get-tuple-element.41), channel_id=1, source_target_pairs={{0,25},{1,24},{8,17},{9,16},{16,9},{17,8},{24,1},{25,0},{2,27},{3,... | collective-permute-start | bytes 417800 | tf_op jit(solution)/shard_map/ppermute | solution.py:221
  23.0 7.3 %collective-permute-start.12 = (bf16[2,2,128,256]{3,2,1,0:T(8,128)(2,1)S(1)}, bf16[2,2,128,256]{3,2,1,0:T(8,128)(2,1)S(1)}, u32[]{:S(2)}, u32[]{:S(2)}) collective-permute-start(bf16[2,2,128,256]{3,2,1,0:T(8,128)(2,1)S(1)} %collective-permute-done.refs_12_), channel_id=1, source_target_pairs={{0,2},{2,0},{4,6},{6,4},{1,3},{3,1},{5,7},{7,5},{8,10},{10,8},{12,... | collective-permute-start | bytes 786440 | tf_op jit(solution)/shard_map/ppermute | solution.py:221
  23.4 2.1 %collective-permute-start.6 = (bf16[272,256]{1,0:T(8,128)(2,1)S(1)}, bf16[272,256]{1,0:T(8,128)(2,1)S(1)}, u32[]{:S(2)}, u32[]{:S(2)}) collective-permute-start(bf16[272,256]{1,0:T(8,128)(2,1)S(1)} %copy-done.8), channel_id=1, source_target_pairs={{0,1},{1,0},{8,9},{9,8},{16,17},{17,16},{24,25},{25,24},{2,3},{3,2... | collective-permute-start | bytes 417800 | tf_op jit(solution)/shard_map/ppermute | solution.py:221
  23.5 6.8 %collective-permute-start.7 = (bf16[272,256]{1,0:T(8,128)(2,1)S(1)}, bf16[272,256]{1,0:T(8,128)(2,1)S(1)}, u32[]{:S(2)}, u32[]{:S(2)}) collective-permute-start(bf16[272,256]{1,0:T(8,128)(2,1)S(1)} %copy-done.7), channel_id=1, source_target_pairs={{0,8},{1,9},{8,0},{9,1},{16,24},{17,25},{24,16},{25,17},{2,10},{3,... | collective-permute-start | bytes 417800 | tf_op jit(solution)/shard_map/ppermute | solution.py:221
  25.0 10.7 %collective-permute-start.9 = (bf16[2,2,128,256]{3,2,1,0:T(8,128)(2,1)S(1)}, bf16[2,2,128,256]{3,2,1,0:T(8,128)(2,1)S(1)}, u32[]{:S(2)}, u32[]{:S(2)}) collective-permute-start(bf16[2,2,128,256]{3,2,1,0:T(8,128)(2,1)S(1)} %copy-done.4), channel_id=1, source_target_pairs={{0,1},{1,0},{2,3},{3,2},{4,5},{5,4},{6,7},{7,6},{8,9},{9,8},{10,11... | collective-permute-start | bytes 786440 | tf_op jit(solution)/shard_map/ppermute | solution.py:221
  25.2 10.6 %collective-permute-start.10 = (bf16[2,2,128,256]{3,2,1,0:T(8,128)(2,1)S(1)}, bf16[2,2,128,256]{3,2,1,0:T(8,128)(2,1)S(1)}, u32[]{:S(2)}, u32[]{:S(2)}) collective-permute-start(bf16[2,2,128,256]{3,2,1,0:T(8,128)(2,1)S(1)} %collective-permute-done.1.refs_10_), channel_id=1, source_target_pairs={{0,1},{1,0},{2,3},{3,2},{4,5},{5,4},{6,7},{7,6},{8,9},{9,8},{10,11... | collective-permute-start | bytes 786440 | tf_op jit(solution)/shard_map/ppermute | solution.py:221
  25.5 10.2 %collective-permute-start.11 = (bf16[2,2,128,256]{3,2,1,0:T(8,128)(2,1)S(1)}, bf16[2,2,128,256]{3,2,1,0:T(8,128)(2,1)S(1)}, u32[]{:S(2)}, u32[]{:S(2)}) collective-permute-start(bf16[2,2,128,256]{3,2,1,0:T(8,128)(2,1)S(1)} %collective-permute-done.refs_12_), channel_id=1, source_target_pairs={{0,1},{1,0},{2,3},{3,2},{4,5},{5,4},{6,7},{7,6},{8,9},{9,8},{10,11... | collective-permute-start | bytes 786440 | tf_op jit(solution)/shard_map/ppermute | solution.py:221
  30.3 5.5 %collective-permute-start.13 = (bf16[2,2,128,256]{3,2,1,0:T(8,128)(2,1)S(1)}, bf16[2,2,128,256]{3,2,1,0:T(8,128)(2,1)S(1)}, u32[]{:S(2)}, u32[]{:S(2)}) collective-permute-start(bf16[2,2,128,256]{3,2,1,0:T(8,128)(2,1)S(1)} %collective-permute-done.12.refs_14_), channel_id=1, source_target_pairs={{0,1},{1,0},{2,3},{3,2},{4,5},{5,4},{6,7},{7,6},{8,9},{9,8},{10,11... | collective-permute-start | bytes 786440 | tf_op jit(solution)/shard_map/ppermute | solution.py:221
  30.3 5.5 %collective-permute-start.8 = (bf16[272,256]{1,0:T(8,128)(2,1)S(1)}, bf16[272,256]{1,0:T(8,128)(2,1)S(1)}, u32[]{:S(2)}, u32[]{:S(2)}) collective-permute-start(bf16[272,256]{1,0:T(8,128)(2,1)S(1)} %copy-done.6), channel_id=1, source_target_pairs={{0,9},{1,8},{8,1},{9,0},{16,25},{17,24},{24,17},{25,16},{2,11},{3,... | collective-permute-start | bytes 417800 | tf_op jit(solution)/shard_map/ppermute | solution.py:221
  43.6 4.3 %collective-permute-start.14 = (bf16[272,256]{1,0:T(8,128)(2,1)S(1)}, bf16[272,256]{1,0:T(8,128)(2,1)S(1)}, u32[]{:S(2)}, u32[]{:S(2)}) collective-permute-start(bf16[272,256]{1,0:T(8,128)(2,1)S(1)} %get-tuple-element.62), channel_id=1, source_target_pairs={{0,1},{1,0},{8,9},{9,8},{16,17},{17,16},{24,25},{25,24},{2,3},{3,2... | collective-permute-start | bytes 417800 | tf_op jit(solution)/shard_map/ppermute | solution.py:221
  44.1 6.5 %collective-permute-start.15 = (bf16[272,256]{1,0:T(8,128)(2,1)S(1)}, bf16[272,256]{1,0:T(8,128)(2,1)S(1)}, u32[]{:S(2)}, u32[]{:S(2)}) collective-permute-start(bf16[272,256]{1,0:T(8,128)(2,1)S(1)} %get-tuple-element.63), channel_id=1, source_target_pairs={{0,8},{1,9},{8,0},{9,1},{16,24},{17,25},{24,16},{25,17},{2,10},{3,... | collective-permute-start | bytes 417800 | tf_op jit(solution)/shard_map/ppermute | solution.py:221
  45.6 7.0 %collective-permute-start.16 = (bf16[272,256]{1,0:T(8,128)(2,1)S(1)}, bf16[272,256]{1,0:T(8,128)(2,1)S(1)}, u32[]{:S(2)}, u32[]{:S(2)}) collective-permute-start(bf16[272,256]{1,0:T(8,128)(2,1)S(1)} %get-tuple-element.64), channel_id=1, source_target_pairs={{0,9},{1,8},{8,1},{9,0},{16,25},{17,24},{24,17},{25,16},{2,11},{3,... | collective-permute-start | bytes 417800 | tf_op jit(solution)/shard_map/ppermute | solution.py:221
  45.6 7.0 %collective-permute-start.17 = (bf16[272,256]{1,0:T(8,128)(2,1)S(1)}, bf16[272,256]{1,0:T(8,128)(2,1)S(1)}, u32[]{:S(2)}, u32[]{:S(2)}) collective-permute-start(bf16[272,256]{1,0:T(8,128)(2,1)S(1)} %get-tuple-element.65), channel_id=1, source_target_pairs={{0,16},{1,17},{8,24},{9,25},{16,0},{17,1},{24,8},{25,9},{2,18},{3,... | collective-permute-start | bytes 417800 | tf_op jit(solution)/shard_map/ppermute | solution.py:221
  47.6 13.3 %collective-permute-start.18 = (bf16[272,256]{1,0:T(8,128)(2,1)S(1)}, bf16[272,256]{1,0:T(8,128)(2,1)S(1)}, u32[]{:S(2)}, u32[]{:S(2)}) collective-permute-start(bf16[272,256]{1,0:T(8,128)(2,1)S(1)} %get-tuple-element.66), channel_id=1, source_target_pairs={{0,17},{1,16},{8,25},{9,24},{16,1},{17,0},{24,9},{25,8},{2,19},{3,... | collective-permute-start | bytes 417800 | tf_op jit(solution)/shard_map/ppermute | solution.py:221
  47.9 13.1 %collective-permute-start.19 = (bf16[272,256]{1,0:T(8,128)(2,1)S(1)}, bf16[272,256]{1,0:T(8,128)(2,1)S(1)}, u32[]{:S(2)}, u32[]{:S(2)}) collective-permute-start(bf16[272,256]{1,0:T(8,128)(2,1)S(1)} %get-tuple-element.67), channel_id=1, source_target_pairs={{0,24},{1,25},{8,16},{9,17},{16,8},{17,9},{24,0},{25,1},{2,26},{3,... | collective-permute-start | bytes 417800 | tf_op jit(solution)/shard_map/ppermute | solution.py:221
  50.6 10.4 %collective-permute-start.20 = (bf16[272,256]{1,0:T(8,128)(2,1)S(1)}, bf16[272,256]{1,0:T(8,128)(2,1)S(1)}, u32[]{:S(2)}, u32[]{:S(2)}) collective-permute-start(bf16[272,256]{1,0:T(8,128)(2,1)S(1)} %get-tuple-element.68), channel_id=1, source_target_pairs={{0,25},{1,24},{8,17},{9,16},{16,9},{17,8},{24,1},{25,0},{2,27},{3,... | collective-permute-start | bytes 417800 | tf_op jit(solution)/shard_map/ppermute | solution.py:221
  61.0 5.7 %collective-permute-start.23 = (f32[16,128]{1,0:T(8,128)S(1)}, f32[16,128]{1,0:T(8,128)S(1)}, u32[]{:S(2)}, u32[]{:S(2)}) collective-permute-start(f32[16,128]{1,0:T(8,128)S(1)} %convert_add_fusion), channel_id=1, source_target_pairs={{0,6},{2,4},{4,2},{6,0},{1,7},{3,5},{5,3},{7,1},{8,14},{10,12},{12... | collective-permute-start | bytes 24584 | tf_op jit(solution)/shard_map/ppermute | solution.py:221
  63.8 4.5 %collective-permute-start.22 = (f32[16,128]{1,0:T(8,128)S(1)}, f32[16,128]{1,0:T(8,128)S(1)}, u32[]{:S(2)}, u32[]{:S(2)}) collective-permute-start(f32[16,128]{1,0:T(8,128)S(1)} %convert_add_fusion), channel_id=1, source_target_pairs={{0,4},{2,6},{4,0},{6,2},{1,5},{3,7},{5,1},{7,3},{8,12},{10,14},{12... | collective-permute-start | bytes 24584 | tf_op jit(solution)/shard_map/ppermute | solution.py:221
  63.8 4.5 %collective-permute-start.21 = (f32[16,128]{1,0:T(8,128)S(1)}, f32[16,128]{1,0:T(8,128)S(1)}, u32[]{:S(2)}, u32[]{:S(2)}) collective-permute-start(f32[16,128]{1,0:T(8,128)S(1)} %convert_add_fusion), channel_id=1, source_target_pairs={{0,2},{2,0},{4,6},{6,4},{1,3},{3,1},{5,7},{7,5},{8,10},{10,8},{12,... | collective-permute-start | bytes 24584 | tf_op jit(solution)/shard_map/ppermute | solution.py:221
  (2 other events, 12.2 us)

commit v2 on v1

--- a/solution.py
+++ b/solution.py
@@ -118,14 +118,14 @@
         dq_ref[:, head_cols(h)] = (dot(ds, k_ref[:, head_cols(h)]) * scale).astype(BF16)
 
 
-def attend_kernel(scale, groups, peers, gate_ref, local_ref, *refs):
-    *refs, k_all, v_all = refs
+def attend_kernel(scale, groups, peers, last, gate_ref, before_ref, *refs):
+    *refs, part_ref, k_all, v_all = refs
     got, mem_refs, back = refs[:peers], refs[peers:-peers], refs[-peers:]
     packet_rows = got[0].shape[0]
     blocks = len(mem_refs)
     rows = mem_refs[0].shape[2]
-    heads = local_ref.shape[0]
-    tok = (back[0].shape[0] - heads) // 2
+    heads = before_ref.shape[0]
+    tok = (back[0].shape[0] - heads * last) // 2
     extra = packet_rows - 2 * tok
     chunk = plane_index()
     lane = lax.broadcasted_iota(jnp.int32, (rows, HEAD_DIM), 1)
@@ -193,9 +193,12 @@
                 back[first + t][tok : 2 * tok, head_cols(h)] = dq[t * tok : (t + 1) * tok]
 
     head = lax.broadcasted_iota(jnp.int32, (heads, HEAD_DIM), 0)
-    total = -local_ref[...]
+    total = before_ref[...]
     for h in range(PAIR):
         total = total + jnp.where(head == chunk * PAIR + h, parts[h], 0.0)
+    if not last:
+        part_ref[...] = total
+        return
     total = jnp.sum(total, axis=1, keepdims=True)
     high = total.astype(BF16).astype(F32)
     middle = (total - high).astype(BF16).astype(F32)
@@ -204,6 +207,7 @@
     terms = jnp.where(lane == 0, high, jnp.where(lane == 1, middle, jnp.where(lane == 2, low, 0.0)))
     for ref in back:
         ref[2 * tok :, :] = terms.astype(BF16)
+    part_ref[...] = terms[:, :HEAD_DIM]
 
 
 def merge_kernel(lo_ref, ldq_ref, *refs):
@@ -258,7 +262,6 @@
     hbm_spec = pl.BlockSpec(memory_space=pltpu.HBM)
     vmem_spec = pl.BlockSpec(memory_space=pltpu.VMEM)
     packet = jax.ShapeDtypeStruct((2 * tok + max(16, blocks), CHUNK), BF16)
-    reply = jax.ShapeDtypeStruct((2 * tok + heads, CHUNK), BF16)
     both, *send = pl.pallas_call(
         functools.partial(prologue_kernel, blocks),
         out_shape=(jax.ShapeDtypeStruct((2, 2, rows, CHUNK), BF16),) + (packet,) * peers,
@@ -298,25 +301,34 @@
         name="local_forward",
     )(query, key, value, d_out)
 
-    spread, (got[4:], local_part) = spread_along(both, "z", (got[4:], local_part))
+    spread, (got[5:], local_part) = spread_along(both, "z", (got[5:], local_part))
     memory = []
     for k in range(blocks // 2):
         memory += [spread[k], send_xor(spread[k], "core", 1)]
 
     keys_shape = (PAIR, blocks * rows, CHUNK)
-    send_back = pl.pallas_call(
-        functools.partial(attend_kernel, scale, groups, peers),
-        out_shape=(reply,) * peers,
-        in_specs=[vmem_spec] * (2 + peers + blocks),
-        out_specs=(vmem_spec,) * peers,
-        scratch_shapes=[pltpu.VMEM(keys_shape, BF16), pltpu.VMEM(keys_shape, BF16)],
-        compiler_params=params,
-        cost_estimate=pl.CostEstimate(
-            flops=8 * peers * tok * blocks * rows * CHUNK, bytes_accessed=10 * tok * width,
-            transcendentals=heads * tok * blocks * rows,
-        ),
-        name="memory_attention",
-    )(gate_cols, local_part.reshape(heads, HEAD_DIM), *got, *memory)
+
+    def attend(before, first, count, last):
+        reply = jax.ShapeDtypeStruct((2 * tok + heads * last, CHUNK), BF16)
+        *replies, part = pl.pallas_call(
+            functools.partial(attend_kernel, scale, groups, count, last),
+            out_shape=(reply,) * count + (jax.ShapeDtypeStruct((heads, HEAD_DIM), F32),),
+            in_specs=[vmem_spec] * (2 + count + blocks),
+            out_specs=(vmem_spec,) * (count + 1),
+            scratch_shapes=[pltpu.VMEM(keys_shape, BF16), pltpu.VMEM(keys_shape, BF16)],
+            compiler_params=params,
+            cost_estimate=pl.CostEstimate(
+                flops=8 * count * tok * blocks * rows * CHUNK,
+                bytes_accessed=10 * tok * count * CHUNK,
+                transcendentals=count * PAIR * tok * blocks * rows,
+            ),
+            name="memory_attention",
+        )(gate_cols, before, *got[first : first + count], *memory)
+        return replies, part
+
+    near = peers // 2
+    far_replies, part = attend(-local_part.reshape(heads, HEAD_DIM), near, peers - near, False)
+    near_replies, part = attend(part, 0, near, True)
     whole = jax.ShapeDtypeStruct((tok, width), BF16)
     local_mix, local_dq = pl.pallas_call(
         functools.partial(local_backward_kernel, scale),
@@ -333,13 +345,21 @@
         name="local_backward",
     )(key, value, d_out, gate_cols, local_out, local_prob)
 
-    send_back = list(send_back)
-    send_back[1], local_mix, local_dq = lax.optimization_barrier(
-        (send_back[1], local_mix, local_dq)
-    )
-    back = exchange(send_back, PLANE)
-
-    sums = functools.reduce(jnp.add, [x[2 * tok :, :HEAD_DIM].astype(F32) for x in back])
+    far = {k: send_xor(far_replies[k - near], PLANE, k) for k in range(near, peers)}
+    back = [near_replies[0]]
+    for k in range(1, near):
+        waits = (far[k + near],) if k > 1 else (far[near], far[near + 1], local_mix, local_dq)
+        reply, waits = lax.optimization_barrier((near_replies[k], waits))
+        if k > 1:
+            (far[k + near],) = waits
+        else:
+            far[near], far[near + 1], local_mix, local_dq = waits
+        back.append(send_xor(reply, PLANE, k))
+    back += [far[k] for k in range(near, peers)]
+
+    parts = [x[2 * tok :, :HEAD_DIM].astype(F32) for x in back[1:near]]
+    parts += [part] + [send_xor(part, PLANE, k) for k in range(near, peers)]
+    sums = functools.reduce(jnp.add, parts)
     sums = jnp.sum(sum_over(sum_over(sums, "z"), "sa")[:, :3], axis=1)
     gate_grad = sums * gate * (1.0 - gate) / math.sqrt(tok * devices)
 

time: 69.2 us -> 70.5 us (1.019)
  starting transfers between devices: 26.8 us -> 29.3 us
  waiting for transfers between devices: 23.4 us -> 22.1 us
    ppermute x24 -> x28, starting transfers between devices: 26.8 us -> 29.3 us  [send_xor(): lax.ppermute(array, axes, [(i, i ^ k) for i in range(lax.axis_size(axes))])]
    ppermute x24 -> x28, waiting for transfers between devices: 23.4 us -> 22.1 us  [send_xor(): lax.ppermute(array, axes, [(i, i ^ k) for i in range(lax.axis_size(axes))])]
    pallas_call x1 -> x2, Pallas kernels: 7.83 us -> 8.04 us  [attend(): pl.pallas_call(functools.partial(attend_kernel, scale, groups, count, las...]
  transfers between devices with their start and end apart: 24 -> 28, of which waited for: 7 -> 7; matrix products, arithmetic and copies ran while one was open for 0% -> 0% of each run, Pallas kernels for 9% -> 20%
where the time goes in v2:
time: 70.5 us; the launch traced here: 70.4 us
  starting transfers between devices  29.3 us (42%)
  waiting for transfers between devices  22.1 us (31%)
  Pallas kernels  17.3 us (25%)
  between operations  0.83 us (1%)
    ppermute x28, starting transfers between devices, send_xor(): lax.ppermute(array, axes, [(i, i ^ k) for i in range(lax.axis_size(axes))])  29.3 us
    ppermute x28, waiting for transfers between devices, send_xor(): lax.ppermute(array, axes, [(i, i ^ k) for i in range(lax.axis_size(axes))])  22.1 us
    pallas_call x2, Pallas kernels, attend(): pl.pallas_call(functools.partial(attend_kernel, scale, groups, count, las...  8.04 us
    pallas_call x1, Pallas kernels, body(): pl.pallas_call(functools.partial(prologue_kernel, blocks), out_shape=(jax...  3.43 us
    pallas_call x1, Pallas kernels, body(): pl.pallas_call(functools.partial(local_forward_kernel, scale), grid=(step...  2.61 us
    pallas_call x1, Pallas kernels, body(): pl.pallas_call(functools.partial(local_backward_kernel, scale), grid=(ste...  2 us
  transfers between devices with their start and end apart: 28, of which 7 were waited for; matrix products, arithmetic and copies ran while one was open for 0% of the time, Pallas kernels for 20%

profile of v2, /device:TPU:0, one launch (start us, length us, event | category | flops | bytes accessed | tf_op | source)
XLA Modules:
  0.0 70.4 jit_solution(10097985360953053980)
XLA Ops:
  0.7 3.4 %chunks.1 = (bf16[2,2,128,256]{3,2,1,0:T(8,128)(2,1)}, bf16[272,256]{1,0:T(8,128)(2,1)}, bf16[272,256]{1,0:T(8,128)(2,1)}, bf16[272,256]{1,0:T(8,128)(2,1)}, bf1...) custom-call(bf16[128,2048]{1,0:T(8,128)(2,1)} %mk_hbm.1, ...), custom_call_target="tpu_custom_call" | custom-call | tf_op jit(solution)/shard_map/chunks/pallas_call | solution.py:265
  4.1 4.1 %collective-permute-start = (bf16[2,2,128,256]{3,2,1,0:T(8,128)(2,1)}, bf16[2,2,128,256]{3,2,1,0:T(8,128)(2,1)S(1)}, u32[]{:S(2)}, u32[]{:S(2)}) collective-permute-start(bf16[2,2,128,256]{3,2,1,0:T(8,128)(2,1)} %get-tuple-element.44.refs_4_), channel_id=1, source_target_pairs={{0,4},{2,6},{4,0},{6,2},{1,5},{3,7},{5,1},{7,3},{8,12},{10,14},{12... | collective-permute-start | bytes 786440 | tf_op jit(solution)/shard_map/ppermute | solution.py:225
  8.2 1.6 %collective-permute-start.1 = (bf16[2,2,128,256]{3,2,1,0:T(8,128)(2,1)}, bf16[2,2,128,256]{3,2,1,0:T(8,128)(2,1)S(1)}, u32[]{:S(2)}, u32[]{:S(2)}) collective-permute-start(bf16[2,2,128,256]{3,2,1,0:T(8,128)(2,1)} %get-tuple-element.44.refs_4_), channel_id=1, source_target_pairs={{0,2},{2,0},{4,6},{6,4},{1,3},{3,1},{5,7},{7,5},{8,10},{10,8},{12,... | collective-permute-start | bytes 786440 | tf_op jit(solution)/shard_map/ppermute | solution.py:225
  10.2 2.1 %collective-permute-start.3 = (bf16[272,256]{1,0:T(8,128)(2,1)}, bf16[272,256]{1,0:T(8,128)(2,1)S(1)}, u32[]{:S(2)}, u32[]{:S(2)}) collective-permute-start(bf16[272,256]{1,0:T(8,128)(2,1)} %get-tuple-element.46), channel_id=1, source_target_pairs={{0,24},{1,25},{8,16},{9,17},{16,8},{17,9},{24,0},{25,1},{2,26},{3,... | collective-permute-start | bytes 417800 | tf_op jit(solution)/shard_map/ppermute | solution.py:225
  12.3 1.5 %collective-permute-start.4 = (bf16[272,256]{1,0:T(8,128)(2,1)}, bf16[272,256]{1,0:T(8,128)(2,1)S(1)}, u32[]{:S(2)}, u32[]{:S(2)}) collective-permute-start(bf16[272,256]{1,0:T(8,128)(2,1)} %get-tuple-element.47), channel_id=1, source_target_pairs={{0,25},{1,24},{8,17},{9,16},{16,9},{17,8},{24,1},{25,0},{2,27},{3,... | collective-permute-start | bytes 417800 | tf_op jit(solution)/shard_map/ppermute | solution.py:225
  13.8 2.6 %local_forward.1 = (f32[128,2048]{1,0:T(8,128)S(1)}, bf16[16,128,128]{2,1,0:T(8,128)(2,1)S(1)}, f32[4,4,128]{2,1,0:T(4,128)S(1)}) custom-call(bf16[128,2048]{1,0:T(8,128)(2,1)S(1)} %copy-done.1, bf16[128,2048]{1,0:T(8,128)(2,1)S(1)} %copy-done.2, bf16[128,2048]{1,0:T(8,128)(2,1)S(1)} %copy-done.3, bf16[128,2048]{1,0:T(8,128)(2,1)S(1)} %copy-done), custom_call_target="tpu_custom_call" | custom-call | flops 134217728 | bytes 3145728 | tf_op jit(solution)/shard_map/local_forward/pallas_call | solution.py:282
  16.4 5.5 %collective-permute-done.2.refs_1_ = bf16[272,256]{1,0:T(8,128)(2,1)S(1)} collective-permute-done((bf16[272,256]{1,0:T(8,128)(2,1)}, bf16[272,256]{1,0:T(8,128)(2,1)S(1)}, u32[]{:S(2)}, u32[]{:S(2)}) %collective-permute-start.2) | collective-permute-done | bytes 139296 | tf_op jit(solution)/shard_map/ppermute | solution.py:225
  21.9 0.5 collective-permute-start.9
  22.9 1.2 %collective-permute-start.5 = (bf16[272,256]{1,0:T(8,128)(2,1)S(1)}, bf16[272,256]{1,0:T(8,128)(2,1)S(1)}, u32[]{:S(2)}, u32[]{:S(2)}) collective-permute-start(bf16[272,256]{1,0:T(8,128)(2,1)S(1)} %copy-done.9), channel_id=1, source_target_pairs={{0,16},{1,17},{8,24},{9,25},{16,0},{17,1},{24,8},{25,9},{2,18},{3,... | collective-permute-start | bytes 417800 | tf_op jit(solution)/shard_map/ppermute | solution.py:225
  24.2 6.1 %collective-permute-done.9.refs_10_ = bf16[2,2,128,256]{3,2,1,0:T(8,128)(2,1)S(1)} collective-permute-done((bf16[2,2,128,256]{3,2,1,0:T(8,128)(2,1)S(1)}, bf16[2,2,128,256]{3,2,1,0:T(8,128)(2,1)S(1)}, u32[]{:S(2)}, u32[]{:S(2)}) %collective-permute-start.9) | collective-permute-done | bytes 262176 | tf_op jit(solution)/shard_map/ppermute | solution.py:225
  30.8 1.6 %collective-permute-start.12 = (bf16[272,256]{1,0:T(8,128)(2,1)S(1)}, bf16[272,256]{1,0:T(8,128)(2,1)S(1)}, u32[]{:S(2)}, u32[]{:S(2)}) collective-permute-start(bf16[272,256]{1,0:T(8,128)(2,1)S(1)} %copy-done.7), channel_id=1, source_target_pairs={{0,8},{1,9},{8,0},{9,1},{16,24},{17,25},{24,16},{25,17},{2,10},{3,... | collective-permute-start | bytes 417800 | tf_op jit(solution)/shard_map/ppermute | solution.py:225
  32.5 4.0 %memory_attention.2 = (bf16[256,256]{1,0:T(8,128)(2,1)S(1)}, bf16[256,256]{1,0:T(8,128)(2,1)S(1)}, bf16[256,256]{1,0:T(8,128)(2,1)S(1)}, bf16[256,256]{1,0:T(8,128)(2,1)S(1)}, f32[16,128]{1,0:T(8,128)S(1)}) custom-call(f32[1,2048]{1,0:T(1,128)S(1)} %bitcast.3, f32[16,128]{1,0:T(8,128)S(1)} %bitcast.6, bf16[272,256]{1,0:T(8,128)(2,1)S(1)} %collective-permute-done.5.refs_0_, ...), custom_call_target="tpu_custom_call" | custom-call | flops 1073741824 | bytes 1310720 | tf_op jit(solution)/shard_map/memory_attention/pallas_call | solution.py:313
  36.5 1.8 %collective-permute-start.19 = (bf16[256,256]{1,0:T(8,128)(2,1)S(1)}, bf16[256,256]{1,0:T(8,128)(2,1)S(1)}, u32[]{:S(2)}, u32[]{:S(2)}) collective-permute-start(bf16[256,256]{1,0:T(8,128)(2,1)S(1)} %get-tuple-element.76), channel_id=1, source_target_pairs={{0,25},{1,24},{8,17},{9,16},{16,9},{17,8},{24,1},{25,0},{2,27},{3,... | collective-permute-start | bytes 393224 | tf_op jit(solution)/shard_map/ppermute | solution.py:225
  38.3 1.4 %collective-permute-start.17 = (bf16[256,256]{1,0:T(8,128)(2,1)S(1)}, bf16[256,256]{1,0:T(8,128)(2,1)S(1)}, u32[]{:S(2)}, u32[]{:S(2)}) collective-permute-start(bf16[256,256]{1,0:T(8,128)(2,1)S(1)} %get-tuple-element.73), channel_id=1, source_target_pairs={{0,24},{1,25},{8,16},{9,17},{16,8},{17,9},{24,0},{25,1},{2,26},{3,... | collective-permute-start | bytes 393224 | tf_op jit(solution)/shard_map/ppermute | solution.py:225
  39.8 0.5 collective-permute-start.14
  40.7 2.0 %local_backward.1 = (bf16[128,2048]{1,0:T(8,128)(2,1)S(1)}, bf16[128,2048]{1,0:T(8,128)(2,1)S(1)}) custom-call(bf16[128,2048]{1,0:T(8,128)(2,1)S(1)} %copy-done.2, bf16[128,2048]{1,0:T(8,128)(2,1)S(1)} %copy-done.3, bf16[128,2048]{1,0:T(8,128)(2,1)S(1)} %copy-done, f32[1,2048]{1,0:T(1,128)S(1)} %bitcast.4, f32[128,2048]{1,0:T(8,128)S(1)} %get-tuple-element.64.out_ref, ...), custom_call_target="tpu_custom_call" | custom-call | flops 134217728 | bytes 4194304 | tf_op jit(solution)/shard_map/local_backward/pallas_call | solution.py:333
  42.7 4.0 %memory_attention.3 = (bf16[272,256]{1,0:T(8,128)(2,1)S(1)}, bf16[272,256]{1,0:T(8,128)(2,1)S(1)}, bf16[272,256]{1,0:T(8,128)(2,1)S(1)}, bf16[272,256]{1,0:T(8,128)(2,1)S(1)}, f32[16,128]{1,0:T(8,128)S(1)}) custom-call(f32[1,2048]{1,0:T(1,128)S(1)} %bitcast.5, f32[16,128]{1,0:T(8,128)S(1)} %get-tuple-element.56.before_ref, bf16[272,256]{1,0:T(8,128)(2,1)S(1)} %copy-done.5, ...), custom_call_target="tpu_custom_call" | custom-call | flops 1073741824 | bytes 1310720 | tf_op jit(solution)/shard_map/memory_attention/pallas_call | solution.py:313
  46.8 2.4 %collective-permute-start.20 = (bf16[272,256]{1,0:T(8,128)(2,1)S(1)}, bf16[272,256]{1,0:T(8,128)(2,1)S(1)}, u32[]{:S(2)}, u32[]{:S(2)}) collective-permute-start(bf16[272,256]{1,0:T(8,128)(2,1)S(1)} %get-tuple-element.77), channel_id=1, source_target_pairs={{0,9},{1,8},{8,1},{9,0},{16,25},{17,24},{24,17},{25,16},{2,11},{3,... | collective-permute-start | bytes 417800 | tf_op jit(solution)/shard_map/ppermute | solution.py:225
  49.1 0.5 collective-permute-start.18
  49.7 1.9 %collective-permute-done.15.refs_5_ = bf16[256,256]{1,0:T(8,128)(2,1)S(1)} collective-permute-done((bf16[256,256]{1,0:T(8,128)(2,1)S(1)}, bf16[256,256]{1,0:T(8,128)(2,1)S(1)}, u32[]{:S(2)}, u32[]{:S(2)}) %collective-permute-start.15) | collective-permute-done | bytes 131104 | tf_op jit(solution)/shard_map/ppermute | solution.py:225
  51.8 0.6 collective-permute-start.21
  52.4 1.1 %collective-permute-start.22 = (f32[16,128]{1,0:T(8,128)S(1)}, f32[16,128]{1,0:T(8,128)S(1)}, u32[]{:S(2)}, u32[]{:S(2)}) collective-permute-start(f32[16,128]{1,0:T(8,128)S(1)} %get-tuple-element.84), channel_id=1, source_target_pairs={{0,17},{1,16},{8,25},{9,24},{16,1},{17,0},{24,9},{25,8},{2,19},{3,... | collective-permute-start | bytes 24584 | tf_op jit(solution)/shard_map/ppermute | solution.py:225
  53.5 2.1 %collective-permute-done.21 = f32[16,128]{1,0:T(8,128)S(1)} collective-permute-done((f32[16,128]{1,0:T(8,128)S(1)}, f32[16,128]{1,0:T(8,128)S(1)}, u32[]{:S(2)}, u32[]{:S(2)}) %collective-permute-start.21) | collective-permute-done | bytes 8224 | tf_op jit(solution)/shard_map/ppermute | solution.py:225
  55.6 1.3 %collective-permute-start.23 = (f32[16,128]{1,0:T(8,128)S(1)}, f32[16,128]{1,0:T(8,128)S(1)}, u32[]{:S(2)}, u32[]{:S(2)}) collective-permute-start(f32[16,128]{1,0:T(8,128)S(1)} %get-tuple-element.84), channel_id=1, source_target_pairs={{0,24},{1,25},{8,16},{9,17},{16,8},{17,9},{24,0},{25,1},{2,26},{3,... | collective-permute-start | bytes 24584 | tf_op jit(solution)/shard_map/ppermute | solution.py:225
  56.9 0.7 collective-permute-start.24
  57.6 2.6 %collective-permute-done.23 = f32[16,128]{1,0:T(8,128)S(1)} collective-permute-done((f32[16,128]{1,0:T(8,128)S(1)}, f32[16,128]{1,0:T(8,128)S(1)}, u32[]{:S(2)}, u32[]{:S(2)}) %collective-permute-start.23) | collective-permute-done | bytes 8224 | tf_op jit(solution)/shard_map/ppermute | solution.py:225
  60.1 0.8 %collective-permute-done.24 = f32[16,128]{1,0:T(8,128)S(1)} collective-permute-done((f32[16,128]{1,0:T(8,128)S(1)}, f32[16,128]{1,0:T(8,128)S(1)}, u32[]{:S(2)}, u32[]{:S(2)}) %collective-permute-start.24) | collective-permute-done | bytes 8224 | tf_op jit(solution)/shard_map/ppermute | solution.py:225
  61.4 2.9 %collective-permute-start.26 = (f32[16,128]{1,0:T(8,128)S(1)}, f32[16,128]{1,0:T(8,128)S(1)}, u32[]{:S(2)}, u32[]{:S(2)}) collective-permute-start(f32[16,128]{1,0:T(8,128)S(1)} %add_add_fusion), channel_id=1, source_target_pairs={{0,4},{2,6},{4,0},{6,2},{1,5},{3,7},{5,1},{7,3},{8,12},{10,14},{12... | collective-permute-start | bytes 24584 | tf_op jit(solution)/shard_map/ppermute | solution.py:225
  64.3 1.1 %collective-permute-start.27 = (f32[16,128]{1,0:T(8,128)S(1)}, f32[16,128]{1,0:T(8,128)S(1)}, u32[]{:S(2)}, u32[]{:S(2)}) collective-permute-start(f32[16,128]{1,0:T(8,128)S(1)} %add_add_fusion), channel_id=1, source_target_pairs={{0,6},{2,4},{4,2},{6,0},{1,7},{3,5},{5,3},{7,1},{8,14},{10,12},{12... | collective-permute-start | bytes 24584 | tf_op jit(solution)/shard_map/ppermute | solution.py:225
  65.4 1.3 %merge.1 = (bf16[128,2048]{1,0:T(8,128)(2,1)}, bf16[128,2048]{1,0:T(8,128)(2,1)}) custom-call(bf16[128,2048]{1,0:T(8,128)(2,1)S(1)} %get-tuple-element.68.lo_ref, bf16[128,2048]{1,0:T(8,128)(2,1)S(1)} %get-tuple-element.69.ldq_ref, bf16[272,256]{1,0:T(8,128)(2,1)S(1)} %get-tuple-element.70.refs_0_, bf16[272,256]{1,0:T(8,128)(2,1)S(1)} %collective-permute-done.16.refs_1_, ...), custom_call_target="tpu_custom_call" | custom-call | tf_op jit(solution)/shard_map/merge/pallas_call | solution.py:366
  66.6 3.1 %collective-permute-done.27 = f32[16,128]{1,0:T(8,128)S(1)} collective-permute-done((f32[16,128]{1,0:T(8,128)S(1)}, f32[16,128]{1,0:T(8,128)S(1)}, u32[]{:S(2)}, u32[]{:S(2)}) %collective-permute-start.27) | collective-permute-done | bytes 8224 | tf_op jit(solution)/shard_map/ppermute | solution.py:225
  69.8 0.5 multiply_multiply_fusion
  (58 shorter events, 2.9 us)
Async XLA Ops:
  0.6 13.1 %copy-start = (bf16[128,2048]{1,0:T(8,128)(2,1)S(1)}, bf16[128,2048]{1,0:T(8,128)(2,1)}, u32[]{:S(2)}) copy-start(bf16[128,2048]{1,0:T(8,128)(2,1)} %g_ref.3) | copy-start | bytes 1572868
  4.1 17.8 %collective-permute-start = (bf16[2,2,128,256]{3,2,1,0:T(8,128)(2,1)}, bf16[2,2,128,256]{3,2,1,0:T(8,128)(2,1)S(1)}, u32[]{:S(2)}, u32[]{:S(2)}) collective-permute-start(bf16[2,2,128,256]{3,2,1,0:T(8,128)(2,1)} %get-tuple-element.44.refs_4_), channel_id=1, source_target_pairs={{0,4},{2,6},{4,0},{6,2},{1,5},{3,7},{5,1},{7,3},{8,12},{10,14},{12... | collective-permute-start | bytes 786440 | tf_op jit(solution)/shard_map/ppermute | solution.py:225
  8.2 13.7 %collective-permute-start.1 = (bf16[2,2,128,256]{3,2,1,0:T(8,128)(2,1)}, bf16[2,2,128,256]{3,2,1,0:T(8,128)(2,1)S(1)}, u32[]{:S(2)}, u32[]{:S(2)}) collective-permute-start(bf16[2,2,128,256]{3,2,1,0:T(8,128)(2,1)} %get-tuple-element.44.refs_4_), channel_id=1, source_target_pairs={{0,2},{2,0},{4,6},{6,4},{1,3},{3,1},{5,7},{7,5},{8,10},{10,8},{12,... | collective-permute-start | bytes 786440 | tf_op jit(solution)/shard_map/ppermute | solution.py:225
  9.8 12.1 %collective-permute-start.2 = (bf16[272,256]{1,0:T(8,128)(2,1)}, bf16[272,256]{1,0:T(8,128)(2,1)S(1)}, u32[]{:S(2)}, u32[]{:S(2)}) collective-permute-start(bf16[272,256]{1,0:T(8,128)(2,1)} %get-tuple-element.45), channel_id=1, source_target_pairs={{0,17},{1,16},{8,25},{9,24},{16,1},{17,0},{24,9},{25,8},{2,19},{3,... | collective-permute-start | bytes 417800 | tf_op jit(solution)/shard_map/ppermute | solution.py:225
  10.2 11.7 %collective-permute-start.3 = (bf16[272,256]{1,0:T(8,128)(2,1)}, bf16[272,256]{1,0:T(8,128)(2,1)S(1)}, u32[]{:S(2)}, u32[]{:S(2)}) collective-permute-start(bf16[272,256]{1,0:T(8,128)(2,1)} %get-tuple-element.46), channel_id=1, source_target_pairs={{0,24},{1,25},{8,16},{9,17},{16,8},{17,9},{24,0},{25,1},{2,26},{3,... | collective-permute-start | bytes 417800 | tf_op jit(solution)/shard_map/ppermute | solution.py:225
  12.2 18.1 %copy-start.8 = (bf16[272,256]{1,0:T(8,128)(2,1)S(1)}, bf16[272,256]{1,0:T(8,128)(2,1)}, u32[]{:S(2)}) copy-start(bf16[272,256]{1,0:T(8,128)(2,1)} %get-tuple-element.58) | copy-start | bytes 417796
  12.2 18.6 %copy-start.7 = (bf16[272,256]{1,0:T(8,128)(2,1)S(1)}, bf16[272,256]{1,0:T(8,128)(2,1)}, u32[]{:S(2)}) copy-start(bf16[272,256]{1,0:T(8,128)(2,1)} %get-tuple-element.59) | copy-start | bytes 417796
  12.2 20.1 %copy-start.6 = (bf16[272,256]{1,0:T(8,128)(2,1)S(1)}, bf16[272,256]{1,0:T(8,128)(2,1)}, u32[]{:S(2)}) copy-start(bf16[272,256]{1,0:T(8,128)(2,1)} %get-tuple-element.60) | copy-start | bytes 417796
  12.3 9.6 %collective-permute-start.4 = (bf16[272,256]{1,0:T(8,128)(2,1)}, bf16[272,256]{1,0:T(8,128)(2,1)S(1)}, u32[]{:S(2)}, u32[]{:S(2)}) collective-permute-start(bf16[272,256]{1,0:T(8,128)(2,1)} %get-tuple-element.47), channel_id=1, source_target_pairs={{0,25},{1,24},{8,17},{9,16},{16,9},{17,8},{24,1},{25,0},{2,27},{3,... | collective-permute-start | bytes 417800 | tf_op jit(solution)/shard_map/ppermute | solution.py:225
  21.9 8.4 %collective-permute-start.9 = (bf16[2,2,128,256]{3,2,1,0:T(8,128)(2,1)S(1)}, bf16[2,2,128,256]{3,2,1,0:T(8,128)(2,1)S(1)}, u32[]{:S(2)}, u32[]{:S(2)}) collective-permute-start(bf16[2,2,128,256]{3,2,1,0:T(8,128)(2,1)S(1)} %collective-permute-done.refs_8_), channel_id=1, source_target_pairs={{0,2},{2,0},{4,6},{6,4},{1,3},{3,1},{5,7},{7,5},{8,10},{10,8},{12,... | collective-permute-start | bytes 786440 | tf_op jit(solution)/shard_map/ppermute | solution.py:225
  22.4 8.4 %collective-permute-start.6 = (bf16[2,2,128,256]{3,2,1,0:T(8,128)(2,1)S(1)}, bf16[2,2,128,256]{3,2,1,0:T(8,128)(2,1)S(1)}, u32[]{:S(2)}, u32[]{:S(2)}) collective-permute-start(bf16[2,2,128,256]{3,2,1,0:T(8,128)(2,1)S(1)} %copy-done.4), channel_id=1, source_target_pairs={{0,1},{1,0},{2,3},{3,2},{4,5},{5,4},{6,7},{7,6},{8,9},{9,8},{10,11... | collective-permute-start | bytes 786440 | tf_op jit(solution)/shard_map/ppermute | solution.py:225
  22.4 10.0 %collective-permute-start.7 = (bf16[2,2,128,256]{3,2,1,0:T(8,128)(2,1)S(1)}, bf16[2,2,128,256]{3,2,1,0:T(8,128)(2,1)S(1)}, u32[]{:S(2)}, u32[]{:S(2)}) collective-permute-start(bf16[2,2,128,256]{3,2,1,0:T(8,128)(2,1)S(1)} %collective-permute-done.1.refs_6_), channel_id=1, source_target_pairs={{0,1},{1,0},{2,3},{3,2},{4,5},{5,4},{6,7},{7,6},{8,9},{9,8},{10,11... | collective-permute-start | bytes 786440 | tf_op jit(solution)/shard_map/ppermute | solution.py:225
  22.9 7.4 %collective-permute-start.5 = (bf16[272,256]{1,0:T(8,128)(2,1)S(1)}, bf16[272,256]{1,0:T(8,128)(2,1)S(1)}, u32[]{:S(2)}, u32[]{:S(2)}) collective-permute-start(bf16[272,256]{1,0:T(8,128)(2,1)S(1)} %copy-done.9), channel_id=1, source_target_pairs={{0,16},{1,17},{8,24},{9,25},{16,0},{17,1},{24,8},{25,9},{2,18},{3,... | collective-permute-start | bytes 417800 | tf_op jit(solution)/shard_map/ppermute | solution.py:225
  24.2 8.2 %collective-permute-start.8 = (bf16[2,2,128,256]{3,2,1,0:T(8,128)(2,1)S(1)}, bf16[2,2,128,256]{3,2,1,0:T(8,128)(2,1)S(1)}, u32[]{:S(2)}, u32[]{:S(2)}) collective-permute-start(bf16[2,2,128,256]{3,2,1,0:T(8,128)(2,1)S(1)} %collective-permute-done.refs_8_), channel_id=1, source_target_pairs={{0,1},{1,0},{2,3},{3,2},{4,5},{5,4},{6,7},{7,6},{8,9},{9,8},{10,11... | collective-permute-start | bytes 786440 | tf_op jit(solution)/shard_map/ppermute | solution.py:225
  30.3 2.1 %collective-permute-start.10 = (bf16[2,2,128,256]{3,2,1,0:T(8,128)(2,1)S(1)}, bf16[2,2,128,256]{3,2,1,0:T(8,128)(2,1)S(1)}, u32[]{:S(2)}, u32[]{:S(2)}) collective-permute-start(bf16[2,2,128,256]{3,2,1,0:T(8,128)(2,1)S(1)} %collective-permute-done.9.refs_10_), channel_id=1, source_target_pairs={{0,1},{1,0},{2,3},{3,2},{4,5},{5,4},{6,7},{7,6},{8,9},{9,8},{10,11... | collective-permute-start | bytes 786440 | tf_op jit(solution)/shard_map/ppermute | solution.py:225
  30.3 9.5 %collective-permute-start.11 = (bf16[272,256]{1,0:T(8,128)(2,1)S(1)}, bf16[272,256]{1,0:T(8,128)(2,1)S(1)}, u32[]{:S(2)}, u32[]{:S(2)}) collective-permute-start(bf16[272,256]{1,0:T(8,128)(2,1)S(1)} %copy-done.8), channel_id=1, source_target_pairs={{0,1},{1,0},{8,9},{9,8},{16,17},{17,16},{24,25},{25,24},{2,3},{3,2... | collective-permute-start | bytes 417800 | tf_op jit(solution)/shard_map/ppermute | solution.py:225
  30.8 9.5 %collective-permute-start.12 = (bf16[272,256]{1,0:T(8,128)(2,1)S(1)}, bf16[272,256]{1,0:T(8,128)(2,1)S(1)}, u32[]{:S(2)}, u32[]{:S(2)}) collective-permute-start(bf16[272,256]{1,0:T(8,128)(2,1)S(1)} %copy-done.7), channel_id=1, source_target_pairs={{0,8},{1,9},{8,0},{9,1},{16,24},{17,25},{24,16},{25,17},{2,10},{3,... | collective-permute-start | bytes 417800 | tf_op jit(solution)/shard_map/ppermute | solution.py:225
  32.4 10.4 %collective-permute-start.13 = (bf16[272,256]{1,0:T(8,128)(2,1)S(1)}, bf16[272,256]{1,0:T(8,128)(2,1)S(1)}, u32[]{:S(2)}, u32[]{:S(2)}) collective-permute-start(bf16[272,256]{1,0:T(8,128)(2,1)S(1)} %copy-done.6), channel_id=1, source_target_pairs={{0,9},{1,8},{8,1},{9,0},{16,25},{17,24},{24,17},{25,16},{2,11},{3,... | collective-permute-start | bytes 417800 | tf_op jit(solution)/shard_map/ppermute | solution.py:225
  36.5 10.2 %collective-permute-start.19 = (bf16[256,256]{1,0:T(8,128)(2,1)S(1)}, bf16[256,256]{1,0:T(8,128)(2,1)S(1)}, u32[]{:S(2)}, u32[]{:S(2)}) collective-permute-start(bf16[256,256]{1,0:T(8,128)(2,1)S(1)} %get-tuple-element.76), channel_id=1, source_target_pairs={{0,25},{1,24},{8,17},{9,16},{16,9},{17,8},{24,1},{25,0},{2,27},{3,... | collective-permute-start | bytes 393224 | tf_op jit(solution)/shard_map/ppermute | solution.py:225
  38.3 10.8 %collective-permute-start.17 = (bf16[256,256]{1,0:T(8,128)(2,1)S(1)}, bf16[256,256]{1,0:T(8,128)(2,1)S(1)}, u32[]{:S(2)}, u32[]{:S(2)}) collective-permute-start(bf16[256,256]{1,0:T(8,128)(2,1)S(1)} %get-tuple-element.73), channel_id=1, source_target_pairs={{0,24},{1,25},{8,16},{9,17},{16,8},{17,9},{24,0},{25,1},{2,26},{3,... | collective-permute-start | bytes 393224 | tf_op jit(solution)/shard_map/ppermute | solution.py:225
  39.8 9.9 %collective-permute-start.14 = (bf16[256,256]{1,0:T(8,128)(2,1)S(1)}, bf16[256,256]{1,0:T(8,128)(2,1)S(1)}, u32[]{:S(2)}, u32[]{:S(2)}) collective-permute-start(bf16[256,256]{1,0:T(8,128)(2,1)S(1)} %get-tuple-element.62), channel_id=1, source_target_pairs={{0,16},{1,17},{8,24},{9,25},{16,0},{17,1},{24,8},{25,9},{2,18},{3,... | collective-permute-start | bytes 393224 | tf_op jit(solution)/shard_map/ppermute | solution.py:225
  40.3 11.3 %collective-permute-start.15 = (bf16[256,256]{1,0:T(8,128)(2,1)S(1)}, bf16[256,256]{1,0:T(8,128)(2,1)S(1)}, u32[]{:S(2)}, u32[]{:S(2)}) collective-permute-start(bf16[256,256]{1,0:T(8,128)(2,1)S(1)} %get-tuple-element.63), channel_id=1, source_target_pairs={{0,17},{1,16},{8,25},{9,24},{16,1},{17,0},{24,9},{25,8},{2,19},{3,... | collective-permute-start | bytes 393224 | tf_op jit(solution)/shard_map/ppermute | solution.py:225
  46.8 14.1 %collective-permute-start.20 = (bf16[272,256]{1,0:T(8,128)(2,1)S(1)}, bf16[272,256]{1,0:T(8,128)(2,1)S(1)}, u32[]{:S(2)}, u32[]{:S(2)}) collective-permute-start(bf16[272,256]{1,0:T(8,128)(2,1)S(1)} %get-tuple-element.77), channel_id=1, source_target_pairs={{0,9},{1,8},{8,1},{9,0},{16,25},{17,24},{24,17},{25,16},{2,11},{3,... | collective-permute-start | bytes 417800 | tf_op jit(solution)/shard_map/ppermute | solution.py:225
  49.1 11.7 %collective-permute-start.18 = (bf16[272,256]{1,0:T(8,128)(2,1)S(1)}, bf16[272,256]{1,0:T(8,128)(2,1)S(1)}, u32[]{:S(2)}, u32[]{:S(2)}) collective-permute-start(bf16[272,256]{1,0:T(8,128)(2,1)S(1)} %get-tuple-element.74), channel_id=1, source_target_pairs={{0,8},{1,9},{8,0},{9,1},{16,24},{17,25},{24,16},{25,17},{2,10},{3,... | collective-permute-start | bytes 417800 | tf_op jit(solution)/shard_map/ppermute | solution.py:225
  51.6 9.3 %collective-permute-start.16 = (bf16[272,256]{1,0:T(8,128)(2,1)S(1)}, bf16[272,256]{1,0:T(8,128)(2,1)S(1)}, u32[]{:S(2)}, u32[]{:S(2)}) collective-permute-start(bf16[272,256]{1,0:T(8,128)(2,1)S(1)} %get-tuple-element.71), channel_id=1, source_target_pairs={{0,1},{1,0},{8,9},{9,8},{16,17},{17,16},{24,25},{25,24},{2,3},{3,2... | collective-permute-start | bytes 417800 | tf_op jit(solution)/shard_map/ppermute | solution.py:225
  51.8 3.7 %collective-permute-start.21 = (f32[16,128]{1,0:T(8,128)S(1)}, f32[16,128]{1,0:T(8,128)S(1)}, u32[]{:S(2)}, u32[]{:S(2)}) collective-permute-start(f32[16,128]{1,0:T(8,128)S(1)} %get-tuple-element.84), channel_id=1, source_target_pairs={{0,16},{1,17},{8,24},{9,25},{16,0},{17,1},{24,8},{25,9},{2,18},{3,... | collective-permute-start | bytes 24584 | tf_op jit(solution)/shard_map/ppermute | solution.py:225
  52.4 4.5 %collective-permute-start.22 = (f32[16,128]{1,0:T(8,128)S(1)}, f32[16,128]{1,0:T(8,128)S(1)}, u32[]{:S(2)}, u32[]{:S(2)}) collective-permute-start(f32[16,128]{1,0:T(8,128)S(1)} %get-tuple-element.84), channel_id=1, source_target_pairs={{0,17},{1,16},{8,25},{9,24},{16,1},{17,0},{24,9},{25,8},{2,19},{3,... | collective-permute-start | bytes 24584 | tf_op jit(solution)/shard_map/ppermute | solution.py:225
  55.6 4.5 %collective-permute-start.23 = (f32[16,128]{1,0:T(8,128)S(1)}, f32[16,128]{1,0:T(8,128)S(1)}, u32[]{:S(2)}, u32[]{:S(2)}) collective-permute-start(f32[16,128]{1,0:T(8,128)S(1)} %get-tuple-element.84), channel_id=1, source_target_pairs={{0,24},{1,25},{8,16},{9,17},{16,8},{17,9},{24,0},{25,1},{2,26},{3,... | collective-permute-start | bytes 24584 | tf_op jit(solution)/shard_map/ppermute | solution.py:225
  56.9 4.0 %collective-permute-start.24 = (f32[16,128]{1,0:T(8,128)S(1)}, f32[16,128]{1,0:T(8,128)S(1)}, u32[]{:S(2)}, u32[]{:S(2)}) collective-permute-start(f32[16,128]{1,0:T(8,128)S(1)} %get-tuple-element.84), channel_id=1, source_target_pairs={{0,25},{1,24},{8,17},{9,16},{16,9},{17,8},{24,1},{25,0},{2,27},{3,... | collective-permute-start | bytes 24584 | tf_op jit(solution)/shard_map/ppermute | solution.py:225
  60.9 5.7 %collective-permute-start.25 = (f32[16,128]{1,0:T(8,128)S(1)}, f32[16,128]{1,0:T(8,128)S(1)}, u32[]{:S(2)}, u32[]{:S(2)}) collective-permute-start(f32[16,128]{1,0:T(8,128)S(1)} %add_add_fusion), channel_id=1, source_target_pairs={{0,2},{2,0},{4,6},{6,4},{1,3},{3,1},{5,7},{7,5},{8,10},{10,8},{12,... | collective-permute-start | bytes 24584 | tf_op jit(solution)/shard_map/ppermute | solution.py:225
  61.4 5.2 %collective-permute-start.26 = (f32[16,128]{1,0:T(8,128)S(1)}, f32[16,128]{1,0:T(8,128)S(1)}, u32[]{:S(2)}, u32[]{:S(2)}) collective-permute-start(f32[16,128]{1,0:T(8,128)S(1)} %add_add_fusion), channel_id=1, source_target_pairs={{0,4},{2,6},{4,0},{6,2},{1,5},{3,7},{5,1},{7,3},{8,12},{10,14},{12... | collective-permute-start | bytes 24584 | tf_op jit(solution)/shard_map/ppermute | solution.py:225
  64.3 5.4 %collective-permute-start.27 = (f32[16,128]{1,0:T(8,128)S(1)}, f32[16,128]{1,0:T(8,128)S(1)}, u32[]{:S(2)}, u32[]{:S(2)}) collective-permute-start(f32[16,128]{1,0:T(8,128)S(1)} %add_add_fusion), channel_id=1, source_target_pairs={{0,6},{2,4},{4,2},{6,0},{1,7},{3,5},{5,3},{7,1},{8,14},{10,12},{12... | collective-permute-start | bytes 24584 | tf_op jit(solution)/shard_map/ppermute | solution.py:225
  (7 other events, 63.8 us)

commit v3 on v1

--- a/solution.py
+++ b/solution.py
@@ -47,7 +47,7 @@
 
 
 def prologue_kernel(
-    blocks, mk_hbm, mv_hbm, q_hbm, g_hbm, ids_ref, both_ref, *refs
+    blocks, mk_hbm, mv_hbm, q_hbm, g_hbm, ids_ref, mine_ref, theirs_ref, *refs
 ):
     *out_refs, mem_sems, in_sems = refs
     tok = q_hbm.shape[0]
@@ -55,9 +55,9 @@
     chunk = plane_index()
     copies = [
         pltpu.make_async_copy(
-            ref.at[:, chunk_columns(chunk ^ i)], both_ref.at[i, t], mem_sems.at[i, t]
+            ref.at[:, chunk_columns(chunk ^ i)], out_ref.at[t], mem_sems.at[i, t]
         )
-        for i in range(2)
+        for i, out_ref in enumerate((mine_ref, theirs_ref))
         for t, ref in enumerate((mk_hbm, mv_hbm))
     ]
     for k, out_ref in enumerate(out_refs):
@@ -83,6 +83,11 @@
         copy.wait()
 
 
+def join_kernel(mine_ref, other_ref, out_ref):
+    out_ref[0] = mine_ref[...]
+    out_ref[1] = other_ref[...]
+
+
 def local_forward_kernel(scale, q_ref, k_ref, v_ref, g_ref, out_ref, prob_ref, part_ref):
     tok = q_ref.shape[0]
     heads = part_ref.shape[1]
@@ -118,19 +123,37 @@
         dq_ref[:, head_cols(h)] = (dot(ds, k_ref[:, head_cols(h)]) * scale).astype(BF16)
 
 
-def attend_kernel(scale, groups, peers, gate_ref, local_ref, *refs):
-    *refs, k_all, v_all = refs
-    got, mem_refs, back = refs[:peers], refs[peers:-peers], refs[-peers:]
-    packet_rows = got[0].shape[0]
-    blocks = len(mem_refs)
+def tile_rows(packets, first, start, count, cols):
+    return jnp.concatenate(
+        [packets[first + t][start : start + count, cols] for t in range(TILE)], axis=0
+    )
+
+
+def gate_of(gate_ref, h):
+    return gate_ref[:, chunk_columns(plane_index())][:, head_cols(h)]
+
+
+def backward(scale, e, dout, delta, inv, k_ref, v_ref, h):
+    keys = k_ref.shape[1]
+    dp = dot(dout, v_ref[h, :, :HEAD_DIM], NT)
+    delta = jnp.concatenate([delta] * (keys // HEAD_DIM), axis=1)
+    ds = (e.astype(F32) * (dp - delta)).astype(BF16)
+    return (dot(ds, k_ref[h, :, :HEAD_DIM]) * (inv * scale)).astype(BF16)
+
+
+def first_kernel(scale, groups, peers, gate_ref, before_ref, *refs):
+    got, refs = refs[:peers], refs[peers:]
+    near = peers // 2
+    mem_refs, refs = refs[: -near - 6], refs[-near - 6 :]
+    back, (part_ref, k_all, v_all, e_ref, stats_ref, mixed_ref) = refs[:near], refs[near:]
     rows = mem_refs[0].shape[2]
-    heads = local_ref.shape[0]
-    tok = (back[0].shape[0] - heads) // 2
-    extra = packet_rows - 2 * tok
-    chunk = plane_index()
+    tok = back[0].shape[0] // 2
+    heads = before_ref.shape[0]
+    extra = got[0].shape[0] - 2 * tok
     lane = lax.broadcasted_iota(jnp.int32, (rows, HEAD_DIM), 1)
     for h in range(PAIR):
-        for b, ref in enumerate(mem_refs):
+        for b in range(2 * len(mem_refs)):
+            ref = mem_refs[b // 2]
             span = slice(b * rows, (b + 1) * rows)
             k_all[h, span, :HEAD_DIM] = ref[b % 2, 0, :, head_cols(h)]
             k_all[h, span, HEAD_DIM:] = jnp.where(lane == b, NEG, 0.0).astype(BF16)
@@ -141,13 +164,7 @@
         == lax.broadcasted_iota(jnp.int32, (tok, groups), 1)
     )
     spread = jnp.where(spread, 1.0, 0.0).astype(BF16)
-    gates = gate_ref[:, chunk_columns(chunk)]
     pad = jnp.zeros((HEAD_DIM - extra, groups), BF16)
-
-    def rows_of(first, start, cols):
-        return jnp.concatenate(
-            [got[first + t][start : start + tok, cols] for t in range(TILE)], axis=0
-        )
 
     units = [(first, h) for first in range(0, peers, TILE) for h in range(PAIR)]
     shunned, scores, weights, parts = {}, {}, {}, [0.0] * PAIR
@@ -162,48 +179,68 @@
                 shunned[first] = jnp.concatenate(
                     [dot(spread, x, NT).astype(BF16) for x in shun], axis=0
                 )
-            q = jnp.concatenate([rows_of(first, 0, head_cols(h)), shunned[first]], axis=1)
-            scores[step] = dot(q, k_all[h], NT)
+            q = tile_rows(got, first, 0, tok, head_cols(h))
+            scores[step] = dot(jnp.concatenate([q, shunned[first]], axis=1), k_all[h], NT)
         if 1 <= step <= len(units):
             u = step - 1
             first, h = units[u]
-            gate = gates[:, head_cols(h)]
+            gate = gate_of(gate_ref, h)
             s = scores.pop(u)
             peak = jnp.max(s, axis=1, keepdims=True)
             e = jnp.exp2((s - peak) * (scale * LOG2E)).astype(BF16)
             o = dot(e, v_all[h])
             inv = 1.0 / o[:, HEAD_DIM:]
             o = o[:, :HEAD_DIM] * inv
-            g32 = rows_of(first, tok, head_cols(h)).astype(F32)
+            g32 = tile_rows(got, first, tok, tok, head_cols(h)).astype(F32)
             dout = (gate * g32).astype(BF16)
             delta = row_sums(dout.astype(F32) * o)
             mixed = (gate * o).astype(BF16)
             for t in range(TILE):
-                back[first + t][:tok, head_cols(h)] = mixed[t * tok : (t + 1) * tok]
+                k = first + t
+                place = mixed_ref.at[k] if k < near else back[k - near]
+                place[:tok, head_cols(h)] = mixed[t * tok : (t + 1) * tok]
             parts[h] = parts[h] + jnp.sum(g32 * o, axis=0, keepdims=True)
-            weights[u] = (e, dout, delta, inv)
-        if 2 <= step:
+            if first < near:
+                e_ref[u] = e
+                stats_ref[u, 0] = delta
+                stats_ref[u, 1] = inv
+            else:
+                weights[u] = (e, dout, delta, inv)
+        if 2 <= step and step - 2 in weights:
             u = step - 2
             first, h = units[u]
-            e, dout, delta, inv = weights.pop(u)
-            dp = dot(dout, v_all[h, :, :HEAD_DIM], NT)
-            ds = (e.astype(F32) * (dp - jnp.concatenate([delta] * blocks, axis=1))).astype(BF16)
-            dq = (dot(ds, k_all[h, :, :HEAD_DIM]) * (inv * scale)).astype(BF16)
+            dq = backward(scale, *weights.pop(u), k_all, v_all, h)
             for t in range(TILE):
-                back[first + t][tok : 2 * tok, head_cols(h)] = dq[t * tok : (t + 1) * tok]
+                back[first + t - near][tok:, head_cols(h)] = dq[t * tok : (t + 1) * tok]
 
     head = lax.broadcasted_iota(jnp.int32, (heads, HEAD_DIM), 0)
-    total = -local_ref[...]
+    total = before_ref[...]
     for h in range(PAIR):
-        total = total + jnp.where(head == chunk * PAIR + h, parts[h], 0.0)
-    total = jnp.sum(total, axis=1, keepdims=True)
+        total = total + jnp.where(head == plane_index() * PAIR + h, parts[h], 0.0)
+    part_ref[...] = total
+
+
+def second_kernel(scale, near, gate_ref, sums_ref, k_all, v_all, e_ref, stats_ref, mixed_ref, *refs):
+    got, back, terms_ref = refs[:near], refs[near:-1], refs[-1]
+    heads = sums_ref.shape[0]
+    tok = mixed_ref.shape[1]
+    units = [(first, h) for first in range(0, near, TILE) for h in range(PAIR)]
+    for u, (first, h) in enumerate(units):
+        g32 = tile_rows(got, first, tok, tok, head_cols(h)).astype(F32)
+        dout = (gate_of(gate_ref, h) * g32).astype(BF16)
+        dq = backward(scale, e_ref[u], dout, stats_ref[u, 0], stats_ref[u, 1], k_all, v_all, h)
+        for t in range(TILE):
+            back[first + t][tok : 2 * tok, head_cols(h)] = dq[t * tok : (t + 1) * tok]
+    total = jnp.sum(sums_ref[...], axis=1, keepdims=True)
     high = total.astype(BF16).astype(F32)
     middle = (total - high).astype(BF16).astype(F32)
     low = total - high - middle
     lane = lax.broadcasted_iota(jnp.int32, (heads, CHUNK), 1)
     terms = jnp.where(lane == 0, high, jnp.where(lane == 1, middle, jnp.where(lane == 2, low, 0.0)))
-    for ref in back:
+    for k, ref in enumerate(back):
+        ref[:tok] = mixed_ref[k]
         ref[2 * tok :, :] = terms.astype(BF16)
+    terms_ref[...] = terms[:, :HEAD_DIM]
 
 
 def merge_kernel(lo_ref, ldq_ref, *refs):
@@ -234,8 +271,11 @@
     return held, ready
 
 
-def exchange(arrays, axes):
-    return [arrays[0]] + [send_xor(arrays[k], axes, k) for k in range(1, len(arrays))]
+def exchange(arrays, axes, order):
+    arrived = list(arrays)
+    for k in order:
+        arrived[k] = send_xor(arrays[k], axes, k)
+    return arrived
 
 
 def sum_over(array, axis):
@@ -258,17 +298,25 @@
     hbm_spec = pl.BlockSpec(memory_space=pltpu.HBM)
     vmem_spec = pl.BlockSpec(memory_space=pltpu.VMEM)
     packet = jax.ShapeDtypeStruct((2 * tok + max(16, blocks), CHUNK), BF16)
-    reply = jax.ShapeDtypeStruct((2 * tok + heads, CHUNK), BF16)
-    both, *send = pl.pallas_call(
+    chunk_shape = jax.ShapeDtypeStruct((2, rows, CHUNK), BF16)
+    mine, theirs, *send = pl.pallas_call(
         functools.partial(prologue_kernel, blocks),
-        out_shape=(jax.ShapeDtypeStruct((2, 2, rows, CHUNK), BF16),) + (packet,) * peers,
+        out_shape=(chunk_shape,) * 2 + (packet,) * peers,
         in_specs=[hbm_spec] * 4 + [vmem_spec],
-        out_specs=(vmem_spec,) * (peers + 1),
+        out_specs=(vmem_spec,) * (peers + 2),
         scratch_shapes=[pltpu.SemaphoreType.DMA((2, 2)), pltpu.SemaphoreType.DMA((peers, 2))],
         compiler_params=alone,
         name="chunks",
     )(mem_key, mem_value, query, d_out, jnp.transpose(block_ids))
-    got = exchange(send, PLANE)
+    both = pl.pallas_call(
+        join_kernel,
+        out_shape=jax.ShapeDtypeStruct((2,) + chunk_shape.shape, BF16),
+        in_specs=[vmem_spec] * 2,
+        out_specs=vmem_spec,
+        compiler_params=params,
+        name="join_cores",
+    )(mine, send_xor(theirs, "core", 1))
+    got = exchange(send, PLANE, (6, 7, 5, 4, 2, 3, 1))
 
     gate = jax.nn.sigmoid(gate_logit)
     gate_cols = jnp.repeat(gate, HEAD_DIM)[None, :]
@@ -298,25 +346,9 @@
         name="local_forward",
     )(query, key, value, d_out)
 
-    spread, (got[4:], local_part) = spread_along(both, "z", (got[4:], local_part))
-    memory = []
-    for k in range(blocks // 2):
-        memory += [spread[k], send_xor(spread[k], "core", 1)]
-
-    keys_shape = (PAIR, blocks * rows, CHUNK)
-    send_back = pl.pallas_call(
-        functools.partial(attend_kernel, scale, groups, peers),
-        out_shape=(reply,) * peers,
-        in_specs=[vmem_spec] * (2 + peers + blocks),
-        out_specs=(vmem_spec,) * peers,
-        scratch_shapes=[pltpu.VMEM(keys_shape, BF16), pltpu.VMEM(keys_shape, BF16)],
-        compiler_params=params,
-        cost_estimate=pl.CostEstimate(
-            flops=8 * peers * tok * blocks * rows * CHUNK, bytes_accessed=10 * tok * width,
-            transcendentals=heads * tok * blocks * rows,
-        ),
-        name="memory_attention",
-    )(gate_cols, local_part.reshape(heads, HEAD_DIM), *got, *memory)
+    spread, (got[5:], local_part) = spread_along(both, "z", (got[5:], local_part))
+    memory = [spread[k] for k in range(blocks // 2)]
+
     whole = jax.ShapeDtypeStruct((tok, width), BF16)
     local_mix, local_dq = pl.pallas_call(
         functools.partial(local_backward_kernel, scale),
@@ -332,15 +364,57 @@
         ),
         name="local_backward",
     )(key, value, d_out, gate_cols, local_out, local_prob)
-
-    send_back = list(send_back)
-    send_back[1], local_mix, local_dq = lax.optimization_barrier(
-        (send_back[1], local_mix, local_dq)
+    memory, local_mix, local_dq = lax.optimization_barrier((memory, local_mix, local_dq))
+
+    keys_shape = (PAIR, blocks * rows, CHUNK)
+
+    near = peers // 2
+    units = near // TILE * PAIR
+    keys_array = jax.ShapeDtypeStruct(keys_shape, BF16)
+    state = (
+        keys_array,
+        keys_array,
+        jax.ShapeDtypeStruct((units, TILE * tok, blocks * rows), BF16),
+        jax.ShapeDtypeStruct((units, 2, TILE * tok, HEAD_DIM), F32),
+        jax.ShapeDtypeStruct((near, tok, CHUNK), BF16),
     )
-    back = exchange(send_back, PLANE)
-
-    sums = functools.reduce(jnp.add, [x[2 * tok :, :HEAD_DIM].astype(F32) for x in back])
-    sums = jnp.sum(sum_over(sum_over(sums, "z"), "sa")[:, :3], axis=1)
+    part_shape = jax.ShapeDtypeStruct((heads, HEAD_DIM), F32)
+    far_reply = jax.ShapeDtypeStruct((2 * tok, CHUNK), BF16)
+    near_reply = jax.ShapeDtypeStruct((2 * tok + heads, CHUNK), BF16)
+    pair_flops = 2 * tok * blocks * rows * CHUNK
+    outs = pl.pallas_call(
+        functools.partial(first_kernel, scale, groups, peers),
+        out_shape=(far_reply,) * (peers - near) + (part_shape,) + state,
+        in_specs=[vmem_spec] * (2 + peers + blocks // 2),
+        out_specs=(vmem_spec,) * (peers - near + 1 + len(state)),
+        compiler_params=params,
+        cost_estimate=pl.CostEstimate(
+            flops=3 * peers * pair_flops, bytes_accessed=20 * tok * width,
+            transcendentals=heads * tok * blocks * rows,
+        ),
+        name="memory_attention",
+    )(gate_cols, -local_part.reshape(heads, HEAD_DIM), *got, *memory)
+    far_replies, part, state = outs[: peers - near], outs[peers - near], outs[peers - near + 1 :]
+    sums = sum_over(sum_over(part, "z"), "sa")
+    *near_replies, terms = pl.pallas_call(
+        functools.partial(second_kernel, scale, near),
+        out_shape=(near_reply,) * near + (part_shape,),
+        in_specs=[vmem_spec] * (2 + len(state) + near),
+        out_specs=(vmem_spec,) * (near + 1),
+        compiler_params=params,
+        cost_estimate=pl.CostEstimate(
+            flops=2 * near * pair_flops, bytes_accessed=10 * tok * width, transcendentals=0
+        ),
+        name="memory_backward",
+    )(gate_cols, sums, *state, *got[:near])
+    far = exchange([None] * near + list(far_replies), PLANE, (6, 7, 4, 5))[near:]
+    core_reply, far = lax.optimization_barrier((near_replies[1], far))
+    near_replies[1] = core_reply
+    back = exchange(near_replies, PLANE, (2, 3, 1)) + far
+
+    parts = [x[2 * tok :, :HEAD_DIM].astype(F32) for x in back[1:near]]
+    sums = functools.reduce(jnp.add, parts, terms)
+    sums = jnp.sum((sums + send_xor(sums, PLANE, near))[:, :3], axis=1)
     gate_grad = sums * gate * (1.0 - gate) / math.sqrt(tok * devices)
 
     out, d_query = pl.pallas_call(

time: 69.2 us -> 66.6 us (0.962)
  waiting for transfers between devices: 23.4 us -> 19.6 us
  local copies, waits for them, and re-layouts: 0.12 us -> 1.02 us
    ppermute x24 -> x22, waiting for transfers between devices: 23.4 us -> 19.6 us  [send_xor(): lax.ppermute(array, axes, [(i, i ^ k) for i in range(lax.axis_size(axes))])]
    unnamed x20 -> x22, local copies, waits for them, and re-layouts: 0.04 us -> 0.95 us
    pallas_call x2 -> x4, Pallas kernels: 11.3 us -> 11.5 us  [the longest x1 6.76 us: body(): pl.pallas_call(functools.partial(first_kernel, scale, groups, peers), out...]
    ppermute x24 -> x22, starting transfers between devices: 26.8 us -> 27 us  [send_xor(): lax.ppermute(array, axes, [(i, i ^ k) for i in range(lax.axis_size(axes))])]
  transfers between devices with their start and end apart: 24 -> 22, of which waited for: 7 -> 9; matrix products, arithmetic and copies ran while one was open for 0% -> 0% of each run, Pallas kernels for 9% -> 11%
where the time goes in v3:
time: 66.6 us; the launch traced here: 66.4 us
  starting transfers between devices  27 us (41%)
  waiting for transfers between devices  19.6 us (29%)
  Pallas kernels  17.4 us (26%)
  local copies, waits for them, and re-layouts  1.02 us (2%)
  between operations  0.78 us (1%)
  other arithmetic  0.67 us (1%)
    ppermute x22, starting transfers between devices, send_xor(): lax.ppermute(array, axes, [(i, i ^ k) for i in range(lax.axis_size(axes))])  27 us
    ppermute x22, waiting for transfers between devices, send_xor(): lax.ppermute(array, axes, [(i, i ^ k) for i in range(lax.axis_size(axes))])  19.6 us
    pallas_call x1, Pallas kernels, body(): pl.pallas_call(functools.partial(first_kernel, scale, groups, peers), out...  6.76 us
    pallas_call x1, Pallas kernels, body(): pl.pallas_call(functools.partial(prologue_kernel, blocks), out_shape=(chu...  3.43 us
    pallas_call x1, Pallas kernels, body(): pl.pallas_call(functools.partial(local_forward_kernel, scale), grid=(step...  2.61 us
    pallas_call x1, Pallas kernels, body(): pl.pallas_call(functools.partial(local_backward_kernel, scale), grid=(ste...  2.01 us
  transfers between devices with their start and end apart: 22, of which 9 were waited for; matrix products, arithmetic and copies ran while one was open for 0% of the time, Pallas kernels for 11%

profile of v3, /device:TPU:0, one launch (start us, length us, event | category | flops | bytes accessed | tf_op | source)
XLA Modules:
  0.0 66.4 jit_solution(13301935455788393874)
XLA Ops:
  0.7 3.4 %chunks.1 = (bf16[2,128,256]{2,1,0:T(8,128)(2,1)}, bf16[2,128,256]{2,1,0:T(8,128)(2,1)}, bf16[272,256]{1,0:T(8,128)(2,1)}, bf16[272,256]{1,0:T(8,128)(2,1)}, bf1...) custom-call(bf16[128,2048]{1,0:T(8,128)(2,1)} %mk_hbm.1, ...), custom_call_target="tpu_custom_call" | custom-call | tf_op jit(solution)/shard_map/chunks/pallas_call | solution.py:302
  4.6 1.2 %collective-permute-done.other_ref = bf16[2,128,256]{2,1,0:T(8,128)(2,1)S(1)} collective-permute-done((bf16[2,128,256]{2,1,0:T(8,128)(2,1)}, bf16[2,128,256]{2,1,0:T(8,128)(2,1)S(1)}, u32[]{:S(2)}, u32[]{:S(2)}) %collective-permute-start) | collective-permute-done | bytes 131104 | tf_op jit(solution)/shard_map/ppermute | solution.py:258
  5.8 0.9 %copy-done.5 = bf16[2,128,256]{2,1,0:T(8,128)(2,1)S(1)} copy-done((bf16[2,128,256]{2,1,0:T(8,128)(2,1)S(1)}, bf16[2,128,256]{2,1,0:T(8,128)(2,1)}, u32[]{:S(2)}) %copy-start.5) | copy-done | bytes 131096
  6.8 3.0 %collective-permute-start.2 = (bf16[2,2,128,256]{3,2,1,0:T(8,128)(2,1)S(1)}, bf16[2,2,128,256]{3,2,1,0:T(8,128)(2,1)S(1)}, u32[]{:S(2)}, u32[]{:S(2)}) collective-permute-start(bf16[2,2,128,256]{3,2,1,0:T(8,128)(2,1)S(1)} %join_cores.1.refs_8_), channel_id=1, source_target_pairs={{0,2},{2,0},{4,6},{6,4},{1,3},{3,1},{5,7},{7,5},{8,10},{10,8},{12,... | collective-permute-start | bytes 786440 | tf_op jit(solution)/shard_map/ppermute | solution.py:258
  9.8 2.6 %collective-permute-start.1 = (bf16[2,2,128,256]{3,2,1,0:T(8,128)(2,1)S(1)}, bf16[2,2,128,256]{3,2,1,0:T(8,128)(2,1)S(1)}, u32[]{:S(2)}, u32[]{:S(2)}) collective-permute-start(bf16[2,2,128,256]{3,2,1,0:T(8,128)(2,1)S(1)} %join_cores.1.refs_8_), channel_id=1, source_target_pairs={{0,4},{2,6},{4,0},{6,2},{1,5},{3,7},{5,1},{7,3},{8,12},{10,14},{12... | collective-permute-start | bytes 786440 | tf_op jit(solution)/shard_map/ppermute | solution.py:258
  12.4 0.7 %collective-permute-start.3 = (bf16[272,256]{1,0:T(8,128)(2,1)}, bf16[272,256]{1,0:T(8,128)(2,1)S(1)}, u32[]{:S(2)}, u32[]{:S(2)}) collective-permute-start(bf16[272,256]{1,0:T(8,128)(2,1)} %get-tuple-element.54), channel_id=1, source_target_pairs={{0,17},{1,16},{8,25},{9,24},{16,1},{17,0},{24,9},{25,8},{2,19},{3,... | collective-permute-start | bytes 417800 | tf_op jit(solution)/shard_map/ppermute | solution.py:258
  13.1 1.7 %collective-permute-start.4 = (bf16[272,256]{1,0:T(8,128)(2,1)}, bf16[272,256]{1,0:T(8,128)(2,1)S(1)}, u32[]{:S(2)}, u32[]{:S(2)}) collective-permute-start(bf16[272,256]{1,0:T(8,128)(2,1)} %get-tuple-element.55), channel_id=1, source_target_pairs={{0,24},{1,25},{8,16},{9,17},{16,8},{17,9},{24,0},{25,1},{2,26},{3,... | collective-permute-start | bytes 417800 | tf_op jit(solution)/shard_map/ppermute | solution.py:258
  14.8 1.4 %collective-permute-start.5 = (bf16[272,256]{1,0:T(8,128)(2,1)}, bf16[272,256]{1,0:T(8,128)(2,1)S(1)}, u32[]{:S(2)}, u32[]{:S(2)}) collective-permute-start(bf16[272,256]{1,0:T(8,128)(2,1)} %get-tuple-element.56), channel_id=1, source_target_pairs={{0,25},{1,24},{8,17},{9,16},{16,9},{17,8},{24,1},{25,0},{2,27},{3,... | collective-permute-start | bytes 417800 | tf_op jit(solution)/shard_map/ppermute | solution.py:258
  16.3 2.6 %local_forward.1 = (f32[128,2048]{1,0:T(8,128)S(1)}, bf16[16,128,128]{2,1,0:T(8,128)(2,1)S(1)}, f32[4,4,128]{2,1,0:T(4,128)S(1)}) custom-call(bf16[128,2048]{1,0:T(8,128)(2,1)S(1)} %copy-done.1, bf16[128,2048]{1,0:T(8,128)(2,1)S(1)} %copy-done.2, bf16[128,2048]{1,0:T(8,128)(2,1)S(1)} %copy-done.3, bf16[128,2048]{1,0:T(8,128)(2,1)S(1)} %copy-done), custom_call_target="tpu_custom_call" | custom-call | flops 134217728 | bytes 3145728 | tf_op jit(solution)/shard_map/local_forward/pallas_call | solution.py:327
  18.9 5.6 %collective-permute-done.3.refs_5_ = bf16[272,256]{1,0:T(8,128)(2,1)S(1)} collective-permute-done((bf16[272,256]{1,0:T(8,128)(2,1)}, bf16[272,256]{1,0:T(8,128)(2,1)S(1)}, u32[]{:S(2)}, u32[]{:S(2)}) %collective-permute-start.3) | collective-permute-done | bytes 139296 | tf_op jit(solution)/shard_map/ppermute | solution.py:258
  25.0 1.6 %collective-permute-start.8 = (bf16[272,256]{1,0:T(8,128)(2,1)S(1)}, bf16[272,256]{1,0:T(8,128)(2,1)S(1)}, u32[]{:S(2)}, u32[]{:S(2)}) collective-permute-start(bf16[272,256]{1,0:T(8,128)(2,1)S(1)} %copy-done.8), channel_id=1, source_target_pairs={{0,8},{1,9},{8,0},{9,1},{16,24},{17,25},{24,16},{25,17},{2,10},{3,... | collective-permute-start | bytes 417800 | tf_op jit(solution)/shard_map/ppermute | solution.py:258
  26.9 1.4 %collective-permute-start.10 = (bf16[272,256]{1,0:T(8,128)(2,1)S(1)}, bf16[272,256]{1,0:T(8,128)(2,1)S(1)}, u32[]{:S(2)}, u32[]{:S(2)}) collective-permute-start(bf16[272,256]{1,0:T(8,128)(2,1)S(1)} %copy-done.6), channel_id=1, source_target_pairs={{0,16},{1,17},{8,24},{9,25},{16,0},{17,1},{24,8},{25,9},{2,18},{3,... | collective-permute-start | bytes 417800 | tf_op jit(solution)/shard_map/ppermute | solution.py:258
  28.4 2.0 %local_backward.1 = (bf16[128,2048]{1,0:T(8,128)(2,1)S(1)}, bf16[128,2048]{1,0:T(8,128)(2,1)S(1)}) custom-call(bf16[128,2048]{1,0:T(8,128)(2,1)S(1)} %copy-done.2, bf16[128,2048]{1,0:T(8,128)(2,1)S(1)} %copy-done.3, bf16[128,2048]{1,0:T(8,128)(2,1)S(1)} %copy-done, f32[1,2048]{1,0:T(1,128)S(1)} %bitcast.3, f32[128,2048]{1,0:T(8,128)S(1)} %get-tuple-element.60.out_ref, ...), custom_call_target="tpu_custom_call" | custom-call | flops 134217728 | bytes 4194304 | tf_op jit(solution)/shard_map/local_backward/pallas_call | solution.py:353
  30.4 2.5 %collective-permute-done.6.refs_11_ = bf16[2,2,128,256]{3,2,1,0:T(8,128)(2,1)S(1)} collective-permute-done((bf16[2,2,128,256]{3,2,1,0:T(8,128)(2,1)S(1)}, bf16[2,2,128,256]{3,2,1,0:T(8,128)(2,1)S(1)}, u32[]{:S(2)}, u32[]{:S(2)}) %collective-permute-start.6) | collective-permute-done | bytes 262176 | tf_op jit(solution)/shard_map/ppermute | solution.py:258
  32.9 0.7 %collective-permute-done.9.refs_3_ = bf16[272,256]{1,0:T(8,128)(2,1)S(1)} collective-permute-done((bf16[272,256]{1,0:T(8,128)(2,1)S(1)}, bf16[272,256]{1,0:T(8,128)(2,1)S(1)}, u32[]{:S(2)}, u32[]{:S(2)}) %collective-permute-start.9) | collective-permute-done | bytes 139296 | tf_op jit(solution)/shard_map/ppermute | solution.py:258
  33.6 6.8 %memory_attention.1 = (bf16[256,256]{1,0:T(8,128)(2,1)S(1)}, bf16[256,256]{1,0:T(8,128)(2,1)S(1)}, bf16[256,256]{1,0:T(8,128)(2,1)S(1)}, bf16[256,256]{1,0:T(8,1...) custom-call(f32[1,2048]{1,0:T(1,128)S(1)} %bitcast.4, ...), custom_call_target="tpu_custom_call" | custom-call | flops 1610612736 | bytes 5242880 | tf_op jit(solution)/shard_map/memory_attention/pallas_call | solution.py:385
  40.4 2.0 %collective-permute-start.13 = (f32[16,128]{1,0:T(8,128)S(1)}, f32[16,128]{1,0:T(8,128)S(1)}, u32[]{:S(2)}, u32[]{:S(2)}) collective-permute-start(f32[16,128]{1,0:T(8,128)S(1)} %get-tuple-element.79), channel_id=1, source_target_pairs={{0,6},{2,4},{4,2},{6,0},{1,7},{3,5},{5,3},{7,1},{8,14},{10,12},{12... | collective-permute-start | bytes 24584 | tf_op jit(solution)/shard_map/ppermute | solution.py:258
  42.4 1.1 %collective-permute-start.12 = (f32[16,128]{1,0:T(8,128)S(1)}, f32[16,128]{1,0:T(8,128)S(1)}, u32[]{:S(2)}, u32[]{:S(2)}) collective-permute-start(f32[16,128]{1,0:T(8,128)S(1)} %get-tuple-element.79), channel_id=1, source_target_pairs={{0,4},{2,6},{4,0},{6,2},{1,5},{3,7},{5,1},{7,3},{8,12},{10,14},{12... | collective-permute-start | bytes 24584 | tf_op jit(solution)/shard_map/ppermute | solution.py:258
  43.5 1.4 %collective-permute-start.11 = (f32[16,128]{1,0:T(8,128)S(1)}, f32[16,128]{1,0:T(8,128)S(1)}, u32[]{:S(2)}, u32[]{:S(2)}) collective-permute-start(f32[16,128]{1,0:T(8,128)S(1)} %get-tuple-element.79), channel_id=1, source_target_pairs={{0,2},{2,0},{4,6},{6,4},{1,3},{3,1},{5,7},{7,5},{8,10},{10,8},{12,... | collective-permute-start | bytes 24584 | tf_op jit(solution)/shard_map/ppermute | solution.py:258
  44.8 1.4 %collective-permute-start.14 = (bf16[256,256]{1,0:T(8,128)(2,1)S(1)}, bf16[256,256]{1,0:T(8,128)(2,1)S(1)}, u32[]{:S(2)}, u32[]{:S(2)}) collective-permute-start(bf16[256,256]{1,0:T(8,128)(2,1)S(1)} %get-tuple-element.87), channel_id=1, source_target_pairs={{0,16},{1,17},{8,24},{9,25},{16,0},{17,1},{24,8},{25,9},{2,18},{3,... | collective-permute-start | bytes 393224 | tf_op jit(solution)/shard_map/ppermute | solution.py:258
  46.2 2.1 %collective-permute-start.16 = (bf16[256,256]{1,0:T(8,128)(2,1)S(1)}, bf16[256,256]{1,0:T(8,128)(2,1)S(1)}, u32[]{:S(2)}, u32[]{:S(2)}) collective-permute-start(bf16[256,256]{1,0:T(8,128)(2,1)S(1)} %get-tuple-element.89), channel_id=1, source_target_pairs={{0,24},{1,25},{8,16},{9,17},{16,8},{17,9},{24,0},{25,1},{2,26},{3,... | collective-permute-start | bytes 393224 | tf_op jit(solution)/shard_map/ppermute | solution.py:258
  48.3 0.9 %collective-permute-start.17 = (bf16[256,256]{1,0:T(8,128)(2,1)S(1)}, bf16[256,256]{1,0:T(8,128)(2,1)S(1)}, u32[]{:S(2)}, u32[]{:S(2)}) collective-permute-start(bf16[256,256]{1,0:T(8,128)(2,1)S(1)} %get-tuple-element.90), channel_id=1, source_target_pairs={{0,25},{1,24},{8,17},{9,16},{16,9},{17,8},{24,1},{25,0},{2,27},{3,... | collective-permute-start | bytes 393224 | tf_op jit(solution)/shard_map/ppermute | solution.py:258
  49.2 1.3 %memory_backward.1 = (bf16[272,256]{1,0:T(8,128)(2,1)S(1)}, bf16[272,256]{1,0:T(8,128)(2,1)S(1)}, bf16[272,256]{1,0:T(8,128)(2,1)S(1)}, bf16[272,256]{1,0:T(8,128)(2,1)S(1)}, f32[16,128]{1,0:T(8,128)S(1)}) custom-call(f32[1,2048]{1,0:T(1,128)S(1)} %bitcast.5, f32[16,128]{1,0:T(8,128)S(1)} %add_add_fusion.sums_ref, ...), custom_call_target="tpu_custom_call" | custom-call | flops 536870912 | bytes 2621440 | tf_op jit(solution)/shard_map/memory_backward/pallas_call | solution.py:399
  50.5 1.6 %collective-permute-start.19 = (bf16[272,256]{1,0:T(8,128)(2,1)S(1)}, bf16[272,256]{1,0:T(8,128)(2,1)S(1)}, u32[]{:S(2)}, u32[]{:S(2)}) collective-permute-start(bf16[272,256]{1,0:T(8,128)(2,1)S(1)} %get-tuple-element.92), channel_id=1, source_target_pairs={{0,8},{1,9},{8,0},{9,1},{16,24},{17,25},{24,16},{25,17},{2,10},{3,... | collective-permute-start | bytes 417800 | tf_op jit(solution)/shard_map/ppermute | solution.py:258
  52.1 3.5 %collective-permute-done.14.refs_4_ = bf16[256,256]{1,0:T(8,128)(2,1)S(1)} collective-permute-done((bf16[256,256]{1,0:T(8,128)(2,1)S(1)}, bf16[256,256]{1,0:T(8,128)(2,1)S(1)}, u32[]{:S(2)}, u32[]{:S(2)}) %collective-permute-start.14) | collective-permute-done | bytes 131104 | tf_op jit(solution)/shard_map/ppermute | solution.py:258
  55.5 2.1 %collective-permute-done.15.refs_5_ = bf16[256,256]{1,0:T(8,128)(2,1)S(1)} collective-permute-done((bf16[256,256]{1,0:T(8,128)(2,1)S(1)}, bf16[256,256]{1,0:T(8,128)(2,1)S(1)}, u32[]{:S(2)}, u32[]{:S(2)}) %collective-permute-start.15) | collective-permute-done | bytes 131104 | tf_op jit(solution)/shard_map/ppermute | solution.py:258
  57.6 0.7 %collective-permute-start.18 = (bf16[272,256]{1,0:T(8,128)(2,1)S(1)}, bf16[272,256]{1,0:T(8,128)(2,1)S(1)}, u32[]{:S(2)}, u32[]{:S(2)}) collective-permute-start(bf16[272,256]{1,0:T(8,128)(2,1)S(1)} %get-tuple-element.91), channel_id=1, source_target_pairs={{0,1},{1,0},{8,9},{9,8},{16,17},{17,16},{24,25},{25,24},{2,3},{3,2... | collective-permute-start | bytes 417800 | tf_op jit(solution)/shard_map/ppermute | solution.py:258
  58.3 0.6 collective-permute-done.19.refs_2_
  59.0 3.0 %collective-permute-done.20.refs_3_ = bf16[272,256]{1,0:T(8,128)(2,1)S(1)} collective-permute-done((bf16[272,256]{1,0:T(8,128)(2,1)S(1)}, bf16[272,256]{1,0:T(8,128)(2,1)S(1)}, u32[]{:S(2)}, u32[]{:S(2)}) %collective-permute-start.20) | collective-permute-done | bytes 139296 | tf_op jit(solution)/shard_map/ppermute | solution.py:258
  62.0 2.1 %collective-permute-start.21 = (f32[16,128]{1,0:T(8,128)S(1)}, f32[16,128]{1,0:T(8,128)S(1)}, u32[]{:S(2)}, u32[]{:S(2)}) collective-permute-start(f32[16,128]{1,0:T(8,128)S(1)} %convert_add_fusion), channel_id=1, source_target_pairs={{0,16},{1,17},{8,24},{9,25},{16,0},{17,1},{24,8},{25,9},{2,18},{3,... | collective-permute-start | bytes 24584 | tf_op jit(solution)/shard_map/ppermute | solution.py:258
  64.1 1.3 %merge.1 = (bf16[128,2048]{1,0:T(8,128)(2,1)}, bf16[128,2048]{1,0:T(8,128)(2,1)}) custom-call(bf16[128,2048]{1,0:T(8,128)(2,1)S(1)} %get-tuple-element.64.lo_ref, bf16[128,2048]{1,0:T(8,128)(2,1)S(1)} %get-tuple-element.65.ldq_ref, bf16[272,256]{1,0:T(8,128)(2,1)S(1)} %get-tuple-element.85.refs_0_, bf16[272,256]{1,0:T(8,128)(2,1)S(1)} %collective-permute-done.18.refs_1_, ...), custom_call_target="tpu_custom_call" | custom-call | tf_op jit(solution)/shard_map/merge/pallas_call | solution.py:420
  65.9 0.5 multiply_multiply_fusion
  (48 shorter events, 2.0 us)
Async XLA Ops:
  0.6 15.6 %copy-start = (bf16[128,2048]{1,0:T(8,128)(2,1)S(1)}, bf16[128,2048]{1,0:T(8,128)(2,1)}, u32[]{:S(2)}) copy-start(bf16[128,2048]{1,0:T(8,128)(2,1)} %g_ref.3) | copy-start | bytes 1572868
  0.6 15.6 %copy-start.1 = (bf16[128,2048]{1,0:T(8,128)(2,1)S(1)}, bf16[128,2048]{1,0:T(8,128)(2,1)}, u32[]{:S(2)}) copy-start(bf16[128,2048]{1,0:T(8,128)(2,1)} %q_ref.1) | copy-start | bytes 1572868
  0.7 15.6 %copy-start.3 = (bf16[128,2048]{1,0:T(8,128)(2,1)S(1)}, bf16[128,2048]{1,0:T(8,128)(2,1)}, u32[]{:S(2)}) copy-start(bf16[128,2048]{1,0:T(8,128)(2,1)} %v_ref.3) | copy-start | bytes 1572868
  0.7 15.6 %copy-start.2 = (bf16[128,2048]{1,0:T(8,128)(2,1)S(1)}, bf16[128,2048]{1,0:T(8,128)(2,1)}, u32[]{:S(2)}) copy-start(bf16[128,2048]{1,0:T(8,128)(2,1)} %k_ref.3) | copy-start | bytes 1572868
  0.7 27.6 %copy-start.10 = (f32[16]{0:T(128)S(1)}, f32[16]{0:T(128)}, u32[]{:S(2)}) copy-start(f32[16]{0:T(128)} %param.14) | copy-start | bytes 196
  4.1 1.7 %collective-permute-start = (bf16[2,128,256]{2,1,0:T(8,128)(2,1)}, bf16[2,128,256]{2,1,0:T(8,128)(2,1)S(1)}, u32[]{:S(2)}, u32[]{:S(2)}) collective-permute-start(bf16[2,128,256]{2,1,0:T(8,128)(2,1)} %get-tuple-element.53), channel_id=1, source_target_pairs={{0,1},{1,0},{2,3},{3,2},{4,5},{5,4},{6,7},{7,6},{8,9},{9,8},{10,11... | collective-permute-start | bytes 393224 | tf_op jit(solution)/shard_map/ppermute | solution.py:258
  6.7 18.2 %copy-start.9 = (bf16[272,256]{1,0:T(8,128)(2,1)S(1)}, bf16[272,256]{1,0:T(8,128)(2,1)}, u32[]{:S(2)}) copy-start(bf16[272,256]{1,0:T(8,128)(2,1)} %get-tuple-element.68) | copy-start | bytes 417796
  6.7 18.3 %copy-start.8 = (bf16[272,256]{1,0:T(8,128)(2,1)S(1)}, bf16[272,256]{1,0:T(8,128)(2,1)}, u32[]{:S(2)}) copy-start(bf16[272,256]{1,0:T(8,128)(2,1)} %get-tuple-element.69) | copy-start | bytes 417796
  6.8 19.8 %copy-start.7 = (bf16[272,256]{1,0:T(8,128)(2,1)S(1)}, bf16[272,256]{1,0:T(8,128)(2,1)}, u32[]{:S(2)}) copy-start(bf16[272,256]{1,0:T(8,128)(2,1)} %get-tuple-element.70) | copy-start | bytes 417796
  6.8 20.1 %copy-start.6 = (bf16[272,256]{1,0:T(8,128)(2,1)S(1)}, bf16[272,256]{1,0:T(8,128)(2,1)}, u32[]{:S(2)}) copy-start(bf16[272,256]{1,0:T(8,128)(2,1)} %get-tuple-element.71) | copy-start | bytes 417796
  6.8 17.7 %collective-permute-start.2 = (bf16[2,2,128,256]{3,2,1,0:T(8,128)(2,1)S(1)}, bf16[2,2,128,256]{3,2,1,0:T(8,128)(2,1)S(1)}, u32[]{:S(2)}, u32[]{:S(2)}) collective-permute-start(bf16[2,2,128,256]{3,2,1,0:T(8,128)(2,1)S(1)} %join_cores.1.refs_8_), channel_id=1, source_target_pairs={{0,2},{2,0},{4,6},{6,4},{1,3},{3,1},{5,7},{7,5},{8,10},{10,8},{12,... | collective-permute-start | bytes 786440 | tf_op jit(solution)/shard_map/ppermute | solution.py:258
  9.8 14.7 %collective-permute-start.1 = (bf16[2,2,128,256]{3,2,1,0:T(8,128)(2,1)S(1)}, bf16[2,2,128,256]{3,2,1,0:T(8,128)(2,1)S(1)}, u32[]{:S(2)}, u32[]{:S(2)}) collective-permute-start(bf16[2,2,128,256]{3,2,1,0:T(8,128)(2,1)S(1)} %join_cores.1.refs_8_), channel_id=1, source_target_pairs={{0,4},{2,6},{4,0},{6,2},{1,5},{3,7},{5,1},{7,3},{8,12},{10,14},{12... | collective-permute-start | bytes 786440 | tf_op jit(solution)/shard_map/ppermute | solution.py:258
  12.4 12.1 %collective-permute-start.3 = (bf16[272,256]{1,0:T(8,128)(2,1)}, bf16[272,256]{1,0:T(8,128)(2,1)S(1)}, u32[]{:S(2)}, u32[]{:S(2)}) collective-permute-start(bf16[272,256]{1,0:T(8,128)(2,1)} %get-tuple-element.54), channel_id=1, source_target_pairs={{0,17},{1,16},{8,25},{9,24},{16,1},{17,0},{24,9},{25,8},{2,19},{3,... | collective-permute-start | bytes 417800 | tf_op jit(solution)/shard_map/ppermute | solution.py:258
  13.1 11.4 %collective-permute-start.4 = (bf16[272,256]{1,0:T(8,128)(2,1)}, bf16[272,256]{1,0:T(8,128)(2,1)S(1)}, u32[]{:S(2)}, u32[]{:S(2)}) collective-permute-start(bf16[272,256]{1,0:T(8,128)(2,1)} %get-tuple-element.55), channel_id=1, source_target_pairs={{0,24},{1,25},{8,16},{9,17},{16,8},{17,9},{24,0},{25,1},{2,26},{3,... | collective-permute-start | bytes 417800 | tf_op jit(solution)/shard_map/ppermute | solution.py:258
  14.8 9.6 %collective-permute-start.5 = (bf16[272,256]{1,0:T(8,128)(2,1)}, bf16[272,256]{1,0:T(8,128)(2,1)S(1)}, u32[]{:S(2)}, u32[]{:S(2)}) collective-permute-start(bf16[272,256]{1,0:T(8,128)(2,1)} %get-tuple-element.56), channel_id=1, source_target_pairs={{0,25},{1,24},{8,17},{9,16},{16,9},{17,8},{24,1},{25,0},{2,27},{3,... | collective-permute-start | bytes 417800 | tf_op jit(solution)/shard_map/ppermute | solution.py:258
  18.9 14.7 %copy-start.4 = (bf16[272,256]{1,0:T(8,128)(2,1)S(1)}, bf16[272,256]{1,0:T(8,128)(2,1)}, u32[]{:S(2)}) copy-start(bf16[272,256]{1,0:T(8,128)(2,1)} %get-tuple-element.67.refs_0_) | copy-start | bytes 417796
  24.5 8.4 %collective-permute-start.6 = (bf16[2,2,128,256]{3,2,1,0:T(8,128)(2,1)S(1)}, bf16[2,2,128,256]{3,2,1,0:T(8,128)(2,1)S(1)}, u32[]{:S(2)}, u32[]{:S(2)}) collective-permute-start(bf16[2,2,128,256]{3,2,1,0:T(8,128)(2,1)S(1)} %collective-permute-done.1.refs_10_), channel_id=1, source_target_pairs={{0,2},{2,0},{4,6},{6,4},{1,3},{3,1},{5,7},{7,5},{8,10},{10,8},{12,... | collective-permute-start | bytes 786440 | tf_op jit(solution)/shard_map/ppermute | solution.py:258
  25.0 7.9 %collective-permute-start.7 = (bf16[272,256]{1,0:T(8,128)(2,1)S(1)}, bf16[272,256]{1,0:T(8,128)(2,1)S(1)}, u32[]{:S(2)}, u32[]{:S(2)}) collective-permute-start(bf16[272,256]{1,0:T(8,128)(2,1)S(1)} %copy-done.9), channel_id=1, source_target_pairs={{0,1},{1,0},{8,9},{9,8},{16,17},{17,16},{24,25},{25,24},{2,3},{3,2... | collective-permute-start | bytes 417800 | tf_op jit(solution)/shard_map/ppermute | solution.py:258
  25.0 7.9 %collective-permute-start.8 = (bf16[272,256]{1,0:T(8,128)(2,1)S(1)}, bf16[272,256]{1,0:T(8,128)(2,1)S(1)}, u32[]{:S(2)}, u32[]{:S(2)}) collective-permute-start(bf16[272,256]{1,0:T(8,128)(2,1)S(1)} %copy-done.8), channel_id=1, source_target_pairs={{0,8},{1,9},{8,0},{9,1},{16,24},{17,25},{24,16},{25,17},{2,10},{3,... | collective-permute-start | bytes 417800 | tf_op jit(solution)/shard_map/ppermute | solution.py:258
  26.6 7.0 %collective-permute-start.9 = (bf16[272,256]{1,0:T(8,128)(2,1)S(1)}, bf16[272,256]{1,0:T(8,128)(2,1)S(1)}, u32[]{:S(2)}, u32[]{:S(2)}) collective-permute-start(bf16[272,256]{1,0:T(8,128)(2,1)S(1)} %copy-done.7), channel_id=1, source_target_pairs={{0,9},{1,8},{8,1},{9,0},{16,25},{17,24},{24,17},{25,16},{2,11},{3,... | collective-permute-start | bytes 417800 | tf_op jit(solution)/shard_map/ppermute | solution.py:258
  26.9 6.7 %collective-permute-start.10 = (bf16[272,256]{1,0:T(8,128)(2,1)S(1)}, bf16[272,256]{1,0:T(8,128)(2,1)S(1)}, u32[]{:S(2)}, u32[]{:S(2)}) collective-permute-start(bf16[272,256]{1,0:T(8,128)(2,1)S(1)} %copy-done.6), channel_id=1, source_target_pairs={{0,16},{1,17},{8,24},{9,25},{16,0},{17,1},{24,8},{25,9},{2,18},{3,... | collective-permute-start | bytes 417800 | tf_op jit(solution)/shard_map/ppermute | solution.py:258
  40.4 5.9 %collective-permute-start.13 = (f32[16,128]{1,0:T(8,128)S(1)}, f32[16,128]{1,0:T(8,128)S(1)}, u32[]{:S(2)}, u32[]{:S(2)}) collective-permute-start(f32[16,128]{1,0:T(8,128)S(1)} %get-tuple-element.79), channel_id=1, source_target_pairs={{0,6},{2,4},{4,2},{6,0},{1,7},{3,5},{5,3},{7,1},{8,14},{10,12},{12... | collective-permute-start | bytes 24584 | tf_op jit(solution)/shard_map/ppermute | solution.py:258
  42.4 5.9 %collective-permute-start.12 = (f32[16,128]{1,0:T(8,128)S(1)}, f32[16,128]{1,0:T(8,128)S(1)}, u32[]{:S(2)}, u32[]{:S(2)}) collective-permute-start(f32[16,128]{1,0:T(8,128)S(1)} %get-tuple-element.79), channel_id=1, source_target_pairs={{0,4},{2,6},{4,0},{6,2},{1,5},{3,7},{5,1},{7,3},{8,12},{10,14},{12... | collective-permute-start | bytes 24584 | tf_op jit(solution)/shard_map/ppermute | solution.py:258
  43.5 5.8 %collective-permute-start.11 = (f32[16,128]{1,0:T(8,128)S(1)}, f32[16,128]{1,0:T(8,128)S(1)}, u32[]{:S(2)}, u32[]{:S(2)}) collective-permute-start(f32[16,128]{1,0:T(8,128)S(1)} %get-tuple-element.79), channel_id=1, source_target_pairs={{0,2},{2,0},{4,6},{6,4},{1,3},{3,1},{5,7},{7,5},{8,10},{10,8},{12,... | collective-permute-start | bytes 24584 | tf_op jit(solution)/shard_map/ppermute | solution.py:258
  44.8 10.7 %collective-permute-start.14 = (bf16[256,256]{1,0:T(8,128)(2,1)S(1)}, bf16[256,256]{1,0:T(8,128)(2,1)S(1)}, u32[]{:S(2)}, u32[]{:S(2)}) collective-permute-start(bf16[256,256]{1,0:T(8,128)(2,1)S(1)} %get-tuple-element.87), channel_id=1, source_target_pairs={{0,16},{1,17},{8,24},{9,25},{16,0},{17,1},{24,8},{25,9},{2,18},{3,... | collective-permute-start | bytes 393224 | tf_op jit(solution)/shard_map/ppermute | solution.py:258
  46.2 11.4 %collective-permute-start.15 = (bf16[256,256]{1,0:T(8,128)(2,1)S(1)}, bf16[256,256]{1,0:T(8,128)(2,1)S(1)}, u32[]{:S(2)}, u32[]{:S(2)}) collective-permute-start(bf16[256,256]{1,0:T(8,128)(2,1)S(1)} %get-tuple-element.88), channel_id=1, source_target_pairs={{0,17},{1,16},{8,25},{9,24},{16,1},{17,0},{24,9},{25,8},{2,19},{3,... | collective-permute-start | bytes 393224 | tf_op jit(solution)/shard_map/ppermute | solution.py:258
  46.2 11.4 %collective-permute-start.16 = (bf16[256,256]{1,0:T(8,128)(2,1)S(1)}, bf16[256,256]{1,0:T(8,128)(2,1)S(1)}, u32[]{:S(2)}, u32[]{:S(2)}) collective-permute-start(bf16[256,256]{1,0:T(8,128)(2,1)S(1)} %get-tuple-element.89), channel_id=1, source_target_pairs={{0,24},{1,25},{8,16},{9,17},{16,8},{17,9},{24,0},{25,1},{2,26},{3,... | collective-permute-start | bytes 393224 | tf_op jit(solution)/shard_map/ppermute | solution.py:258
  48.3 9.3 %collective-permute-start.17 = (bf16[256,256]{1,0:T(8,128)(2,1)S(1)}, bf16[256,256]{1,0:T(8,128)(2,1)S(1)}, u32[]{:S(2)}, u32[]{:S(2)}) collective-permute-start(bf16[256,256]{1,0:T(8,128)(2,1)S(1)} %get-tuple-element.90), channel_id=1, source_target_pairs={{0,25},{1,24},{8,17},{9,16},{16,9},{17,8},{24,1},{25,0},{2,27},{3,... | collective-permute-start | bytes 393224 | tf_op jit(solution)/shard_map/ppermute | solution.py:258
  50.5 8.5 %collective-permute-start.19 = (bf16[272,256]{1,0:T(8,128)(2,1)S(1)}, bf16[272,256]{1,0:T(8,128)(2,1)S(1)}, u32[]{:S(2)}, u32[]{:S(2)}) collective-permute-start(bf16[272,256]{1,0:T(8,128)(2,1)S(1)} %get-tuple-element.92), channel_id=1, source_target_pairs={{0,8},{1,9},{8,0},{9,1},{16,24},{17,25},{24,16},{25,17},{2,10},{3,... | collective-permute-start | bytes 417800 | tf_op jit(solution)/shard_map/ppermute | solution.py:258
  55.5 6.5 %collective-permute-start.20 = (bf16[272,256]{1,0:T(8,128)(2,1)S(1)}, bf16[272,256]{1,0:T(8,128)(2,1)S(1)}, u32[]{:S(2)}, u32[]{:S(2)}) collective-permute-start(bf16[272,256]{1,0:T(8,128)(2,1)S(1)} %get-tuple-element.93), channel_id=1, source_target_pairs={{0,9},{1,8},{8,1},{9,0},{16,25},{17,24},{24,17},{25,16},{2,11},{3,... | collective-permute-start | bytes 417800 | tf_op jit(solution)/shard_map/ppermute | solution.py:258
  57.6 4.4 %collective-permute-start.18 = (bf16[272,256]{1,0:T(8,128)(2,1)S(1)}, bf16[272,256]{1,0:T(8,128)(2,1)S(1)}, u32[]{:S(2)}, u32[]{:S(2)}) collective-permute-start(bf16[272,256]{1,0:T(8,128)(2,1)S(1)} %get-tuple-element.91), channel_id=1, source_target_pairs={{0,1},{1,0},{8,9},{9,8},{16,17},{17,16},{24,25},{25,24},{2,3},{3,2... | collective-permute-start | bytes 417800 | tf_op jit(solution)/shard_map/ppermute | solution.py:258
  62.0 3.8 %collective-permute-start.21 = (f32[16,128]{1,0:T(8,128)S(1)}, f32[16,128]{1,0:T(8,128)S(1)}, u32[]{:S(2)}, u32[]{:S(2)}) collective-permute-start(f32[16,128]{1,0:T(8,128)S(1)} %convert_add_fusion), channel_id=1, source_target_pairs={{0,16},{1,17},{8,24},{9,25},{16,0},{17,1},{24,8},{25,9},{2,18},{3,... | collective-permute-start | bytes 24584 | tf_op jit(solution)/shard_map/ppermute | solution.py:258
  (1 other events, 0.9 us)

commit v4 on v3

--- a/solution.py
+++ b/solution.py
@@ -46,6 +46,16 @@
     return dot(jnp.concatenate([high, low], axis=1), jnp.ones((2 * HEAD_DIM, HEAD_DIM), BF16))
 
 
+def packets_of(refs):
+    own, core, *pairs = refs
+    return [own, core] + [pair.at[lane] for pair in pairs for lane in range(2)]
+
+
+def arrivals_of(refs):
+    own, core, *pairs = refs
+    return [own, core] + [pair.at[i % 2] for i, pair in enumerate(pairs)]
+
+
 def prologue_kernel(
     blocks, mk_hbm, mv_hbm, q_hbm, g_hbm, ids_ref, mine_ref, theirs_ref, *refs
 ):
@@ -60,12 +70,12 @@
         for i, out_ref in enumerate((mine_ref, theirs_ref))
         for t, ref in enumerate((mk_hbm, mv_hbm))
     ]
-    for k, out_ref in enumerate(out_refs):
+    for k, packet in enumerate(out_refs):
         for t, ref in enumerate((q_hbm, g_hbm)):
             span = slice(t * tok, (t + 1) * tok)
             copies.append(
                 pltpu.make_async_copy(
-                    ref.at[:, chunk_columns(chunk ^ k)], out_ref.at[span], in_sems.at[k, t]
+                    ref.at[:, chunk_columns(chunk ^ k)], packet.at[span], in_sems.at[k, t]
                 )
             )
     for copy in copies:
@@ -77,8 +87,8 @@
         for t in range(fetched):
             hot = hot | (row == (ids_ref[t : t + 1, :] ^ owner ^ core))
         shun = jnp.where(hot, 0.0, 1.0).astype(BF16)
-        for out_ref in out_refs[core::2]:
-            out_ref[2 * tok :, :groups] = shun
+        for packet in out_refs[core::2]:
+            packet[2 * tok :, :groups] = shun
     for copy in copies:
         copy.wait()
 
@@ -141,14 +151,14 @@
     return (dot(ds, k_ref[h, :, :HEAD_DIM]) * (inv * scale)).astype(BF16)
 
 
-def first_kernel(scale, groups, peers, gate_ref, before_ref, *refs):
+def attend_kernel(scale, groups, peers, gate_ref, before_ref, *refs):
+    *refs, k_all, v_all = refs
     got, refs = refs[:peers], refs[peers:]
-    near = peers // 2
-    mem_refs, refs = refs[: -near - 6], refs[-near - 6 :]
-    back, (part_ref, k_all, v_all, e_ref, stats_ref, mixed_ref) = refs[:near], refs[near:]
+    pairs = peers // 2 - 1
+    mem_refs, back = refs[: -pairs - 2], packets_of(refs[-pairs - 2 :])
     rows = mem_refs[0].shape[2]
-    tok = back[0].shape[0] // 2
     heads = before_ref.shape[0]
+    tok = (back[0].shape[0] - heads) // 2
     extra = got[0].shape[0] - 2 * tok
     lane = lax.broadcasted_iota(jnp.int32, (rows, HEAD_DIM), 1)
     for h in range(PAIR):
@@ -196,55 +206,33 @@
             delta = row_sums(dout.astype(F32) * o)
             mixed = (gate * o).astype(BF16)
             for t in range(TILE):
-                k = first + t
-                place = mixed_ref.at[k] if k < near else back[k - near]
-                place[:tok, head_cols(h)] = mixed[t * tok : (t + 1) * tok]
+                back[first + t][:tok, head_cols(h)] = mixed[t * tok : (t + 1) * tok]
             parts[h] = parts[h] + jnp.sum(g32 * o, axis=0, keepdims=True)
-            if first < near:
-                e_ref[u] = e
-                stats_ref[u, 0] = delta
-                stats_ref[u, 1] = inv
-            else:
-                weights[u] = (e, dout, delta, inv)
-        if 2 <= step and step - 2 in weights:
+            weights[u] = (e, dout, delta, inv)
+        if 2 <= step:
             u = step - 2
             first, h = units[u]
             dq = backward(scale, *weights.pop(u), k_all, v_all, h)
             for t in range(TILE):
-                back[first + t - near][tok:, head_cols(h)] = dq[t * tok : (t + 1) * tok]
+                back[first + t][tok : 2 * tok, head_cols(h)] = dq[t * tok : (t + 1) * tok]
 
     head = lax.broadcasted_iota(jnp.int32, (heads, HEAD_DIM), 0)
     total = before_ref[...]
     for h in range(PAIR):
         total = total + jnp.where(head == plane_index() * PAIR + h, parts[h], 0.0)
-    part_ref[...] = total
-
-
-def second_kernel(scale, near, gate_ref, sums_ref, k_all, v_all, e_ref, stats_ref, mixed_ref, *refs):
-    got, back, terms_ref = refs[:near], refs[near:-1], refs[-1]
-    heads = sums_ref.shape[0]
-    tok = mixed_ref.shape[1]
-    units = [(first, h) for first in range(0, near, TILE) for h in range(PAIR)]
-    for u, (first, h) in enumerate(units):
-        g32 = tile_rows(got, first, tok, tok, head_cols(h)).astype(F32)
-        dout = (gate_of(gate_ref, h) * g32).astype(BF16)
-        dq = backward(scale, e_ref[u], dout, stats_ref[u, 0], stats_ref[u, 1], k_all, v_all, h)
-        for t in range(TILE):
-            back[first + t][tok : 2 * tok, head_cols(h)] = dq[t * tok : (t + 1) * tok]
-    total = jnp.sum(sums_ref[...], axis=1, keepdims=True)
+    total = jnp.sum(total, axis=1, keepdims=True)
     high = total.astype(BF16).astype(F32)
     middle = (total - high).astype(BF16).astype(F32)
     low = total - high - middle
     lane = lax.broadcasted_iota(jnp.int32, (heads, CHUNK), 1)
     terms = jnp.where(lane == 0, high, jnp.where(lane == 1, middle, jnp.where(lane == 2, low, 0.0)))
-    for k, ref in enumerate(back):
-        ref[:tok] = mixed_ref[k]
-        ref[2 * tok :, :] = terms.astype(BF16)
-    terms_ref[...] = terms[:, :HEAD_DIM]
+    for reply in back:
+        reply[2 * tok :, :] = terms.astype(BF16)
 
 
 def merge_kernel(lo_ref, ldq_ref, *refs):
     *back_refs, out_ref, dq_ref = refs
+    back_refs = arrivals_of(back_refs)
     tok = lo_ref.shape[0]
     chunk = plane_index()
     for k, back_ref in enumerate(back_refs):
@@ -271,11 +259,13 @@
     return held, ready
 
 
-def exchange(arrays, axes, order):
-    arrived = list(arrays)
-    for k in order:
-        arrived[k] = send_xor(arrays[k], axes, k)
-    return arrived
+def across(pairs):
+    order = reversed(range(len(pairs)))
+    return [send_xor(pairs[i], PLANE, 2 * i + 2) for i in order][::-1]
+
+
+def forward(pairs):
+    return [x for pair in pairs for x in (pair, send_xor(pair, PLANE, 1))]
 
 
 def sum_over(array, axis):
@@ -298,12 +288,13 @@
     hbm_spec = pl.BlockSpec(memory_space=pltpu.HBM)
     vmem_spec = pl.BlockSpec(memory_space=pltpu.VMEM)
     packet = jax.ShapeDtypeStruct((2 * tok + max(16, blocks), CHUNK), BF16)
+    pairs = peers // 2 - 1
     chunk_shape = jax.ShapeDtypeStruct((2, rows, CHUNK), BF16)
     mine, theirs, *send = pl.pallas_call(
         functools.partial(prologue_kernel, blocks),
         out_shape=(chunk_shape,) * 2 + (packet,) * peers,
         in_specs=[hbm_spec] * 4 + [vmem_spec],
-        out_specs=(vmem_spec,) * (peers + 2),
+        out_specs=(vmem_spec,) * (2 + peers),
         scratch_shapes=[pltpu.SemaphoreType.DMA((2, 2)), pltpu.SemaphoreType.DMA((peers, 2))],
         compiler_params=alone,
         name="chunks",
@@ -316,7 +307,6 @@
         compiler_params=params,
         name="join_cores",
     )(mine, send_xor(theirs, "core", 1))
-    got = exchange(send, PLANE, (6, 7, 5, 4, 2, 3, 1))
 
     gate = jax.nn.sigmoid(gate_logit)
     gate_cols = jnp.repeat(gate, HEAD_DIM)[None, :]
@@ -346,6 +336,9 @@
         name="local_forward",
     )(query, key, value, d_out)
 
+    got = list(send)
+    for k in (6, 7, 5, 4, 2, 3, 1):
+        got[k] = send_xor(send[k], PLANE, k)
     spread, (got[5:], local_part) = spread_along(both, "z", (got[5:], local_part))
     memory = [spread[k] for k in range(blocks // 2)]
 
@@ -368,53 +361,27 @@
 
     keys_shape = (PAIR, blocks * rows, CHUNK)
 
-    near = peers // 2
-    units = near // TILE * PAIR
-    keys_array = jax.ShapeDtypeStruct(keys_shape, BF16)
-    state = (
-        keys_array,
-        keys_array,
-        jax.ShapeDtypeStruct((units, TILE * tok, blocks * rows), BF16),
-        jax.ShapeDtypeStruct((units, 2, TILE * tok, HEAD_DIM), F32),
-        jax.ShapeDtypeStruct((near, tok, CHUNK), BF16),
-    )
-    part_shape = jax.ShapeDtypeStruct((heads, HEAD_DIM), F32)
-    far_reply = jax.ShapeDtypeStruct((2 * tok, CHUNK), BF16)
-    near_reply = jax.ShapeDtypeStruct((2 * tok + heads, CHUNK), BF16)
-    pair_flops = 2 * tok * blocks * rows * CHUNK
-    outs = pl.pallas_call(
-        functools.partial(first_kernel, scale, groups, peers),
-        out_shape=(far_reply,) * (peers - near) + (part_shape,) + state,
+    reply = jax.ShapeDtypeStruct((2 * tok + heads, CHUNK), BF16)
+    pair_reply = jax.ShapeDtypeStruct((2,) + reply.shape, BF16)
+    replies = pl.pallas_call(
+        functools.partial(attend_kernel, scale, groups, peers),
+        out_shape=(reply,) * 2 + (pair_reply,) * pairs,
         in_specs=[vmem_spec] * (2 + peers + blocks // 2),
-        out_specs=(vmem_spec,) * (peers - near + 1 + len(state)),
+        out_specs=(vmem_spec,) * (2 + pairs),
+        scratch_shapes=[pltpu.VMEM(keys_shape, BF16), pltpu.VMEM(keys_shape, BF16)],
         compiler_params=params,
         cost_estimate=pl.CostEstimate(
-            flops=3 * peers * pair_flops, bytes_accessed=20 * tok * width,
+            flops=8 * peers * tok * blocks * rows * CHUNK, bytes_accessed=10 * tok * width,
             transcendentals=heads * tok * blocks * rows,
         ),
         name="memory_attention",
     )(gate_cols, -local_part.reshape(heads, HEAD_DIM), *got, *memory)
-    far_replies, part, state = outs[: peers - near], outs[peers - near], outs[peers - near + 1 :]
-    sums = sum_over(sum_over(part, "z"), "sa")
-    *near_replies, terms = pl.pallas_call(
-        functools.partial(second_kernel, scale, near),
-        out_shape=(near_reply,) * near + (part_shape,),
-        in_specs=[vmem_spec] * (2 + len(state) + near),
-        out_specs=(vmem_spec,) * (near + 1),
-        compiler_params=params,
-        cost_estimate=pl.CostEstimate(
-            flops=2 * near * pair_flops, bytes_accessed=10 * tok * width, transcendentals=0
-        ),
-        name="memory_backward",
-    )(gate_cols, sums, *state, *got[:near])
-    far = exchange([None] * near + list(far_replies), PLANE, (6, 7, 4, 5))[near:]
-    core_reply, far = lax.optimization_barrier((near_replies[1], far))
-    near_replies[1] = core_reply
-    back = exchange(near_replies, PLANE, (2, 3, 1)) + far
-
-    parts = [x[2 * tok :, :HEAD_DIM].astype(F32) for x in back[1:near]]
-    sums = functools.reduce(jnp.add, parts, terms)
-    sums = jnp.sum((sums + send_xor(sums, PLANE, near))[:, :3], axis=1)
+    back = [replies[0], send_xor(replies[1], PLANE, 1)] + forward(across(replies[2:]))
+
+    rows_of = [x[2 * tok :, :HEAD_DIM] for x in back[:2]]
+    rows_of += [x[i % 2, 2 * tok :, :HEAD_DIM] for i, x in enumerate(back[2:])]
+    sums = functools.reduce(jnp.add, [x.astype(F32) for x in rows_of])
+    sums = jnp.sum(sum_over(sum_over(sums, "z"), "sa")[:, :3], axis=1)
     gate_grad = sums * gate * (1.0 - gate) / math.sqrt(tok * devices)
 
     out, d_query = pl.pallas_call(

time: 66.6 us -> 67.3 us (1.011)
  waiting for transfers between devices: 19.6 us -> 25.1 us
  starting transfers between devices: 27 us -> 22.4 us
    ppermute x22 -> x21, waiting for transfers between devices: 19.6 us -> 25.1 us  [send_xor(): lax.ppermute(array, axes, [(i, i ^ k) for i in range(lax.axis_size(axes))])]
    ppermute x22 -> x21, starting transfers between devices: 27 us -> 22.4 us  [send_xor(): lax.ppermute(array, axes, [(i, i ^ k) for i in range(lax.axis_size(axes))])]
    pallas_call x2 -> x1, Pallas kernels: 8.03 us -> 7.82 us  [body(): pl.pallas_call(functools.partial(attend_kernel, scale, groups, peers), ou...]
  transfers between devices with their start and end apart: 22 -> 21, of which waited for: 9 -> 9; matrix products, arithmetic and copies ran while one was open for 0% -> 0% of each run, Pallas kernels for 11% -> 9%
where the time goes in v4:
time: 67.3 us; the launch traced here: 67.1 us
  waiting for transfers between devices  25.1 us (37%)
  starting transfers between devices  22.4 us (33%)
  Pallas kernels  17.1 us (25%)
  local copies, waits for them, and re-layouts  1.02 us (2%)
  between operations  0.76 us (1%)
    ppermute x21, waiting for transfers between devices, send_xor(): lax.ppermute(array, axes, [(i, i ^ k) for i in range(lax.axis_size(axes))])  25.1 us
    ppermute x21, starting transfers between devices, send_xor(): lax.ppermute(array, axes, [(i, i ^ k) for i in range(lax.axis_size(axes))])  22.4 us
    pallas_call x1, Pallas kernels, body(): pl.pallas_call(functools.partial(attend_kernel, scale, groups, peers), ou...  7.82 us
    pallas_call x1, Pallas kernels, body(): pl.pallas_call(functools.partial(prologue_kernel, blocks), out_shape=(chu...  3.39 us
    pallas_call x1, Pallas kernels, body(): pl.pallas_call(functools.partial(local_forward_kernel, scale), grid=(step...  2.61 us
    pallas_call x1, Pallas kernels, body(): pl.pallas_call(functools.partial(local_backward_kernel, scale), grid=(ste...  2.02 us
  transfers between devices with their start and end apart: 21, of which 9 were waited for; matrix products, arithmetic and copies ran while one was open for 0% of the time, Pallas kernels for 9%

profile of v4, /device:TPU:0, one launch (start us, length us, event | category | flops | bytes accessed | tf_op | source)
XLA Modules:
  0.0 67.1 jit_solution(10889830272873730953)
XLA Ops:
  0.7 3.4 %chunks.1 = (bf16[2,128,256]{2,1,0:T(8,128)(2,1)}, bf16[2,128,256]{2,1,0:T(8,128)(2,1)}, bf16[272,256]{1,0:T(8,128)(2,1)}, bf16[272,256]{1,0:T(8,128)(2,1)}, bf1...) custom-call(bf16[128,2048]{1,0:T(8,128)(2,1)} %mk_hbm.1, ...), custom_call_target="tpu_custom_call" | custom-call | tf_op jit(solution)/shard_map/chunks/pallas_call | solution.py:293
  4.1 0.5 collective-permute-start
  4.6 1.2 %collective-permute-done.other_ref = bf16[2,128,256]{2,1,0:T(8,128)(2,1)S(1)} collective-permute-done((bf16[2,128,256]{2,1,0:T(8,128)(2,1)}, bf16[2,128,256]{2,1,0:T(8,128)(2,1)S(1)}, u32[]{:S(2)}, u32[]{:S(2)}) %collective-permute-start) | collective-permute-done | bytes 131104 | tf_op jit(solution)/shard_map/ppermute | solution.py:246
  5.8 0.9 %copy-done.4 = bf16[2,128,256]{2,1,0:T(8,128)(2,1)S(1)} copy-done((bf16[2,128,256]{2,1,0:T(8,128)(2,1)S(1)}, bf16[2,128,256]{2,1,0:T(8,128)(2,1)}, u32[]{:S(2)}) %copy-start.4) | copy-done | bytes 131096
  6.7 3.0 %collective-permute-start.2 = (bf16[2,2,128,256]{3,2,1,0:T(8,128)(2,1)S(1)}, bf16[2,2,128,256]{3,2,1,0:T(8,128)(2,1)S(1)}, u32[]{:S(2)}, u32[]{:S(2)}) collective-permute-start(bf16[2,2,128,256]{3,2,1,0:T(8,128)(2,1)S(1)} %join_cores.1.refs_8_), channel_id=1, source_target_pairs={{0,2},{2,0},{4,6},{6,4},{1,3},{3,1},{5,7},{7,5},{8,10},{10,8},{12,... | collective-permute-start | bytes 786440 | tf_op jit(solution)/shard_map/ppermute | solution.py:246
  9.7 2.6 %collective-permute-start.1 = (bf16[2,2,128,256]{3,2,1,0:T(8,128)(2,1)S(1)}, bf16[2,2,128,256]{3,2,1,0:T(8,128)(2,1)S(1)}, u32[]{:S(2)}, u32[]{:S(2)}) collective-permute-start(bf16[2,2,128,256]{3,2,1,0:T(8,128)(2,1)S(1)} %join_cores.1.refs_8_), channel_id=1, source_target_pairs={{0,4},{2,6},{4,0},{6,2},{1,5},{3,7},{5,1},{7,3},{8,12},{10,14},{12... | collective-permute-start | bytes 786440 | tf_op jit(solution)/shard_map/ppermute | solution.py:246
  12.3 0.7 %collective-permute-start.3 = (bf16[272,256]{1,0:T(8,128)(2,1)}, bf16[272,256]{1,0:T(8,128)(2,1)S(1)}, u32[]{:S(2)}, u32[]{:S(2)}) collective-permute-start(bf16[272,256]{1,0:T(8,128)(2,1)} %get-tuple-element.39), channel_id=1, source_target_pairs={{0,17},{1,16},{8,25},{9,24},{16,1},{17,0},{24,9},{25,8},{2,19},{3,... | collective-permute-start | bytes 417800 | tf_op jit(solution)/shard_map/ppermute | solution.py:246
  13.0 1.7 %collective-permute-start.4 = (bf16[272,256]{1,0:T(8,128)(2,1)}, bf16[272,256]{1,0:T(8,128)(2,1)S(1)}, u32[]{:S(2)}, u32[]{:S(2)}) collective-permute-start(bf16[272,256]{1,0:T(8,128)(2,1)} %get-tuple-element.40), channel_id=1, source_target_pairs={{0,24},{1,25},{8,16},{9,17},{16,8},{17,9},{24,0},{25,1},{2,26},{3,... | collective-permute-start | bytes 417800 | tf_op jit(solution)/shard_map/ppermute | solution.py:246
  14.8 1.5 %collective-permute-start.5 = (bf16[272,256]{1,0:T(8,128)(2,1)}, bf16[272,256]{1,0:T(8,128)(2,1)S(1)}, u32[]{:S(2)}, u32[]{:S(2)}) collective-permute-start(bf16[272,256]{1,0:T(8,128)(2,1)} %get-tuple-element.41), channel_id=1, source_target_pairs={{0,25},{1,24},{8,17},{9,16},{16,9},{17,8},{24,1},{25,0},{2,27},{3,... | collective-permute-start | bytes 417800 | tf_op jit(solution)/shard_map/ppermute | solution.py:246
  16.3 2.6 %local_forward.1 = (f32[128,2048]{1,0:T(8,128)S(1)}, bf16[16,128,128]{2,1,0:T(8,128)(2,1)S(1)}, f32[4,4,128]{2,1,0:T(4,128)S(1)}) custom-call(bf16[128,2048]{1,0:T(8,128)(2,1)S(1)} %copy-done.1, bf16[128,2048]{1,0:T(8,128)(2,1)S(1)} %copy-done.2, bf16[128,2048]{1,0:T(8,128)(2,1)S(1)} %copy-done.3, bf16[128,2048]{1,0:T(8,128)(2,1)S(1)} %copy-done), custom_call_target="tpu_custom_call" | custom-call | flops 134217728 | bytes 3145728 | tf_op jit(solution)/shard_map/local_forward/pallas_call | solution.py:317
  18.9 5.5 %collective-permute-done.3.refs_5_ = bf16[272,256]{1,0:T(8,128)(2,1)S(1)} collective-permute-done((bf16[272,256]{1,0:T(8,128)(2,1)}, bf16[272,256]{1,0:T(8,128)(2,1)S(1)}, u32[]{:S(2)}, u32[]{:S(2)}) %collective-permute-start.3) | collective-permute-done | bytes 139296 | tf_op jit(solution)/shard_map/ppermute | solution.py:246
  24.4 0.5 collective-permute-start.6
  24.9 1.6 %collective-permute-start.8 = (bf16[272,256]{1,0:T(8,128)(2,1)S(1)}, bf16[272,256]{1,0:T(8,128)(2,1)S(1)}, u32[]{:S(2)}, u32[]{:S(2)}) collective-permute-start(bf16[272,256]{1,0:T(8,128)(2,1)S(1)} %copy-done.8), channel_id=1, source_target_pairs={{0,8},{1,9},{8,0},{9,1},{16,24},{17,25},{24,16},{25,17},{2,10},{3,... | collective-permute-start | bytes 417800 | tf_op jit(solution)/shard_map/ppermute | solution.py:246
  26.5 0.3 collective-permute-start.9
  26.8 1.4 %collective-permute-start.10 = (bf16[272,256]{1,0:T(8,128)(2,1)S(1)}, bf16[272,256]{1,0:T(8,128)(2,1)S(1)}, u32[]{:S(2)}, u32[]{:S(2)}) collective-permute-start(bf16[272,256]{1,0:T(8,128)(2,1)S(1)} %copy-done.6), channel_id=1, source_target_pairs={{0,16},{1,17},{8,24},{9,25},{16,0},{17,1},{24,8},{25,9},{2,18},{3,... | collective-permute-start | bytes 417800 | tf_op jit(solution)/shard_map/ppermute | solution.py:246
  28.3 2.0 %local_backward.1 = (bf16[128,2048]{1,0:T(8,128)(2,1)S(1)}, bf16[128,2048]{1,0:T(8,128)(2,1)S(1)}) custom-call(bf16[128,2048]{1,0:T(8,128)(2,1)S(1)} %copy-done.2, bf16[128,2048]{1,0:T(8,128)(2,1)S(1)} %copy-done.3, bf16[128,2048]{1,0:T(8,128)(2,1)S(1)} %copy-done, f32[1,2048]{1,0:T(1,128)S(1)} %bitcast.33, f32[128,2048]{1,0:T(8,128)S(1)} %get-tuple-element.45.out_ref, ...), custom_call_target="tpu_custom_call" | custom-call | flops 134217728 | bytes 4194304 | tf_op jit(solution)/shard_map/local_backward/pallas_call | solution.py:346
  30.3 2.5 %collective-permute-done.6.refs_11_ = bf16[2,2,128,256]{3,2,1,0:T(8,128)(2,1)S(1)} collective-permute-done((bf16[2,2,128,256]{3,2,1,0:T(8,128)(2,1)S(1)}, bf16[2,2,128,256]{3,2,1,0:T(8,128)(2,1)S(1)}, u32[]{:S(2)}, u32[]{:S(2)}) %collective-permute-start.6) | collective-permute-done | bytes 262176 | tf_op jit(solution)/shard_map/ppermute | solution.py:246
  32.8 0.7 %collective-permute-done.9.refs_3_ = bf16[272,256]{1,0:T(8,128)(2,1)S(1)} collective-permute-done((bf16[272,256]{1,0:T(8,128)(2,1)S(1)}, bf16[272,256]{1,0:T(8,128)(2,1)S(1)}, u32[]{:S(2)}, u32[]{:S(2)}) %collective-permute-start.9) | collective-permute-done | bytes 139296 | tf_op jit(solution)/shard_map/ppermute | solution.py:246
  33.5 7.8 %memory_attention.1 = (bf16[272,256]{1,0:T(8,128)(2,1)S(1)}, bf16[272,256]{1,0:T(8,128)(2,1)S(1)}, bf16[2,272,256]{2,1,0:T(8,128)(2,1)S(1)}, bf16[2,272,256]{2,1,0:T(8,128)(2,1)S(1)}, bf16[2,272,256]{2,1,0:T(8,128)(2,1)S(1)}) custom-call(f32[1,2048]{1,0:T(1,128)S(1)} %bitcast.34, f32[16,128]{1,0:T(8,128)S(1)} %bitcast.35, bf16[272,256]{1,0:T(8,128)(2,1)S(1)} %copy-done.5, ...), custom_call_target="tpu_custom_call" | custom-call | flops 2147483648 | bytes 2621440 | tf_op jit(solution)/shard_map/memory_attention/pallas_call | solution.py:366
  41.4 1.5 %collective-permute-start.12 = (bf16[2,272,256]{2,1,0:T(8,128)(2,1)S(1)}, bf16[2,272,256]{2,1,0:T(8,128)(2,1)S(1)}, u32[]{:S(2)}, u32[]{:S(2)}) collective-permute-start(bf16[2,272,256]{2,1,0:T(8,128)(2,1)S(1)} %get-tuple-element.66), channel_id=1, source_target_pairs={{0,8},{1,9},{8,0},{9,1},{16,24},{17,25},{24,16},{25,17},{2,10},{3,... | collective-permute-start | bytes 835592 | tf_op jit(solution)/shard_map/ppermute | solution.py:246
  42.9 1.4 %collective-permute-start.14 = (bf16[2,272,256]{2,1,0:T(8,128)(2,1)S(1)}, bf16[2,272,256]{2,1,0:T(8,128)(2,1)S(1)}, u32[]{:S(2)}, u32[]{:S(2)}) collective-permute-start(bf16[2,272,256]{2,1,0:T(8,128)(2,1)S(1)} %get-tuple-element.67), channel_id=1, source_target_pairs={{0,16},{1,17},{8,24},{9,25},{16,0},{17,1},{24,8},{25,9},{2,18},{3,... | collective-permute-start | bytes 835592 | tf_op jit(solution)/shard_map/ppermute | solution.py:246
  44.3 0.6 collective-permute-start.16
  44.9 6.0 %collective-permute-done.12.refs_2_ = bf16[2,272,256]{2,1,0:T(8,128)(2,1)S(1)} collective-permute-done((bf16[2,272,256]{2,1,0:T(8,128)(2,1)S(1)}, bf16[2,272,256]{2,1,0:T(8,128)(2,1)S(1)}, u32[]{:S(2)}, u32[]{:S(2)}) %collective-permute-start.12) | collective-permute-done | bytes 278560 | tf_op jit(solution)/shard_map/ppermute | solution.py:246
  50.9 6.5 %collective-permute-done.14.refs_4_ = bf16[2,272,256]{2,1,0:T(8,128)(2,1)S(1)} collective-permute-done((bf16[2,272,256]{2,1,0:T(8,128)(2,1)S(1)}, bf16[2,272,256]{2,1,0:T(8,128)(2,1)S(1)}, u32[]{:S(2)}, u32[]{:S(2)}) %collective-permute-start.14) | collective-permute-done | bytes 278560 | tf_op jit(solution)/shard_map/ppermute | solution.py:246
  57.5 0.5 collective-permute-start.17
  58.0 1.6 %collective-permute-done.11.refs_1_ = bf16[272,256]{1,0:T(8,128)(2,1)S(1)} collective-permute-done((bf16[272,256]{1,0:T(8,128)(2,1)S(1)}, bf16[272,256]{1,0:T(8,128)(2,1)S(1)}, u32[]{:S(2)}, u32[]{:S(2)}) %collective-permute-start.11) | collective-permute-done | bytes 139296 | tf_op jit(solution)/shard_map/ppermute | solution.py:246
  59.7 2.0 %collective-permute-start.20 = (f32[16,128]{1,0:T(8,128)S(1)}, f32[16,128]{1,0:T(8,128)S(1)}, u32[]{:S(2)}, u32[]{:S(2)}) collective-permute-start(f32[16,128]{1,0:T(8,128)S(1)} %convert_add_fusion), channel_id=1, source_target_pairs={{0,6},{2,4},{4,2},{6,0},{1,7},{3,5},{5,3},{7,1},{8,14},{10,12},{12... | collective-permute-start | bytes 24584 | tf_op jit(solution)/shard_map/ppermute | solution.py:246
  61.6 1.1 %collective-permute-start.19 = (f32[16,128]{1,0:T(8,128)S(1)}, f32[16,128]{1,0:T(8,128)S(1)}, u32[]{:S(2)}, u32[]{:S(2)}) collective-permute-start(f32[16,128]{1,0:T(8,128)S(1)} %convert_add_fusion), channel_id=1, source_target_pairs={{0,4},{2,6},{4,0},{6,2},{1,5},{3,7},{5,1},{7,3},{8,12},{10,14},{12... | collective-permute-start | bytes 24584 | tf_op jit(solution)/shard_map/ppermute | solution.py:246
  62.8 1.4 %collective-permute-start.18 = (f32[16,128]{1,0:T(8,128)S(1)}, f32[16,128]{1,0:T(8,128)S(1)}, u32[]{:S(2)}, u32[]{:S(2)}) collective-permute-start(f32[16,128]{1,0:T(8,128)S(1)} %convert_add_fusion), channel_id=1, source_target_pairs={{0,2},{2,0},{4,6},{6,4},{1,3},{3,1},{5,7},{7,5},{8,10},{10,8},{12,... | collective-permute-start | bytes 24584 | tf_op jit(solution)/shard_map/ppermute | solution.py:246
  64.1 1.3 %merge.1 = (bf16[128,2048]{1,0:T(8,128)(2,1)}, bf16[128,2048]{1,0:T(8,128)(2,1)}) custom-call(bf16[128,2048]{1,0:T(8,128)(2,1)S(1)} %get-tuple-element.49.lo_ref, bf16[128,2048]{1,0:T(8,128)(2,1)S(1)} %get-tuple-element.50.ldq_ref, bf16[272,256]{1,0:T(8,128)(2,1)S(1)} %get-tuple-element.64.refs_0_, bf16[272,256]{1,0:T(8,128)(2,1)S(1)} %collective-permute-done.11.refs_1_, ...), custom_call_target="tpu_custom_call" | custom-call | tf_op jit(solution)/shard_map/merge/pallas_call | solution.py:387
  65.4 0.8 %collective-permute-done.19 = f32[16,128]{1,0:T(8,128)S(1)} collective-permute-done((f32[16,128]{1,0:T(8,128)S(1)}, f32[16,128]{1,0:T(8,128)S(1)}, u32[]{:S(2)}, u32[]{:S(2)}) %collective-permute-start.19) | collective-permute-done | bytes 8224 | tf_op jit(solution)/shard_map/ppermute | solution.py:246
  66.5 0.5 multiply_multiply_fusion
  (44 shorter events, 0.5 us)
Async XLA Ops:
  0.6 15.6 %copy-start.1 = (bf16[128,2048]{1,0:T(8,128)(2,1)S(1)}, bf16[128,2048]{1,0:T(8,128)(2,1)}, u32[]{:S(2)}) copy-start(bf16[128,2048]{1,0:T(8,128)(2,1)} %q_ref.1) | copy-start | bytes 1572868
  0.6 15.6 %copy-start.2 = (bf16[128,2048]{1,0:T(8,128)(2,1)S(1)}, bf16[128,2048]{1,0:T(8,128)(2,1)}, u32[]{:S(2)}) copy-start(bf16[128,2048]{1,0:T(8,128)(2,1)} %k_ref.3) | copy-start | bytes 1572868
  0.7 15.6 %copy-start.3 = (bf16[128,2048]{1,0:T(8,128)(2,1)S(1)}, bf16[128,2048]{1,0:T(8,128)(2,1)}, u32[]{:S(2)}) copy-start(bf16[128,2048]{1,0:T(8,128)(2,1)} %v_ref.3) | copy-start | bytes 1572868
  4.1 12.2 %copy-start = (bf16[128,2048]{1,0:T(8,128)(2,1)S(1)}, bf16[128,2048]{1,0:T(8,128)(2,1)}, u32[]{:S(2)}) copy-start(bf16[128,2048]{1,0:T(8,128)(2,1)} %g_ref.3) | copy-start | bytes 1572868
  4.1 1.7 %collective-permute-start = (bf16[2,128,256]{2,1,0:T(8,128)(2,1)}, bf16[2,128,256]{2,1,0:T(8,128)(2,1)S(1)}, u32[]{:S(2)}, u32[]{:S(2)}) collective-permute-start(bf16[2,128,256]{2,1,0:T(8,128)(2,1)} %get-tuple-element.38), channel_id=1, source_target_pairs={{0,1},{1,0},{2,3},{3,2},{4,5},{5,4},{6,7},{7,6},{8,9},{9,8},{10,11... | collective-permute-start | bytes 393224 | tf_op jit(solution)/shard_map/ppermute | solution.py:246
  5.8 0.9 %copy-start.4 = (bf16[2,128,256]{2,1,0:T(8,128)(2,1)S(1)}, bf16[2,128,256]{2,1,0:T(8,128)(2,1)}, u32[]{:S(2)}) copy-start(bf16[2,128,256]{2,1,0:T(8,128)(2,1)} %get-tuple-element.37.mine_ref) | copy-start | bytes 393220
  6.7 17.7 %collective-permute-start.2 = (bf16[2,2,128,256]{3,2,1,0:T(8,128)(2,1)S(1)}, bf16[2,2,128,256]{3,2,1,0:T(8,128)(2,1)S(1)}, u32[]{:S(2)}, u32[]{:S(2)}) collective-permute-start(bf16[2,2,128,256]{3,2,1,0:T(8,128)(2,1)S(1)} %join_cores.1.refs_8_), channel_id=1, source_target_pairs={{0,2},{2,0},{4,6},{6,4},{1,3},{3,1},{5,7},{7,5},{8,10},{10,8},{12,... | collective-permute-start | bytes 786440 | tf_op jit(solution)/shard_map/ppermute | solution.py:246
  9.7 14.7 %collective-permute-start.1 = (bf16[2,2,128,256]{3,2,1,0:T(8,128)(2,1)S(1)}, bf16[2,2,128,256]{3,2,1,0:T(8,128)(2,1)S(1)}, u32[]{:S(2)}, u32[]{:S(2)}) collective-permute-start(bf16[2,2,128,256]{3,2,1,0:T(8,128)(2,1)S(1)} %join_cores.1.refs_8_), channel_id=1, source_target_pairs={{0,4},{2,6},{4,0},{6,2},{1,5},{3,7},{5,1},{7,3},{8,12},{10,14},{12... | collective-permute-start | bytes 786440 | tf_op jit(solution)/shard_map/ppermute | solution.py:246
  12.3 12.1 %collective-permute-start.3 = (bf16[272,256]{1,0:T(8,128)(2,1)}, bf16[272,256]{1,0:T(8,128)(2,1)S(1)}, u32[]{:S(2)}, u32[]{:S(2)}) collective-permute-start(bf16[272,256]{1,0:T(8,128)(2,1)} %get-tuple-element.39), channel_id=1, source_target_pairs={{0,17},{1,16},{8,25},{9,24},{16,1},{17,0},{24,9},{25,8},{2,19},{3,... | collective-permute-start | bytes 417800 | tf_op jit(solution)/shard_map/ppermute | solution.py:246
  13.0 11.4 %collective-permute-start.4 = (bf16[272,256]{1,0:T(8,128)(2,1)}, bf16[272,256]{1,0:T(8,128)(2,1)S(1)}, u32[]{:S(2)}, u32[]{:S(2)}) collective-permute-start(bf16[272,256]{1,0:T(8,128)(2,1)} %get-tuple-element.40), channel_id=1, source_target_pairs={{0,24},{1,25},{8,16},{9,17},{16,8},{17,9},{24,0},{25,1},{2,26},{3,... | collective-permute-start | bytes 417800 | tf_op jit(solution)/shard_map/ppermute | solution.py:246
  14.8 10.2 %copy-start.9 = (bf16[272,256]{1,0:T(8,128)(2,1)S(1)}, bf16[272,256]{1,0:T(8,128)(2,1)}, u32[]{:S(2)}) copy-start(bf16[272,256]{1,0:T(8,128)(2,1)} %get-tuple-element.53) | copy-start | bytes 417796
  14.8 10.2 %copy-start.8 = (bf16[272,256]{1,0:T(8,128)(2,1)S(1)}, bf16[272,256]{1,0:T(8,128)(2,1)}, u32[]{:S(2)}) copy-start(bf16[272,256]{1,0:T(8,128)(2,1)} %get-tuple-element.54) | copy-start | bytes 417796
  14.8 11.7 %copy-start.7 = (bf16[272,256]{1,0:T(8,128)(2,1)S(1)}, bf16[272,256]{1,0:T(8,128)(2,1)}, u32[]{:S(2)}) copy-start(bf16[272,256]{1,0:T(8,128)(2,1)} %get-tuple-element.55) | copy-start | bytes 417796
  14.8 12.0 %copy-start.6 = (bf16[272,256]{1,0:T(8,128)(2,1)S(1)}, bf16[272,256]{1,0:T(8,128)(2,1)}, u32[]{:S(2)}) copy-start(bf16[272,256]{1,0:T(8,128)(2,1)} %get-tuple-element.56) | copy-start | bytes 417796
  14.8 9.6 %collective-permute-start.5 = (bf16[272,256]{1,0:T(8,128)(2,1)}, bf16[272,256]{1,0:T(8,128)(2,1)S(1)}, u32[]{:S(2)}, u32[]{:S(2)}) collective-permute-start(bf16[272,256]{1,0:T(8,128)(2,1)} %get-tuple-element.41), channel_id=1, source_target_pairs={{0,25},{1,24},{8,17},{9,16},{16,9},{17,8},{24,1},{25,0},{2,27},{3,... | collective-permute-start | bytes 417800 | tf_op jit(solution)/shard_map/ppermute | solution.py:246
  24.4 8.4 %collective-permute-start.6 = (bf16[2,2,128,256]{3,2,1,0:T(8,128)(2,1)S(1)}, bf16[2,2,128,256]{3,2,1,0:T(8,128)(2,1)S(1)}, u32[]{:S(2)}, u32[]{:S(2)}) collective-permute-start(bf16[2,2,128,256]{3,2,1,0:T(8,128)(2,1)S(1)} %collective-permute-done.1.refs_10_), channel_id=1, source_target_pairs={{0,2},{2,0},{4,6},{6,4},{1,3},{3,1},{5,7},{7,5},{8,10},{10,8},{12,... | collective-permute-start | bytes 786440 | tf_op jit(solution)/shard_map/ppermute | solution.py:246
  24.9 7.9 %collective-permute-start.7 = (bf16[272,256]{1,0:T(8,128)(2,1)S(1)}, bf16[272,256]{1,0:T(8,128)(2,1)S(1)}, u32[]{:S(2)}, u32[]{:S(2)}) collective-permute-start(bf16[272,256]{1,0:T(8,128)(2,1)S(1)} %copy-done.9), channel_id=1, source_target_pairs={{0,1},{1,0},{8,9},{9,8},{16,17},{17,16},{24,25},{25,24},{2,3},{3,2... | collective-permute-start | bytes 417800 | tf_op jit(solution)/shard_map/ppermute | solution.py:246
  24.9 7.9 %collective-permute-start.8 = (bf16[272,256]{1,0:T(8,128)(2,1)S(1)}, bf16[272,256]{1,0:T(8,128)(2,1)S(1)}, u32[]{:S(2)}, u32[]{:S(2)}) collective-permute-start(bf16[272,256]{1,0:T(8,128)(2,1)S(1)} %copy-done.8), channel_id=1, source_target_pairs={{0,8},{1,9},{8,0},{9,1},{16,24},{17,25},{24,16},{25,17},{2,10},{3,... | collective-permute-start | bytes 417800 | tf_op jit(solution)/shard_map/ppermute | solution.py:246
  26.5 1.7 %copy-start.10 = (f32[16]{0:T(128)S(1)}, f32[16]{0:T(128)}, u32[]{:S(2)}) copy-start(f32[16]{0:T(128)} %param.14) | copy-start | bytes 196
  26.5 7.0 %collective-permute-start.9 = (bf16[272,256]{1,0:T(8,128)(2,1)S(1)}, bf16[272,256]{1,0:T(8,128)(2,1)S(1)}, u32[]{:S(2)}, u32[]{:S(2)}) collective-permute-start(bf16[272,256]{1,0:T(8,128)(2,1)S(1)} %copy-done.7), channel_id=1, source_target_pairs={{0,9},{1,8},{8,1},{9,0},{16,25},{17,24},{24,17},{25,16},{2,11},{3,... | collective-permute-start | bytes 417800 | tf_op jit(solution)/shard_map/ppermute | solution.py:246
  26.8 6.7 %collective-permute-start.10 = (bf16[272,256]{1,0:T(8,128)(2,1)S(1)}, bf16[272,256]{1,0:T(8,128)(2,1)S(1)}, u32[]{:S(2)}, u32[]{:S(2)}) collective-permute-start(bf16[272,256]{1,0:T(8,128)(2,1)S(1)} %copy-done.6), channel_id=1, source_target_pairs={{0,16},{1,17},{8,24},{9,25},{16,0},{17,1},{24,8},{25,9},{2,18},{3,... | collective-permute-start | bytes 417800 | tf_op jit(solution)/shard_map/ppermute | solution.py:246
  28.3 5.3 %copy-start.5 = (bf16[272,256]{1,0:T(8,128)(2,1)S(1)}, bf16[272,256]{1,0:T(8,128)(2,1)}, u32[]{:S(2)}) copy-start(bf16[272,256]{1,0:T(8,128)(2,1)} %get-tuple-element.52.refs_0_) | copy-start | bytes 417796
  41.4 9.6 %collective-permute-start.12 = (bf16[2,272,256]{2,1,0:T(8,128)(2,1)S(1)}, bf16[2,272,256]{2,1,0:T(8,128)(2,1)S(1)}, u32[]{:S(2)}, u32[]{:S(2)}) collective-permute-start(bf16[2,272,256]{2,1,0:T(8,128)(2,1)S(1)} %get-tuple-element.66), channel_id=1, source_target_pairs={{0,8},{1,9},{8,0},{9,1},{16,24},{17,25},{24,16},{25,17},{2,10},{3,... | collective-permute-start | bytes 835592 | tf_op jit(solution)/shard_map/ppermute | solution.py:246
  42.9 14.6 %collective-permute-start.14 = (bf16[2,272,256]{2,1,0:T(8,128)(2,1)S(1)}, bf16[2,272,256]{2,1,0:T(8,128)(2,1)S(1)}, u32[]{:S(2)}, u32[]{:S(2)}) collective-permute-start(bf16[2,272,256]{2,1,0:T(8,128)(2,1)S(1)} %get-tuple-element.67), channel_id=1, source_target_pairs={{0,16},{1,17},{8,24},{9,25},{16,0},{17,1},{24,8},{25,9},{2,18},{3,... | collective-permute-start | bytes 835592 | tf_op jit(solution)/shard_map/ppermute | solution.py:246
  44.3 13.1 %collective-permute-start.16 = (bf16[2,272,256]{2,1,0:T(8,128)(2,1)S(1)}, bf16[2,272,256]{2,1,0:T(8,128)(2,1)S(1)}, u32[]{:S(2)}, u32[]{:S(2)}) collective-permute-start(bf16[2,272,256]{2,1,0:T(8,128)(2,1)S(1)} %get-tuple-element.68), channel_id=1, source_target_pairs={{0,24},{1,25},{8,16},{9,17},{16,8},{17,9},{24,0},{25,1},{2,26},{3,... | collective-permute-start | bytes 835592 | tf_op jit(solution)/shard_map/ppermute | solution.py:246
  50.9 8.7 %collective-permute-start.13 = (bf16[2,272,256]{2,1,0:T(8,128)(2,1)S(1)}, bf16[2,272,256]{2,1,0:T(8,128)(2,1)S(1)}, u32[]{:S(2)}, u32[]{:S(2)}) collective-permute-start(bf16[2,272,256]{2,1,0:T(8,128)(2,1)S(1)} %collective-permute-done.12.refs_2_), channel_id=1, source_target_pairs={{0,1},{1,0},{8,9},{9,8},{16,17},{17,16},{24,25},{25,24},{2,3},{3,2... | collective-permute-start | bytes 835592 | tf_op jit(solution)/shard_map/ppermute | solution.py:246
  57.5 2.2 %collective-permute-start.15 = (bf16[2,272,256]{2,1,0:T(8,128)(2,1)S(1)}, bf16[2,272,256]{2,1,0:T(8,128)(2,1)S(1)}, u32[]{:S(2)}, u32[]{:S(2)}) collective-permute-start(bf16[2,272,256]{2,1,0:T(8,128)(2,1)S(1)} %collective-permute-done.14.refs_4_), channel_id=1, source_target_pairs={{0,1},{1,0},{8,9},{9,8},{16,17},{17,16},{24,25},{25,24},{2,3},{3,2... | collective-permute-start | bytes 835592 | tf_op jit(solution)/shard_map/ppermute | solution.py:246
  57.5 2.2 %collective-permute-start.17 = (bf16[2,272,256]{2,1,0:T(8,128)(2,1)S(1)}, bf16[2,272,256]{2,1,0:T(8,128)(2,1)S(1)}, u32[]{:S(2)}, u32[]{:S(2)}) collective-permute-start(bf16[2,272,256]{2,1,0:T(8,128)(2,1)S(1)} %collective-permute-done.16.refs_6_), channel_id=1, source_target_pairs={{0,1},{1,0},{8,9},{9,8},{16,17},{17,16},{24,25},{25,24},{2,3},{3,2... | collective-permute-start | bytes 835592 | tf_op jit(solution)/shard_map/ppermute | solution.py:246
  58.0 1.6 %collective-permute-start.11 = (bf16[272,256]{1,0:T(8,128)(2,1)S(1)}, bf16[272,256]{1,0:T(8,128)(2,1)S(1)}, u32[]{:S(2)}, u32[]{:S(2)}) collective-permute-start(bf16[272,256]{1,0:T(8,128)(2,1)S(1)} %get-tuple-element.65), channel_id=1, source_target_pairs={{0,1},{1,0},{8,9},{9,8},{16,17},{17,16},{24,25},{25,24},{2,3},{3,2... | collective-permute-start | bytes 417800 | tf_op jit(solution)/shard_map/ppermute | solution.py:246
  59.7 5.7 %collective-permute-start.20 = (f32[16,128]{1,0:T(8,128)S(1)}, f32[16,128]{1,0:T(8,128)S(1)}, u32[]{:S(2)}, u32[]{:S(2)}) collective-permute-start(f32[16,128]{1,0:T(8,128)S(1)} %convert_add_fusion), channel_id=1, source_target_pairs={{0,6},{2,4},{4,2},{6,0},{1,7},{3,5},{5,3},{7,1},{8,14},{10,12},{12... | collective-permute-start | bytes 24584 | tf_op jit(solution)/shard_map/ppermute | solution.py:246
  61.6 4.5 %collective-permute-start.19 = (f32[16,128]{1,0:T(8,128)S(1)}, f32[16,128]{1,0:T(8,128)S(1)}, u32[]{:S(2)}, u32[]{:S(2)}) collective-permute-start(f32[16,128]{1,0:T(8,128)S(1)} %convert_add_fusion), channel_id=1, source_target_pairs={{0,4},{2,6},{4,0},{6,2},{1,5},{3,7},{5,1},{7,3},{8,12},{10,14},{12... | collective-permute-start | bytes 24584 | tf_op jit(solution)/shard_map/ppermute | solution.py:246
  62.8 3.7 %collective-permute-start.18 = (f32[16,128]{1,0:T(8,128)S(1)}, f32[16,128]{1,0:T(8,128)S(1)}, u32[]{:S(2)}, u32[]{:S(2)}) collective-permute-start(f32[16,128]{1,0:T(8,128)S(1)} %convert_add_fusion), channel_id=1, source_target_pairs={{0,2},{2,0},{4,6},{6,4},{1,3},{3,1},{5,7},{7,5},{8,10},{10,8},{12,... | collective-permute-start | bytes 24584 | tf_op jit(solution)/shard_map/ppermute | solution.py:246

commit v5 on v4

--- a/solution.py
+++ b/solution.py
@@ -152,13 +152,13 @@
 
 
 def attend_kernel(scale, groups, peers, gate_ref, before_ref, *refs):
-    *refs, k_all, v_all = refs
+    *refs, part_ref, k_all, v_all = refs
     got, refs = refs[:peers], refs[peers:]
     pairs = peers // 2 - 1
     mem_refs, back = refs[: -pairs - 2], packets_of(refs[-pairs - 2 :])
     rows = mem_refs[0].shape[2]
     heads = before_ref.shape[0]
-    tok = (back[0].shape[0] - heads) // 2
+    tok = back[0].shape[0] // 2
     extra = got[0].shape[0] - 2 * tok
     lane = lax.broadcasted_iota(jnp.int32, (rows, HEAD_DIM), 1)
     for h in range(PAIR):
@@ -220,14 +220,7 @@
     total = before_ref[...]
     for h in range(PAIR):
         total = total + jnp.where(head == plane_index() * PAIR + h, parts[h], 0.0)
-    total = jnp.sum(total, axis=1, keepdims=True)
-    high = total.astype(BF16).astype(F32)
-    middle = (total - high).astype(BF16).astype(F32)
-    low = total - high - middle
-    lane = lax.broadcasted_iota(jnp.int32, (heads, CHUNK), 1)
-    terms = jnp.where(lane == 0, high, jnp.where(lane == 1, middle, jnp.where(lane == 2, low, 0.0)))
-    for reply in back:
-        reply[2 * tok :, :] = terms.astype(BF16)
+    part_ref[...] = total
 
 
 def merge_kernel(lo_ref, ldq_ref, *refs):
@@ -361,13 +354,15 @@
 
     keys_shape = (PAIR, blocks * rows, CHUNK)
 
-    reply = jax.ShapeDtypeStruct((2 * tok + heads, CHUNK), BF16)
+    reply = jax.ShapeDtypeStruct((2 * tok, CHUNK), BF16)
     pair_reply = jax.ShapeDtypeStruct((2,) + reply.shape, BF16)
-    replies = pl.pallas_call(
+    *replies, part = pl.pallas_call(
         functools.partial(attend_kernel, scale, groups, peers),
-        out_shape=(reply,) * 2 + (pair_reply,) * pairs,
+        out_shape=(reply,) * 2
+        + (pair_reply,) * pairs
+        + (jax.ShapeDtypeStruct((heads, HEAD_DIM), F32),),
         in_specs=[vmem_spec] * (2 + peers + blocks // 2),
-        out_specs=(vmem_spec,) * (2 + pairs),
+        out_specs=(vmem_spec,) * (3 + pairs),
         scratch_shapes=[pltpu.VMEM(keys_shape, BF16), pltpu.VMEM(keys_shape, BF16)],
         compiler_params=params,
         cost_estimate=pl.CostEstimate(
@@ -376,12 +371,15 @@
         ),
         name="memory_attention",
     )(gate_cols, -local_part.reshape(heads, HEAD_DIM), *got, *memory)
-    back = [replies[0], send_xor(replies[1], PLANE, 1)] + forward(across(replies[2:]))
-
-    rows_of = [x[2 * tok :, :HEAD_DIM] for x in back[:2]]
-    rows_of += [x[i % 2, 2 * tok :, :HEAD_DIM] for i, x in enumerate(back[2:])]
-    sums = functools.reduce(jnp.add, [x.astype(F32) for x in rows_of])
-    sums = jnp.sum(sum_over(sum_over(sums, "z"), "sa")[:, :3], axis=1)
+    arrived = across(replies[2:])
+    core_back = send_xor(replies[1], PLANE, 1)
+    core_back, arrived[0] = lax.optimization_barrier((core_back, arrived[0]))
+    back = [replies[0], core_back] + forward(arrived)
+
+    sums = sum_over(sum_over(part, "z"), "sa")
+    for step in (1, 2, 4):
+        sums = sums + send_xor(sums, PLANE, step)
+    sums = jnp.sum(sums, axis=1)
     gate_grad = sums * gate * (1.0 - gate) / math.sqrt(tok * devices)
 
     out, d_query = pl.pallas_call(

time: 67.3 us -> 63.2 us (0.939)
  waiting for transfers between devices: 25.1 us -> 17.7 us
  starting transfers between devices: 22.4 us -> 25.7 us
    ppermute x21 -> x24, waiting for transfers between devices: 25.1 us -> 17.7 us  [send_xor(): lax.ppermute(array, axes, [(i, i ^ k) for i in range(lax.axis_size(axes))])]
    ppermute x21 -> x24, starting transfers between devices: 22.4 us -> 25.7 us  [send_xor(): lax.ppermute(array, axes, [(i, i ^ k) for i in range(lax.axis_size(axes))])]
  transfers between devices with their start and end apart: 21 -> 24, of which waited for: 9 -> 9; matrix products, arithmetic and copies ran while one was open for 0% -> 1% of each run, Pallas kernels for 9% -> 7%
where the time goes in v5:
time: 63.2 us; the launch traced here: 63 us
  starting transfers between devices  25.7 us (41%)
  waiting for transfers between devices  17.7 us (28%)
  Pallas kernels  17.1 us (27%)
  local copies, waits for them, and re-layouts  1.02 us (2%)
  between operations  0.77 us (1%)
  other arithmetic  0.67 us (1%)
    ppermute x24, starting transfers between devices, send_xor(): lax.ppermute(array, axes, [(i, i ^ k) for i in range(lax.axis_size(axes))])  25.7 us
    ppermute x24, waiting for transfers between devices, send_xor(): lax.ppermute(array, axes, [(i, i ^ k) for i in range(lax.axis_size(axes))])  17.7 us
    pallas_call x1, Pallas kernels, body(): pl.pallas_call(functools.partial(attend_kernel, scale, groups, peers), ou...  7.83 us
    pallas_call x1, Pallas kernels, body(): pl.pallas_call(functools.partial(prologue_kernel, blocks), out_shape=(chu...  3.41 us
    pallas_call x1, Pallas kernels, body(): pl.pallas_call(functools.partial(local_forward_kernel, scale), grid=(step...  2.61 us
    pallas_call x1, Pallas kernels, body(): pl.pallas_call(functools.partial(local_backward_kernel, scale), grid=(ste...  2.01 us
    pallas_call x1, Pallas kernels, body(): pl.pallas_call(merge_kernel, out_shape=(whole, whole), in_specs=[vmem_spe...  1.27 us
  transfers between devices with their start and end apart: 24, of which 9 were waited for; matrix products, arithmetic and copies ran while one was open for 1% of the time, Pallas kernels for 7%

profile of v5, /device:TPU:0, one launch (start us, length us, event | category | flops | bytes accessed | tf_op | source)
XLA Modules:
  0.0 63.0 jit_solution(1507073100433030210)
XLA Ops:
  0.7 3.4 %chunks.1 = (bf16[2,128,256]{2,1,0:T(8,128)(2,1)}, bf16[2,128,256]{2,1,0:T(8,128)(2,1)}, bf16[272,256]{1,0:T(8,128)(2,1)}, bf16[272,256]{1,0:T(8,128)(2,1)}, bf1...) custom-call(bf16[128,2048]{1,0:T(8,128)(2,1)} %mk_hbm.1, ...), custom_call_target="tpu_custom_call" | custom-call | tf_op jit(solution)/shard_map/chunks/pallas_call | solution.py:286
  4.1 0.5 collective-permute-start
  4.6 1.2 %collective-permute-done.other_ref = bf16[2,128,256]{2,1,0:T(8,128)(2,1)S(1)} collective-permute-done((bf16[2,128,256]{2,1,0:T(8,128)(2,1)}, bf16[2,128,256]{2,1,0:T(8,128)(2,1)S(1)}, u32[]{:S(2)}, u32[]{:S(2)}) %collective-permute-start) | collective-permute-done | bytes 131104 | tf_op jit(solution)/shard_map/ppermute | solution.py:239
  5.8 0.9 %copy-done.4 = bf16[2,128,256]{2,1,0:T(8,128)(2,1)S(1)} copy-done((bf16[2,128,256]{2,1,0:T(8,128)(2,1)S(1)}, bf16[2,128,256]{2,1,0:T(8,128)(2,1)}, u32[]{:S(2)}) %copy-start.4) | copy-done | bytes 131096
  6.7 3.0 %collective-permute-start.2 = (bf16[2,2,128,256]{3,2,1,0:T(8,128)(2,1)S(1)}, bf16[2,2,128,256]{3,2,1,0:T(8,128)(2,1)S(1)}, u32[]{:S(2)}, u32[]{:S(2)}) collective-permute-start(bf16[2,2,128,256]{3,2,1,0:T(8,128)(2,1)S(1)} %join_cores.1.refs_8_), channel_id=1, source_target_pairs={{0,2},{2,0},{4,6},{6,4},{1,3},{3,1},{5,7},{7,5},{8,10},{10,8},{12,... | collective-permute-start | bytes 786440 | tf_op jit(solution)/shard_map/ppermute | solution.py:239
  9.7 2.6 %collective-permute-start.1 = (bf16[2,2,128,256]{3,2,1,0:T(8,128)(2,1)S(1)}, bf16[2,2,128,256]{3,2,1,0:T(8,128)(2,1)S(1)}, u32[]{:S(2)}, u32[]{:S(2)}) collective-permute-start(bf16[2,2,128,256]{3,2,1,0:T(8,128)(2,1)S(1)} %join_cores.1.refs_8_), channel_id=1, source_target_pairs={{0,4},{2,6},{4,0},{6,2},{1,5},{3,7},{5,1},{7,3},{8,12},{10,14},{12... | collective-permute-start | bytes 786440 | tf_op jit(solution)/shard_map/ppermute | solution.py:239
  12.3 0.7 %collective-permute-start.3 = (bf16[272,256]{1,0:T(8,128)(2,1)}, bf16[272,256]{1,0:T(8,128)(2,1)S(1)}, u32[]{:S(2)}, u32[]{:S(2)}) collective-permute-start(bf16[272,256]{1,0:T(8,128)(2,1)} %get-tuple-element.42), channel_id=1, source_target_pairs={{0,17},{1,16},{8,25},{9,24},{16,1},{17,0},{24,9},{25,8},{2,19},{3,... | collective-permute-start | bytes 417800 | tf_op jit(solution)/shard_map/ppermute | solution.py:239
  13.0 1.7 %collective-permute-start.4 = (bf16[272,256]{1,0:T(8,128)(2,1)}, bf16[272,256]{1,0:T(8,128)(2,1)S(1)}, u32[]{:S(2)}, u32[]{:S(2)}) collective-permute-start(bf16[272,256]{1,0:T(8,128)(2,1)} %get-tuple-element.43), channel_id=1, source_target_pairs={{0,24},{1,25},{8,16},{9,17},{16,8},{17,9},{24,0},{25,1},{2,26},{3,... | collective-permute-start | bytes 417800 | tf_op jit(solution)/shard_map/ppermute | solution.py:239
  14.8 1.5 %collective-permute-start.5 = (bf16[272,256]{1,0:T(8,128)(2,1)}, bf16[272,256]{1,0:T(8,128)(2,1)S(1)}, u32[]{:S(2)}, u32[]{:S(2)}) collective-permute-start(bf16[272,256]{1,0:T(8,128)(2,1)} %get-tuple-element.44), channel_id=1, source_target_pairs={{0,25},{1,24},{8,17},{9,16},{16,9},{17,8},{24,1},{25,0},{2,27},{3,... | collective-permute-start | bytes 417800 | tf_op jit(solution)/shard_map/ppermute | solution.py:239
  16.3 2.6 %local_forward.1 = (f32[128,2048]{1,0:T(8,128)S(1)}, bf16[16,128,128]{2,1,0:T(8,128)(2,1)S(1)}, f32[4,4,128]{2,1,0:T(4,128)S(1)}) custom-call(bf16[128,2048]{1,0:T(8,128)(2,1)S(1)} %copy-done.1, bf16[128,2048]{1,0:T(8,128)(2,1)S(1)} %copy-done.2, bf16[128,2048]{1,0:T(8,128)(2,1)S(1)} %copy-done.3, bf16[128,2048]{1,0:T(8,128)(2,1)S(1)} %copy-done), custom_call_target="tpu_custom_call" | custom-call | flops 134217728 | bytes 3145728 | tf_op jit(solution)/shard_map/local_forward/pallas_call | solution.py:310
  18.9 5.5 %collective-permute-done.3.refs_5_ = bf16[272,256]{1,0:T(8,128)(2,1)S(1)} collective-permute-done((bf16[272,256]{1,0:T(8,128)(2,1)}, bf16[272,256]{1,0:T(8,128)(2,1)S(1)}, u32[]{:S(2)}, u32[]{:S(2)}) %collective-permute-start.3) | collective-permute-done | bytes 139296 | tf_op jit(solution)/shard_map/ppermute | solution.py:239
  24.4 0.5 collective-permute-start.6
  25.0 1.6 %collective-permute-start.8 = (bf16[272,256]{1,0:T(8,128)(2,1)S(1)}, bf16[272,256]{1,0:T(8,128)(2,1)S(1)}, u32[]{:S(2)}, u32[]{:S(2)}) collective-permute-start(bf16[272,256]{1,0:T(8,128)(2,1)S(1)} %copy-done.8), channel_id=1, source_target_pairs={{0,8},{1,9},{8,0},{9,1},{16,24},{17,25},{24,16},{25,17},{2,10},{3,... | collective-permute-start | bytes 417800 | tf_op jit(solution)/shard_map/ppermute | solution.py:239
  26.8 1.4 %collective-permute-start.10 = (bf16[272,256]{1,0:T(8,128)(2,1)S(1)}, bf16[272,256]{1,0:T(8,128)(2,1)S(1)}, u32[]{:S(2)}, u32[]{:S(2)}) collective-permute-start(bf16[272,256]{1,0:T(8,128)(2,1)S(1)} %copy-done.6), channel_id=1, source_target_pairs={{0,16},{1,17},{8,24},{9,25},{16,0},{17,1},{24,8},{25,9},{2,18},{3,... | collective-permute-start | bytes 417800 | tf_op jit(solution)/shard_map/ppermute | solution.py:239
  28.3 2.0 %local_backward.1 = (bf16[128,2048]{1,0:T(8,128)(2,1)S(1)}, bf16[128,2048]{1,0:T(8,128)(2,1)S(1)}) custom-call(bf16[128,2048]{1,0:T(8,128)(2,1)S(1)} %copy-done.2, bf16[128,2048]{1,0:T(8,128)(2,1)S(1)} %copy-done.3, bf16[128,2048]{1,0:T(8,128)(2,1)S(1)} %copy-done, f32[1,2048]{1,0:T(1,128)S(1)} %bitcast.3, f32[128,2048]{1,0:T(8,128)S(1)} %get-tuple-element.48.out_ref, ...), custom_call_target="tpu_custom_call" | custom-call | flops 134217728 | bytes 4194304 | tf_op jit(solution)/shard_map/local_backward/pallas_call | solution.py:339
  30.3 2.5 %collective-permute-done.6.refs_11_ = bf16[2,2,128,256]{3,2,1,0:T(8,128)(2,1)S(1)} collective-permute-done((bf16[2,2,128,256]{3,2,1,0:T(8,128)(2,1)S(1)}, bf16[2,2,128,256]{3,2,1,0:T(8,128)(2,1)S(1)}, u32[]{:S(2)}, u32[]{:S(2)}) %collective-permute-start.6) | collective-permute-done | bytes 262176 | tf_op jit(solution)/shard_map/ppermute | solution.py:239
  32.8 0.7 %collective-permute-done.9.refs_3_ = bf16[272,256]{1,0:T(8,128)(2,1)S(1)} collective-permute-done((bf16[272,256]{1,0:T(8,128)(2,1)S(1)}, bf16[272,256]{1,0:T(8,128)(2,1)S(1)}, u32[]{:S(2)}, u32[]{:S(2)}) %collective-permute-start.9) | collective-permute-done | bytes 139296 | tf_op jit(solution)/shard_map/ppermute | solution.py:239
  33.6 7.8 %memory_attention.1 = (bf16[256,256]{1,0:T(8,128)(2,1)S(1)}, bf16[256,256]{1,0:T(8,128)(2,1)S(1)}, bf16[2,256,256]{2,1,0:T(8,128)(2,1)S(1)}, bf16[2,256,256]{2,1...) custom-call(f32[1,2048]{1,0:T(1,128)S(1)} %bitcast.4, f32[16,128]{1,0:T(8,128)S(1)} %bitcast.5, ...), custom_call_target="tpu_custom_call" | custom-call | flops 2147483648 | bytes 2621440 | tf_op jit(solution)/shard_map/memory_attention/pallas_call | solution.py:359
  41.4 2.0 %collective-permute-start.20 = (f32[16,128]{1,0:T(8,128)S(1)}, f32[16,128]{1,0:T(8,128)S(1)}, u32[]{:S(2)}, u32[]{:S(2)}) collective-permute-start(f32[16,128]{1,0:T(8,128)S(1)} %get-tuple-element.76), channel_id=1, source_target_pairs={{0,6},{2,4},{4,2},{6,0},{1,7},{3,5},{5,3},{7,1},{8,14},{10,12},{12... | collective-permute-start | bytes 24584 | tf_op jit(solution)/shard_map/ppermute | solution.py:239
  43.4 1.5 %collective-permute-start.12 = (bf16[2,256,256]{2,1,0:T(8,128)(2,1)S(1)}, bf16[2,256,256]{2,1,0:T(8,128)(2,1)S(1)}, u32[]{:S(2)}, u32[]{:S(2)}) collective-permute-start(bf16[2,256,256]{2,1,0:T(8,128)(2,1)S(1)} %get-tuple-element.69), channel_id=1, source_target_pairs={{0,8},{1,9},{8,0},{9,1},{16,24},{17,25},{24,16},{25,17},{2,10},{3,... | collective-permute-start | bytes 786440 | tf_op jit(solution)/shard_map/ppermute | solution.py:239
  44.9 1.5 %collective-permute-start.14 = (bf16[2,256,256]{2,1,0:T(8,128)(2,1)S(1)}, bf16[2,256,256]{2,1,0:T(8,128)(2,1)S(1)}, u32[]{:S(2)}, u32[]{:S(2)}) collective-permute-start(bf16[2,256,256]{2,1,0:T(8,128)(2,1)S(1)} %get-tuple-element.72), channel_id=1, source_target_pairs={{0,16},{1,17},{8,24},{9,25},{16,0},{17,1},{24,8},{25,9},{2,18},{3,... | collective-permute-start | bytes 786440 | tf_op jit(solution)/shard_map/ppermute | solution.py:239
  46.9 1.1 %collective-permute-start.19 = (f32[16,128]{1,0:T(8,128)S(1)}, f32[16,128]{1,0:T(8,128)S(1)}, u32[]{:S(2)}, u32[]{:S(2)}) collective-permute-start(f32[16,128]{1,0:T(8,128)S(1)} %get-tuple-element.76), channel_id=1, source_target_pairs={{0,4},{2,6},{4,0},{6,2},{1,5},{3,7},{5,1},{7,3},{8,12},{10,14},{12... | collective-permute-start | bytes 24584 | tf_op jit(solution)/shard_map/ppermute | solution.py:239
  48.0 1.4 %collective-permute-start.18 = (f32[16,128]{1,0:T(8,128)S(1)}, f32[16,128]{1,0:T(8,128)S(1)}, u32[]{:S(2)}, u32[]{:S(2)}) collective-permute-start(f32[16,128]{1,0:T(8,128)S(1)} %get-tuple-element.76), channel_id=1, source_target_pairs={{0,2},{2,0},{4,6},{6,4},{1,3},{3,1},{5,7},{7,5},{8,10},{10,8},{12,... | collective-permute-start | bytes 24584 | tf_op jit(solution)/shard_map/ppermute | solution.py:239
  49.3 2.1 %collective-permute-done.19 = f32[16,128]{1,0:T(8,128)S(1)} collective-permute-done((f32[16,128]{1,0:T(8,128)S(1)}, f32[16,128]{1,0:T(8,128)S(1)}, u32[]{:S(2)}, u32[]{:S(2)}) %collective-permute-start.19) | collective-permute-done | bytes 8224 | tf_op jit(solution)/shard_map/ppermute | solution.py:239
  52.0 0.8 %collective-permute-done.21 = f32[16,128]{1,0:T(8,128)S(1)} collective-permute-done((f32[16,128]{1,0:T(8,128)S(1)}, f32[16,128]{1,0:T(8,128)S(1)}, u32[]{:S(2)}, u32[]{:S(2)}) %collective-permute-start.21) | collective-permute-done | bytes 8224 | tf_op jit(solution)/shard_map/ppermute | solution.py:239
  52.8 1.5 %collective-permute-start.22 = (f32[16,128]{1,0:T(8,128)S(1)}, f32[16,128]{1,0:T(8,128)S(1)}, u32[]{:S(2)}, u32[]{:S(2)}) collective-permute-start(f32[16,128]{1,0:T(8,128)S(1)} %add.25), channel_id=1, source_target_pairs={{0,8},{1,9},{8,0},{9,1},{16,24},{17,25},{24,16},{25,17},{2,10},{3,... | collective-permute-start | bytes 24584 | tf_op jit(solution)/shard_map/ppermute | solution.py:239
  54.3 3.1 %collective-permute-done.22 = f32[16,128]{1,0:T(8,128)S(1)} collective-permute-done((f32[16,128]{1,0:T(8,128)S(1)}, f32[16,128]{1,0:T(8,128)S(1)}, u32[]{:S(2)}, u32[]{:S(2)}) %collective-permute-start.22) | collective-permute-done | bytes 8224 | tf_op jit(solution)/shard_map/ppermute | solution.py:239
  57.4 1.5 %collective-permute-start.23 = (f32[16,128]{1,0:T(8,128)S(1)}, f32[16,128]{1,0:T(8,128)S(1)}, u32[]{:S(2)}, u32[]{:S(2)}) collective-permute-start(f32[16,128]{1,0:T(8,128)S(1)} %add.26), channel_id=1, source_target_pairs={{0,16},{1,17},{8,24},{9,25},{16,0},{17,1},{24,8},{25,9},{2,18},{3,... | collective-permute-start | bytes 24584 | tf_op jit(solution)/shard_map/ppermute | solution.py:239
  59.0 0.5 collective-permute-start.15
  59.6 1.5 %collective-permute-done.23 = f32[16,128]{1,0:T(8,128)S(1)} collective-permute-done((f32[16,128]{1,0:T(8,128)S(1)}, f32[16,128]{1,0:T(8,128)S(1)}, u32[]{:S(2)}, u32[]{:S(2)}) %collective-permute-start.23) | collective-permute-done | bytes 8224 | tf_op jit(solution)/shard_map/ppermute | solution.py:239
  61.2 0.5 multiply_multiply_fusion
  61.8 1.3 %merge.1 = (bf16[128,2048]{1,0:T(8,128)(2,1)}, bf16[128,2048]{1,0:T(8,128)(2,1)}) custom-call(bf16[128,2048]{1,0:T(8,128)(2,1)S(1)} %get-tuple-element.52.lo_ref, bf16[128,2048]{1,0:T(8,128)(2,1)S(1)} %get-tuple-element.53.ldq_ref, bf16[256,256]{1,0:T(8,128)(2,1)S(1)} %get-tuple-element.67.refs_0_, bf16[256,256]{1,0:T(8,128)(2,1)S(1)} %collective-permute-done.11.refs_1_, ...), custom_call_target="tpu_custom_call" | custom-call | tf_op jit(solution)/shard_map/merge/pallas_call | solution.py:385
  (52 shorter events, 1.7 us)
Async XLA Ops:
  0.6 15.7 %copy-start.1 = (bf16[128,2048]{1,0:T(8,128)(2,1)S(1)}, bf16[128,2048]{1,0:T(8,128)(2,1)}, u32[]{:S(2)}) copy-start(bf16[128,2048]{1,0:T(8,128)(2,1)} %q_ref.1) | copy-start | bytes 1572868
  0.6 15.6 %copy-start.2 = (bf16[128,2048]{1,0:T(8,128)(2,1)S(1)}, bf16[128,2048]{1,0:T(8,128)(2,1)}, u32[]{:S(2)}) copy-start(bf16[128,2048]{1,0:T(8,128)(2,1)} %k_ref.3) | copy-start | bytes 1572868
  0.7 15.6 %copy-start.3 = (bf16[128,2048]{1,0:T(8,128)(2,1)S(1)}, bf16[128,2048]{1,0:T(8,128)(2,1)}, u32[]{:S(2)}) copy-start(bf16[128,2048]{1,0:T(8,128)(2,1)} %v_ref.3) | copy-start | bytes 1572868
  4.1 12.2 %copy-start = (bf16[128,2048]{1,0:T(8,128)(2,1)S(1)}, bf16[128,2048]{1,0:T(8,128)(2,1)}, u32[]{:S(2)}) copy-start(bf16[128,2048]{1,0:T(8,128)(2,1)} %g_ref.3) | copy-start | bytes 1572868
  4.1 1.7 %collective-permute-start = (bf16[2,128,256]{2,1,0:T(8,128)(2,1)}, bf16[2,128,256]{2,1,0:T(8,128)(2,1)S(1)}, u32[]{:S(2)}, u32[]{:S(2)}) collective-permute-start(bf16[2,128,256]{2,1,0:T(8,128)(2,1)} %get-tuple-element.41), channel_id=1, source_target_pairs={{0,1},{1,0},{2,3},{3,2},{4,5},{5,4},{6,7},{7,6},{8,9},{9,8},{10,11... | collective-permute-start | bytes 393224 | tf_op jit(solution)/shard_map/ppermute | solution.py:239
  6.7 17.7 %collective-permute-start.2 = (bf16[2,2,128,256]{3,2,1,0:T(8,128)(2,1)S(1)}, bf16[2,2,128,256]{3,2,1,0:T(8,128)(2,1)S(1)}, u32[]{:S(2)}, u32[]{:S(2)}) collective-permute-start(bf16[2,2,128,256]{3,2,1,0:T(8,128)(2,1)S(1)} %join_cores.1.refs_8_), channel_id=1, source_target_pairs={{0,2},{2,0},{4,6},{6,4},{1,3},{3,1},{5,7},{7,5},{8,10},{10,8},{12,... | collective-permute-start | bytes 786440 | tf_op jit(solution)/shard_map/ppermute | solution.py:239
  9.7 14.7 %collective-permute-start.1 = (bf16[2,2,128,256]{3,2,1,0:T(8,128)(2,1)S(1)}, bf16[2,2,128,256]{3,2,1,0:T(8,128)(2,1)S(1)}, u32[]{:S(2)}, u32[]{:S(2)}) collective-permute-start(bf16[2,2,128,256]{3,2,1,0:T(8,128)(2,1)S(1)} %join_cores.1.refs_8_), channel_id=1, source_target_pairs={{0,4},{2,6},{4,0},{6,2},{1,5},{3,7},{5,1},{7,3},{8,12},{10,14},{12... | collective-permute-start | bytes 786440 | tf_op jit(solution)/shard_map/ppermute | solution.py:239
  12.3 12.1 %collective-permute-start.3 = (bf16[272,256]{1,0:T(8,128)(2,1)}, bf16[272,256]{1,0:T(8,128)(2,1)S(1)}, u32[]{:S(2)}, u32[]{:S(2)}) collective-permute-start(bf16[272,256]{1,0:T(8,128)(2,1)} %get-tuple-element.42), channel_id=1, source_target_pairs={{0,17},{1,16},{8,25},{9,24},{16,1},{17,0},{24,9},{25,8},{2,19},{3,... | collective-permute-start | bytes 417800 | tf_op jit(solution)/shard_map/ppermute | solution.py:239
  13.0 11.4 %collective-permute-start.4 = (bf16[272,256]{1,0:T(8,128)(2,1)}, bf16[272,256]{1,0:T(8,128)(2,1)S(1)}, u32[]{:S(2)}, u32[]{:S(2)}) collective-permute-start(bf16[272,256]{1,0:T(8,128)(2,1)} %get-tuple-element.43), channel_id=1, source_target_pairs={{0,24},{1,25},{8,16},{9,17},{16,8},{17,9},{24,0},{25,1},{2,26},{3,... | collective-permute-start | bytes 417800 | tf_op jit(solution)/shard_map/ppermute | solution.py:239
  14.8 10.2 %copy-start.9 = (bf16[272,256]{1,0:T(8,128)(2,1)S(1)}, bf16[272,256]{1,0:T(8,128)(2,1)}, u32[]{:S(2)}) copy-start(bf16[272,256]{1,0:T(8,128)(2,1)} %get-tuple-element.56) | copy-start | bytes 417796
  14.8 10.2 %copy-start.8 = (bf16[272,256]{1,0:T(8,128)(2,1)S(1)}, bf16[272,256]{1,0:T(8,128)(2,1)}, u32[]{:S(2)}) copy-start(bf16[272,256]{1,0:T(8,128)(2,1)} %get-tuple-element.57) | copy-start | bytes 417796
  14.8 11.7 %copy-start.7 = (bf16[272,256]{1,0:T(8,128)(2,1)S(1)}, bf16[272,256]{1,0:T(8,128)(2,1)}, u32[]{:S(2)}) copy-start(bf16[272,256]{1,0:T(8,128)(2,1)} %get-tuple-element.58) | copy-start | bytes 417796
  14.8 12.0 %copy-start.6 = (bf16[272,256]{1,0:T(8,128)(2,1)S(1)}, bf16[272,256]{1,0:T(8,128)(2,1)}, u32[]{:S(2)}) copy-start(bf16[272,256]{1,0:T(8,128)(2,1)} %get-tuple-element.59) | copy-start | bytes 417796
  14.8 9.6 %collective-permute-start.5 = (bf16[272,256]{1,0:T(8,128)(2,1)}, bf16[272,256]{1,0:T(8,128)(2,1)S(1)}, u32[]{:S(2)}, u32[]{:S(2)}) collective-permute-start(bf16[272,256]{1,0:T(8,128)(2,1)} %get-tuple-element.44), channel_id=1, source_target_pairs={{0,25},{1,24},{8,17},{9,16},{16,9},{17,8},{24,1},{25,0},{2,27},{3,... | collective-permute-start | bytes 417800 | tf_op jit(solution)/shard_map/ppermute | solution.py:239
  24.4 8.4 %collective-permute-start.6 = (bf16[2,2,128,256]{3,2,1,0:T(8,128)(2,1)S(1)}, bf16[2,2,128,256]{3,2,1,0:T(8,128)(2,1)S(1)}, u32[]{:S(2)}, u32[]{:S(2)}) collective-permute-start(bf16[2,2,128,256]{3,2,1,0:T(8,128)(2,1)S(1)} %collective-permute-done.1.refs_10_), channel_id=1, source_target_pairs={{0,2},{2,0},{4,6},{6,4},{1,3},{3,1},{5,7},{7,5},{8,10},{10,8},{12,... | collective-permute-start | bytes 786440 | tf_op jit(solution)/shard_map/ppermute | solution.py:239
  24.9 7.9 %collective-permute-start.7 = (bf16[272,256]{1,0:T(8,128)(2,1)S(1)}, bf16[272,256]{1,0:T(8,128)(2,1)S(1)}, u32[]{:S(2)}, u32[]{:S(2)}) collective-permute-start(bf16[272,256]{1,0:T(8,128)(2,1)S(1)} %copy-done.9), channel_id=1, source_target_pairs={{0,1},{1,0},{8,9},{9,8},{16,17},{17,16},{24,25},{25,24},{2,3},{3,2... | collective-permute-start | bytes 417800 | tf_op jit(solution)/shard_map/ppermute | solution.py:239
  25.0 7.9 %collective-permute-start.8 = (bf16[272,256]{1,0:T(8,128)(2,1)S(1)}, bf16[272,256]{1,0:T(8,128)(2,1)S(1)}, u32[]{:S(2)}, u32[]{:S(2)}) collective-permute-start(bf16[272,256]{1,0:T(8,128)(2,1)S(1)} %copy-done.8), channel_id=1, source_target_pairs={{0,8},{1,9},{8,0},{9,1},{16,24},{17,25},{24,16},{25,17},{2,10},{3,... | collective-permute-start | bytes 417800 | tf_op jit(solution)/shard_map/ppermute | solution.py:239
  26.5 7.0 %collective-permute-start.9 = (bf16[272,256]{1,0:T(8,128)(2,1)S(1)}, bf16[272,256]{1,0:T(8,128)(2,1)S(1)}, u32[]{:S(2)}, u32[]{:S(2)}) collective-permute-start(bf16[272,256]{1,0:T(8,128)(2,1)S(1)} %copy-done.7), channel_id=1, source_target_pairs={{0,9},{1,8},{8,1},{9,0},{16,25},{17,24},{24,17},{25,16},{2,11},{3,... | collective-permute-start | bytes 417800 | tf_op jit(solution)/shard_map/ppermute | solution.py:239
  26.8 6.7 %collective-permute-start.10 = (bf16[272,256]{1,0:T(8,128)(2,1)S(1)}, bf16[272,256]{1,0:T(8,128)(2,1)S(1)}, u32[]{:S(2)}, u32[]{:S(2)}) collective-permute-start(bf16[272,256]{1,0:T(8,128)(2,1)S(1)} %copy-done.6), channel_id=1, source_target_pairs={{0,16},{1,17},{8,24},{9,25},{16,0},{17,1},{24,8},{25,9},{2,18},{3,... | collective-permute-start | bytes 417800 | tf_op jit(solution)/shard_map/ppermute | solution.py:239
  41.4 6.6 %collective-permute-start.20 = (f32[16,128]{1,0:T(8,128)S(1)}, f32[16,128]{1,0:T(8,128)S(1)}, u32[]{:S(2)}, u32[]{:S(2)}) collective-permute-start(f32[16,128]{1,0:T(8,128)S(1)} %get-tuple-element.76), channel_id=1, source_target_pairs={{0,6},{2,4},{4,2},{6,0},{1,7},{3,5},{5,3},{7,1},{8,14},{10,12},{12... | collective-permute-start | bytes 24584 | tf_op jit(solution)/shard_map/ppermute | solution.py:239
  43.4 15.6 %collective-permute-start.12 = (bf16[2,256,256]{2,1,0:T(8,128)(2,1)S(1)}, bf16[2,256,256]{2,1,0:T(8,128)(2,1)S(1)}, u32[]{:S(2)}, u32[]{:S(2)}) collective-permute-start(bf16[2,256,256]{2,1,0:T(8,128)(2,1)S(1)} %get-tuple-element.69), channel_id=1, source_target_pairs={{0,8},{1,9},{8,0},{9,1},{16,24},{17,25},{24,16},{25,17},{2,10},{3,... | collective-permute-start | bytes 786440 | tf_op jit(solution)/shard_map/ppermute | solution.py:239
  44.9 14.1 %collective-permute-start.14 = (bf16[2,256,256]{2,1,0:T(8,128)(2,1)S(1)}, bf16[2,256,256]{2,1,0:T(8,128)(2,1)S(1)}, u32[]{:S(2)}, u32[]{:S(2)}) collective-permute-start(bf16[2,256,256]{2,1,0:T(8,128)(2,1)S(1)} %get-tuple-element.72), channel_id=1, source_target_pairs={{0,16},{1,17},{8,24},{9,25},{16,0},{17,1},{24,8},{25,9},{2,18},{3,... | collective-permute-start | bytes 786440 | tf_op jit(solution)/shard_map/ppermute | solution.py:239
  46.4 13.1 %collective-permute-start.16 = (bf16[2,256,256]{2,1,0:T(8,128)(2,1)S(1)}, bf16[2,256,256]{2,1,0:T(8,128)(2,1)S(1)}, u32[]{:S(2)}, u32[]{:S(2)}) collective-permute-start(bf16[2,256,256]{2,1,0:T(8,128)(2,1)S(1)} %get-tuple-element.73), channel_id=1, source_target_pairs={{0,24},{1,25},{8,16},{9,17},{16,8},{17,9},{24,0},{25,1},{2,26},{3,... | collective-permute-start | bytes 786440 | tf_op jit(solution)/shard_map/ppermute | solution.py:239
  46.9 4.5 %collective-permute-start.19 = (f32[16,128]{1,0:T(8,128)S(1)}, f32[16,128]{1,0:T(8,128)S(1)}, u32[]{:S(2)}, u32[]{:S(2)}) collective-permute-start(f32[16,128]{1,0:T(8,128)S(1)} %get-tuple-element.76), channel_id=1, source_target_pairs={{0,4},{2,6},{4,0},{6,2},{1,5},{3,7},{5,1},{7,3},{8,12},{10,14},{12... | collective-permute-start | bytes 24584 | tf_op jit(solution)/shard_map/ppermute | solution.py:239
  48.0 3.7 %collective-permute-start.18 = (f32[16,128]{1,0:T(8,128)S(1)}, f32[16,128]{1,0:T(8,128)S(1)}, u32[]{:S(2)}, u32[]{:S(2)}) collective-permute-start(f32[16,128]{1,0:T(8,128)S(1)} %get-tuple-element.76), channel_id=1, source_target_pairs={{0,2},{2,0},{4,6},{6,4},{1,3},{3,1},{5,7},{7,5},{8,10},{10,8},{12,... | collective-permute-start | bytes 24584 | tf_op jit(solution)/shard_map/ppermute | solution.py:239
  51.4 7.5 %collective-permute-start.11 = (bf16[256,256]{1,0:T(8,128)(2,1)S(1)}, bf16[256,256]{1,0:T(8,128)(2,1)S(1)}, u32[]{:S(2)}, u32[]{:S(2)}) collective-permute-start(bf16[256,256]{1,0:T(8,128)(2,1)S(1)} %get-tuple-element.68), channel_id=1, source_target_pairs={{0,1},{1,0},{8,9},{9,8},{16,17},{17,16},{24,25},{25,24},{2,3},{3,2... | collective-permute-start | bytes 393224 | tf_op jit(solution)/shard_map/ppermute | solution.py:239
  51.6 1.2 %collective-permute-start.21 = (f32[16,128]{1,0:T(8,128)S(1)}, f32[16,128]{1,0:T(8,128)S(1)}, u32[]{:S(2)}, u32[]{:S(2)}) collective-permute-start(f32[16,128]{1,0:T(8,128)S(1)} %add_add_fusion), channel_id=1, source_target_pairs={{0,1},{1,0},{8,9},{9,8},{16,17},{17,16},{24,25},{25,24},{2,3},{3,2... | collective-permute-start | bytes 24584 | tf_op jit(solution)/shard_map/ppermute | solution.py:239
  52.8 4.6 %collective-permute-start.22 = (f32[16,128]{1,0:T(8,128)S(1)}, f32[16,128]{1,0:T(8,128)S(1)}, u32[]{:S(2)}, u32[]{:S(2)}) collective-permute-start(f32[16,128]{1,0:T(8,128)S(1)} %add.25), channel_id=1, source_target_pairs={{0,8},{1,9},{8,0},{9,1},{16,24},{17,25},{24,16},{25,17},{2,10},{3,... | collective-permute-start | bytes 24584 | tf_op jit(solution)/shard_map/ppermute | solution.py:239
  57.4 3.7 %collective-permute-start.23 = (f32[16,128]{1,0:T(8,128)S(1)}, f32[16,128]{1,0:T(8,128)S(1)}, u32[]{:S(2)}, u32[]{:S(2)}) collective-permute-start(f32[16,128]{1,0:T(8,128)S(1)} %add.26), channel_id=1, source_target_pairs={{0,16},{1,17},{8,24},{9,25},{16,0},{17,1},{24,8},{25,9},{2,18},{3,... | collective-permute-start | bytes 24584 | tf_op jit(solution)/shard_map/ppermute | solution.py:239
  59.0 2.8 %collective-permute-start.13 = (bf16[2,256,256]{2,1,0:T(8,128)(2,1)S(1)}, bf16[2,256,256]{2,1,0:T(8,128)(2,1)S(1)}, u32[]{:S(2)}, u32[]{:S(2)}) collective-permute-start(bf16[2,256,256]{2,1,0:T(8,128)(2,1)S(1)} %collective-permute-done.12.refs_2_), channel_id=1, source_target_pairs={{0,1},{1,0},{8,9},{9,8},{16,17},{17,16},{24,25},{25,24},{2,3},{3,2... | collective-permute-start | bytes 786440 | tf_op jit(solution)/shard_map/ppermute | solution.py:239
  59.0 2.8 %collective-permute-start.15 = (bf16[2,256,256]{2,1,0:T(8,128)(2,1)S(1)}, bf16[2,256,256]{2,1,0:T(8,128)(2,1)S(1)}, u32[]{:S(2)}, u32[]{:S(2)}) collective-permute-start(bf16[2,256,256]{2,1,0:T(8,128)(2,1)S(1)} %collective-permute-done.14.refs_4_), channel_id=1, source_target_pairs={{0,1},{1,0},{8,9},{9,8},{16,17},{17,16},{24,25},{25,24},{2,3},{3,2... | collective-permute-start | bytes 786440 | tf_op jit(solution)/shard_map/ppermute | solution.py:239
  59.5 2.3 %collective-permute-start.17 = (bf16[2,256,256]{2,1,0:T(8,128)(2,1)S(1)}, bf16[2,256,256]{2,1,0:T(8,128)(2,1)S(1)}, u32[]{:S(2)}, u32[]{:S(2)}) collective-permute-start(bf16[2,256,256]{2,1,0:T(8,128)(2,1)S(1)} %collective-permute-done.16.refs_6_), channel_id=1, source_target_pairs={{0,1},{1,0},{8,9},{9,8},{16,17},{17,16},{24,25},{25,24},{2,3},{3,2... | collective-permute-start | bytes 786440 | tf_op jit(solution)/shard_map/ppermute | solution.py:239
  (3 other events, 7.9 us)

commit v6 on v5

--- a/solution.py
+++ b/solution.py
@@ -377,8 +377,8 @@
     back = [replies[0], core_back] + forward(arrived)
 
     sums = sum_over(sum_over(part, "z"), "sa")
-    for step in (1, 2, 4):
-        sums = sums + send_xor(sums, PLANE, step)
+    sums = sums + send_xor(sums, PLANE, 1)
+    sums = functools.reduce(jnp.add, across([sums] * pairs), sums)
     sums = jnp.sum(sums, axis=1)
     gate_grad = sums * gate * (1.0 - gate) / math.sqrt(tok * devices)
 

time: 63.2 us -> 64 us (1.013)
  waiting for transfers between devices: 17.7 us -> 19.7 us
  starting transfers between devices: 25.7 us -> 24.5 us
    ppermute x24 -> x25, waiting for transfers between devices: 17.7 us -> 19.7 us  [send_xor(): lax.ppermute(array, axes, [(i, i ^ k) for i in range(lax.axis_size(axes))])]
    ppermute x24 -> x25, starting transfers between devices: 25.7 us -> 24.5 us  [send_xor(): lax.ppermute(array, axes, [(i, i ^ k) for i in range(lax.axis_size(axes))])]
  transfers between devices with their start and end apart: 24 -> 25, of which waited for: 9 -> 11; matrix products, arithmetic and copies ran while one was open for 1% -> 1% of each run, Pallas kernels for 7% -> 7%
where the time goes in v6:
time: 64 us; the launch traced here: 63.8 us
  starting transfers between devices  24.5 us (38%)
  waiting for transfers between devices  19.7 us (31%)
  Pallas kernels  17.1 us (27%)
  local copies, waits for them, and re-layouts  1.02 us (2%)
  between operations  0.76 us (1%)
  other arithmetic  0.67 us (1%)
    ppermute x25, starting transfers between devices, send_xor(): lax.ppermute(array, axes, [(i, i ^ k) for i in range(lax.axis_size(axes))])  24.5 us
    ppermute x25, waiting for transfers between devices, send_xor(): lax.ppermute(array, axes, [(i, i ^ k) for i in range(lax.axis_size(axes))])  19.7 us
    pallas_call x1, Pallas kernels, body(): pl.pallas_call(functools.partial(attend_kernel, scale, groups, peers), ou...  7.82 us
    pallas_call x1, Pallas kernels, body(): pl.pallas_call(functools.partial(prologue_kernel, blocks), out_shape=(chu...  3.42 us
    pallas_call x1, Pallas kernels, body(): pl.pallas_call(functools.partial(local_forward_kernel, scale), grid=(step...  2.6 us
    pallas_call x1, Pallas kernels, body(): pl.pallas_call(functools.partial(local_backward_kernel, scale), grid=(ste...  2 us
  transfers between devices with their start and end apart: 25, of which 11 were waited for; matrix products, arithmetic and copies ran while one was open for 1% of the time, Pallas kernels for 7%

profile of v6, /device:TPU:0, one launch (start us, length us, event | category | flops | bytes accessed | tf_op | source)
XLA Modules:
  0.0 63.8 jit_solution(8493785346123717374)
XLA Ops:
  0.7 3.4 %chunks.1 = (bf16[2,128,256]{2,1,0:T(8,128)(2,1)}, bf16[2,128,256]{2,1,0:T(8,128)(2,1)}, bf16[272,256]{1,0:T(8,128)(2,1)}, bf16[272,256]{1,0:T(8,128)(2,1)}, bf1...) custom-call(bf16[128,2048]{1,0:T(8,128)(2,1)} %mk_hbm.1, ...), custom_call_target="tpu_custom_call" | custom-call | tf_op jit(solution)/shard_map/chunks/pallas_call | solution.py:286
  4.6 1.2 %collective-permute-done.other_ref = bf16[2,128,256]{2,1,0:T(8,128)(2,1)S(1)} collective-permute-done((bf16[2,128,256]{2,1,0:T(8,128)(2,1)}, bf16[2,128,256]{2,1,0:T(8,128)(2,1)S(1)}, u32[]{:S(2)}, u32[]{:S(2)}) %collective-permute-start) | collective-permute-done | bytes 131104 | tf_op jit(solution)/shard_map/ppermute | solution.py:239
  5.8 0.9 %copy-done.4 = bf16[2,128,256]{2,1,0:T(8,128)(2,1)S(1)} copy-done((bf16[2,128,256]{2,1,0:T(8,128)(2,1)S(1)}, bf16[2,128,256]{2,1,0:T(8,128)(2,1)}, u32[]{:S(2)}) %copy-start.4) | copy-done | bytes 131096
  6.7 3.0 %collective-permute-start.2 = (bf16[2,2,128,256]{3,2,1,0:T(8,128)(2,1)S(1)}, bf16[2,2,128,256]{3,2,1,0:T(8,128)(2,1)S(1)}, u32[]{:S(2)}, u32[]{:S(2)}) collective-permute-start(bf16[2,2,128,256]{3,2,1,0:T(8,128)(2,1)S(1)} %join_cores.1.refs_8_), channel_id=1, source_target_pairs={{0,2},{2,0},{4,6},{6,4},{1,3},{3,1},{5,7},{7,5},{8,10},{10,8},{12,... | collective-permute-start | bytes 786440 | tf_op jit(solution)/shard_map/ppermute | solution.py:239
  9.7 2.6 %collective-permute-start.1 = (bf16[2,2,128,256]{3,2,1,0:T(8,128)(2,1)S(1)}, bf16[2,2,128,256]{3,2,1,0:T(8,128)(2,1)S(1)}, u32[]{:S(2)}, u32[]{:S(2)}) collective-permute-start(bf16[2,2,128,256]{3,2,1,0:T(8,128)(2,1)S(1)} %join_cores.1.refs_8_), channel_id=1, source_target_pairs={{0,4},{2,6},{4,0},{6,2},{1,5},{3,7},{5,1},{7,3},{8,12},{10,14},{12... | collective-permute-start | bytes 786440 | tf_op jit(solution)/shard_map/ppermute | solution.py:239
  12.3 0.7 %collective-permute-start.3 = (bf16[272,256]{1,0:T(8,128)(2,1)}, bf16[272,256]{1,0:T(8,128)(2,1)S(1)}, u32[]{:S(2)}, u32[]{:S(2)}) collective-permute-start(bf16[272,256]{1,0:T(8,128)(2,1)} %get-tuple-element.42), channel_id=1, source_target_pairs={{0,17},{1,16},{8,25},{9,24},{16,1},{17,0},{24,9},{25,8},{2,19},{3,... | collective-permute-start | bytes 417800 | tf_op jit(solution)/shard_map/ppermute | solution.py:239
  13.0 1.7 %collective-permute-start.4 = (bf16[272,256]{1,0:T(8,128)(2,1)}, bf16[272,256]{1,0:T(8,128)(2,1)S(1)}, u32[]{:S(2)}, u32[]{:S(2)}) collective-permute-start(bf16[272,256]{1,0:T(8,128)(2,1)} %get-tuple-element.43), channel_id=1, source_target_pairs={{0,24},{1,25},{8,16},{9,17},{16,8},{17,9},{24,0},{25,1},{2,26},{3,... | collective-permute-start | bytes 417800 | tf_op jit(solution)/shard_map/ppermute | solution.py:239
  14.8 1.5 %collective-permute-start.5 = (bf16[272,256]{1,0:T(8,128)(2,1)}, bf16[272,256]{1,0:T(8,128)(2,1)S(1)}, u32[]{:S(2)}, u32[]{:S(2)}) collective-permute-start(bf16[272,256]{1,0:T(8,128)(2,1)} %get-tuple-element.44), channel_id=1, source_target_pairs={{0,25},{1,24},{8,17},{9,16},{16,9},{17,8},{24,1},{25,0},{2,27},{3,... | collective-permute-start | bytes 417800 | tf_op jit(solution)/shard_map/ppermute | solution.py:239
  16.3 2.6 %local_forward.1 = (f32[128,2048]{1,0:T(8,128)S(1)}, bf16[16,128,128]{2,1,0:T(8,128)(2,1)S(1)}, f32[4,4,128]{2,1,0:T(4,128)S(1)}) custom-call(bf16[128,2048]{1,0:T(8,128)(2,1)S(1)} %copy-done.1, bf16[128,2048]{1,0:T(8,128)(2,1)S(1)} %copy-done.2, bf16[128,2048]{1,0:T(8,128)(2,1)S(1)} %copy-done.3, bf16[128,2048]{1,0:T(8,128)(2,1)S(1)} %copy-done), custom_call_target="tpu_custom_call" | custom-call | flops 134217728 | bytes 3145728 | tf_op jit(solution)/shard_map/local_forward/pallas_call | solution.py:310
  18.9 5.5 %collective-permute-done.3.refs_5_ = bf16[272,256]{1,0:T(8,128)(2,1)S(1)} collective-permute-done((bf16[272,256]{1,0:T(8,128)(2,1)}, bf16[272,256]{1,0:T(8,128)(2,1)S(1)}, u32[]{:S(2)}, u32[]{:S(2)}) %collective-permute-start.3) | collective-permute-done | bytes 139296 | tf_op jit(solution)/shard_map/ppermute | solution.py:239
  25.0 1.6 %collective-permute-start.8 = (bf16[272,256]{1,0:T(8,128)(2,1)S(1)}, bf16[272,256]{1,0:T(8,128)(2,1)S(1)}, u32[]{:S(2)}, u32[]{:S(2)}) collective-permute-start(bf16[272,256]{1,0:T(8,128)(2,1)S(1)} %copy-done.8), channel_id=1, source_target_pairs={{0,8},{1,9},{8,0},{9,1},{16,24},{17,25},{24,16},{25,17},{2,10},{3,... | collective-permute-start | bytes 417800 | tf_op jit(solution)/shard_map/ppermute | solution.py:239
  26.8 1.4 %collective-permute-start.10 = (bf16[272,256]{1,0:T(8,128)(2,1)S(1)}, bf16[272,256]{1,0:T(8,128)(2,1)S(1)}, u32[]{:S(2)}, u32[]{:S(2)}) collective-permute-start(bf16[272,256]{1,0:T(8,128)(2,1)S(1)} %copy-done.6), channel_id=1, source_target_pairs={{0,16},{1,17},{8,24},{9,25},{16,0},{17,1},{24,8},{25,9},{2,18},{3,... | collective-permute-start | bytes 417800 | tf_op jit(solution)/shard_map/ppermute | solution.py:239
  28.3 2.0 %local_backward.1 = (bf16[128,2048]{1,0:T(8,128)(2,1)S(1)}, bf16[128,2048]{1,0:T(8,128)(2,1)S(1)}) custom-call(bf16[128,2048]{1,0:T(8,128)(2,1)S(1)} %copy-done.2, bf16[128,2048]{1,0:T(8,128)(2,1)S(1)} %copy-done.3, bf16[128,2048]{1,0:T(8,128)(2,1)S(1)} %copy-done, f32[1,2048]{1,0:T(1,128)S(1)} %bitcast.3, f32[128,2048]{1,0:T(8,128)S(1)} %get-tuple-element.48.out_ref, ...), custom_call_target="tpu_custom_call" | custom-call | flops 134217728 | bytes 4194304 | tf_op jit(solution)/shard_map/local_backward/pallas_call | solution.py:339
  30.3 2.5 %collective-permute-done.6.refs_11_ = bf16[2,2,128,256]{3,2,1,0:T(8,128)(2,1)S(1)} collective-permute-done((bf16[2,2,128,256]{3,2,1,0:T(8,128)(2,1)S(1)}, bf16[2,2,128,256]{3,2,1,0:T(8,128)(2,1)S(1)}, u32[]{:S(2)}, u32[]{:S(2)}) %collective-permute-start.6) | collective-permute-done | bytes 262176 | tf_op jit(solution)/shard_map/ppermute | solution.py:239
  32.8 0.7 %collective-permute-done.9.refs_3_ = bf16[272,256]{1,0:T(8,128)(2,1)S(1)} collective-permute-done((bf16[272,256]{1,0:T(8,128)(2,1)S(1)}, bf16[272,256]{1,0:T(8,128)(2,1)S(1)}, u32[]{:S(2)}, u32[]{:S(2)}) %collective-permute-start.9) | collective-permute-done | bytes 139296 | tf_op jit(solution)/shard_map/ppermute | solution.py:239
  33.6 7.8 %memory_attention.1 = (bf16[256,256]{1,0:T(8,128)(2,1)S(1)}, bf16[256,256]{1,0:T(8,128)(2,1)S(1)}, bf16[2,256,256]{2,1,0:T(8,128)(2,1)S(1)}, bf16[2,256,256]{2,1...) custom-call(f32[1,2048]{1,0:T(1,128)S(1)} %bitcast.4, f32[16,128]{1,0:T(8,128)S(1)} %bitcast.5, ...), custom_call_target="tpu_custom_call" | custom-call | flops 2147483648 | bytes 2621440 | tf_op jit(solution)/shard_map/memory_attention/pallas_call | solution.py:359
  41.4 1.6 %collective-permute-start.12 = (bf16[2,256,256]{2,1,0:T(8,128)(2,1)S(1)}, bf16[2,256,256]{2,1,0:T(8,128)(2,1)S(1)}, u32[]{:S(2)}, u32[]{:S(2)}) collective-permute-start(bf16[2,256,256]{2,1,0:T(8,128)(2,1)S(1)} %get-tuple-element.69), channel_id=1, source_target_pairs={{0,8},{1,9},{8,0},{9,1},{16,24},{17,25},{24,16},{25,17},{2,10},{3,... | collective-permute-start | bytes 786440 | tf_op jit(solution)/shard_map/ppermute | solution.py:239
  42.9 1.4 %collective-permute-start.14 = (bf16[2,256,256]{2,1,0:T(8,128)(2,1)S(1)}, bf16[2,256,256]{2,1,0:T(8,128)(2,1)S(1)}, u32[]{:S(2)}, u32[]{:S(2)}) collective-permute-start(bf16[2,256,256]{2,1,0:T(8,128)(2,1)S(1)} %get-tuple-element.72), channel_id=1, source_target_pairs={{0,16},{1,17},{8,24},{9,25},{16,0},{17,1},{24,8},{25,9},{2,18},{3,... | collective-permute-start | bytes 786440 | tf_op jit(solution)/shard_map/ppermute | solution.py:239
  44.4 0.6 collective-permute-start.16
  44.9 1.9 %collective-permute-start.20 = (f32[16,128]{1,0:T(8,128)S(1)}, f32[16,128]{1,0:T(8,128)S(1)}, u32[]{:S(2)}, u32[]{:S(2)}) collective-permute-start(f32[16,128]{1,0:T(8,128)S(1)} %get-tuple-element.76), channel_id=1, source_target_pairs={{0,6},{2,4},{4,2},{6,0},{1,7},{3,5},{5,3},{7,1},{8,14},{10,12},{12... | collective-permute-start | bytes 24584 | tf_op jit(solution)/shard_map/ppermute | solution.py:239
  46.9 1.1 %collective-permute-start.19 = (f32[16,128]{1,0:T(8,128)S(1)}, f32[16,128]{1,0:T(8,128)S(1)}, u32[]{:S(2)}, u32[]{:S(2)}) collective-permute-start(f32[16,128]{1,0:T(8,128)S(1)} %get-tuple-element.76), channel_id=1, source_target_pairs={{0,4},{2,6},{4,0},{6,2},{1,5},{3,7},{5,1},{7,3},{8,12},{10,14},{12... | collective-permute-start | bytes 24584 | tf_op jit(solution)/shard_map/ppermute | solution.py:239
  48.0 2.4 %collective-permute-done.20 = f32[16,128]{1,0:T(8,128)S(1)} collective-permute-done((f32[16,128]{1,0:T(8,128)S(1)}, f32[16,128]{1,0:T(8,128)S(1)}, u32[]{:S(2)}, u32[]{:S(2)}) %collective-permute-start.20) | collective-permute-done | bytes 8224 | tf_op jit(solution)/shard_map/ppermute | solution.py:239
  50.4 1.1 %collective-permute-done.19 = f32[16,128]{1,0:T(8,128)S(1)} collective-permute-done((f32[16,128]{1,0:T(8,128)S(1)}, f32[16,128]{1,0:T(8,128)S(1)}, u32[]{:S(2)}, u32[]{:S(2)}) %collective-permute-start.19) | collective-permute-done | bytes 8224 | tf_op jit(solution)/shard_map/ppermute | solution.py:239
  51.5 2.6 %collective-permute-done.18 = f32[16,128]{1,0:T(8,128)S(1)} collective-permute-done((f32[16,128]{1,0:T(8,128)S(1)}, f32[16,128]{1,0:T(8,128)S(1)}, u32[]{:S(2)}, u32[]{:S(2)}) %collective-permute-start.18) | collective-permute-done | bytes 8224 | tf_op jit(solution)/shard_map/ppermute | solution.py:239
  54.1 1.2 %collective-permute-done.21 = f32[16,128]{1,0:T(8,128)S(1)} collective-permute-done((f32[16,128]{1,0:T(8,128)S(1)}, f32[16,128]{1,0:T(8,128)S(1)}, u32[]{:S(2)}, u32[]{:S(2)}) %collective-permute-start.21) | collective-permute-done | bytes 8224 | tf_op jit(solution)/shard_map/ppermute | solution.py:239
  55.2 2.3 %collective-permute-start.24 = (f32[16,128]{1,0:T(8,128)S(1)}, f32[16,128]{1,0:T(8,128)S(1)}, u32[]{:S(2)}, u32[]{:S(2)}) collective-permute-start(f32[16,128]{1,0:T(8,128)S(1)} %add.28), channel_id=1, source_target_pairs={{0,24},{1,25},{8,16},{9,17},{16,8},{17,9},{24,0},{25,1},{2,26},{3,... | collective-permute-start | bytes 24584 | tf_op jit(solution)/shard_map/ppermute | solution.py:239
  57.6 0.6 collective-permute-start.23
  58.2 0.5 collective-permute-start.22
  58.7 1.1 %collective-permute-done.24 = f32[16,128]{1,0:T(8,128)S(1)} collective-permute-done((f32[16,128]{1,0:T(8,128)S(1)}, f32[16,128]{1,0:T(8,128)S(1)}, u32[]{:S(2)}, u32[]{:S(2)}) %collective-permute-start.24) | collective-permute-done | bytes 8224 | tf_op jit(solution)/shard_map/ppermute | solution.py:239
  60.4 0.8 %collective-permute-done.23 = f32[16,128]{1,0:T(8,128)S(1)} collective-permute-done((f32[16,128]{1,0:T(8,128)S(1)}, f32[16,128]{1,0:T(8,128)S(1)}, u32[]{:S(2)}, u32[]{:S(2)}) %collective-permute-start.23) | collective-permute-done | bytes 8224 | tf_op jit(solution)/shard_map/ppermute | solution.py:239
  61.2 0.6 collective-permute-done.22
  62.5 1.3 %merge.1 = (bf16[128,2048]{1,0:T(8,128)(2,1)}, bf16[128,2048]{1,0:T(8,128)(2,1)}) custom-call(bf16[128,2048]{1,0:T(8,128)(2,1)S(1)} %get-tuple-element.52.lo_ref, bf16[128,2048]{1,0:T(8,128)(2,1)S(1)} %get-tuple-element.53.ldq_ref, bf16[256,256]{1,0:T(8,128)(2,1)S(1)} %get-tuple-element.67.refs_0_, bf16[256,256]{1,0:T(8,128)(2,1)S(1)} %collective-permute-done.11.refs_1_, ...), custom_call_target="tpu_custom_call" | custom-call | tf_op jit(solution)/shard_map/merge/pallas_call | solution.py:385
  (53 shorter events, 2.8 us)
Async XLA Ops:
  0.6 15.7 %copy-start.1 = (bf16[128,2048]{1,0:T(8,128)(2,1)S(1)}, bf16[128,2048]{1,0:T(8,128)(2,1)}, u32[]{:S(2)}) copy-start(bf16[128,2048]{1,0:T(8,128)(2,1)} %q_ref.1) | copy-start | bytes 1572868
  0.6 15.7 %copy-start.2 = (bf16[128,2048]{1,0:T(8,128)(2,1)S(1)}, bf16[128,2048]{1,0:T(8,128)(2,1)}, u32[]{:S(2)}) copy-start(bf16[128,2048]{1,0:T(8,128)(2,1)} %k_ref.3) | copy-start | bytes 1572868
  0.7 15.6 %copy-start.3 = (bf16[128,2048]{1,0:T(8,128)(2,1)S(1)}, bf16[128,2048]{1,0:T(8,128)(2,1)}, u32[]{:S(2)}) copy-start(bf16[128,2048]{1,0:T(8,128)(2,1)} %v_ref.3) | copy-start | bytes 1572868
  4.1 12.2 %copy-start = (bf16[128,2048]{1,0:T(8,128)(2,1)S(1)}, bf16[128,2048]{1,0:T(8,128)(2,1)}, u32[]{:S(2)}) copy-start(bf16[128,2048]{1,0:T(8,128)(2,1)} %g_ref.3) | copy-start | bytes 1572868
  4.1 1.7 %collective-permute-start = (bf16[2,128,256]{2,1,0:T(8,128)(2,1)}, bf16[2,128,256]{2,1,0:T(8,128)(2,1)S(1)}, u32[]{:S(2)}, u32[]{:S(2)}) collective-permute-start(bf16[2,128,256]{2,1,0:T(8,128)(2,1)} %get-tuple-element.41), channel_id=1, source_target_pairs={{0,1},{1,0},{2,3},{3,2},{4,5},{5,4},{6,7},{7,6},{8,9},{9,8},{10,11... | collective-permute-start | bytes 393224 | tf_op jit(solution)/shard_map/ppermute | solution.py:239
  6.7 17.7 %collective-permute-start.2 = (bf16[2,2,128,256]{3,2,1,0:T(8,128)(2,1)S(1)}, bf16[2,2,128,256]{3,2,1,0:T(8,128)(2,1)S(1)}, u32[]{:S(2)}, u32[]{:S(2)}) collective-permute-start(bf16[2,2,128,256]{3,2,1,0:T(8,128)(2,1)S(1)} %join_cores.1.refs_8_), channel_id=1, source_target_pairs={{0,2},{2,0},{4,6},{6,4},{1,3},{3,1},{5,7},{7,5},{8,10},{10,8},{12,... | collective-permute-start | bytes 786440 | tf_op jit(solution)/shard_map/ppermute | solution.py:239
  9.7 14.7 %collective-permute-start.1 = (bf16[2,2,128,256]{3,2,1,0:T(8,128)(2,1)S(1)}, bf16[2,2,128,256]{3,2,1,0:T(8,128)(2,1)S(1)}, u32[]{:S(2)}, u32[]{:S(2)}) collective-permute-start(bf16[2,2,128,256]{3,2,1,0:T(8,128)(2,1)S(1)} %join_cores.1.refs_8_), channel_id=1, source_target_pairs={{0,4},{2,6},{4,0},{6,2},{1,5},{3,7},{5,1},{7,3},{8,12},{10,14},{12... | collective-permute-start | bytes 786440 | tf_op jit(solution)/shard_map/ppermute | solution.py:239
  12.3 12.1 %collective-permute-start.3 = (bf16[272,256]{1,0:T(8,128)(2,1)}, bf16[272,256]{1,0:T(8,128)(2,1)S(1)}, u32[]{:S(2)}, u32[]{:S(2)}) collective-permute-start(bf16[272,256]{1,0:T(8,128)(2,1)} %get-tuple-element.42), channel_id=1, source_target_pairs={{0,17},{1,16},{8,25},{9,24},{16,1},{17,0},{24,9},{25,8},{2,19},{3,... | collective-permute-start | bytes 417800 | tf_op jit(solution)/shard_map/ppermute | solution.py:239
  13.0 11.4 %collective-permute-start.4 = (bf16[272,256]{1,0:T(8,128)(2,1)}, bf16[272,256]{1,0:T(8,128)(2,1)S(1)}, u32[]{:S(2)}, u32[]{:S(2)}) collective-permute-start(bf16[272,256]{1,0:T(8,128)(2,1)} %get-tuple-element.43), channel_id=1, source_target_pairs={{0,24},{1,25},{8,16},{9,17},{16,8},{17,9},{24,0},{25,1},{2,26},{3,... | collective-permute-start | bytes 417800 | tf_op jit(solution)/shard_map/ppermute | solution.py:239
  14.8 10.2 %copy-start.8 = (bf16[272,256]{1,0:T(8,128)(2,1)S(1)}, bf16[272,256]{1,0:T(8,128)(2,1)}, u32[]{:S(2)}) copy-start(bf16[272,256]{1,0:T(8,128)(2,1)} %get-tuple-element.57) | copy-start | bytes 417796
  14.8 11.7 %copy-start.7 = (bf16[272,256]{1,0:T(8,128)(2,1)S(1)}, bf16[272,256]{1,0:T(8,128)(2,1)}, u32[]{:S(2)}) copy-start(bf16[272,256]{1,0:T(8,128)(2,1)} %get-tuple-element.58) | copy-start | bytes 417796
  14.8 12.0 %copy-start.6 = (bf16[272,256]{1,0:T(8,128)(2,1)S(1)}, bf16[272,256]{1,0:T(8,128)(2,1)}, u32[]{:S(2)}) copy-start(bf16[272,256]{1,0:T(8,128)(2,1)} %get-tuple-element.59) | copy-start | bytes 417796
  14.8 9.6 %collective-permute-start.5 = (bf16[272,256]{1,0:T(8,128)(2,1)}, bf16[272,256]{1,0:T(8,128)(2,1)S(1)}, u32[]{:S(2)}, u32[]{:S(2)}) collective-permute-start(bf16[272,256]{1,0:T(8,128)(2,1)} %get-tuple-element.44), channel_id=1, source_target_pairs={{0,25},{1,24},{8,17},{9,16},{16,9},{17,8},{24,1},{25,0},{2,27},{3,... | collective-permute-start | bytes 417800 | tf_op jit(solution)/shard_map/ppermute | solution.py:239
  24.4 8.4 %collective-permute-start.6 = (bf16[2,2,128,256]{3,2,1,0:T(8,128)(2,1)S(1)}, bf16[2,2,128,256]{3,2,1,0:T(8,128)(2,1)S(1)}, u32[]{:S(2)}, u32[]{:S(2)}) collective-permute-start(bf16[2,2,128,256]{3,2,1,0:T(8,128)(2,1)S(1)} %collective-permute-done.1.refs_10_), channel_id=1, source_target_pairs={{0,2},{2,0},{4,6},{6,4},{1,3},{3,1},{5,7},{7,5},{8,10},{10,8},{12,... | collective-permute-start | bytes 786440 | tf_op jit(solution)/shard_map/ppermute | solution.py:239
  25.0 7.9 %collective-permute-start.7 = (bf16[272,256]{1,0:T(8,128)(2,1)S(1)}, bf16[272,256]{1,0:T(8,128)(2,1)S(1)}, u32[]{:S(2)}, u32[]{:S(2)}) collective-permute-start(bf16[272,256]{1,0:T(8,128)(2,1)S(1)} %copy-done.9), channel_id=1, source_target_pairs={{0,1},{1,0},{8,9},{9,8},{16,17},{17,16},{24,25},{25,24},{2,3},{3,2... | collective-permute-start | bytes 417800 | tf_op jit(solution)/shard_map/ppermute | solution.py:239
  25.0 7.9 %collective-permute-start.8 = (bf16[272,256]{1,0:T(8,128)(2,1)S(1)}, bf16[272,256]{1,0:T(8,128)(2,1)S(1)}, u32[]{:S(2)}, u32[]{:S(2)}) collective-permute-start(bf16[272,256]{1,0:T(8,128)(2,1)S(1)} %copy-done.8), channel_id=1, source_target_pairs={{0,8},{1,9},{8,0},{9,1},{16,24},{17,25},{24,16},{25,17},{2,10},{3,... | collective-permute-start | bytes 417800 | tf_op jit(solution)/shard_map/ppermute | solution.py:239
  26.5 7.0 %collective-permute-start.9 = (bf16[272,256]{1,0:T(8,128)(2,1)S(1)}, bf16[272,256]{1,0:T(8,128)(2,1)S(1)}, u32[]{:S(2)}, u32[]{:S(2)}) collective-permute-start(bf16[272,256]{1,0:T(8,128)(2,1)S(1)} %copy-done.7), channel_id=1, source_target_pairs={{0,9},{1,8},{8,1},{9,0},{16,25},{17,24},{24,17},{25,16},{2,11},{3,... | collective-permute-start | bytes 417800 | tf_op jit(solution)/shard_map/ppermute | solution.py:239
  26.8 6.7 %collective-permute-start.10 = (bf16[272,256]{1,0:T(8,128)(2,1)S(1)}, bf16[272,256]{1,0:T(8,128)(2,1)S(1)}, u32[]{:S(2)}, u32[]{:S(2)}) collective-permute-start(bf16[272,256]{1,0:T(8,128)(2,1)S(1)} %copy-done.6), channel_id=1, source_target_pairs={{0,16},{1,17},{8,24},{9,25},{16,0},{17,1},{24,8},{25,9},{2,18},{3,... | collective-permute-start | bytes 417800 | tf_op jit(solution)/shard_map/ppermute | solution.py:239
  41.4 16.8 %collective-permute-start.12 = (bf16[2,256,256]{2,1,0:T(8,128)(2,1)S(1)}, bf16[2,256,256]{2,1,0:T(8,128)(2,1)S(1)}, u32[]{:S(2)}, u32[]{:S(2)}) collective-permute-start(bf16[2,256,256]{2,1,0:T(8,128)(2,1)S(1)} %get-tuple-element.69), channel_id=1, source_target_pairs={{0,8},{1,9},{8,0},{9,1},{16,24},{17,25},{24,16},{25,17},{2,10},{3,... | collective-permute-start | bytes 786440 | tf_op jit(solution)/shard_map/ppermute | solution.py:239
  42.9 16.8 %collective-permute-start.14 = (bf16[2,256,256]{2,1,0:T(8,128)(2,1)S(1)}, bf16[2,256,256]{2,1,0:T(8,128)(2,1)S(1)}, u32[]{:S(2)}, u32[]{:S(2)}) collective-permute-start(bf16[2,256,256]{2,1,0:T(8,128)(2,1)S(1)} %get-tuple-element.72), channel_id=1, source_target_pairs={{0,16},{1,17},{8,24},{9,25},{16,0},{17,1},{24,8},{25,9},{2,18},{3,... | collective-permute-start | bytes 786440 | tf_op jit(solution)/shard_map/ppermute | solution.py:239
  44.4 15.9 %collective-permute-start.16 = (bf16[2,256,256]{2,1,0:T(8,128)(2,1)S(1)}, bf16[2,256,256]{2,1,0:T(8,128)(2,1)S(1)}, u32[]{:S(2)}, u32[]{:S(2)}) collective-permute-start(bf16[2,256,256]{2,1,0:T(8,128)(2,1)S(1)} %get-tuple-element.73), channel_id=1, source_target_pairs={{0,24},{1,25},{8,16},{9,17},{16,8},{17,9},{24,0},{25,1},{2,26},{3,... | collective-permute-start | bytes 786440 | tf_op jit(solution)/shard_map/ppermute | solution.py:239
  44.9 5.4 %collective-permute-start.20 = (f32[16,128]{1,0:T(8,128)S(1)}, f32[16,128]{1,0:T(8,128)S(1)}, u32[]{:S(2)}, u32[]{:S(2)}) collective-permute-start(f32[16,128]{1,0:T(8,128)S(1)} %get-tuple-element.76), channel_id=1, source_target_pairs={{0,6},{2,4},{4,2},{6,0},{1,7},{3,5},{5,3},{7,1},{8,14},{10,12},{12... | collective-permute-start | bytes 24584 | tf_op jit(solution)/shard_map/ppermute | solution.py:239
  46.9 4.6 %collective-permute-start.19 = (f32[16,128]{1,0:T(8,128)S(1)}, f32[16,128]{1,0:T(8,128)S(1)}, u32[]{:S(2)}, u32[]{:S(2)}) collective-permute-start(f32[16,128]{1,0:T(8,128)S(1)} %get-tuple-element.76), channel_id=1, source_target_pairs={{0,4},{2,6},{4,0},{6,2},{1,5},{3,7},{5,1},{7,3},{8,12},{10,14},{12... | collective-permute-start | bytes 24584 | tf_op jit(solution)/shard_map/ppermute | solution.py:239
  50.4 3.7 %collective-permute-start.18 = (f32[16,128]{1,0:T(8,128)S(1)}, f32[16,128]{1,0:T(8,128)S(1)}, u32[]{:S(2)}, u32[]{:S(2)}) collective-permute-start(f32[16,128]{1,0:T(8,128)S(1)} %get-tuple-element.76), channel_id=1, source_target_pairs={{0,2},{2,0},{4,6},{6,4},{1,3},{3,1},{5,7},{7,5},{8,10},{10,8},{12,... | collective-permute-start | bytes 24584 | tf_op jit(solution)/shard_map/ppermute | solution.py:239
  51.5 6.1 %collective-permute-start.11 = (bf16[256,256]{1,0:T(8,128)(2,1)S(1)}, bf16[256,256]{1,0:T(8,128)(2,1)S(1)}, u32[]{:S(2)}, u32[]{:S(2)}) collective-permute-start(bf16[256,256]{1,0:T(8,128)(2,1)S(1)} %get-tuple-element.68), channel_id=1, source_target_pairs={{0,1},{1,0},{8,9},{9,8},{16,17},{17,16},{24,25},{25,24},{2,3},{3,2... | collective-permute-start | bytes 393224 | tf_op jit(solution)/shard_map/ppermute | solution.py:239
  54.1 1.2 %collective-permute-start.21 = (f32[16,128]{1,0:T(8,128)S(1)}, f32[16,128]{1,0:T(8,128)S(1)}, u32[]{:S(2)}, u32[]{:S(2)}) collective-permute-start(f32[16,128]{1,0:T(8,128)S(1)} %add_add_fusion), channel_id=1, source_target_pairs={{0,1},{1,0},{8,9},{9,8},{16,17},{17,16},{24,25},{25,24},{2,3},{3,2... | collective-permute-start | bytes 24584 | tf_op jit(solution)/shard_map/ppermute | solution.py:239
  55.2 4.5 %collective-permute-start.24 = (f32[16,128]{1,0:T(8,128)S(1)}, f32[16,128]{1,0:T(8,128)S(1)}, u32[]{:S(2)}, u32[]{:S(2)}) collective-permute-start(f32[16,128]{1,0:T(8,128)S(1)} %add.28), channel_id=1, source_target_pairs={{0,24},{1,25},{8,16},{9,17},{16,8},{17,9},{24,0},{25,1},{2,26},{3,... | collective-permute-start | bytes 24584 | tf_op jit(solution)/shard_map/ppermute | solution.py:239
  57.6 3.7 %collective-permute-start.23 = (f32[16,128]{1,0:T(8,128)S(1)}, f32[16,128]{1,0:T(8,128)S(1)}, u32[]{:S(2)}, u32[]{:S(2)}) collective-permute-start(f32[16,128]{1,0:T(8,128)S(1)} %add.28), channel_id=1, source_target_pairs={{0,16},{1,17},{8,24},{9,25},{16,0},{17,1},{24,8},{25,9},{2,18},{3,... | collective-permute-start | bytes 24584 | tf_op jit(solution)/shard_map/ppermute | solution.py:239
  58.2 3.7 %collective-permute-start.22 = (f32[16,128]{1,0:T(8,128)S(1)}, f32[16,128]{1,0:T(8,128)S(1)}, u32[]{:S(2)}, u32[]{:S(2)}) collective-permute-start(f32[16,128]{1,0:T(8,128)S(1)} %add.28), channel_id=1, source_target_pairs={{0,8},{1,9},{8,0},{9,1},{16,24},{17,25},{24,16},{25,17},{2,10},{3,... | collective-permute-start | bytes 24584 | tf_op jit(solution)/shard_map/ppermute | solution.py:239
  59.8 2.7 %collective-permute-start.13 = (bf16[2,256,256]{2,1,0:T(8,128)(2,1)S(1)}, bf16[2,256,256]{2,1,0:T(8,128)(2,1)S(1)}, u32[]{:S(2)}, u32[]{:S(2)}) collective-permute-start(bf16[2,256,256]{2,1,0:T(8,128)(2,1)S(1)} %collective-permute-done.12.refs_2_), channel_id=1, source_target_pairs={{0,1},{1,0},{8,9},{9,8},{16,17},{17,16},{24,25},{25,24},{2,3},{3,2... | collective-permute-start | bytes 786440 | tf_op jit(solution)/shard_map/ppermute | solution.py:239
  59.8 2.7 %collective-permute-start.15 = (bf16[2,256,256]{2,1,0:T(8,128)(2,1)S(1)}, bf16[2,256,256]{2,1,0:T(8,128)(2,1)S(1)}, u32[]{:S(2)}, u32[]{:S(2)}) collective-permute-start(bf16[2,256,256]{2,1,0:T(8,128)(2,1)S(1)} %collective-permute-done.14.refs_4_), channel_id=1, source_target_pairs={{0,1},{1,0},{8,9},{9,8},{16,17},{17,16},{24,25},{25,24},{2,3},{3,2... | collective-permute-start | bytes 786440 | tf_op jit(solution)/shard_map/ppermute | solution.py:239
  60.3 2.2 %collective-permute-start.17 = (bf16[2,256,256]{2,1,0:T(8,128)(2,1)S(1)}, bf16[2,256,256]{2,1,0:T(8,128)(2,1)S(1)}, u32[]{:S(2)}, u32[]{:S(2)}) collective-permute-start(bf16[2,256,256]{2,1,0:T(8,128)(2,1)S(1)} %collective-permute-done.16.refs_6_), channel_id=1, source_target_pairs={{0,1},{1,0},{8,9},{9,8},{16,17},{17,16},{24,25},{25,24},{2,3},{3,2... | collective-permute-start | bytes 786440 | tf_op jit(solution)/shard_map/ppermute | solution.py:239
  (4 other events, 18.0 us)

commit v7 on v5

--- a/solution.py
+++ b/solution.py
@@ -11,7 +11,7 @@
 HEAD_DIM = 128
 PAIR = 2
 CHUNK = PAIR * HEAD_DIM
-TILE = 2
+TILE = 4
 NEG = -1e30
 LOG2E = math.log2(math.e)
 MIB = 1024 * 1024

time: 63.2 us -> 62.3 us (0.986)
  Pallas kernels: 17.1 us -> 16.3 us
    pallas_call x1, Pallas kernels: 7.83 us -> 6.94 us  [body(): pl.pallas_call(functools.partial(attend_kernel, scale, groups, peers), ou...]
where the time goes in v7:
time: 62.3 us; the launch traced here: 62.1 us
  starting transfers between devices  25.7 us (41%)
  waiting for transfers between devices  17.7 us (28%)
  Pallas kernels  16.3 us (26%)
  local copies, waits for them, and re-layouts  1.02 us (2%)
  between operations  0.78 us (1%)
  other arithmetic  0.67 us (1%)
    ppermute x24, starting transfers between devices, send_xor(): lax.ppermute(array, axes, [(i, i ^ k) for i in range(lax.axis_size(axes))])  25.7 us
    ppermute x24, waiting for transfers between devices, send_xor(): lax.ppermute(array, axes, [(i, i ^ k) for i in range(lax.axis_size(axes))])  17.7 us
    pallas_call x1, Pallas kernels, body(): pl.pallas_call(functools.partial(attend_kernel, scale, groups, peers), ou...  6.94 us
    pallas_call x1, Pallas kernels, body(): pl.pallas_call(functools.partial(prologue_kernel, blocks), out_shape=(chu...  3.41 us
    pallas_call x1, Pallas kernels, body(): pl.pallas_call(functools.partial(local_forward_kernel, scale), grid=(step...  2.61 us
    pallas_call x1, Pallas kernels, body(): pl.pallas_call(functools.partial(local_backward_kernel, scale), grid=(ste...  2.01 us
    pallas_call x1, Pallas kernels, body(): pl.pallas_call(merge_kernel, out_shape=(whole, whole), in_specs=[vmem_spe...  1.27 us
  transfers between devices with their start and end apart: 24, of which 9 were waited for; matrix products, arithmetic and copies ran while one was open for 1% of the time, Pallas kernels for 7%

profile of v7, /device:TPU:0, one launch (start us, length us, event | category | flops | bytes accessed | tf_op | source)
XLA Modules:
  0.0 62.1 jit_solution(13336077737796108752)
XLA Ops:
  0.7 3.4 %chunks.1 = (bf16[2,128,256]{2,1,0:T(8,128)(2,1)}, bf16[2,128,256]{2,1,0:T(8,128)(2,1)}, bf16[272,256]{1,0:T(8,128)(2,1)}, bf16[272,256]{1,0:T(8,128)(2,1)}, bf1...) custom-call(bf16[128,2048]{1,0:T(8,128)(2,1)} %mk_hbm.1, ...), custom_call_target="tpu_custom_call" | custom-call | tf_op jit(solution)/shard_map/chunks/pallas_call | solution.py:286
  4.1 0.5 collective-permute-start
  4.6 1.2 %collective-permute-done.other_ref = bf16[2,128,256]{2,1,0:T(8,128)(2,1)S(1)} collective-permute-done((bf16[2,128,256]{2,1,0:T(8,128)(2,1)}, bf16[2,128,256]{2,1,0:T(8,128)(2,1)S(1)}, u32[]{:S(2)}, u32[]{:S(2)}) %collective-permute-start) | collective-permute-done | bytes 131104 | tf_op jit(solution)/shard_map/ppermute | solution.py:239
  5.8 0.9 %copy-done.4 = bf16[2,128,256]{2,1,0:T(8,128)(2,1)S(1)} copy-done((bf16[2,128,256]{2,1,0:T(8,128)(2,1)S(1)}, bf16[2,128,256]{2,1,0:T(8,128)(2,1)}, u32[]{:S(2)}) %copy-start.4) | copy-done | bytes 131096
  6.7 3.0 %collective-permute-start.2 = (bf16[2,2,128,256]{3,2,1,0:T(8,128)(2,1)S(1)}, bf16[2,2,128,256]{3,2,1,0:T(8,128)(2,1)S(1)}, u32[]{:S(2)}, u32[]{:S(2)}) collective-permute-start(bf16[2,2,128,256]{3,2,1,0:T(8,128)(2,1)S(1)} %join_cores.1.refs_8_), channel_id=1, source_target_pairs={{0,2},{2,0},{4,6},{6,4},{1,3},{3,1},{5,7},{7,5},{8,10},{10,8},{12,... | collective-permute-start | bytes 786440 | tf_op jit(solution)/shard_map/ppermute | solution.py:239
  9.7 2.6 %collective-permute-start.1 = (bf16[2,2,128,256]{3,2,1,0:T(8,128)(2,1)S(1)}, bf16[2,2,128,256]{3,2,1,0:T(8,128)(2,1)S(1)}, u32[]{:S(2)}, u32[]{:S(2)}) collective-permute-start(bf16[2,2,128,256]{3,2,1,0:T(8,128)(2,1)S(1)} %join_cores.1.refs_8_), channel_id=1, source_target_pairs={{0,4},{2,6},{4,0},{6,2},{1,5},{3,7},{5,1},{7,3},{8,12},{10,14},{12... | collective-permute-start | bytes 786440 | tf_op jit(solution)/shard_map/ppermute | solution.py:239
  12.3 0.7 %collective-permute-start.3 = (bf16[272,256]{1,0:T(8,128)(2,1)}, bf16[272,256]{1,0:T(8,128)(2,1)S(1)}, u32[]{:S(2)}, u32[]{:S(2)}) collective-permute-start(bf16[272,256]{1,0:T(8,128)(2,1)} %get-tuple-element.42), channel_id=1, source_target_pairs={{0,17},{1,16},{8,25},{9,24},{16,1},{17,0},{24,9},{25,8},{2,19},{3,... | collective-permute-start | bytes 417800 | tf_op jit(solution)/shard_map/ppermute | solution.py:239
  13.0 1.7 %collective-permute-start.4 = (bf16[272,256]{1,0:T(8,128)(2,1)}, bf16[272,256]{1,0:T(8,128)(2,1)S(1)}, u32[]{:S(2)}, u32[]{:S(2)}) collective-permute-start(bf16[272,256]{1,0:T(8,128)(2,1)} %get-tuple-element.43), channel_id=1, source_target_pairs={{0,24},{1,25},{8,16},{9,17},{16,8},{17,9},{24,0},{25,1},{2,26},{3,... | collective-permute-start | bytes 417800 | tf_op jit(solution)/shard_map/ppermute | solution.py:239
  14.8 1.5 %collective-permute-start.5 = (bf16[272,256]{1,0:T(8,128)(2,1)}, bf16[272,256]{1,0:T(8,128)(2,1)S(1)}, u32[]{:S(2)}, u32[]{:S(2)}) collective-permute-start(bf16[272,256]{1,0:T(8,128)(2,1)} %get-tuple-element.44), channel_id=1, source_target_pairs={{0,25},{1,24},{8,17},{9,16},{16,9},{17,8},{24,1},{25,0},{2,27},{3,... | collective-permute-start | bytes 417800 | tf_op jit(solution)/shard_map/ppermute | solution.py:239
  16.3 2.6 %local_forward.1 = (f32[128,2048]{1,0:T(8,128)S(1)}, bf16[16,128,128]{2,1,0:T(8,128)(2,1)S(1)}, f32[4,4,128]{2,1,0:T(4,128)S(1)}) custom-call(bf16[128,2048]{1,0:T(8,128)(2,1)S(1)} %copy-done.1, bf16[128,2048]{1,0:T(8,128)(2,1)S(1)} %copy-done.2, bf16[128,2048]{1,0:T(8,128)(2,1)S(1)} %copy-done.3, bf16[128,2048]{1,0:T(8,128)(2,1)S(1)} %copy-done), custom_call_target="tpu_custom_call" | custom-call | flops 134217728 | bytes 3145728 | tf_op jit(solution)/shard_map/local_forward/pallas_call | solution.py:310
  18.9 5.5 %collective-permute-done.3.refs_5_ = bf16[272,256]{1,0:T(8,128)(2,1)S(1)} collective-permute-done((bf16[272,256]{1,0:T(8,128)(2,1)}, bf16[272,256]{1,0:T(8,128)(2,1)S(1)}, u32[]{:S(2)}, u32[]{:S(2)}) %collective-permute-start.3) | collective-permute-done | bytes 139296 | tf_op jit(solution)/shard_map/ppermute | solution.py:239
  24.4 0.5 collective-permute-start.6
  25.0 1.6 %collective-permute-start.8 = (bf16[272,256]{1,0:T(8,128)(2,1)S(1)}, bf16[272,256]{1,0:T(8,128)(2,1)S(1)}, u32[]{:S(2)}, u32[]{:S(2)}) collective-permute-start(bf16[272,256]{1,0:T(8,128)(2,1)S(1)} %copy-done.8), channel_id=1, source_target_pairs={{0,8},{1,9},{8,0},{9,1},{16,24},{17,25},{24,16},{25,17},{2,10},{3,... | collective-permute-start | bytes 417800 | tf_op jit(solution)/shard_map/ppermute | solution.py:239
  26.8 1.4 %collective-permute-start.10 = (bf16[272,256]{1,0:T(8,128)(2,1)S(1)}, bf16[272,256]{1,0:T(8,128)(2,1)S(1)}, u32[]{:S(2)}, u32[]{:S(2)}) collective-permute-start(bf16[272,256]{1,0:T(8,128)(2,1)S(1)} %copy-done.6), channel_id=1, source_target_pairs={{0,16},{1,17},{8,24},{9,25},{16,0},{17,1},{24,8},{25,9},{2,18},{3,... | collective-permute-start | bytes 417800 | tf_op jit(solution)/shard_map/ppermute | solution.py:239
  28.3 2.0 %local_backward.1 = (bf16[128,2048]{1,0:T(8,128)(2,1)S(1)}, bf16[128,2048]{1,0:T(8,128)(2,1)S(1)}) custom-call(bf16[128,2048]{1,0:T(8,128)(2,1)S(1)} %copy-done.2, bf16[128,2048]{1,0:T(8,128)(2,1)S(1)} %copy-done.3, bf16[128,2048]{1,0:T(8,128)(2,1)S(1)} %copy-done, f32[1,2048]{1,0:T(1,128)S(1)} %bitcast.3, f32[128,2048]{1,0:T(8,128)S(1)} %get-tuple-element.48.out_ref, ...), custom_call_target="tpu_custom_call" | custom-call | flops 134217728 | bytes 4194304 | tf_op jit(solution)/shard_map/local_backward/pallas_call | solution.py:339
  30.3 2.5 %collective-permute-done.6.refs_11_ = bf16[2,2,128,256]{3,2,1,0:T(8,128)(2,1)S(1)} collective-permute-done((bf16[2,2,128,256]{3,2,1,0:T(8,128)(2,1)S(1)}, bf16[2,2,128,256]{3,2,1,0:T(8,128)(2,1)S(1)}, u32[]{:S(2)}, u32[]{:S(2)}) %collective-permute-start.6) | collective-permute-done | bytes 262176 | tf_op jit(solution)/shard_map/ppermute | solution.py:239
  32.8 0.7 %collective-permute-done.9.refs_3_ = bf16[272,256]{1,0:T(8,128)(2,1)S(1)} collective-permute-done((bf16[272,256]{1,0:T(8,128)(2,1)S(1)}, bf16[272,256]{1,0:T(8,128)(2,1)S(1)}, u32[]{:S(2)}, u32[]{:S(2)}) %collective-permute-start.9) | collective-permute-done | bytes 139296 | tf_op jit(solution)/shard_map/ppermute | solution.py:239
  33.6 6.9 %memory_attention.1 = (bf16[256,256]{1,0:T(8,128)(2,1)S(1)}, bf16[256,256]{1,0:T(8,128)(2,1)S(1)}, bf16[2,256,256]{2,1,0:T(8,128)(2,1)S(1)}, bf16[2,256,256]{2,1...) custom-call(f32[1,2048]{1,0:T(1,128)S(1)} %bitcast.4, f32[16,128]{1,0:T(8,128)S(1)} %bitcast.5, ...), custom_call_target="tpu_custom_call" | custom-call | flops 2147483648 | bytes 2621440 | tf_op jit(solution)/shard_map/memory_attention/pallas_call | solution.py:359
  40.5 2.0 %collective-permute-start.20 = (f32[16,128]{1,0:T(8,128)S(1)}, f32[16,128]{1,0:T(8,128)S(1)}, u32[]{:S(2)}, u32[]{:S(2)}) collective-permute-start(f32[16,128]{1,0:T(8,128)S(1)} %get-tuple-element.76), channel_id=1, source_target_pairs={{0,6},{2,4},{4,2},{6,0},{1,7},{3,5},{5,3},{7,1},{8,14},{10,12},{12... | collective-permute-start | bytes 24584 | tf_op jit(solution)/shard_map/ppermute | solution.py:239
  42.5 1.5 %collective-permute-start.12 = (bf16[2,256,256]{2,1,0:T(8,128)(2,1)S(1)}, bf16[2,256,256]{2,1,0:T(8,128)(2,1)S(1)}, u32[]{:S(2)}, u32[]{:S(2)}) collective-permute-start(bf16[2,256,256]{2,1,0:T(8,128)(2,1)S(1)} %get-tuple-element.69), channel_id=1, source_target_pairs={{0,8},{1,9},{8,0},{9,1},{16,24},{17,25},{24,16},{25,17},{2,10},{3,... | collective-permute-start | bytes 786440 | tf_op jit(solution)/shard_map/ppermute | solution.py:239
  44.0 1.5 %collective-permute-start.14 = (bf16[2,256,256]{2,1,0:T(8,128)(2,1)S(1)}, bf16[2,256,256]{2,1,0:T(8,128)(2,1)S(1)}, u32[]{:S(2)}, u32[]{:S(2)}) collective-permute-start(bf16[2,256,256]{2,1,0:T(8,128)(2,1)S(1)} %get-tuple-element.72), channel_id=1, source_target_pairs={{0,16},{1,17},{8,24},{9,25},{16,0},{17,1},{24,8},{25,9},{2,18},{3,... | collective-permute-start | bytes 786440 | tf_op jit(solution)/shard_map/ppermute | solution.py:239
  46.0 1.1 %collective-permute-start.19 = (f32[16,128]{1,0:T(8,128)S(1)}, f32[16,128]{1,0:T(8,128)S(1)}, u32[]{:S(2)}, u32[]{:S(2)}) collective-permute-start(f32[16,128]{1,0:T(8,128)S(1)} %get-tuple-element.76), channel_id=1, source_target_pairs={{0,4},{2,6},{4,0},{6,2},{1,5},{3,7},{5,1},{7,3},{8,12},{10,14},{12... | collective-permute-start | bytes 24584 | tf_op jit(solution)/shard_map/ppermute | solution.py:239
  47.1 1.3 %collective-permute-start.18 = (f32[16,128]{1,0:T(8,128)S(1)}, f32[16,128]{1,0:T(8,128)S(1)}, u32[]{:S(2)}, u32[]{:S(2)}) collective-permute-start(f32[16,128]{1,0:T(8,128)S(1)} %get-tuple-element.76), channel_id=1, source_target_pairs={{0,2},{2,0},{4,6},{6,4},{1,3},{3,1},{5,7},{7,5},{8,10},{10,8},{12,... | collective-permute-start | bytes 24584 | tf_op jit(solution)/shard_map/ppermute | solution.py:239
  48.5 2.1 %collective-permute-done.19 = f32[16,128]{1,0:T(8,128)S(1)} collective-permute-done((f32[16,128]{1,0:T(8,128)S(1)}, f32[16,128]{1,0:T(8,128)S(1)}, u32[]{:S(2)}, u32[]{:S(2)}) %collective-permute-start.19) | collective-permute-done | bytes 8224 | tf_op jit(solution)/shard_map/ppermute | solution.py:239
  51.1 0.8 %collective-permute-done.21 = f32[16,128]{1,0:T(8,128)S(1)} collective-permute-done((f32[16,128]{1,0:T(8,128)S(1)}, f32[16,128]{1,0:T(8,128)S(1)}, u32[]{:S(2)}, u32[]{:S(2)}) %collective-permute-start.21) | collective-permute-done | bytes 8224 | tf_op jit(solution)/shard_map/ppermute | solution.py:239
  52.0 1.5 %collective-permute-start.22 = (f32[16,128]{1,0:T(8,128)S(1)}, f32[16,128]{1,0:T(8,128)S(1)}, u32[]{:S(2)}, u32[]{:S(2)}) collective-permute-start(f32[16,128]{1,0:T(8,128)S(1)} %add.25), channel_id=1, source_target_pairs={{0,8},{1,9},{8,0},{9,1},{16,24},{17,25},{24,16},{25,17},{2,10},{3,... | collective-permute-start | bytes 24584 | tf_op jit(solution)/shard_map/ppermute | solution.py:239
  53.5 3.1 %collective-permute-done.22 = f32[16,128]{1,0:T(8,128)S(1)} collective-permute-done((f32[16,128]{1,0:T(8,128)S(1)}, f32[16,128]{1,0:T(8,128)S(1)}, u32[]{:S(2)}, u32[]{:S(2)}) %collective-permute-start.22) | collective-permute-done | bytes 8224 | tf_op jit(solution)/shard_map/ppermute | solution.py:239
  56.6 1.5 %collective-permute-start.23 = (f32[16,128]{1,0:T(8,128)S(1)}, f32[16,128]{1,0:T(8,128)S(1)}, u32[]{:S(2)}, u32[]{:S(2)}) collective-permute-start(f32[16,128]{1,0:T(8,128)S(1)} %add.26), channel_id=1, source_target_pairs={{0,16},{1,17},{8,24},{9,25},{16,0},{17,1},{24,8},{25,9},{2,18},{3,... | collective-permute-start | bytes 24584 | tf_op jit(solution)/shard_map/ppermute | solution.py:239
  58.1 0.5 collective-permute-start.15
  58.7 1.5 %collective-permute-done.23 = f32[16,128]{1,0:T(8,128)S(1)} collective-permute-done((f32[16,128]{1,0:T(8,128)S(1)}, f32[16,128]{1,0:T(8,128)S(1)}, u32[]{:S(2)}, u32[]{:S(2)}) %collective-permute-start.23) | collective-permute-done | bytes 8224 | tf_op jit(solution)/shard_map/ppermute | solution.py:239
  60.3 0.5 multiply_multiply_fusion
  60.9 1.3 %merge.1 = (bf16[128,2048]{1,0:T(8,128)(2,1)}, bf16[128,2048]{1,0:T(8,128)(2,1)}) custom-call(bf16[128,2048]{1,0:T(8,128)(2,1)S(1)} %get-tuple-element.52.lo_ref, bf16[128,2048]{1,0:T(8,128)(2,1)S(1)} %get-tuple-element.53.ldq_ref, bf16[256,256]{1,0:T(8,128)(2,1)S(1)} %get-tuple-element.67.refs_0_, bf16[256,256]{1,0:T(8,128)(2,1)S(1)} %collective-permute-done.11.refs_1_, ...), custom_call_target="tpu_custom_call" | custom-call | tf_op jit(solution)/shard_map/merge/pallas_call | solution.py:385
  (52 shorter events, 1.7 us)
Async XLA Ops:
  0.6 15.7 %copy-start.1 = (bf16[128,2048]{1,0:T(8,128)(2,1)S(1)}, bf16[128,2048]{1,0:T(8,128)(2,1)}, u32[]{:S(2)}) copy-start(bf16[128,2048]{1,0:T(8,128)(2,1)} %q_ref.1) | copy-start | bytes 1572868
  0.6 15.6 %copy-start.2 = (bf16[128,2048]{1,0:T(8,128)(2,1)S(1)}, bf16[128,2048]{1,0:T(8,128)(2,1)}, u32[]{:S(2)}) copy-start(bf16[128,2048]{1,0:T(8,128)(2,1)} %k_ref.3) | copy-start | bytes 1572868
  0.7 15.6 %copy-start.3 = (bf16[128,2048]{1,0:T(8,128)(2,1)S(1)}, bf16[128,2048]{1,0:T(8,128)(2,1)}, u32[]{:S(2)}) copy-start(bf16[128,2048]{1,0:T(8,128)(2,1)} %v_ref.3) | copy-start | bytes 1572868
  4.1 12.2 %copy-start = (bf16[128,2048]{1,0:T(8,128)(2,1)S(1)}, bf16[128,2048]{1,0:T(8,128)(2,1)}, u32[]{:S(2)}) copy-start(bf16[128,2048]{1,0:T(8,128)(2,1)} %g_ref.3) | copy-start | bytes 1572868
  4.1 1.7 %collective-permute-start = (bf16[2,128,256]{2,1,0:T(8,128)(2,1)}, bf16[2,128,256]{2,1,0:T(8,128)(2,1)S(1)}, u32[]{:S(2)}, u32[]{:S(2)}) collective-permute-start(bf16[2,128,256]{2,1,0:T(8,128)(2,1)} %get-tuple-element.41), channel_id=1, source_target_pairs={{0,1},{1,0},{2,3},{3,2},{4,5},{5,4},{6,7},{7,6},{8,9},{9,8},{10,11... | collective-permute-start | bytes 393224 | tf_op jit(solution)/shard_map/ppermute | solution.py:239
  6.7 17.7 %collective-permute-start.2 = (bf16[2,2,128,256]{3,2,1,0:T(8,128)(2,1)S(1)}, bf16[2,2,128,256]{3,2,1,0:T(8,128)(2,1)S(1)}, u32[]{:S(2)}, u32[]{:S(2)}) collective-permute-start(bf16[2,2,128,256]{3,2,1,0:T(8,128)(2,1)S(1)} %join_cores.1.refs_8_), channel_id=1, source_target_pairs={{0,2},{2,0},{4,6},{6,4},{1,3},{3,1},{5,7},{7,5},{8,10},{10,8},{12,... | collective-permute-start | bytes 786440 | tf_op jit(solution)/shard_map/ppermute | solution.py:239
  9.7 14.7 %collective-permute-start.1 = (bf16[2,2,128,256]{3,2,1,0:T(8,128)(2,1)S(1)}, bf16[2,2,128,256]{3,2,1,0:T(8,128)(2,1)S(1)}, u32[]{:S(2)}, u32[]{:S(2)}) collective-permute-start(bf16[2,2,128,256]{3,2,1,0:T(8,128)(2,1)S(1)} %join_cores.1.refs_8_), channel_id=1, source_target_pairs={{0,4},{2,6},{4,0},{6,2},{1,5},{3,7},{5,1},{7,3},{8,12},{10,14},{12... | collective-permute-start | bytes 786440 | tf_op jit(solution)/shard_map/ppermute | solution.py:239
  12.3 12.1 %collective-permute-start.3 = (bf16[272,256]{1,0:T(8,128)(2,1)}, bf16[272,256]{1,0:T(8,128)(2,1)S(1)}, u32[]{:S(2)}, u32[]{:S(2)}) collective-permute-start(bf16[272,256]{1,0:T(8,128)(2,1)} %get-tuple-element.42), channel_id=1, source_target_pairs={{0,17},{1,16},{8,25},{9,24},{16,1},{17,0},{24,9},{25,8},{2,19},{3,... | collective-permute-start | bytes 417800 | tf_op jit(solution)/shard_map/ppermute | solution.py:239
  13.0 11.4 %collective-permute-start.4 = (bf16[272,256]{1,0:T(8,128)(2,1)}, bf16[272,256]{1,0:T(8,128)(2,1)S(1)}, u32[]{:S(2)}, u32[]{:S(2)}) collective-permute-start(bf16[272,256]{1,0:T(8,128)(2,1)} %get-tuple-element.43), channel_id=1, source_target_pairs={{0,24},{1,25},{8,16},{9,17},{16,8},{17,9},{24,0},{25,1},{2,26},{3,... | collective-permute-start | bytes 417800 | tf_op jit(solution)/shard_map/ppermute | solution.py:239
  14.8 10.2 %copy-start.9 = (bf16[272,256]{1,0:T(8,128)(2,1)S(1)}, bf16[272,256]{1,0:T(8,128)(2,1)}, u32[]{:S(2)}) copy-start(bf16[272,256]{1,0:T(8,128)(2,1)} %get-tuple-element.56) | copy-start | bytes 417796
  14.8 10.2 %copy-start.8 = (bf16[272,256]{1,0:T(8,128)(2,1)S(1)}, bf16[272,256]{1,0:T(8,128)(2,1)}, u32[]{:S(2)}) copy-start(bf16[272,256]{1,0:T(8,128)(2,1)} %get-tuple-element.57) | copy-start | bytes 417796
  14.8 11.7 %copy-start.7 = (bf16[272,256]{1,0:T(8,128)(2,1)S(1)}, bf16[272,256]{1,0:T(8,128)(2,1)}, u32[]{:S(2)}) copy-start(bf16[272,256]{1,0:T(8,128)(2,1)} %get-tuple-element.58) | copy-start | bytes 417796
  14.8 12.0 %copy-start.6 = (bf16[272,256]{1,0:T(8,128)(2,1)S(1)}, bf16[272,256]{1,0:T(8,128)(2,1)}, u32[]{:S(2)}) copy-start(bf16[272,256]{1,0:T(8,128)(2,1)} %get-tuple-element.59) | copy-start | bytes 417796
  14.8 9.6 %collective-permute-start.5 = (bf16[272,256]{1,0:T(8,128)(2,1)}, bf16[272,256]{1,0:T(8,128)(2,1)S(1)}, u32[]{:S(2)}, u32[]{:S(2)}) collective-permute-start(bf16[272,256]{1,0:T(8,128)(2,1)} %get-tuple-element.44), channel_id=1, source_target_pairs={{0,25},{1,24},{8,17},{9,16},{16,9},{17,8},{24,1},{25,0},{2,27},{3,... | collective-permute-start | bytes 417800 | tf_op jit(solution)/shard_map/ppermute | solution.py:239
  24.4 8.4 %collective-permute-start.6 = (bf16[2,2,128,256]{3,2,1,0:T(8,128)(2,1)S(1)}, bf16[2,2,128,256]{3,2,1,0:T(8,128)(2,1)S(1)}, u32[]{:S(2)}, u32[]{:S(2)}) collective-permute-start(bf16[2,2,128,256]{3,2,1,0:T(8,128)(2,1)S(1)} %collective-permute-done.1.refs_10_), channel_id=1, source_target_pairs={{0,2},{2,0},{4,6},{6,4},{1,3},{3,1},{5,7},{7,5},{8,10},{10,8},{12,... | collective-permute-start | bytes 786440 | tf_op jit(solution)/shard_map/ppermute | solution.py:239
  24.9 7.9 %collective-permute-start.7 = (bf16[272,256]{1,0:T(8,128)(2,1)S(1)}, bf16[272,256]{1,0:T(8,128)(2,1)S(1)}, u32[]{:S(2)}, u32[]{:S(2)}) collective-permute-start(bf16[272,256]{1,0:T(8,128)(2,1)S(1)} %copy-done.9), channel_id=1, source_target_pairs={{0,1},{1,0},{8,9},{9,8},{16,17},{17,16},{24,25},{25,24},{2,3},{3,2... | collective-permute-start | bytes 417800 | tf_op jit(solution)/shard_map/ppermute | solution.py:239
  25.0 7.9 %collective-permute-start.8 = (bf16[272,256]{1,0:T(8,128)(2,1)S(1)}, bf16[272,256]{1,0:T(8,128)(2,1)S(1)}, u32[]{:S(2)}, u32[]{:S(2)}) collective-permute-start(bf16[272,256]{1,0:T(8,128)(2,1)S(1)} %copy-done.8), channel_id=1, source_target_pairs={{0,8},{1,9},{8,0},{9,1},{16,24},{17,25},{24,16},{25,17},{2,10},{3,... | collective-permute-start | bytes 417800 | tf_op jit(solution)/shard_map/ppermute | solution.py:239
  26.5 7.0 %collective-permute-start.9 = (bf16[272,256]{1,0:T(8,128)(2,1)S(1)}, bf16[272,256]{1,0:T(8,128)(2,1)S(1)}, u32[]{:S(2)}, u32[]{:S(2)}) collective-permute-start(bf16[272,256]{1,0:T(8,128)(2,1)S(1)} %copy-done.7), channel_id=1, source_target_pairs={{0,9},{1,8},{8,1},{9,0},{16,25},{17,24},{24,17},{25,16},{2,11},{3,... | collective-permute-start | bytes 417800 | tf_op jit(solution)/shard_map/ppermute | solution.py:239
  26.8 6.7 %collective-permute-start.10 = (bf16[272,256]{1,0:T(8,128)(2,1)S(1)}, bf16[272,256]{1,0:T(8,128)(2,1)S(1)}, u32[]{:S(2)}, u32[]{:S(2)}) collective-permute-start(bf16[272,256]{1,0:T(8,128)(2,1)S(1)} %copy-done.6), channel_id=1, source_target_pairs={{0,16},{1,17},{8,24},{9,25},{16,0},{17,1},{24,8},{25,9},{2,18},{3,... | collective-permute-start | bytes 417800 | tf_op jit(solution)/shard_map/ppermute | solution.py:239
  40.5 6.6 %collective-permute-start.20 = (f32[16,128]{1,0:T(8,128)S(1)}, f32[16,128]{1,0:T(8,128)S(1)}, u32[]{:S(2)}, u32[]{:S(2)}) collective-permute-start(f32[16,128]{1,0:T(8,128)S(1)} %get-tuple-element.76), channel_id=1, source_target_pairs={{0,6},{2,4},{4,2},{6,0},{1,7},{3,5},{5,3},{7,1},{8,14},{10,12},{12... | collective-permute-start | bytes 24584 | tf_op jit(solution)/shard_map/ppermute | solution.py:239
  42.5 15.6 %collective-permute-start.12 = (bf16[2,256,256]{2,1,0:T(8,128)(2,1)S(1)}, bf16[2,256,256]{2,1,0:T(8,128)(2,1)S(1)}, u32[]{:S(2)}, u32[]{:S(2)}) collective-permute-start(bf16[2,256,256]{2,1,0:T(8,128)(2,1)S(1)} %get-tuple-element.69), channel_id=1, source_target_pairs={{0,8},{1,9},{8,0},{9,1},{16,24},{17,25},{24,16},{25,17},{2,10},{3,... | collective-permute-start | bytes 786440 | tf_op jit(solution)/shard_map/ppermute | solution.py:239
  44.0 14.1 %collective-permute-start.14 = (bf16[2,256,256]{2,1,0:T(8,128)(2,1)S(1)}, bf16[2,256,256]{2,1,0:T(8,128)(2,1)S(1)}, u32[]{:S(2)}, u32[]{:S(2)}) collective-permute-start(bf16[2,256,256]{2,1,0:T(8,128)(2,1)S(1)} %get-tuple-element.72), channel_id=1, source_target_pairs={{0,16},{1,17},{8,24},{9,25},{16,0},{17,1},{24,8},{25,9},{2,18},{3,... | collective-permute-start | bytes 786440 | tf_op jit(solution)/shard_map/ppermute | solution.py:239
  45.5 13.1 %collective-permute-start.16 = (bf16[2,256,256]{2,1,0:T(8,128)(2,1)S(1)}, bf16[2,256,256]{2,1,0:T(8,128)(2,1)S(1)}, u32[]{:S(2)}, u32[]{:S(2)}) collective-permute-start(bf16[2,256,256]{2,1,0:T(8,128)(2,1)S(1)} %get-tuple-element.73), channel_id=1, source_target_pairs={{0,24},{1,25},{8,16},{9,17},{16,8},{17,9},{24,0},{25,1},{2,26},{3,... | collective-permute-start | bytes 786440 | tf_op jit(solution)/shard_map/ppermute | solution.py:239
  46.0 4.5 %collective-permute-start.19 = (f32[16,128]{1,0:T(8,128)S(1)}, f32[16,128]{1,0:T(8,128)S(1)}, u32[]{:S(2)}, u32[]{:S(2)}) collective-permute-start(f32[16,128]{1,0:T(8,128)S(1)} %get-tuple-element.76), channel_id=1, source_target_pairs={{0,4},{2,6},{4,0},{6,2},{1,5},{3,7},{5,1},{7,3},{8,12},{10,14},{12... | collective-permute-start | bytes 24584 | tf_op jit(solution)/shard_map/ppermute | solution.py:239
  47.1 3.7 %collective-permute-start.18 = (f32[16,128]{1,0:T(8,128)S(1)}, f32[16,128]{1,0:T(8,128)S(1)}, u32[]{:S(2)}, u32[]{:S(2)}) collective-permute-start(f32[16,128]{1,0:T(8,128)S(1)} %get-tuple-element.76), channel_id=1, source_target_pairs={{0,2},{2,0},{4,6},{6,4},{1,3},{3,1},{5,7},{7,5},{8,10},{10,8},{12,... | collective-permute-start | bytes 24584 | tf_op jit(solution)/shard_map/ppermute | solution.py:239
  50.5 7.5 %collective-permute-start.11 = (bf16[256,256]{1,0:T(8,128)(2,1)S(1)}, bf16[256,256]{1,0:T(8,128)(2,1)S(1)}, u32[]{:S(2)}, u32[]{:S(2)}) collective-permute-start(bf16[256,256]{1,0:T(8,128)(2,1)S(1)} %get-tuple-element.68), channel_id=1, source_target_pairs={{0,1},{1,0},{8,9},{9,8},{16,17},{17,16},{24,25},{25,24},{2,3},{3,2... | collective-permute-start | bytes 393224 | tf_op jit(solution)/shard_map/ppermute | solution.py:239
  50.8 1.2 %collective-permute-start.21 = (f32[16,128]{1,0:T(8,128)S(1)}, f32[16,128]{1,0:T(8,128)S(1)}, u32[]{:S(2)}, u32[]{:S(2)}) collective-permute-start(f32[16,128]{1,0:T(8,128)S(1)} %add_add_fusion), channel_id=1, source_target_pairs={{0,1},{1,0},{8,9},{9,8},{16,17},{17,16},{24,25},{25,24},{2,3},{3,2... | collective-permute-start | bytes 24584 | tf_op jit(solution)/shard_map/ppermute | solution.py:239
  52.0 4.6 %collective-permute-start.22 = (f32[16,128]{1,0:T(8,128)S(1)}, f32[16,128]{1,0:T(8,128)S(1)}, u32[]{:S(2)}, u32[]{:S(2)}) collective-permute-start(f32[16,128]{1,0:T(8,128)S(1)} %add.25), channel_id=1, source_target_pairs={{0,8},{1,9},{8,0},{9,1},{16,24},{17,25},{24,16},{25,17},{2,10},{3,... | collective-permute-start | bytes 24584 | tf_op jit(solution)/shard_map/ppermute | solution.py:239
  56.6 3.7 %collective-permute-start.23 = (f32[16,128]{1,0:T(8,128)S(1)}, f32[16,128]{1,0:T(8,128)S(1)}, u32[]{:S(2)}, u32[]{:S(2)}) collective-permute-start(f32[16,128]{1,0:T(8,128)S(1)} %add.26), channel_id=1, source_target_pairs={{0,16},{1,17},{8,24},{9,25},{16,0},{17,1},{24,8},{25,9},{2,18},{3,... | collective-permute-start | bytes 24584 | tf_op jit(solution)/shard_map/ppermute | solution.py:239
  58.1 2.8 %collective-permute-start.13 = (bf16[2,256,256]{2,1,0:T(8,128)(2,1)S(1)}, bf16[2,256,256]{2,1,0:T(8,128)(2,1)S(1)}, u32[]{:S(2)}, u32[]{:S(2)}) collective-permute-start(bf16[2,256,256]{2,1,0:T(8,128)(2,1)S(1)} %collective-permute-done.12.refs_2_), channel_id=1, source_target_pairs={{0,1},{1,0},{8,9},{9,8},{16,17},{17,16},{24,25},{25,24},{2,3},{3,2... | collective-permute-start | bytes 786440 | tf_op jit(solution)/shard_map/ppermute | solution.py:239
  58.1 2.8 %collective-permute-start.15 = (bf16[2,256,256]{2,1,0:T(8,128)(2,1)S(1)}, bf16[2,256,256]{2,1,0:T(8,128)(2,1)S(1)}, u32[]{:S(2)}, u32[]{:S(2)}) collective-permute-start(bf16[2,256,256]{2,1,0:T(8,128)(2,1)S(1)} %collective-permute-done.14.refs_4_), channel_id=1, source_target_pairs={{0,1},{1,0},{8,9},{9,8},{16,17},{17,16},{24,25},{25,24},{2,3},{3,2... | collective-permute-start | bytes 786440 | tf_op jit(solution)/shard_map/ppermute | solution.py:239
  58.6 2.3 %collective-permute-start.17 = (bf16[2,256,256]{2,1,0:T(8,128)(2,1)S(1)}, bf16[2,256,256]{2,1,0:T(8,128)(2,1)S(1)}, u32[]{:S(2)}, u32[]{:S(2)}) collective-permute-start(bf16[2,256,256]{2,1,0:T(8,128)(2,1)S(1)} %collective-permute-done.16.refs_6_), channel_id=1, source_target_pairs={{0,1},{1,0},{8,9},{9,8},{16,17},{17,16},{24,25},{25,24},{2,3},{3,2... | collective-permute-start | bytes 786440 | tf_op jit(solution)/shard_map/ppermute | solution.py:239
  (3 other events, 7.9 us)

commit v8 on v7

--- a/solution.py
+++ b/solution.py
@@ -70,7 +70,8 @@
         for i, out_ref in enumerate((mine_ref, theirs_ref))
         for t, ref in enumerate((mk_hbm, mv_hbm))
     ]
-    for k, packet in enumerate(out_refs):
+    packets = packets_of(out_refs)
+    for k, packet in enumerate(packets):
         for t, ref in enumerate((q_hbm, g_hbm)):
             span = slice(t * tok, (t + 1) * tok)
             copies.append(
@@ -80,14 +81,14 @@
             )
     for copy in copies:
         copy.start()
-    row = lax.broadcasted_iota(jnp.int32, (out_refs[0].shape[0] - 2 * tok, groups), 0)
+    row = lax.broadcasted_iota(jnp.int32, (packets[0].shape[0] - 2 * tok, groups), 0)
     owner = lax.axis_index("z") * 2 + lax.axis_index("core")
     for core in range(2):
         hot = row >= blocks
         for t in range(fetched):
             hot = hot | (row == (ids_ref[t : t + 1, :] ^ owner ^ core))
         shun = jnp.where(hot, 0.0, 1.0).astype(BF16)
-        for packet in out_refs[core::2]:
+        for packet in packets[core::2]:
             packet[2 * tok :, :groups] = shun
     for copy in copies:
         copy.wait()
@@ -153,7 +154,7 @@
 
 def attend_kernel(scale, groups, peers, gate_ref, before_ref, *refs):
     *refs, part_ref, k_all, v_all = refs
-    got, refs = refs[:peers], refs[peers:]
+    got, refs = arrivals_of(refs[:peers]), refs[peers:]
     pairs = peers // 2 - 1
     mem_refs, back = refs[: -pairs - 2], packets_of(refs[-pairs - 2 :])
     rows = mem_refs[0].shape[2]
@@ -282,12 +283,13 @@
     vmem_spec = pl.BlockSpec(memory_space=pltpu.VMEM)
     packet = jax.ShapeDtypeStruct((2 * tok + max(16, blocks), CHUNK), BF16)
     pairs = peers // 2 - 1
+    pair_packet = jax.ShapeDtypeStruct((2,) + packet.shape, BF16)
     chunk_shape = jax.ShapeDtypeStruct((2, rows, CHUNK), BF16)
     mine, theirs, *send = pl.pallas_call(
         functools.partial(prologue_kernel, blocks),
-        out_shape=(chunk_shape,) * 2 + (packet,) * peers,
+        out_shape=(chunk_shape,) * 2 + (packet,) * 2 + (pair_packet,) * pairs,
         in_specs=[hbm_spec] * 4 + [vmem_spec],
-        out_specs=(vmem_spec,) * (2 + peers),
+        out_specs=(vmem_spec,) * (4 + pairs),
         scratch_shapes=[pltpu.SemaphoreType.DMA((2, 2)), pltpu.SemaphoreType.DMA((peers, 2))],
         compiler_params=alone,
         name="chunks",
@@ -329,10 +331,10 @@
         name="local_forward",
     )(query, key, value, d_out)
 
-    got = list(send)
-    for k in (6, 7, 5, 4, 2, 3, 1):
-        got[k] = send_xor(send[k], PLANE, k)
-    spread, (got[5:], local_part) = spread_along(both, "z", (got[5:], local_part))
+    both, pair_packets = lax.optimization_barrier((both, send[2:]))
+    arrived = across(pair_packets)
+    spread, (arrived, local_part) = spread_along(both, "z", (arrived, local_part))
+    got = [send[0], send_xor(send[1], PLANE, 1)] + forward(arrived)
     memory = [spread[k] for k in range(blocks // 2)]
 
     whole = jax.ShapeDtypeStruct((tok, width), BF16)

time: 62.3 us -> 64.7 us (1.039)
  waiting for transfers between devices: 17.7 us -> 21.9 us
  starting transfers between devices: 25.7 us -> 24 us
    ppermute x24, waiting for transfers between devices: 17.7 us -> 21.9 us  [send_xor(): lax.ppermute(array, axes, [(i, i ^ k) for i in range(lax.axis_size(axes))])]
    ppermute x24, starting transfers between devices: 25.7 us -> 24 us  [send_xor(): lax.ppermute(array, axes, [(i, i ^ k) for i in range(lax.axis_size(axes))])]
  transfers between devices with their start and end apart: 24 -> 24, of which waited for: 9 -> 8; matrix products, arithmetic and copies ran while one was open for 1% -> 1% of each run, Pallas kernels for 7% -> 7%
where the time goes in v8:
time: 64.7 us; the launch traced here: 64.5 us
  starting transfers between devices  24 us (37%)
  waiting for transfers between devices  21.9 us (34%)
  Pallas kernels  16.2 us (25%)
  local copies, waits for them, and re-layouts  1.01 us (2%)
  between operations  0.8 us (1%)
  other arithmetic  0.67 us (1%)
    ppermute x24, starting transfers between devices, send_xor(): lax.ppermute(array, axes, [(i, i ^ k) for i in range(lax.axis_size(axes))])  24 us
    ppermute x24, waiting for transfers between devices, send_xor(): lax.ppermute(array, axes, [(i, i ^ k) for i in range(lax.axis_size(axes))])  21.9 us
    pallas_call x1, Pallas kernels, body(): pl.pallas_call(functools.partial(attend_kernel, scale, groups, peers), ou...  6.9 us
    pallas_call x1, Pallas kernels, body(): pl.pallas_call(functools.partial(prologue_kernel, blocks), out_shape=(chu...  3.39 us
    pallas_call x1, Pallas kernels, body(): pl.pallas_call(functools.partial(local_forward_kernel, scale), grid=(step...  2.61 us
    pallas_call x1, Pallas kernels, body(): pl.pallas_call(functools.partial(local_backward_kernel, scale), grid=(ste...  2.02 us
  transfers between devices with their start and end apart: 24, of which 8 were waited for; matrix products, arithmetic and copies ran while one was open for 1% of the time, Pallas kernels for 7%

profile of v8, /device:TPU:0, one launch (start us, length us, event | category | flops | bytes accessed | tf_op | source)
XLA Modules:
  0.0 64.5 jit_solution(5198595750746999331)
XLA Ops:
  0.7 3.4 %chunks.1 = (bf16[2,128,256]{2,1,0:T(8,128)(2,1)}, bf16[2,128,256]{2,1,0:T(8,128)(2,1)}, bf16[272,256]{1,0:T(8,128)(2,1)}, bf16[272,256]{1,0:T(8,128)(2,1)}, bf1...) custom-call(bf16[128,2048]{1,0:T(8,128)(2,1)} %mk_hbm.1, ...), custom_call_target="tpu_custom_call" | custom-call | tf_op jit(solution)/shard_map/chunks/pallas_call | solution.py:288
  4.1 0.5 collective-permute-start
  4.6 1.2 %collective-permute-done.other_ref = bf16[2,128,256]{2,1,0:T(8,128)(2,1)S(1)} collective-permute-done((bf16[2,128,256]{2,1,0:T(8,128)(2,1)}, bf16[2,128,256]{2,1,0:T(8,128)(2,1)S(1)}, u32[]{:S(2)}, u32[]{:S(2)}) %collective-permute-start) | collective-permute-done | bytes 131104 | tf_op jit(solution)/shard_map/ppermute | solution.py:240
  5.8 0.9 %copy-done.4 = bf16[2,128,256]{2,1,0:T(8,128)(2,1)S(1)} copy-done((bf16[2,128,256]{2,1,0:T(8,128)(2,1)S(1)}, bf16[2,128,256]{2,1,0:T(8,128)(2,1)}, u32[]{:S(2)}) %copy-start.4) | copy-done | bytes 131096
  6.7 2.9 %collective-permute-start.3 = (bf16[2,272,256]{2,1,0:T(8,128)(2,1)}, bf16[2,272,256]{2,1,0:T(8,128)(2,1)S(1)}, u32[]{:S(2)}, u32[]{:S(2)}) collective-permute-start(bf16[2,272,256]{2,1,0:T(8,128)(2,1)} %get-tuple-element.47), channel_id=1, source_target_pairs={{0,8},{1,9},{8,0},{9,1},{16,24},{17,25},{24,16},{25,17},{2,10},{3,... | collective-permute-start | bytes 835592 | tf_op jit(solution)/shard_map/ppermute | solution.py:240
  9.6 1.5 %collective-permute-start.4 = (bf16[2,272,256]{2,1,0:T(8,128)(2,1)}, bf16[2,272,256]{2,1,0:T(8,128)(2,1)S(1)}, u32[]{:S(2)}, u32[]{:S(2)}) collective-permute-start(bf16[2,272,256]{2,1,0:T(8,128)(2,1)} %get-tuple-element.48), channel_id=1, source_target_pairs={{0,16},{1,17},{8,24},{9,25},{16,0},{17,1},{24,8},{25,9},{2,18},{3,... | collective-permute-start | bytes 835592 | tf_op jit(solution)/shard_map/ppermute | solution.py:240
  11.2 3.0 %collective-permute-start.1 = (bf16[2,2,128,256]{3,2,1,0:T(8,128)(2,1)S(1)}, bf16[2,2,128,256]{3,2,1,0:T(8,128)(2,1)S(1)}, u32[]{:S(2)}, u32[]{:S(2)}) collective-permute-start(bf16[2,2,128,256]{3,2,1,0:T(8,128)(2,1)S(1)} %join_cores.1.refs_8_), channel_id=1, source_target_pairs={{0,4},{2,6},{4,0},{6,2},{1,5},{3,7},{5,1},{7,3},{8,12},{10,14},{12... | collective-permute-start | bytes 786440 | tf_op jit(solution)/shard_map/ppermute | solution.py:240
  14.2 1.6 %collective-permute-start.2 = (bf16[2,2,128,256]{3,2,1,0:T(8,128)(2,1)S(1)}, bf16[2,2,128,256]{3,2,1,0:T(8,128)(2,1)S(1)}, u32[]{:S(2)}, u32[]{:S(2)}) collective-permute-start(bf16[2,2,128,256]{3,2,1,0:T(8,128)(2,1)S(1)} %join_cores.1.refs_8_), channel_id=1, source_target_pairs={{0,2},{2,0},{4,6},{6,4},{1,3},{3,1},{5,7},{7,5},{8,10},{10,8},{12,... | collective-permute-start | bytes 786440 | tf_op jit(solution)/shard_map/ppermute | solution.py:240
  15.8 2.6 %local_forward.1 = (f32[128,2048]{1,0:T(8,128)S(1)}, bf16[16,128,128]{2,1,0:T(8,128)(2,1)S(1)}, f32[4,4,128]{2,1,0:T(4,128)S(1)}) custom-call(bf16[128,2048]{1,0:T(8,128)(2,1)S(1)} %copy-done.1, bf16[128,2048]{1,0:T(8,128)(2,1)S(1)} %copy-done.2, bf16[128,2048]{1,0:T(8,128)(2,1)S(1)} %copy-done.3, bf16[128,2048]{1,0:T(8,128)(2,1)S(1)} %copy-done), custom_call_target="tpu_custom_call" | custom-call | flops 134217728 | bytes 3145728 | tf_op jit(solution)/shard_map/local_forward/pallas_call | solution.py:312
  18.4 7.3 %collective-permute-done.1.refs_10_ = bf16[2,2,128,256]{3,2,1,0:T(8,128)(2,1)S(1)} collective-permute-done((bf16[2,2,128,256]{3,2,1,0:T(8,128)(2,1)S(1)}, bf16[2,2,128,256]{3,2,1,0:T(8,128)(2,1)S(1)}, u32[]{:S(2)}, u32[]{:S(2)}) %collective-permute-start.1) | collective-permute-done | bytes 262176 | tf_op jit(solution)/shard_map/ppermute | solution.py:240
  25.7 0.2 collective-permute-done.2.refs_9_
  26.0 0.5 collective-permute-start.9
  26.6 1.5 %collective-permute-start.6 = (bf16[2,2,128,256]{3,2,1,0:T(8,128)(2,1)S(1)}, bf16[2,2,128,256]{3,2,1,0:T(8,128)(2,1)S(1)}, u32[]{:S(2)}, u32[]{:S(2)}) collective-permute-start(bf16[2,2,128,256]{3,2,1,0:T(8,128)(2,1)S(1)} %collective-permute-done.1.refs_10_), channel_id=1, source_target_pairs={{0,2},{2,0},{4,6},{6,4},{1,3},{3,1},{5,7},{7,5},{8,10},{10,8},{12,... | collective-permute-start | bytes 786440 | tf_op jit(solution)/shard_map/ppermute | solution.py:240
  28.1 0.2 collective-permute-start.7
  28.3 2.0 %local_backward.1 = (bf16[128,2048]{1,0:T(8,128)(2,1)S(1)}, bf16[128,2048]{1,0:T(8,128)(2,1)S(1)}) custom-call(bf16[128,2048]{1,0:T(8,128)(2,1)S(1)} %copy-done.2, bf16[128,2048]{1,0:T(8,128)(2,1)S(1)} %copy-done.3, bf16[128,2048]{1,0:T(8,128)(2,1)S(1)} %copy-done, f32[1,2048]{1,0:T(1,128)S(1)} %bitcast.3, f32[128,2048]{1,0:T(8,128)S(1)} %get-tuple-element.53.out_ref, ...), custom_call_target="tpu_custom_call" | custom-call | flops 134217728 | bytes 4194304 | tf_op jit(solution)/shard_map/local_backward/pallas_call | solution.py:341
  30.4 4.9 %collective-permute-done.6.refs_11_ = bf16[2,2,128,256]{3,2,1,0:T(8,128)(2,1)S(1)} collective-permute-done((bf16[2,2,128,256]{3,2,1,0:T(8,128)(2,1)S(1)}, bf16[2,2,128,256]{3,2,1,0:T(8,128)(2,1)S(1)}, u32[]{:S(2)}, u32[]{:S(2)}) %collective-permute-start.6) | collective-permute-done | bytes 262176 | tf_op jit(solution)/shard_map/ppermute | solution.py:240
  35.3 6.9 %memory_attention.1 = (bf16[256,256]{1,0:T(8,128)(2,1)S(1)}, bf16[256,256]{1,0:T(8,128)(2,1)S(1)}, bf16[2,256,256]{2,1,0:T(8,128)(2,1)S(1)}, bf16[2,256,256]{2,1...) custom-call(f32[1,2048]{1,0:T(1,128)S(1)} %bitcast.4, f32[16,128]{1,0:T(8,128)S(1)} %bitcast.5, ...), custom_call_target="tpu_custom_call" | custom-call | flops 2147483648 | bytes 2621440 | tf_op jit(solution)/shard_map/memory_attention/pallas_call | solution.py:361
  42.2 3.3 %collective-permute-start.20 = (f32[16,128]{1,0:T(8,128)S(1)}, f32[16,128]{1,0:T(8,128)S(1)}, u32[]{:S(2)}, u32[]{:S(2)}) collective-permute-start(f32[16,128]{1,0:T(8,128)S(1)} %get-tuple-element.78), channel_id=1, source_target_pairs={{0,6},{2,4},{4,2},{6,0},{1,7},{3,5},{5,3},{7,1},{8,14},{10,12},{12... | collective-permute-start | bytes 24584 | tf_op jit(solution)/shard_map/ppermute | solution.py:240
  45.5 1.5 %collective-permute-start.12 = (bf16[2,256,256]{2,1,0:T(8,128)(2,1)S(1)}, bf16[2,256,256]{2,1,0:T(8,128)(2,1)S(1)}, u32[]{:S(2)}, u32[]{:S(2)}) collective-permute-start(bf16[2,256,256]{2,1,0:T(8,128)(2,1)S(1)} %get-tuple-element.71), channel_id=1, source_target_pairs={{0,8},{1,9},{8,0},{9,1},{16,24},{17,25},{24,16},{25,17},{2,10},{3,... | collective-permute-start | bytes 786440 | tf_op jit(solution)/shard_map/ppermute | solution.py:240
  47.0 1.5 %collective-permute-start.14 = (bf16[2,256,256]{2,1,0:T(8,128)(2,1)S(1)}, bf16[2,256,256]{2,1,0:T(8,128)(2,1)S(1)}, u32[]{:S(2)}, u32[]{:S(2)}) collective-permute-start(bf16[2,256,256]{2,1,0:T(8,128)(2,1)S(1)} %get-tuple-element.74), channel_id=1, source_target_pairs={{0,16},{1,17},{8,24},{9,25},{16,0},{17,1},{24,8},{25,9},{2,18},{3,... | collective-permute-start | bytes 786440 | tf_op jit(solution)/shard_map/ppermute | solution.py:240
  48.5 0.5 collective-permute-start.16
  49.0 1.1 %collective-permute-start.18 = (f32[16,128]{1,0:T(8,128)S(1)}, f32[16,128]{1,0:T(8,128)S(1)}, u32[]{:S(2)}, u32[]{:S(2)}) collective-permute-start(f32[16,128]{1,0:T(8,128)S(1)} %get-tuple-element.78), channel_id=1, source_target_pairs={{0,2},{2,0},{4,6},{6,4},{1,3},{3,1},{5,7},{7,5},{8,10},{10,8},{12,... | collective-permute-start | bytes 24584 | tf_op jit(solution)/shard_map/ppermute | solution.py:240
  50.1 3.4 %collective-permute-done.19 = f32[16,128]{1,0:T(8,128)S(1)} collective-permute-done((f32[16,128]{1,0:T(8,128)S(1)}, f32[16,128]{1,0:T(8,128)S(1)}, u32[]{:S(2)}, u32[]{:S(2)}) %collective-permute-start.19) | collective-permute-done | bytes 8224 | tf_op jit(solution)/shard_map/ppermute | solution.py:240
  53.6 0.6 collective-permute-start.21
  54.1 0.8 %collective-permute-done.21 = f32[16,128]{1,0:T(8,128)S(1)} collective-permute-done((f32[16,128]{1,0:T(8,128)S(1)}, f32[16,128]{1,0:T(8,128)S(1)}, u32[]{:S(2)}, u32[]{:S(2)}) %collective-permute-start.21) | collective-permute-done | bytes 8224 | tf_op jit(solution)/shard_map/ppermute | solution.py:240
  55.0 1.5 %collective-permute-start.22 = (f32[16,128]{1,0:T(8,128)S(1)}, f32[16,128]{1,0:T(8,128)S(1)}, u32[]{:S(2)}, u32[]{:S(2)}) collective-permute-start(f32[16,128]{1,0:T(8,128)S(1)} %add.25), channel_id=1, source_target_pairs={{0,8},{1,9},{8,0},{9,1},{16,24},{17,25},{24,16},{25,17},{2,10},{3,... | collective-permute-start | bytes 24584 | tf_op jit(solution)/shard_map/ppermute | solution.py:240
  56.5 2.5 %collective-permute-done.22 = f32[16,128]{1,0:T(8,128)S(1)} collective-permute-done((f32[16,128]{1,0:T(8,128)S(1)}, f32[16,128]{1,0:T(8,128)S(1)}, u32[]{:S(2)}, u32[]{:S(2)}) %collective-permute-start.22) | collective-permute-done | bytes 8224 | tf_op jit(solution)/shard_map/ppermute | solution.py:240
  58.9 1.5 %collective-permute-start.23 = (f32[16,128]{1,0:T(8,128)S(1)}, f32[16,128]{1,0:T(8,128)S(1)}, u32[]{:S(2)}, u32[]{:S(2)}) collective-permute-start(f32[16,128]{1,0:T(8,128)S(1)} %add.26), channel_id=1, source_target_pairs={{0,16},{1,17},{8,24},{9,25},{16,0},{17,1},{24,8},{25,9},{2,18},{3,... | collective-permute-start | bytes 24584 | tf_op jit(solution)/shard_map/ppermute | solution.py:240
  60.5 0.5 collective-permute-start.15
  61.1 1.5 %collective-permute-done.23 = f32[16,128]{1,0:T(8,128)S(1)} collective-permute-done((f32[16,128]{1,0:T(8,128)S(1)}, f32[16,128]{1,0:T(8,128)S(1)}, u32[]{:S(2)}, u32[]{:S(2)}) %collective-permute-start.23) | collective-permute-done | bytes 8224 | tf_op jit(solution)/shard_map/ppermute | solution.py:240
  62.7 0.5 multiply_multiply_fusion
  63.3 1.3 %merge.1 = (bf16[128,2048]{1,0:T(8,128)(2,1)}, bf16[128,2048]{1,0:T(8,128)(2,1)}) custom-call(bf16[128,2048]{1,0:T(8,128)(2,1)S(1)} %get-tuple-element.57.lo_ref, bf16[128,2048]{1,0:T(8,128)(2,1)S(1)} %get-tuple-element.58.ldq_ref, bf16[256,256]{1,0:T(8,128)(2,1)S(1)} %get-tuple-element.69.refs_0_, bf16[256,256]{1,0:T(8,128)(2,1)S(1)} %collective-permute-done.11.refs_1_, ...), custom_call_target="tpu_custom_call" | custom-call | tf_op jit(solution)/shard_map/merge/pallas_call | solution.py:387
  (46 shorter events, 0.6 us)
Async XLA Ops:
  0.6 15.2 %copy-start.1 = (bf16[128,2048]{1,0:T(8,128)(2,1)S(1)}, bf16[128,2048]{1,0:T(8,128)(2,1)}, u32[]{:S(2)}) copy-start(bf16[128,2048]{1,0:T(8,128)(2,1)} %q_ref.1) | copy-start | bytes 1572868
  0.6 15.2 %copy-start.2 = (bf16[128,2048]{1,0:T(8,128)(2,1)S(1)}, bf16[128,2048]{1,0:T(8,128)(2,1)}, u32[]{:S(2)}) copy-start(bf16[128,2048]{1,0:T(8,128)(2,1)} %k_ref.3) | copy-start | bytes 1572868
  0.7 15.2 %copy-start.3 = (bf16[128,2048]{1,0:T(8,128)(2,1)S(1)}, bf16[128,2048]{1,0:T(8,128)(2,1)}, u32[]{:S(2)}) copy-start(bf16[128,2048]{1,0:T(8,128)(2,1)} %v_ref.3) | copy-start | bytes 1572868
  4.1 11.8 %copy-start = (bf16[128,2048]{1,0:T(8,128)(2,1)S(1)}, bf16[128,2048]{1,0:T(8,128)(2,1)}, u32[]{:S(2)}) copy-start(bf16[128,2048]{1,0:T(8,128)(2,1)} %g_ref.3) | copy-start | bytes 1572868
  4.1 1.7 %collective-permute-start = (bf16[2,128,256]{2,1,0:T(8,128)(2,1)}, bf16[2,128,256]{2,1,0:T(8,128)(2,1)S(1)}, u32[]{:S(2)}, u32[]{:S(2)}) collective-permute-start(bf16[2,128,256]{2,1,0:T(8,128)(2,1)} %get-tuple-element.42), channel_id=1, source_target_pairs={{0,1},{1,0},{2,3},{3,2},{4,5},{5,4},{6,7},{7,6},{8,9},{9,8},{10,11... | collective-permute-start | bytes 393224 | tf_op jit(solution)/shard_map/ppermute | solution.py:240
  5.8 0.9 %copy-start.4 = (bf16[2,128,256]{2,1,0:T(8,128)(2,1)S(1)}, bf16[2,128,256]{2,1,0:T(8,128)(2,1)}, u32[]{:S(2)}) copy-start(bf16[2,128,256]{2,1,0:T(8,128)(2,1)} %get-tuple-element.41.mine_ref) | copy-start | bytes 393220
  6.7 21.4 %copy-start.6 = (bf16[272,256]{1,0:T(8,128)(2,1)S(1)}, bf16[272,256]{1,0:T(8,128)(2,1)}, u32[]{:S(2)}) copy-start(bf16[272,256]{1,0:T(8,128)(2,1)} %get-tuple-element.61) | copy-start | bytes 417796
  6.7 19.2 %collective-permute-start.3 = (bf16[2,272,256]{2,1,0:T(8,128)(2,1)}, bf16[2,272,256]{2,1,0:T(8,128)(2,1)S(1)}, u32[]{:S(2)}, u32[]{:S(2)}) collective-permute-start(bf16[2,272,256]{2,1,0:T(8,128)(2,1)} %get-tuple-element.47), channel_id=1, source_target_pairs={{0,8},{1,9},{8,0},{9,1},{16,24},{17,25},{24,16},{25,17},{2,10},{3,... | collective-permute-start | bytes 835592 | tf_op jit(solution)/shard_map/ppermute | solution.py:240
  9.6 16.3 %collective-permute-start.4 = (bf16[2,272,256]{2,1,0:T(8,128)(2,1)}, bf16[2,272,256]{2,1,0:T(8,128)(2,1)S(1)}, u32[]{:S(2)}, u32[]{:S(2)}) collective-permute-start(bf16[2,272,256]{2,1,0:T(8,128)(2,1)} %get-tuple-element.48), channel_id=1, source_target_pairs={{0,16},{1,17},{8,24},{9,25},{16,0},{17,1},{24,8},{25,9},{2,18},{3,... | collective-permute-start | bytes 835592 | tf_op jit(solution)/shard_map/ppermute | solution.py:240
  11.2 14.8 %collective-permute-start.5 = (bf16[2,272,256]{2,1,0:T(8,128)(2,1)}, bf16[2,272,256]{2,1,0:T(8,128)(2,1)S(1)}, u32[]{:S(2)}, u32[]{:S(2)}) collective-permute-start(bf16[2,272,256]{2,1,0:T(8,128)(2,1)} %get-tuple-element.49), channel_id=1, source_target_pairs={{0,24},{1,25},{8,16},{9,17},{16,8},{17,9},{24,0},{25,1},{2,26},{3,... | collective-permute-start | bytes 835592 | tf_op jit(solution)/shard_map/ppermute | solution.py:240
  11.2 14.5 %collective-permute-start.1 = (bf16[2,2,128,256]{3,2,1,0:T(8,128)(2,1)S(1)}, bf16[2,2,128,256]{3,2,1,0:T(8,128)(2,1)S(1)}, u32[]{:S(2)}, u32[]{:S(2)}) collective-permute-start(bf16[2,2,128,256]{3,2,1,0:T(8,128)(2,1)S(1)} %join_cores.1.refs_8_), channel_id=1, source_target_pairs={{0,4},{2,6},{4,0},{6,2},{1,5},{3,7},{5,1},{7,3},{8,12},{10,14},{12... | collective-permute-start | bytes 786440 | tf_op jit(solution)/shard_map/ppermute | solution.py:240
  14.2 11.7 %collective-permute-start.2 = (bf16[2,2,128,256]{3,2,1,0:T(8,128)(2,1)S(1)}, bf16[2,2,128,256]{3,2,1,0:T(8,128)(2,1)S(1)}, u32[]{:S(2)}, u32[]{:S(2)}) collective-permute-start(bf16[2,2,128,256]{3,2,1,0:T(8,128)(2,1)S(1)} %join_cores.1.refs_8_), channel_id=1, source_target_pairs={{0,2},{2,0},{4,6},{6,4},{1,3},{3,1},{5,7},{7,5},{8,10},{10,8},{12,... | collective-permute-start | bytes 786440 | tf_op jit(solution)/shard_map/ppermute | solution.py:240
  25.9 2.3 %copy-start.7 = (f32[16]{0:T(128)S(1)}, f32[16]{0:T(128)}, u32[]{:S(2)}) copy-start(f32[16]{0:T(128)} %param.14) | copy-start | bytes 196
  25.9 9.3 %collective-permute-start.8 = (bf16[2,272,256]{2,1,0:T(8,128)(2,1)S(1)}, bf16[2,272,256]{2,1,0:T(8,128)(2,1)S(1)}, u32[]{:S(2)}, u32[]{:S(2)}) collective-permute-start(bf16[2,272,256]{2,1,0:T(8,128)(2,1)S(1)} %collective-permute-done.3.refs_2_), channel_id=1, source_target_pairs={{0,1},{1,0},{8,9},{9,8},{16,17},{17,16},{24,25},{25,24},{2,3},{3,2... | collective-permute-start | bytes 835592 | tf_op jit(solution)/shard_map/ppermute | solution.py:240
  26.0 9.2 %collective-permute-start.9 = (bf16[2,272,256]{2,1,0:T(8,128)(2,1)S(1)}, bf16[2,272,256]{2,1,0:T(8,128)(2,1)S(1)}, u32[]{:S(2)}, u32[]{:S(2)}) collective-permute-start(bf16[2,272,256]{2,1,0:T(8,128)(2,1)S(1)} %collective-permute-done.4.refs_4_), channel_id=1, source_target_pairs={{0,1},{1,0},{8,9},{9,8},{16,17},{17,16},{24,25},{25,24},{2,3},{3,2... | collective-permute-start | bytes 835592 | tf_op jit(solution)/shard_map/ppermute | solution.py:240
  26.5 8.8 %collective-permute-start.10 = (bf16[2,272,256]{2,1,0:T(8,128)(2,1)S(1)}, bf16[2,272,256]{2,1,0:T(8,128)(2,1)S(1)}, u32[]{:S(2)}, u32[]{:S(2)}) collective-permute-start(bf16[2,272,256]{2,1,0:T(8,128)(2,1)S(1)} %collective-permute-done.5.refs_6_), channel_id=1, source_target_pairs={{0,1},{1,0},{8,9},{9,8},{16,17},{17,16},{24,25},{25,24},{2,3},{3,2... | collective-permute-start | bytes 835592 | tf_op jit(solution)/shard_map/ppermute | solution.py:240
  26.6 8.7 %collective-permute-start.6 = (bf16[2,2,128,256]{3,2,1,0:T(8,128)(2,1)S(1)}, bf16[2,2,128,256]{3,2,1,0:T(8,128)(2,1)S(1)}, u32[]{:S(2)}, u32[]{:S(2)}) collective-permute-start(bf16[2,2,128,256]{3,2,1,0:T(8,128)(2,1)S(1)} %collective-permute-done.1.refs_10_), channel_id=1, source_target_pairs={{0,2},{2,0},{4,6},{6,4},{1,3},{3,1},{5,7},{7,5},{8,10},{10,8},{12,... | collective-permute-start | bytes 786440 | tf_op jit(solution)/shard_map/ppermute | solution.py:240
  28.1 7.2 %collective-permute-start.7 = (bf16[272,256]{1,0:T(8,128)(2,1)S(1)}, bf16[272,256]{1,0:T(8,128)(2,1)S(1)}, u32[]{:S(2)}, u32[]{:S(2)}) collective-permute-start(bf16[272,256]{1,0:T(8,128)(2,1)S(1)} %copy-done.6), channel_id=1, source_target_pairs={{0,1},{1,0},{8,9},{9,8},{16,17},{17,16},{24,25},{25,24},{2,3},{3,2... | collective-permute-start | bytes 417800 | tf_op jit(solution)/shard_map/ppermute | solution.py:240
  28.3 6.9 %copy-start.5 = (bf16[272,256]{1,0:T(8,128)(2,1)S(1)}, bf16[272,256]{1,0:T(8,128)(2,1)}, u32[]{:S(2)}) copy-start(bf16[272,256]{1,0:T(8,128)(2,1)} %get-tuple-element.60.refs_0_) | copy-start | bytes 417796
  42.2 6.8 %collective-permute-start.20 = (f32[16,128]{1,0:T(8,128)S(1)}, f32[16,128]{1,0:T(8,128)S(1)}, u32[]{:S(2)}, u32[]{:S(2)}) collective-permute-start(f32[16,128]{1,0:T(8,128)S(1)} %get-tuple-element.78), channel_id=1, source_target_pairs={{0,6},{2,4},{4,2},{6,0},{1,7},{3,5},{5,3},{7,1},{8,14},{10,12},{12... | collective-permute-start | bytes 24584 | tf_op jit(solution)/shard_map/ppermute | solution.py:240
  45.5 15.0 %collective-permute-start.12 = (bf16[2,256,256]{2,1,0:T(8,128)(2,1)S(1)}, bf16[2,256,256]{2,1,0:T(8,128)(2,1)S(1)}, u32[]{:S(2)}, u32[]{:S(2)}) collective-permute-start(bf16[2,256,256]{2,1,0:T(8,128)(2,1)S(1)} %get-tuple-element.71), channel_id=1, source_target_pairs={{0,8},{1,9},{8,0},{9,1},{16,24},{17,25},{24,16},{25,17},{2,10},{3,... | collective-permute-start | bytes 786440 | tf_op jit(solution)/shard_map/ppermute | solution.py:240
  47.0 13.5 %collective-permute-start.14 = (bf16[2,256,256]{2,1,0:T(8,128)(2,1)S(1)}, bf16[2,256,256]{2,1,0:T(8,128)(2,1)S(1)}, u32[]{:S(2)}, u32[]{:S(2)}) collective-permute-start(bf16[2,256,256]{2,1,0:T(8,128)(2,1)S(1)} %get-tuple-element.74), channel_id=1, source_target_pairs={{0,16},{1,17},{8,24},{9,25},{16,0},{17,1},{24,8},{25,9},{2,18},{3,... | collective-permute-start | bytes 786440 | tf_op jit(solution)/shard_map/ppermute | solution.py:240
  48.5 12.5 %collective-permute-start.16 = (bf16[2,256,256]{2,1,0:T(8,128)(2,1)S(1)}, bf16[2,256,256]{2,1,0:T(8,128)(2,1)S(1)}, u32[]{:S(2)}, u32[]{:S(2)}) collective-permute-start(bf16[2,256,256]{2,1,0:T(8,128)(2,1)S(1)} %get-tuple-element.75), channel_id=1, source_target_pairs={{0,24},{1,25},{8,16},{9,17},{16,8},{17,9},{24,0},{25,1},{2,26},{3,... | collective-permute-start | bytes 786440 | tf_op jit(solution)/shard_map/ppermute | solution.py:240
  49.0 4.5 %collective-permute-start.19 = (f32[16,128]{1,0:T(8,128)S(1)}, f32[16,128]{1,0:T(8,128)S(1)}, u32[]{:S(2)}, u32[]{:S(2)}) collective-permute-start(f32[16,128]{1,0:T(8,128)S(1)} %get-tuple-element.78), channel_id=1, source_target_pairs={{0,4},{2,6},{4,0},{6,2},{1,5},{3,7},{5,1},{7,3},{8,12},{10,14},{12... | collective-permute-start | bytes 24584 | tf_op jit(solution)/shard_map/ppermute | solution.py:240
  49.0 4.5 %collective-permute-start.18 = (f32[16,128]{1,0:T(8,128)S(1)}, f32[16,128]{1,0:T(8,128)S(1)}, u32[]{:S(2)}, u32[]{:S(2)}) collective-permute-start(f32[16,128]{1,0:T(8,128)S(1)} %get-tuple-element.78), channel_id=1, source_target_pairs={{0,2},{2,0},{4,6},{6,4},{1,3},{3,1},{5,7},{7,5},{8,10},{10,8},{12,... | collective-permute-start | bytes 24584 | tf_op jit(solution)/shard_map/ppermute | solution.py:240
  53.6 6.9 %collective-permute-start.11 = (bf16[256,256]{1,0:T(8,128)(2,1)S(1)}, bf16[256,256]{1,0:T(8,128)(2,1)S(1)}, u32[]{:S(2)}, u32[]{:S(2)}) collective-permute-start(bf16[256,256]{1,0:T(8,128)(2,1)S(1)} %get-tuple-element.70), channel_id=1, source_target_pairs={{0,1},{1,0},{8,9},{9,8},{16,17},{17,16},{24,25},{25,24},{2,3},{3,2... | collective-permute-start | bytes 393224 | tf_op jit(solution)/shard_map/ppermute | solution.py:240
  53.6 1.4 %collective-permute-start.21 = (f32[16,128]{1,0:T(8,128)S(1)}, f32[16,128]{1,0:T(8,128)S(1)}, u32[]{:S(2)}, u32[]{:S(2)}) collective-permute-start(f32[16,128]{1,0:T(8,128)S(1)} %add_add_fusion), channel_id=1, source_target_pairs={{0,1},{1,0},{8,9},{9,8},{16,17},{17,16},{24,25},{25,24},{2,3},{3,2... | collective-permute-start | bytes 24584 | tf_op jit(solution)/shard_map/ppermute | solution.py:240
  55.0 4.0 %collective-permute-start.22 = (f32[16,128]{1,0:T(8,128)S(1)}, f32[16,128]{1,0:T(8,128)S(1)}, u32[]{:S(2)}, u32[]{:S(2)}) collective-permute-start(f32[16,128]{1,0:T(8,128)S(1)} %add.25), channel_id=1, source_target_pairs={{0,8},{1,9},{8,0},{9,1},{16,24},{17,25},{24,16},{25,17},{2,10},{3,... | collective-permute-start | bytes 24584 | tf_op jit(solution)/shard_map/ppermute | solution.py:240
  58.9 3.7 %collective-permute-start.23 = (f32[16,128]{1,0:T(8,128)S(1)}, f32[16,128]{1,0:T(8,128)S(1)}, u32[]{:S(2)}, u32[]{:S(2)}) collective-permute-start(f32[16,128]{1,0:T(8,128)S(1)} %add.26), channel_id=1, source_target_pairs={{0,16},{1,17},{8,24},{9,25},{16,0},{17,1},{24,8},{25,9},{2,18},{3,... | collective-permute-start | bytes 24584 | tf_op jit(solution)/shard_map/ppermute | solution.py:240
  60.5 2.8 %collective-permute-start.13 = (bf16[2,256,256]{2,1,0:T(8,128)(2,1)S(1)}, bf16[2,256,256]{2,1,0:T(8,128)(2,1)S(1)}, u32[]{:S(2)}, u32[]{:S(2)}) collective-permute-start(bf16[2,256,256]{2,1,0:T(8,128)(2,1)S(1)} %collective-permute-done.12.refs_2_), channel_id=1, source_target_pairs={{0,1},{1,0},{8,9},{9,8},{16,17},{17,16},{24,25},{25,24},{2,3},{3,2... | collective-permute-start | bytes 786440 | tf_op jit(solution)/shard_map/ppermute | solution.py:240
  60.5 2.8 %collective-permute-start.15 = (bf16[2,256,256]{2,1,0:T(8,128)(2,1)S(1)}, bf16[2,256,256]{2,1,0:T(8,128)(2,1)S(1)}, u32[]{:S(2)}, u32[]{:S(2)}) collective-permute-start(bf16[2,256,256]{2,1,0:T(8,128)(2,1)S(1)} %collective-permute-done.14.refs_4_), channel_id=1, source_target_pairs={{0,1},{1,0},{8,9},{9,8},{16,17},{17,16},{24,25},{25,24},{2,3},{3,2... | collective-permute-start | bytes 786440 | tf_op jit(solution)/shard_map/ppermute | solution.py:240
  61.0 2.3 %collective-permute-start.17 = (bf16[2,256,256]{2,1,0:T(8,128)(2,1)S(1)}, bf16[2,256,256]{2,1,0:T(8,128)(2,1)S(1)}, u32[]{:S(2)}, u32[]{:S(2)}) collective-permute-start(bf16[2,256,256]{2,1,0:T(8,128)(2,1)S(1)} %collective-permute-done.16.refs_6_), channel_id=1, source_target_pairs={{0,1},{1,0},{8,9},{9,8},{16,17},{17,16},{24,25},{25,24},{2,3},{3,2... | collective-permute-start | bytes 786440 | tf_op jit(solution)/shard_map/ppermute | solution.py:240

commit v9 on v7

--- a/solution.py
+++ b/solution.py
@@ -11,7 +11,7 @@
 HEAD_DIM = 128
 PAIR = 2
 CHUNK = PAIR * HEAD_DIM
-TILE = 4
+TILE = 8
 NEG = -1e30
 LOG2E = math.log2(math.e)
 MIB = 1024 * 1024

time: 62.3 us -> 62.4 us (level)
  no operation moved by 1% of the time
where the time goes in v9:
time: 62.4 us; the launch traced here: 62.2 us
  starting transfers between devices  25.7 us (41%)
  waiting for transfers between devices  17.7 us (28%)
  Pallas kernels  16.3 us (26%)
  local copies, waits for them, and re-layouts  1.02 us (2%)
  between operations  0.78 us (1%)
  other arithmetic  0.67 us (1%)
    ppermute x24, starting transfers between devices, send_xor(): lax.ppermute(array, axes, [(i, i ^ k) for i in range(lax.axis_size(axes))])  25.7 us
    ppermute x24, waiting for transfers between devices, send_xor(): lax.ppermute(array, axes, [(i, i ^ k) for i in range(lax.axis_size(axes))])  17.7 us
    pallas_call x1, Pallas kernels, body(): pl.pallas_call(functools.partial(attend_kernel, scale, groups, peers), ou...  7.02 us
    pallas_call x1, Pallas kernels, body(): pl.pallas_call(functools.partial(prologue_kernel, blocks), out_shape=(chu...  3.41 us
    pallas_call x1, Pallas kernels, body(): pl.pallas_call(functools.partial(local_forward_kernel, scale), grid=(step...  2.61 us
    pallas_call x1, Pallas kernels, body(): pl.pallas_call(functools.partial(local_backward_kernel, scale), grid=(ste...  2.01 us
    pallas_call x1, Pallas kernels, body(): pl.pallas_call(merge_kernel, out_shape=(whole, whole), in_specs=[vmem_spe...  1.27 us
  transfers between devices with their start and end apart: 24, of which 9 were waited for; matrix products, arithmetic and copies ran while one was open for 1% of the time, Pallas kernels for 7%

profile of v9, /device:TPU:0, one launch (start us, length us, event | category | flops | bytes accessed | tf_op | source)
XLA Modules:
  0.0 62.2 jit_solution(10323363261816174963)
XLA Ops:
  0.7 3.4 %chunks.1 = (bf16[2,128,256]{2,1,0:T(8,128)(2,1)}, bf16[2,128,256]{2,1,0:T(8,128)(2,1)}, bf16[272,256]{1,0:T(8,128)(2,1)}, bf16[272,256]{1,0:T(8,128)(2,1)}, bf1...) custom-call(bf16[128,2048]{1,0:T(8,128)(2,1)} %mk_hbm.1, ...), custom_call_target="tpu_custom_call" | custom-call | tf_op jit(solution)/shard_map/chunks/pallas_call | solution.py:286
  4.1 0.5 collective-permute-start
  4.6 1.2 %collective-permute-done.other_ref = bf16[2,128,256]{2,1,0:T(8,128)(2,1)S(1)} collective-permute-done((bf16[2,128,256]{2,1,0:T(8,128)(2,1)}, bf16[2,128,256]{2,1,0:T(8,128)(2,1)S(1)}, u32[]{:S(2)}, u32[]{:S(2)}) %collective-permute-start) | collective-permute-done | bytes 131104 | tf_op jit(solution)/shard_map/ppermute | solution.py:239
  5.8 0.9 %copy-done.4 = bf16[2,128,256]{2,1,0:T(8,128)(2,1)S(1)} copy-done((bf16[2,128,256]{2,1,0:T(8,128)(2,1)S(1)}, bf16[2,128,256]{2,1,0:T(8,128)(2,1)}, u32[]{:S(2)}) %copy-start.4) | copy-done | bytes 131096
  6.7 3.0 %collective-permute-start.2 = (bf16[2,2,128,256]{3,2,1,0:T(8,128)(2,1)S(1)}, bf16[2,2,128,256]{3,2,1,0:T(8,128)(2,1)S(1)}, u32[]{:S(2)}, u32[]{:S(2)}) collective-permute-start(bf16[2,2,128,256]{3,2,1,0:T(8,128)(2,1)S(1)} %join_cores.1.refs_8_), channel_id=1, source_target_pairs={{0,2},{2,0},{4,6},{6,4},{1,3},{3,1},{5,7},{7,5},{8,10},{10,8},{12,... | collective-permute-start | bytes 786440 | tf_op jit(solution)/shard_map/ppermute | solution.py:239
  9.7 2.6 %collective-permute-start.1 = (bf16[2,2,128,256]{3,2,1,0:T(8,128)(2,1)S(1)}, bf16[2,2,128,256]{3,2,1,0:T(8,128)(2,1)S(1)}, u32[]{:S(2)}, u32[]{:S(2)}) collective-permute-start(bf16[2,2,128,256]{3,2,1,0:T(8,128)(2,1)S(1)} %join_cores.1.refs_8_), channel_id=1, source_target_pairs={{0,4},{2,6},{4,0},{6,2},{1,5},{3,7},{5,1},{7,3},{8,12},{10,14},{12... | collective-permute-start | bytes 786440 | tf_op jit(solution)/shard_map/ppermute | solution.py:239
  12.3 0.7 %collective-permute-start.3 = (bf16[272,256]{1,0:T(8,128)(2,1)}, bf16[272,256]{1,0:T(8,128)(2,1)S(1)}, u32[]{:S(2)}, u32[]{:S(2)}) collective-permute-start(bf16[272,256]{1,0:T(8,128)(2,1)} %get-tuple-element.42), channel_id=1, source_target_pairs={{0,17},{1,16},{8,25},{9,24},{16,1},{17,0},{24,9},{25,8},{2,19},{3,... | collective-permute-start | bytes 417800 | tf_op jit(solution)/shard_map/ppermute | solution.py:239
  13.0 1.7 %collective-permute-start.4 = (bf16[272,256]{1,0:T(8,128)(2,1)}, bf16[272,256]{1,0:T(8,128)(2,1)S(1)}, u32[]{:S(2)}, u32[]{:S(2)}) collective-permute-start(bf16[272,256]{1,0:T(8,128)(2,1)} %get-tuple-element.43), channel_id=1, source_target_pairs={{0,24},{1,25},{8,16},{9,17},{16,8},{17,9},{24,0},{25,1},{2,26},{3,... | collective-permute-start | bytes 417800 | tf_op jit(solution)/shard_map/ppermute | solution.py:239
  14.8 1.5 %collective-permute-start.5 = (bf16[272,256]{1,0:T(8,128)(2,1)}, bf16[272,256]{1,0:T(8,128)(2,1)S(1)}, u32[]{:S(2)}, u32[]{:S(2)}) collective-permute-start(bf16[272,256]{1,0:T(8,128)(2,1)} %get-tuple-element.44), channel_id=1, source_target_pairs={{0,25},{1,24},{8,17},{9,16},{16,9},{17,8},{24,1},{25,0},{2,27},{3,... | collective-permute-start | bytes 417800 | tf_op jit(solution)/shard_map/ppermute | solution.py:239
  16.3 2.6 %local_forward.1 = (f32[128,2048]{1,0:T(8,128)S(1)}, bf16[16,128,128]{2,1,0:T(8,128)(2,1)S(1)}, f32[4,4,128]{2,1,0:T(4,128)S(1)}) custom-call(bf16[128,2048]{1,0:T(8,128)(2,1)S(1)} %copy-done.1, bf16[128,2048]{1,0:T(8,128)(2,1)S(1)} %copy-done.2, bf16[128,2048]{1,0:T(8,128)(2,1)S(1)} %copy-done.3, bf16[128,2048]{1,0:T(8,128)(2,1)S(1)} %copy-done), custom_call_target="tpu_custom_call" | custom-call | flops 134217728 | bytes 3145728 | tf_op jit(solution)/shard_map/local_forward/pallas_call | solution.py:310
  18.9 5.5 %collective-permute-done.3.refs_5_ = bf16[272,256]{1,0:T(8,128)(2,1)S(1)} collective-permute-done((bf16[272,256]{1,0:T(8,128)(2,1)}, bf16[272,256]{1,0:T(8,128)(2,1)S(1)}, u32[]{:S(2)}, u32[]{:S(2)}) %collective-permute-start.3) | collective-permute-done | bytes 139296 | tf_op jit(solution)/shard_map/ppermute | solution.py:239
  24.4 0.5 collective-permute-start.6
  25.0 1.6 %collective-permute-start.8 = (bf16[272,256]{1,0:T(8,128)(2,1)S(1)}, bf16[272,256]{1,0:T(8,128)(2,1)S(1)}, u32[]{:S(2)}, u32[]{:S(2)}) collective-permute-start(bf16[272,256]{1,0:T(8,128)(2,1)S(1)} %copy-done.8), channel_id=1, source_target_pairs={{0,8},{1,9},{8,0},{9,1},{16,24},{17,25},{24,16},{25,17},{2,10},{3,... | collective-permute-start | bytes 417800 | tf_op jit(solution)/shard_map/ppermute | solution.py:239
  26.8 1.4 %collective-permute-start.10 = (bf16[272,256]{1,0:T(8,128)(2,1)S(1)}, bf16[272,256]{1,0:T(8,128)(2,1)S(1)}, u32[]{:S(2)}, u32[]{:S(2)}) collective-permute-start(bf16[272,256]{1,0:T(8,128)(2,1)S(1)} %copy-done.6), channel_id=1, source_target_pairs={{0,16},{1,17},{8,24},{9,25},{16,0},{17,1},{24,8},{25,9},{2,18},{3,... | collective-permute-start | bytes 417800 | tf_op jit(solution)/shard_map/ppermute | solution.py:239
  28.3 2.0 %local_backward.1 = (bf16[128,2048]{1,0:T(8,128)(2,1)S(1)}, bf16[128,2048]{1,0:T(8,128)(2,1)S(1)}) custom-call(bf16[128,2048]{1,0:T(8,128)(2,1)S(1)} %copy-done.2, bf16[128,2048]{1,0:T(8,128)(2,1)S(1)} %copy-done.3, bf16[128,2048]{1,0:T(8,128)(2,1)S(1)} %copy-done, f32[1,2048]{1,0:T(1,128)S(1)} %bitcast.3, f32[128,2048]{1,0:T(8,128)S(1)} %get-tuple-element.48.out_ref, ...), custom_call_target="tpu_custom_call" | custom-call | flops 134217728 | bytes 4194304 | tf_op jit(solution)/shard_map/local_backward/pallas_call | solution.py:339
  30.3 2.5 %collective-permute-done.6.refs_11_ = bf16[2,2,128,256]{3,2,1,0:T(8,128)(2,1)S(1)} collective-permute-done((bf16[2,2,128,256]{3,2,1,0:T(8,128)(2,1)S(1)}, bf16[2,2,128,256]{3,2,1,0:T(8,128)(2,1)S(1)}, u32[]{:S(2)}, u32[]{:S(2)}) %collective-permute-start.6) | collective-permute-done | bytes 262176 | tf_op jit(solution)/shard_map/ppermute | solution.py:239
  32.8 0.7 %collective-permute-done.9.refs_3_ = bf16[272,256]{1,0:T(8,128)(2,1)S(1)} collective-permute-done((bf16[272,256]{1,0:T(8,128)(2,1)S(1)}, bf16[272,256]{1,0:T(8,128)(2,1)S(1)}, u32[]{:S(2)}, u32[]{:S(2)}) %collective-permute-start.9) | collective-permute-done | bytes 139296 | tf_op jit(solution)/shard_map/ppermute | solution.py:239
  33.6 7.0 %memory_attention.1 = (bf16[256,256]{1,0:T(8,128)(2,1)S(1)}, bf16[256,256]{1,0:T(8,128)(2,1)S(1)}, bf16[2,256,256]{2,1,0:T(8,128)(2,1)S(1)}, bf16[2,256,256]{2,1...) custom-call(f32[1,2048]{1,0:T(1,128)S(1)} %bitcast.4, f32[16,128]{1,0:T(8,128)S(1)} %bitcast.5, ...), custom_call_target="tpu_custom_call" | custom-call | flops 2147483648 | bytes 2621440 | tf_op jit(solution)/shard_map/memory_attention/pallas_call | solution.py:359
  40.6 2.0 %collective-permute-start.20 = (f32[16,128]{1,0:T(8,128)S(1)}, f32[16,128]{1,0:T(8,128)S(1)}, u32[]{:S(2)}, u32[]{:S(2)}) collective-permute-start(f32[16,128]{1,0:T(8,128)S(1)} %get-tuple-element.76), channel_id=1, source_target_pairs={{0,6},{2,4},{4,2},{6,0},{1,7},{3,5},{5,3},{7,1},{8,14},{10,12},{12... | collective-permute-start | bytes 24584 | tf_op jit(solution)/shard_map/ppermute | solution.py:239
  42.6 1.5 %collective-permute-start.12 = (bf16[2,256,256]{2,1,0:T(8,128)(2,1)S(1)}, bf16[2,256,256]{2,1,0:T(8,128)(2,1)S(1)}, u32[]{:S(2)}, u32[]{:S(2)}) collective-permute-start(bf16[2,256,256]{2,1,0:T(8,128)(2,1)S(1)} %get-tuple-element.69), channel_id=1, source_target_pairs={{0,8},{1,9},{8,0},{9,1},{16,24},{17,25},{24,16},{25,17},{2,10},{3,... | collective-permute-start | bytes 786440 | tf_op jit(solution)/shard_map/ppermute | solution.py:239
  44.1 1.5 %collective-permute-start.14 = (bf16[2,256,256]{2,1,0:T(8,128)(2,1)S(1)}, bf16[2,256,256]{2,1,0:T(8,128)(2,1)S(1)}, u32[]{:S(2)}, u32[]{:S(2)}) collective-permute-start(bf16[2,256,256]{2,1,0:T(8,128)(2,1)S(1)} %get-tuple-element.72), channel_id=1, source_target_pairs={{0,16},{1,17},{8,24},{9,25},{16,0},{17,1},{24,8},{25,9},{2,18},{3,... | collective-permute-start | bytes 786440 | tf_op jit(solution)/shard_map/ppermute | solution.py:239
  46.1 1.1 %collective-permute-start.19 = (f32[16,128]{1,0:T(8,128)S(1)}, f32[16,128]{1,0:T(8,128)S(1)}, u32[]{:S(2)}, u32[]{:S(2)}) collective-permute-start(f32[16,128]{1,0:T(8,128)S(1)} %get-tuple-element.76), channel_id=1, source_target_pairs={{0,4},{2,6},{4,0},{6,2},{1,5},{3,7},{5,1},{7,3},{8,12},{10,14},{12... | collective-permute-start | bytes 24584 | tf_op jit(solution)/shard_map/ppermute | solution.py:239
  47.2 1.4 %collective-permute-start.18 = (f32[16,128]{1,0:T(8,128)S(1)}, f32[16,128]{1,0:T(8,128)S(1)}, u32[]{:S(2)}, u32[]{:S(2)}) collective-permute-start(f32[16,128]{1,0:T(8,128)S(1)} %get-tuple-element.76), channel_id=1, source_target_pairs={{0,2},{2,0},{4,6},{6,4},{1,3},{3,1},{5,7},{7,5},{8,10},{10,8},{12,... | collective-permute-start | bytes 24584 | tf_op jit(solution)/shard_map/ppermute | solution.py:239
  48.5 2.1 %collective-permute-done.19 = f32[16,128]{1,0:T(8,128)S(1)} collective-permute-done((f32[16,128]{1,0:T(8,128)S(1)}, f32[16,128]{1,0:T(8,128)S(1)}, u32[]{:S(2)}, u32[]{:S(2)}) %collective-permute-start.19) | collective-permute-done | bytes 8224 | tf_op jit(solution)/shard_map/ppermute | solution.py:239
  51.2 0.8 %collective-permute-done.21 = f32[16,128]{1,0:T(8,128)S(1)} collective-permute-done((f32[16,128]{1,0:T(8,128)S(1)}, f32[16,128]{1,0:T(8,128)S(1)}, u32[]{:S(2)}, u32[]{:S(2)}) %collective-permute-start.21) | collective-permute-done | bytes 8224 | tf_op jit(solution)/shard_map/ppermute | solution.py:239
  52.0 1.5 %collective-permute-start.22 = (f32[16,128]{1,0:T(8,128)S(1)}, f32[16,128]{1,0:T(8,128)S(1)}, u32[]{:S(2)}, u32[]{:S(2)}) collective-permute-start(f32[16,128]{1,0:T(8,128)S(1)} %add.25), channel_id=1, source_target_pairs={{0,8},{1,9},{8,0},{9,1},{16,24},{17,25},{24,16},{25,17},{2,10},{3,... | collective-permute-start | bytes 24584 | tf_op jit(solution)/shard_map/ppermute | solution.py:239
  53.5 3.1 %collective-permute-done.22 = f32[16,128]{1,0:T(8,128)S(1)} collective-permute-done((f32[16,128]{1,0:T(8,128)S(1)}, f32[16,128]{1,0:T(8,128)S(1)}, u32[]{:S(2)}, u32[]{:S(2)}) %collective-permute-start.22) | collective-permute-done | bytes 8224 | tf_op jit(solution)/shard_map/ppermute | solution.py:239
  56.6 1.5 %collective-permute-start.23 = (f32[16,128]{1,0:T(8,128)S(1)}, f32[16,128]{1,0:T(8,128)S(1)}, u32[]{:S(2)}, u32[]{:S(2)}) collective-permute-start(f32[16,128]{1,0:T(8,128)S(1)} %add.26), channel_id=1, source_target_pairs={{0,16},{1,17},{8,24},{9,25},{16,0},{17,1},{24,8},{25,9},{2,18},{3,... | collective-permute-start | bytes 24584 | tf_op jit(solution)/shard_map/ppermute | solution.py:239
  58.2 0.5 collective-permute-start.15
  58.8 1.5 %collective-permute-done.23 = f32[16,128]{1,0:T(8,128)S(1)} collective-permute-done((f32[16,128]{1,0:T(8,128)S(1)}, f32[16,128]{1,0:T(8,128)S(1)}, u32[]{:S(2)}, u32[]{:S(2)}) %collective-permute-start.23) | collective-permute-done | bytes 8224 | tf_op jit(solution)/shard_map/ppermute | solution.py:239
  60.4 0.5 multiply_multiply_fusion
  60.9 1.3 %merge.1 = (bf16[128,2048]{1,0:T(8,128)(2,1)}, bf16[128,2048]{1,0:T(8,128)(2,1)}) custom-call(bf16[128,2048]{1,0:T(8,128)(2,1)S(1)} %get-tuple-element.52.lo_ref, bf16[128,2048]{1,0:T(8,128)(2,1)S(1)} %get-tuple-element.53.ldq_ref, bf16[256,256]{1,0:T(8,128)(2,1)S(1)} %get-tuple-element.67.refs_0_, bf16[256,256]{1,0:T(8,128)(2,1)S(1)} %collective-permute-done.11.refs_1_, ...), custom_call_target="tpu_custom_call" | custom-call | tf_op jit(solution)/shard_map/merge/pallas_call | solution.py:385
  (52 shorter events, 1.7 us)
Async XLA Ops:
  0.6 15.7 %copy-start.1 = (bf16[128,2048]{1,0:T(8,128)(2,1)S(1)}, bf16[128,2048]{1,0:T(8,128)(2,1)}, u32[]{:S(2)}) copy-start(bf16[128,2048]{1,0:T(8,128)(2,1)} %q_ref.1) | copy-start | bytes 1572868
  0.6 15.6 %copy-start.2 = (bf16[128,2048]{1,0:T(8,128)(2,1)S(1)}, bf16[128,2048]{1,0:T(8,128)(2,1)}, u32[]{:S(2)}) copy-start(bf16[128,2048]{1,0:T(8,128)(2,1)} %k_ref.3) | copy-start | bytes 1572868
  0.7 15.6 %copy-start.3 = (bf16[128,2048]{1,0:T(8,128)(2,1)S(1)}, bf16[128,2048]{1,0:T(8,128)(2,1)}, u32[]{:S(2)}) copy-start(bf16[128,2048]{1,0:T(8,128)(2,1)} %v_ref.3) | copy-start | bytes 1572868
  4.1 12.2 %copy-start = (bf16[128,2048]{1,0:T(8,128)(2,1)S(1)}, bf16[128,2048]{1,0:T(8,128)(2,1)}, u32[]{:S(2)}) copy-start(bf16[128,2048]{1,0:T(8,128)(2,1)} %g_ref.3) | copy-start | bytes 1572868
  4.1 1.7 %collective-permute-start = (bf16[2,128,256]{2,1,0:T(8,128)(2,1)}, bf16[2,128,256]{2,1,0:T(8,128)(2,1)S(1)}, u32[]{:S(2)}, u32[]{:S(2)}) collective-permute-start(bf16[2,128,256]{2,1,0:T(8,128)(2,1)} %get-tuple-element.41), channel_id=1, source_target_pairs={{0,1},{1,0},{2,3},{3,2},{4,5},{5,4},{6,7},{7,6},{8,9},{9,8},{10,11... | collective-permute-start | bytes 393224 | tf_op jit(solution)/shard_map/ppermute | solution.py:239
  6.7 17.7 %collective-permute-start.2 = (bf16[2,2,128,256]{3,2,1,0:T(8,128)(2,1)S(1)}, bf16[2,2,128,256]{3,2,1,0:T(8,128)(2,1)S(1)}, u32[]{:S(2)}, u32[]{:S(2)}) collective-permute-start(bf16[2,2,128,256]{3,2,1,0:T(8,128)(2,1)S(1)} %join_cores.1.refs_8_), channel_id=1, source_target_pairs={{0,2},{2,0},{4,6},{6,4},{1,3},{3,1},{5,7},{7,5},{8,10},{10,8},{12,... | collective-permute-start | bytes 786440 | tf_op jit(solution)/shard_map/ppermute | solution.py:239
  9.7 14.7 %collective-permute-start.1 = (bf16[2,2,128,256]{3,2,1,0:T(8,128)(2,1)S(1)}, bf16[2,2,128,256]{3,2,1,0:T(8,128)(2,1)S(1)}, u32[]{:S(2)}, u32[]{:S(2)}) collective-permute-start(bf16[2,2,128,256]{3,2,1,0:T(8,128)(2,1)S(1)} %join_cores.1.refs_8_), channel_id=1, source_target_pairs={{0,4},{2,6},{4,0},{6,2},{1,5},{3,7},{5,1},{7,3},{8,12},{10,14},{12... | collective-permute-start | bytes 786440 | tf_op jit(solution)/shard_map/ppermute | solution.py:239
  12.3 12.1 %collective-permute-start.3 = (bf16[272,256]{1,0:T(8,128)(2,1)}, bf16[272,256]{1,0:T(8,128)(2,1)S(1)}, u32[]{:S(2)}, u32[]{:S(2)}) collective-permute-start(bf16[272,256]{1,0:T(8,128)(2,1)} %get-tuple-element.42), channel_id=1, source_target_pairs={{0,17},{1,16},{8,25},{9,24},{16,1},{17,0},{24,9},{25,8},{2,19},{3,... | collective-permute-start | bytes 417800 | tf_op jit(solution)/shard_map/ppermute | solution.py:239
  13.0 11.4 %collective-permute-start.4 = (bf16[272,256]{1,0:T(8,128)(2,1)}, bf16[272,256]{1,0:T(8,128)(2,1)S(1)}, u32[]{:S(2)}, u32[]{:S(2)}) collective-permute-start(bf16[272,256]{1,0:T(8,128)(2,1)} %get-tuple-element.43), channel_id=1, source_target_pairs={{0,24},{1,25},{8,16},{9,17},{16,8},{17,9},{24,0},{25,1},{2,26},{3,... | collective-permute-start | bytes 417800 | tf_op jit(solution)/shard_map/ppermute | solution.py:239
  14.8 10.2 %copy-start.9 = (bf16[272,256]{1,0:T(8,128)(2,1)S(1)}, bf16[272,256]{1,0:T(8,128)(2,1)}, u32[]{:S(2)}) copy-start(bf16[272,256]{1,0:T(8,128)(2,1)} %get-tuple-element.56) | copy-start | bytes 417796
  14.8 10.2 %copy-start.8 = (bf16[272,256]{1,0:T(8,128)(2,1)S(1)}, bf16[272,256]{1,0:T(8,128)(2,1)}, u32[]{:S(2)}) copy-start(bf16[272,256]{1,0:T(8,128)(2,1)} %get-tuple-element.57) | copy-start | bytes 417796
  14.8 11.7 %copy-start.7 = (bf16[272,256]{1,0:T(8,128)(2,1)S(1)}, bf16[272,256]{1,0:T(8,128)(2,1)}, u32[]{:S(2)}) copy-start(bf16[272,256]{1,0:T(8,128)(2,1)} %get-tuple-element.58) | copy-start | bytes 417796
  14.8 12.0 %copy-start.6 = (bf16[272,256]{1,0:T(8,128)(2,1)S(1)}, bf16[272,256]{1,0:T(8,128)(2,1)}, u32[]{:S(2)}) copy-start(bf16[272,256]{1,0:T(8,128)(2,1)} %get-tuple-element.59) | copy-start | bytes 417796
  14.8 9.6 %collective-permute-start.5 = (bf16[272,256]{1,0:T(8,128)(2,1)}, bf16[272,256]{1,0:T(8,128)(2,1)S(1)}, u32[]{:S(2)}, u32[]{:S(2)}) collective-permute-start(bf16[272,256]{1,0:T(8,128)(2,1)} %get-tuple-element.44), channel_id=1, source_target_pairs={{0,25},{1,24},{8,17},{9,16},{16,9},{17,8},{24,1},{25,0},{2,27},{3,... | collective-permute-start | bytes 417800 | tf_op jit(solution)/shard_map/ppermute | solution.py:239
  24.4 8.4 %collective-permute-start.6 = (bf16[2,2,128,256]{3,2,1,0:T(8,128)(2,1)S(1)}, bf16[2,2,128,256]{3,2,1,0:T(8,128)(2,1)S(1)}, u32[]{:S(2)}, u32[]{:S(2)}) collective-permute-start(bf16[2,2,128,256]{3,2,1,0:T(8,128)(2,1)S(1)} %collective-permute-done.1.refs_10_), channel_id=1, source_target_pairs={{0,2},{2,0},{4,6},{6,4},{1,3},{3,1},{5,7},{7,5},{8,10},{10,8},{12,... | collective-permute-start | bytes 786440 | tf_op jit(solution)/shard_map/ppermute | solution.py:239
  24.9 7.9 %collective-permute-start.7 = (bf16[272,256]{1,0:T(8,128)(2,1)S(1)}, bf16[272,256]{1,0:T(8,128)(2,1)S(1)}, u32[]{:S(2)}, u32[]{:S(2)}) collective-permute-start(bf16[272,256]{1,0:T(8,128)(2,1)S(1)} %copy-done.9), channel_id=1, source_target_pairs={{0,1},{1,0},{8,9},{9,8},{16,17},{17,16},{24,25},{25,24},{2,3},{3,2... | collective-permute-start | bytes 417800 | tf_op jit(solution)/shard_map/ppermute | solution.py:239
  25.0 7.9 %collective-permute-start.8 = (bf16[272,256]{1,0:T(8,128)(2,1)S(1)}, bf16[272,256]{1,0:T(8,128)(2,1)S(1)}, u32[]{:S(2)}, u32[]{:S(2)}) collective-permute-start(bf16[272,256]{1,0:T(8,128)(2,1)S(1)} %copy-done.8), channel_id=1, source_target_pairs={{0,8},{1,9},{8,0},{9,1},{16,24},{17,25},{24,16},{25,17},{2,10},{3,... | collective-permute-start | bytes 417800 | tf_op jit(solution)/shard_map/ppermute | solution.py:239
  26.5 7.0 %collective-permute-start.9 = (bf16[272,256]{1,0:T(8,128)(2,1)S(1)}, bf16[272,256]{1,0:T(8,128)(2,1)S(1)}, u32[]{:S(2)}, u32[]{:S(2)}) collective-permute-start(bf16[272,256]{1,0:T(8,128)(2,1)S(1)} %copy-done.7), channel_id=1, source_target_pairs={{0,9},{1,8},{8,1},{9,0},{16,25},{17,24},{24,17},{25,16},{2,11},{3,... | collective-permute-start | bytes 417800 | tf_op jit(solution)/shard_map/ppermute | solution.py:239
  26.8 6.7 %collective-permute-start.10 = (bf16[272,256]{1,0:T(8,128)(2,1)S(1)}, bf16[272,256]{1,0:T(8,128)(2,1)S(1)}, u32[]{:S(2)}, u32[]{:S(2)}) collective-permute-start(bf16[272,256]{1,0:T(8,128)(2,1)S(1)} %copy-done.6), channel_id=1, source_target_pairs={{0,16},{1,17},{8,24},{9,25},{16,0},{17,1},{24,8},{25,9},{2,18},{3,... | collective-permute-start | bytes 417800 | tf_op jit(solution)/shard_map/ppermute | solution.py:239
  40.6 6.6 %collective-permute-start.20 = (f32[16,128]{1,0:T(8,128)S(1)}, f32[16,128]{1,0:T(8,128)S(1)}, u32[]{:S(2)}, u32[]{:S(2)}) collective-permute-start(f32[16,128]{1,0:T(8,128)S(1)} %get-tuple-element.76), channel_id=1, source_target_pairs={{0,6},{2,4},{4,2},{6,0},{1,7},{3,5},{5,3},{7,1},{8,14},{10,12},{12... | collective-permute-start | bytes 24584 | tf_op jit(solution)/shard_map/ppermute | solution.py:239
  42.6 15.6 %collective-permute-start.12 = (bf16[2,256,256]{2,1,0:T(8,128)(2,1)S(1)}, bf16[2,256,256]{2,1,0:T(8,128)(2,1)S(1)}, u32[]{:S(2)}, u32[]{:S(2)}) collective-permute-start(bf16[2,256,256]{2,1,0:T(8,128)(2,1)S(1)} %get-tuple-element.69), channel_id=1, source_target_pairs={{0,8},{1,9},{8,0},{9,1},{16,24},{17,25},{24,16},{25,17},{2,10},{3,... | collective-permute-start | bytes 786440 | tf_op jit(solution)/shard_map/ppermute | solution.py:239
  44.1 14.1 %collective-permute-start.14 = (bf16[2,256,256]{2,1,0:T(8,128)(2,1)S(1)}, bf16[2,256,256]{2,1,0:T(8,128)(2,1)S(1)}, u32[]{:S(2)}, u32[]{:S(2)}) collective-permute-start(bf16[2,256,256]{2,1,0:T(8,128)(2,1)S(1)} %get-tuple-element.72), channel_id=1, source_target_pairs={{0,16},{1,17},{8,24},{9,25},{16,0},{17,1},{24,8},{25,9},{2,18},{3,... | collective-permute-start | bytes 786440 | tf_op jit(solution)/shard_map/ppermute | solution.py:239
  45.6 13.1 %collective-permute-start.16 = (bf16[2,256,256]{2,1,0:T(8,128)(2,1)S(1)}, bf16[2,256,256]{2,1,0:T(8,128)(2,1)S(1)}, u32[]{:S(2)}, u32[]{:S(2)}) collective-permute-start(bf16[2,256,256]{2,1,0:T(8,128)(2,1)S(1)} %get-tuple-element.73), channel_id=1, source_target_pairs={{0,24},{1,25},{8,16},{9,17},{16,8},{17,9},{24,0},{25,1},{2,26},{3,... | collective-permute-start | bytes 786440 | tf_op jit(solution)/shard_map/ppermute | solution.py:239
  46.1 4.5 %collective-permute-start.19 = (f32[16,128]{1,0:T(8,128)S(1)}, f32[16,128]{1,0:T(8,128)S(1)}, u32[]{:S(2)}, u32[]{:S(2)}) collective-permute-start(f32[16,128]{1,0:T(8,128)S(1)} %get-tuple-element.76), channel_id=1, source_target_pairs={{0,4},{2,6},{4,0},{6,2},{1,5},{3,7},{5,1},{7,3},{8,12},{10,14},{12... | collective-permute-start | bytes 24584 | tf_op jit(solution)/shard_map/ppermute | solution.py:239
  47.2 3.7 %collective-permute-start.18 = (f32[16,128]{1,0:T(8,128)S(1)}, f32[16,128]{1,0:T(8,128)S(1)}, u32[]{:S(2)}, u32[]{:S(2)}) collective-permute-start(f32[16,128]{1,0:T(8,128)S(1)} %get-tuple-element.76), channel_id=1, source_target_pairs={{0,2},{2,0},{4,6},{6,4},{1,3},{3,1},{5,7},{7,5},{8,10},{10,8},{12,... | collective-permute-start | bytes 24584 | tf_op jit(solution)/shard_map/ppermute | solution.py:239
  50.6 7.5 %collective-permute-start.11 = (bf16[256,256]{1,0:T(8,128)(2,1)S(1)}, bf16[256,256]{1,0:T(8,128)(2,1)S(1)}, u32[]{:S(2)}, u32[]{:S(2)}) collective-permute-start(bf16[256,256]{1,0:T(8,128)(2,1)S(1)} %get-tuple-element.68), channel_id=1, source_target_pairs={{0,1},{1,0},{8,9},{9,8},{16,17},{17,16},{24,25},{25,24},{2,3},{3,2... | collective-permute-start | bytes 393224 | tf_op jit(solution)/shard_map/ppermute | solution.py:239
  50.8 1.2 %collective-permute-start.21 = (f32[16,128]{1,0:T(8,128)S(1)}, f32[16,128]{1,0:T(8,128)S(1)}, u32[]{:S(2)}, u32[]{:S(2)}) collective-permute-start(f32[16,128]{1,0:T(8,128)S(1)} %add_add_fusion), channel_id=1, source_target_pairs={{0,1},{1,0},{8,9},{9,8},{16,17},{17,16},{24,25},{25,24},{2,3},{3,2... | collective-permute-start | bytes 24584 | tf_op jit(solution)/shard_map/ppermute | solution.py:239
  52.0 4.6 %collective-permute-start.22 = (f32[16,128]{1,0:T(8,128)S(1)}, f32[16,128]{1,0:T(8,128)S(1)}, u32[]{:S(2)}, u32[]{:S(2)}) collective-permute-start(f32[16,128]{1,0:T(8,128)S(1)} %add.25), channel_id=1, source_target_pairs={{0,8},{1,9},{8,0},{9,1},{16,24},{17,25},{24,16},{25,17},{2,10},{3,... | collective-permute-start | bytes 24584 | tf_op jit(solution)/shard_map/ppermute | solution.py:239
  56.6 3.7 %collective-permute-start.23 = (f32[16,128]{1,0:T(8,128)S(1)}, f32[16,128]{1,0:T(8,128)S(1)}, u32[]{:S(2)}, u32[]{:S(2)}) collective-permute-start(f32[16,128]{1,0:T(8,128)S(1)} %add.26), channel_id=1, source_target_pairs={{0,16},{1,17},{8,24},{9,25},{16,0},{17,1},{24,8},{25,9},{2,18},{3,... | collective-permute-start | bytes 24584 | tf_op jit(solution)/shard_map/ppermute | solution.py:239
  58.2 2.8 %collective-permute-start.13 = (bf16[2,256,256]{2,1,0:T(8,128)(2,1)S(1)}, bf16[2,256,256]{2,1,0:T(8,128)(2,1)S(1)}, u32[]{:S(2)}, u32[]{:S(2)}) collective-permute-start(bf16[2,256,256]{2,1,0:T(8,128)(2,1)S(1)} %collective-permute-done.12.refs_2_), channel_id=1, source_target_pairs={{0,1},{1,0},{8,9},{9,8},{16,17},{17,16},{24,25},{25,24},{2,3},{3,2... | collective-permute-start | bytes 786440 | tf_op jit(solution)/shard_map/ppermute | solution.py:239
  58.2 2.8 %collective-permute-start.15 = (bf16[2,256,256]{2,1,0:T(8,128)(2,1)S(1)}, bf16[2,256,256]{2,1,0:T(8,128)(2,1)S(1)}, u32[]{:S(2)}, u32[]{:S(2)}) collective-permute-start(bf16[2,256,256]{2,1,0:T(8,128)(2,1)S(1)} %collective-permute-done.14.refs_4_), channel_id=1, source_target_pairs={{0,1},{1,0},{8,9},{9,8},{16,17},{17,16},{24,25},{25,24},{2,3},{3,2... | collective-permute-start | bytes 786440 | tf_op jit(solution)/shard_map/ppermute | solution.py:239
  58.7 2.3 %collective-permute-start.17 = (bf16[2,256,256]{2,1,0:T(8,128)(2,1)S(1)}, bf16[2,256,256]{2,1,0:T(8,128)(2,1)S(1)}, u32[]{:S(2)}, u32[]{:S(2)}) collective-permute-start(bf16[2,256,256]{2,1,0:T(8,128)(2,1)S(1)} %collective-permute-done.16.refs_6_), channel_id=1, source_target_pairs={{0,1},{1,0},{8,9},{9,8},{16,17},{17,16},{24,25},{25,24},{2,3},{3,2... | collective-permute-start | bytes 786440 | tf_op jit(solution)/shard_map/ppermute | solution.py:239
  (3 other events, 7.9 us)
